TPU v7x, 128 devices: a whole 4x4x4 slice. The times are simulated.
128 devices in a mesh: blk: 32 (over y, x, z_lo), rep: 4 (over z_hi, core).
Axes of the slice: x: 4, y: 4, z: 4 (z_hi: 2, z_lo: 2; z = z_hi * 2 + z_lo), core: 2. Of those that a mesh axis runs over, the one named last changes fastest.
Arguments:
- features: bfloat16 [32768, 256], P('blk'), may hold values from -6 to 6
- tiles: bfloat16 [256, 32, 6, 128, 128], P('blk', 'rep'), may hold values from -0.375 to 0.375
- tile_cols: int32 [256, 32, 6], P('blk', 'rep'), may hold values from 0 to 7
- counts: int32 [256, 32], P('blk', 'rep'), may hold values from 0 to 6
- degree: int32 [32768], P('blk'), may hold values from 1 to 16
- train_mask: int32 [32768], P('blk'), may hold values 0 or 1
- cotangent: bfloat16 [32768, 256], P('blk'), may hold values from -6 to 6
- w_self: bfloat16 [256, 256], replicated, may hold values from -0.375 to 0.375
- w_neigh: bfloat16 [256, 256], replicated, may hold values from -0.375 to 0.375
- bias_term: float32 [256], replicated, may hold values from -3 to 3
Outputs:
- activation: bfloat16 [32768, 256], P(('blk', 'rep'))
- grad_features: bfloat16 [32768, 256], P(('blk', 'rep'))
- grad_self: float32 [256, 256], replicated
- grad_neigh: float32 [256, 256], replicated
- grad_bias: float32 [256], replicated
Inputs may be any that keep to these rules, and one draw needn't show every extreme that they name: `tile_cols`: a column block index inside the owner's 8 blocks. `counts`: tiles at positions of count or more are ignored.
All inputs are finite; a program needn't handle non-finite values. No bound on the sum of `train_mask` on one device may be relied on, other than what follows from the above.
Results may differ from a plain program's by a relative error of at most 0.0075.
Values may be sent and summed in bfloat16 or wider, within the bound.
No kernel may reach another device: no remote copies, remote signals or barrier semaphores. Data moves between devices by JAX's collectives and lax.ppermute only.
A program may use at most 128 MiB of HBM per device.

v0:
```python
import jax
import jax.numpy as jnp
from jax import lax
from jax.sharding import PartitionSpec as P


def passed_along(value, axis, by):
    size = lax.axis_size(axis)
    return lax.ppermute(value, axis, [(i, (i + by) % size) for i in range(size)])


def dense_rows(own_rows, aggregate, cot_rows, mask_rows, w_self, w_neigh, bias_term):
    pre_act = (
        jnp.dot(own_rows, w_self, preferred_element_type=jnp.float32)
        + jnp.dot(aggregate, w_neigh, preferred_element_type=jnp.float32)
        + bias_term
    )
    sigm = jax.nn.sigmoid(pre_act)
    activation = (pre_act * sigm).astype(jnp.bfloat16)
    slope = sigm * (1.0 + pre_act * (1.0 - sigm))
    grad_pre = (
        mask_rows.astype(jnp.float32)[:, None] * cot_rows.astype(jnp.float32) * slope
    ).astype(jnp.bfloat16)
    return (activation, grad_pre)


def shards(
    features, tiles, tile_cols, counts, degree, train_mask, cotangent, w_self, w_neigh, bias_term
):
    rows_dev, feat_width = features.shape
    nblocks, cycle_span, slot_count, bsize, _ = tiles.shape
    rep_count = lax.axis_size("rep")
    quarter = rows_dev // rep_count
    rep_index = lax.axis_index("rep")
    rep_bits = rep_count.bit_length() - 1
    row_start = rep_index * quarter
    slot_ids = jnp.arange(slot_count, dtype=jnp.int32)
    block_ids = jnp.arange(nblocks, dtype=jnp.int32)

    def live_of(distance):
        return slot_ids[None, :] < counts[:, distance][:, None]

    def gather_part(shard, distance):
        shard_blocks = shard.reshape(nblocks, bsize, feat_width)
        picked = jnp.take(shard_blocks, tile_cols[:, distance], axis=0)
        picked = jnp.where(live_of(distance)[:, :, None, None], picked, jnp.zeros((), jnp.bfloat16))
        summed = jnp.einsum(
            "bsij,bsjf->bif", tiles[:, distance], picked, preferred_element_type=jnp.float32
        )
        return summed.reshape(rows_dev, feat_width)

    current = features
    for bit_pos in range(rep_bits):
        moved = passed_along(current, "blk", cycle_span << bit_pos)
        current = jnp.where(rep_index >> bit_pos & 1 == 1, moved, current)
    partial_value = gather_part(current, 0)
    for distance in range(1, cycle_span):
        current = passed_along(current, "blk", 1)
        partial_value = partial_value + gather_part(current, distance)
    inv_degree = 1.0 / degree.astype(jnp.float32)
    own_rows = lax.dynamic_slice_in_dim(features, row_start, quarter, 0)
    cot_rows = lax.dynamic_slice_in_dim(cotangent, row_start, quarter, 0)
    mask_rows = lax.dynamic_slice_in_dim(train_mask, row_start, quarter, 0)
    scale_rows = lax.dynamic_slice_in_dim(inv_degree, row_start, quarter, 0)
    agg_sum = lax.psum_scatter(partial_value, "rep", scatter_dimension=0, tiled=True)
    aggregate = (agg_sum * scale_rows[:, None]).astype(jnp.bfloat16)
    activation, grad_pre = dense_rows(
        own_rows, aggregate, cot_rows, mask_rows, w_self, w_neigh, bias_term
    )
    back_part = (
        jnp.dot(grad_pre, w_neigh.T, preferred_element_type=jnp.float32) * scale_rows[:, None]
    ).astype(jnp.bfloat16)
    back_msg = lax.all_gather(back_part, "rep", axis=0, tiled=True)
    local_self = jnp.einsum("nf,ng->fg", own_rows, grad_pre, preferred_element_type=jnp.float32)
    local_neigh = jnp.einsum("nf,ng->fg", aggregate, grad_pre, preferred_element_type=jnp.float32)
    local_bias = jnp.sum(grad_pre.astype(jnp.float32), axis=0)
    grad_self, grad_neigh, grad_bias = lax.psum(
        (local_self, local_neigh, local_bias), ("blk", "rep")
    )
    norm_factor = 1.0 / jnp.sqrt(jnp.float32(rows_dev * lax.axis_size("blk")))
    grad_self = grad_self * norm_factor
    grad_neigh = grad_neigh * norm_factor
    grad_bias = grad_bias * norm_factor
    back_blocks = back_msg.reshape(nblocks, bsize, feat_width)

    def spread_part(distance):
        onehot = (
            (tile_cols[:, distance][:, :, None] == block_ids[None, None, :])
            & live_of(distance)[:, :, None]
        ).astype(jnp.float32)
        products = jnp.einsum(
            "bsji,bjf->bsif", tiles[:, distance], back_blocks, preferred_element_type=jnp.float32
        )
        placed = jnp.einsum("bsc,bsif->cif", onehot, products, precision=lax.Precision.HIGHEST)
        return placed.reshape(rows_dev, feat_width)

    zero_rows = jnp.zeros((rows_dev, feat_width), jnp.float32)
    carried = zero_rows
    for distance in range(cycle_span - 1, 0, -1):
        carried = passed_along(carried + spread_part(distance), "blk", -1)
    carried = carried + spread_part(0)
    for bit_pos in range(rep_bits):
        moved = passed_along(carried, "blk", -(cycle_span << bit_pos))
        carried = jnp.where(rep_index >> bit_pos & 1 == 1, moved, carried)
    spread = lax.psum_scatter(carried, "rep", scatter_dimension=0, tiled=True)
    own_term = jnp.dot(grad_pre, w_self.T, preferred_element_type=jnp.float32)
    grad_features = (own_term + spread).astype(jnp.bfloat16)
    return (activation, grad_features, grad_self, grad_neigh, grad_bias)


def solution(mesh):
    return jax.shard_map(
        shards,
        mesh=mesh,
        in_specs=(
            P("blk", None),
            P("blk", "rep", None, None, None),
            P("blk", "rep", None),
            P("blk", "rep"),
            P("blk"),
            P("blk"),
            P("blk", None),
            P(),
            P(),
            P(),
        ),
        out_specs=(P(("blk", "rep"), None), P(("blk", "rep"), None), P(), P(), P()),
        check_vma=False,
    )
```

profile of v0, /device:TPU:1, one launch (start us, length us, event | category | flops | bytes accessed | tf_op | source)
XLA Modules:
  0.0 638.7 jit_solution(9774339680790928754)
XLA Ops:
  14.6 8.0 %collective-permute-done = bf16[1024,256]{1,0:T(8,128)(2,1)S(1)} collective-permute-done((bf16[1024,256]{1,0:T(8,128)(2,1)}, bf16[1024,256]{1,0:T(8,128)(2,1)S(1)}, u32[]{:S(2)}, u32[]{:S(2)}) %collective-permute-start) | collective-permute-done | bytes 524320 | tf_op jit(solution)/shard_map/ppermute | solution.py:9
  24.2 11.0 %collective-permute-done.1 = bf16[1024,256]{1,0:T(8,128)(2,1)S(1)} collective-permute-done((bf16[1024,256]{1,0:T(8,128)(2,1)S(1)}, bf16[1024,256]{1,0:T(8,128)(2,1)S(1)}, u32[]{:S(2)}, u32[]{:S(2)}) %collective-permute-start.1) | collective-permute-done | bytes 524320 | tf_op jit(solution)/shard_map/ppermute | solution.py:9
  36.8 2.5 gather_fusion
  39.3 10.3 %collective-permute-done.2 = bf16[1024,256]{1,0:T(8,128)(2,1)S(1)} collective-permute-done((bf16[1024,256]{1,0:T(8,128)(2,1)S(1)}, bf16[1024,256]{1,0:T(8,128)(2,1)S(1)}, u32[]{:S(2)}, u32[]{:S(2)}) %collective-permute-start.2) | collective-permute-done | bytes 524320 | tf_op jit(solution)/shard_map/ppermute | solution.py:9
  49.6 2.5 gather_fusion.1
  52.2 3.3 fusion.99
  57.9 11.0 %collective-permute-done.3 = bf16[1024,256]{1,0:T(8,128)(2,1)S(1)} collective-permute-done((bf16[1024,256]{1,0:T(8,128)(2,1)S(1)}, bf16[1024,256]{1,0:T(8,128)(2,1)S(1)}, u32[]{:S(2)}, u32[]{:S(2)}) %collective-permute-start.3) | collective-permute-done | bytes 524320 | tf_op jit(solution)/shard_map/ppermute | solution.py:9
  68.9 2.5 gather_fusion.2
  71.5 4.2 fusion.159
  75.7 8.0 %collective-permute-done.4 = bf16[1024,256]{1,0:T(8,128)(2,1)S(1)} collective-permute-done((bf16[1024,256]{1,0:T(8,128)(2,1)S(1)}, bf16[1024,256]{1,0:T(8,128)(2,1)S(1)}, u32[]{:S(2)}, u32[]{:S(2)}) %collective-permute-start.4) | collective-permute-done | bytes 524320 | tf_op jit(solution)/shard_map/ppermute | solution.py:9
  83.7 2.5 gather_fusion.3
  86.2 4.2 fusion.156
  90.4 8.0 %collective-permute-done.5 = bf16[1024,256]{1,0:T(8,128)(2,1)S(1)} collective-permute-done((bf16[1024,256]{1,0:T(8,128)(2,1)S(1)}, bf16[1024,256]{1,0:T(8,128)(2,1)S(1)}, u32[]{:S(2)}, u32[]{:S(2)}) %collective-permute-start.5) | collective-permute-done | bytes 524320 | tf_op jit(solution)/shard_map/ppermute | solution.py:9
  98.5 2.5 gather_fusion.4
  101.0 4.2 fusion.153
  105.2 8.0 %collective-permute-done.6 = bf16[1024,256]{1,0:T(8,128)(2,1)S(1)} collective-permute-done((bf16[1024,256]{1,0:T(8,128)(2,1)S(1)}, bf16[1024,256]{1,0:T(8,128)(2,1)S(1)}, u32[]{:S(2)}, u32[]{:S(2)}) %collective-permute-start.6) | collective-permute-done | bytes 524320 | tf_op jit(solution)/shard_map/ppermute | solution.py:9
  113.2 2.5 gather_fusion.5
  115.7 4.2 fusion.150
  120.0 8.0 %collective-permute-done.7 = bf16[1024,256]{1,0:T(8,128)(2,1)S(1)} collective-permute-done((bf16[1024,256]{1,0:T(8,128)(2,1)S(1)}, bf16[1024,256]{1,0:T(8,128)(2,1)S(1)}, u32[]{:S(2)}, u32[]{:S(2)}) %collective-permute-start.7) | collective-permute-done | bytes 524320 | tf_op jit(solution)/shard_map/ppermute | solution.py:9
  128.0 2.5 gather_fusion.6
  130.7 4.2 fusion.147
  134.9 8.0 %collective-permute-done.8 = bf16[1024,256]{1,0:T(8,128)(2,1)S(1)} collective-permute-done((bf16[1024,256]{1,0:T(8,128)(2,1)S(1)}, bf16[1024,256]{1,0:T(8,128)(2,1)S(1)}, u32[]{:S(2)}, u32[]{:S(2)}) %collective-permute-start.8) | collective-permute-done | bytes 524320 | tf_op jit(solution)/shard_map/ppermute | solution.py:9
  142.9 2.5 gather_fusion.7
  145.4 4.6 fusion.144
  151.2 38.0 %reduce-scatter.3.cloned.1.call-done = f32[256,256]{1,0:T(8,128)} async-done(((f32[1024,256]{1,0:T(8,128)}), f32[256,256]{1,0:T(8,128)}) %reduce-scatter.3.cloned.1.call-update) | async-done | bytes 262160 | tf_op jit(solution)/shard_map/reduce_scatter | solution.py:65
  191.4 8.8 %all_gather.3 = bf16[1024,256]{1,0:T(8,128)(2,1)S(1)} all-gather(bf16[256,256]{1,0:T(8,128)(2,1)S(1)} %fusion.166), channel_id=1, replica_groups=mesh['blk'=32,'rep'=4] {'rep'}, dimensions={0}, use_global_device_ids=true | all-gather | bytes 655360 | tf_op jit(solution)/shard_map/all_gather | solution.py:73
  200.2 5.1 fusion.40
  205.3 6.7 %copy.64 = f32[8,256,6,128]{1,0,2,3:T(8,128)} copy(f32[8,256,6,128]{3,1,2,0:T(8,128)} %fusion.40) | data formatting | bytes 12582912 | tf_op jit(solution)/shard_map/bsji,bjf->bsif/dot_general | solution.py:91
  211.9 6.2 fusion.120
  218.5 4.8 collective-permute-start.9
  223.4 5.1 fusion.43
  228.5 6.7 %copy.66 = f32[8,256,6,128]{1,0,2,3:T(8,128)} copy(f32[8,256,6,128]{3,1,2,0:T(8,128)} %fusion.43) | data formatting | bytes 12582912 | tf_op jit(solution)/shard_map/bsji,bjf->bsif/dot_general | solution.py:91
  235.1 6.2 fusion.123
  241.7 4.0 collective-permute-done.9
  247.0 6.8 %collective-permute-start.10 = (f32[1024,256]{1,0:T(8,128)S(1)}, f32[1024,256]{1,0:T(8,128)}, u32[]{:S(2)}, u32[]{:S(2)}) collective-permute-start(f32[1024,256]{1,0:T(8,128)S(1)} %bitcast_add_fusion.6), channel_id=1, source_target_pairs={{0,124},{4,0},{8,4},{12,8},{16,12},{20,16},{24,20},{28,24},{32,28}... | collective-permute-start | bytes 3145736 | tf_op jit(solution)/shard_map/ppermute | solution.py:9
  253.9 5.1 fusion.46
  259.0 6.7 %copy.68 = f32[8,256,6,128]{1,0,2,3:T(8,128)} copy(f32[8,256,6,128]{3,1,2,0:T(8,128)} %fusion.46) | data formatting | bytes 12582912 | tf_op jit(solution)/shard_map/bsji,bjf->bsif/dot_general | solution.py:91
  265.7 6.2 fusion.126
  272.2 3.0 collective-permute-done.10
  276.6 6.6 %collective-permute-start.11 = (f32[1024,256]{1,0:T(8,128)S(1)}, f32[1024,256]{1,0:T(8,128)}, u32[]{:S(2)}, u32[]{:S(2)}) collective-permute-start(f32[1024,256]{1,0:T(8,128)S(1)} %bitcast_add_fusion.5), channel_id=1, source_target_pairs={{0,124},{4,0},{8,4},{12,8},{16,12},{20,16},{24,20},{28,24},{32,28}... | collective-permute-start | bytes 3145736 | tf_op jit(solution)/shard_map/ppermute | solution.py:9
  283.3 5.1 fusion.49
  288.4 6.7 %copy.70 = f32[8,256,6,128]{1,0,2,3:T(8,128)} copy(f32[8,256,6,128]{3,1,2,0:T(8,128)} %fusion.49) | data formatting | bytes 12582912 | tf_op jit(solution)/shard_map/bsji,bjf->bsif/dot_general | solution.py:91
  295.1 6.2 fusion.129
  305.1 7.0 %collective-permute-start.12 = (f32[1024,256]{1,0:T(8,128)S(1)}, f32[1024,256]{1,0:T(8,128)}, u32[]{:S(2)}, u32[]{:S(2)}) collective-permute-start(f32[1024,256]{1,0:T(8,128)S(1)} %bitcast_add_fusion.4), channel_id=1, source_target_pairs={{0,124},{4,0},{8,4},{12,8},{16,12},{20,16},{24,20},{28,24},{32,28}... | collective-permute-start | bytes 3145736 | tf_op jit(solution)/shard_map/ppermute | solution.py:9
  312.2 5.1 fusion.52
  317.3 6.7 %copy.72 = f32[8,256,6,128]{1,0,2,3:T(8,128)} copy(f32[8,256,6,128]{3,1,2,0:T(8,128)} %fusion.52) | data formatting | bytes 12582912 | tf_op jit(solution)/shard_map/bsji,bjf->bsif/dot_general | solution.py:91
  324.0 6.2 fusion.132
  333.1 6.6 %collective-permute-start.13 = (f32[1024,256]{1,0:T(8,128)S(1)}, f32[1024,256]{1,0:T(8,128)}, u32[]{:S(2)}, u32[]{:S(2)}) collective-permute-start(f32[1024,256]{1,0:T(8,128)S(1)} %bitcast_add_fusion.3), channel_id=1, source_target_pairs={{0,124},{4,0},{8,4},{12,8},{16,12},{20,16},{24,20},{28,24},{32,28}... | collective-permute-start | bytes 3145736 | tf_op jit(solution)/shard_map/ppermute | solution.py:9
  339.8 5.1 fusion.55
  344.9 6.7 %copy.74 = f32[8,256,6,128]{1,0,2,3:T(8,128)} copy(f32[8,256,6,128]{3,1,2,0:T(8,128)} %fusion.55) | data formatting | bytes 12582912 | tf_op jit(solution)/shard_map/bsji,bjf->bsif/dot_general | solution.py:91
  351.6 6.2 fusion.135
  359.7 6.8 %collective-permute-start.14 = (f32[1024,256]{1,0:T(8,128)S(1)}, f32[1024,256]{1,0:T(8,128)}, u32[]{:S(2)}, u32[]{:S(2)}) collective-permute-start(f32[1024,256]{1,0:T(8,128)S(1)} %bitcast_add_fusion.2), channel_id=1, source_target_pairs={{0,124},{4,0},{8,4},{12,8},{16,12},{20,16},{24,20},{28,24},{32,28}... | collective-permute-start | bytes 3145736 | tf_op jit(solution)/shard_map/ppermute | solution.py:9
  366.6 5.1 fusion.58
  371.7 6.7 %copy.76 = f32[8,256,6,128]{1,0,2,3:T(8,128)} copy(f32[8,256,6,128]{3,1,2,0:T(8,128)} %fusion.58) | data formatting | bytes 12582912 | tf_op jit(solution)/shard_map/bsji,bjf->bsif/dot_general | solution.py:91
  378.4 6.2 fusion.138
  386.3 5.9 collective-permute-start.15
  392.3 5.1 fusion.61
  397.4 6.7 %copy.78 = f32[8,256,6,128]{1,0,2,3:T(8,128)} copy(f32[8,256,6,128]{3,1,2,0:T(8,128)} %fusion.61) | data formatting | bytes 12582912 | tf_op jit(solution)/shard_map/bsji,bjf->bsif/dot_general | solution.py:91
  404.1 6.2 fusion.141
  412.1 18.8 %collective-permute-done.16 = f32[1024,256]{1,0:T(8,128)S(1)} collective-permute-done((f32[1024,256]{1,0:T(8,128)S(1)}, f32[1024,256]{1,0:T(8,128)S(1)}, u32[]{:S(2)}, u32[]{:S(2)}) %collective-permute-start.16) | collective-permute-done | bytes 1048608 | tf_op jit(solution)/shard_map/ppermute | solution.py:9
  433.2 14.6 %collective-permute-done.17 = f32[1024,256]{1,0:T(8,128)S(1)} collective-permute-done((f32[1024,256]{1,0:T(8,128)S(1)}, f32[1024,256]{1,0:T(8,128)S(1)}, u32[]{:S(2)}, u32[]{:S(2)}) %collective-permute-start.17) | collective-permute-done | bytes 1048608 | tf_op jit(solution)/shard_map/ppermute | solution.py:9
  448.9 81.5 %psum.23 = f32[256]{0:T(256)S(1)} all-reduce(f32[256]{0:T(256)S(1)} %get-tuple-element.16), channel_id=1, replica_groups=mesh['blk'=32,'rep'=4] {'blk','rep'}, use_global_device_ids=true, to_apply=%region_5.7 | all-reduce | flops 256 | bytes 2048 | tf_op jit(solution)/shard_map/psum | solution.py:77
  531.2 65.9 %all-reduce.3.cloned.1.call-done = (f32[256,256]{1,0:T(8,128)}, f32[256,256]{1,0:T(8,128)}) async-done(((f32[256,256]{1,0:T(8,128)}, f32[256,256]{1,0:T(8,128)}), (f32[256,256]{1,0:T(8,128)}, f32[256,256]{1,0:T(8,128)})) %all-reduce.3.cloned.1.call-update) | async-done | bytes 524304 | tf_op jit(solution)/shard_map/psum | solution.py:77
  598.9 31.4 %reduce-scatter.5.cloned.1.call-done = f32[256,256]{1,0:T(8,128)} async-done(((f32[1024,256]{1,0:T(8,128)}), f32[256,256]{1,0:T(8,128)}) %reduce-scatter.5.cloned.1.call-update) | async-done | bytes 262160 | tf_op jit(solution)/shard_map/reduce_scatter | solution.py:105
  (144 shorter events, 40.7 us)
Async XLA Ops:
  7.2 182.0 %copy-start = (bf16[256,256]{1,0:T(8,128)(2,1)S(1)}, bf16[256,256]{1,0:T(8,128)(2,1)}, u32[]{:S(2)}) copy-start(bf16[256,256]{1,0:T(8,128)(2,1)} %param.20) | copy-start | bytes 393220
  7.2 182.0 %reduce-scatter.3.cloned.1.call-start = ((), (), s32[]{:S(2)}) async-start(), calls=%async_computation.2 | async-start | bytes 1310720 | tf_op jit(solution)/shard_map/reduce_scatter | solution.py:65
  7.2 15.3 %collective-permute-start = (bf16[1024,256]{1,0:T(8,128)(2,1)}, bf16[1024,256]{1,0:T(8,128)(2,1)S(1)}, u32[]{:S(2)}, u32[]{:S(2)}) collective-permute-start(bf16[1024,256]{1,0:T(8,128)(2,1)} %param.12), channel_id=1, source_target_pairs={{0,32},{4,36},{8,40},{12,44},{16,48},{20,52},{24,56},{28,60},{32,6... | collective-permute-start | bytes 1572872 | tf_op jit(solution)/shard_map/ppermute | solution.py:9
  22.6 12.6 %collective-permute-start.1 = (bf16[1024,256]{1,0:T(8,128)(2,1)S(1)}, bf16[1024,256]{1,0:T(8,128)(2,1)S(1)}, u32[]{:S(2)}, u32[]{:S(2)}) collective-permute-start(bf16[1024,256]{1,0:T(8,128)(2,1)S(1)} %broadcast_select_fusion.1), channel_id=1, source_target_pairs={{0,64},{4,68},{8,72},{12,76},{16,80},{20,84},{24,88},{28,92},{32,9... | collective-permute-start | bytes 1572872 | tf_op jit(solution)/shard_map/ppermute | solution.py:9
  35.3 14.4 %collective-permute-start.2 = (bf16[1024,256]{1,0:T(8,128)(2,1)S(1)}, bf16[1024,256]{1,0:T(8,128)(2,1)S(1)}, u32[]{:S(2)}, u32[]{:S(2)}) collective-permute-start(bf16[1024,256]{1,0:T(8,128)(2,1)S(1)} %broadcast_select_fusion.3), channel_id=1, source_target_pairs={{0,4},{4,8},{8,12},{12,16},{16,20},{20,24},{24,28},{28,32},{32,36}... | collective-permute-start | bytes 1572872 | tf_op jit(solution)/shard_map/ppermute | solution.py:9
  52.2 3.4 copy-start.2
  55.5 13.4 %collective-permute-start.3 = (bf16[1024,256]{1,0:T(8,128)(2,1)S(1)}, bf16[1024,256]{1,0:T(8,128)(2,1)S(1)}, u32[]{:S(2)}, u32[]{:S(2)}) collective-permute-start(bf16[1024,256]{1,0:T(8,128)(2,1)S(1)} %collective-permute-done.2), channel_id=1, source_target_pairs={{0,4},{4,8},{8,12},{12,16},{16,20},{20,24},{24,28},{28,32},{32,36}... | collective-permute-start | bytes 1572872 | tf_op jit(solution)/shard_map/ppermute | solution.py:9
  71.5 12.3 %collective-permute-start.4 = (bf16[1024,256]{1,0:T(8,128)(2,1)S(1)}, bf16[1024,256]{1,0:T(8,128)(2,1)S(1)}, u32[]{:S(2)}, u32[]{:S(2)}) collective-permute-start(bf16[1024,256]{1,0:T(8,128)(2,1)S(1)} %collective-permute-done.3), channel_id=1, source_target_pairs={{0,4},{4,8},{8,12},{12,16},{16,20},{20,24},{24,28},{28,32},{32,36}... | collective-permute-start | bytes 1572872 | tf_op jit(solution)/shard_map/ppermute | solution.py:9
  83.7 2.5 copy-start.8
  86.2 12.3 %collective-permute-start.5 = (bf16[1024,256]{1,0:T(8,128)(2,1)S(1)}, bf16[1024,256]{1,0:T(8,128)(2,1)S(1)}, u32[]{:S(2)}, u32[]{:S(2)}) collective-permute-start(bf16[1024,256]{1,0:T(8,128)(2,1)S(1)} %collective-permute-done.4), channel_id=1, source_target_pairs={{0,4},{4,8},{8,12},{12,16},{16,20},{20,24},{24,28},{28,32},{32,36}... | collective-permute-start | bytes 1572872 | tf_op jit(solution)/shard_map/ppermute | solution.py:9
  98.5 2.5 copy-start.9
  101.0 12.3 %collective-permute-start.6 = (bf16[1024,256]{1,0:T(8,128)(2,1)S(1)}, bf16[1024,256]{1,0:T(8,128)(2,1)S(1)}, u32[]{:S(2)}, u32[]{:S(2)}) collective-permute-start(bf16[1024,256]{1,0:T(8,128)(2,1)S(1)} %collective-permute-done.5), channel_id=1, source_target_pairs={{0,4},{4,8},{8,12},{12,16},{16,20},{20,24},{24,28},{28,32},{32,36}... | collective-permute-start | bytes 1572872 | tf_op jit(solution)/shard_map/ppermute | solution.py:9
  113.2 2.5 copy-start.10
  115.7 12.3 %collective-permute-start.7 = (bf16[1024,256]{1,0:T(8,128)(2,1)S(1)}, bf16[1024,256]{1,0:T(8,128)(2,1)S(1)}, u32[]{:S(2)}, u32[]{:S(2)}) collective-permute-start(bf16[1024,256]{1,0:T(8,128)(2,1)S(1)} %collective-permute-done.6), channel_id=1, source_target_pairs={{0,4},{4,8},{8,12},{12,16},{16,20},{20,24},{24,28},{28,32},{32,36}... | collective-permute-start | bytes 1572872 | tf_op jit(solution)/shard_map/ppermute | solution.py:9
  128.0 2.7 copy-start.11
  130.5 12.4 %collective-permute-start.8 = (bf16[1024,256]{1,0:T(8,128)(2,1)S(1)}, bf16[1024,256]{1,0:T(8,128)(2,1)S(1)}, u32[]{:S(2)}, u32[]{:S(2)}) collective-permute-start(bf16[1024,256]{1,0:T(8,128)(2,1)S(1)} %collective-permute-done.7), channel_id=1, source_target_pairs={{0,4},{4,8},{8,12},{12,16},{16,20},{20,24},{24,28},{28,32},{32,36}... | collective-permute-start | bytes 1572872 | tf_op jit(solution)/shard_map/ppermute | solution.py:9
  145.4 4.8 copy-start.6
  145.4 5.6 copy-start.3
  145.4 5.6 copy-start.4
  145.4 43.8 %copy-start.7 = (f32[256]{0:T(256)S(1)}, f32[256]{0:T(256)}, u32[]{:S(2)}) copy-start(f32[256]{0:T(256)} %param.21) | copy-start | bytes 3076
  150.0 447.1 %all-reduce.3.cloned.1.call-start = ((), (), s32[]{:S(2)}) async-start(), calls=%async_computation.4 | async-start | bytes 1048576 | tf_op jit(solution)/shard_map/psum | solution.py:77
  218.5 27.2 %collective-permute-start.9 = (f32[1024,256]{1,0:T(8,128)S(1)}, f32[1024,256]{1,0:T(8,128)}, u32[]{:S(2)}, u32[]{:S(2)}) collective-permute-start(f32[1024,256]{1,0:T(8,128)S(1)} %bitcast.332), channel_id=1, source_target_pairs={{0,124},{4,0},{8,4},{12,8},{16,12},{20,16},{24,20},{28,24},{32,28}... | collective-permute-start | bytes 3145736 | tf_op jit(solution)/shard_map/ppermute | solution.py:9
  247.0 28.3 %collective-permute-start.10 = (f32[1024,256]{1,0:T(8,128)S(1)}, f32[1024,256]{1,0:T(8,128)}, u32[]{:S(2)}, u32[]{:S(2)}) collective-permute-start(f32[1024,256]{1,0:T(8,128)S(1)} %bitcast_add_fusion.6), channel_id=1, source_target_pairs={{0,124},{4,0},{8,4},{12,8},{16,12},{20,16},{24,20},{28,24},{32,28}... | collective-permute-start | bytes 3145736 | tf_op jit(solution)/shard_map/ppermute | solution.py:9
  276.6 27.2 %collective-permute-start.11 = (f32[1024,256]{1,0:T(8,128)S(1)}, f32[1024,256]{1,0:T(8,128)}, u32[]{:S(2)}, u32[]{:S(2)}) collective-permute-start(f32[1024,256]{1,0:T(8,128)S(1)} %bitcast_add_fusion.5), channel_id=1, source_target_pairs={{0,124},{4,0},{8,4},{12,8},{16,12},{20,16},{24,20},{28,24},{32,28}... | collective-permute-start | bytes 3145736 | tf_op jit(solution)/shard_map/ppermute | solution.py:9
  305.1 26.7 %collective-permute-start.12 = (f32[1024,256]{1,0:T(8,128)S(1)}, f32[1024,256]{1,0:T(8,128)}, u32[]{:S(2)}, u32[]{:S(2)}) collective-permute-start(f32[1024,256]{1,0:T(8,128)S(1)} %bitcast_add_fusion.4), channel_id=1, source_target_pairs={{0,124},{4,0},{8,4},{12,8},{16,12},{20,16},{24,20},{28,24},{32,28}... | collective-permute-start | bytes 3145736 | tf_op jit(solution)/shard_map/ppermute | solution.py:9
  333.1 25.3 %collective-permute-start.13 = (f32[1024,256]{1,0:T(8,128)S(1)}, f32[1024,256]{1,0:T(8,128)}, u32[]{:S(2)}, u32[]{:S(2)}) collective-permute-start(f32[1024,256]{1,0:T(8,128)S(1)} %bitcast_add_fusion.3), channel_id=1, source_target_pairs={{0,124},{4,0},{8,4},{12,8},{16,12},{20,16},{24,20},{28,24},{32,28}... | collective-permute-start | bytes 3145736 | tf_op jit(solution)/shard_map/ppermute | solution.py:9
  359.7 25.2 %collective-permute-start.14 = (f32[1024,256]{1,0:T(8,128)S(1)}, f32[1024,256]{1,0:T(8,128)}, u32[]{:S(2)}, u32[]{:S(2)}) collective-permute-start(f32[1024,256]{1,0:T(8,128)S(1)} %bitcast_add_fusion.2), channel_id=1, source_target_pairs={{0,124},{4,0},{8,4},{12,8},{16,12},{20,16},{24,20},{28,24},{32,28}... | collective-permute-start | bytes 3145736 | tf_op jit(solution)/shard_map/ppermute | solution.py:9
  386.3 24.4 %collective-permute-start.15 = (f32[1024,256]{1,0:T(8,128)S(1)}, f32[1024,256]{1,0:T(8,128)}, u32[]{:S(2)}, u32[]{:S(2)}) collective-permute-start(f32[1024,256]{1,0:T(8,128)S(1)} %bitcast_add_fusion.1), channel_id=1, source_target_pairs={{0,124},{4,0},{8,4},{12,8},{16,12},{20,16},{24,20},{28,24},{32,28}... | collective-permute-start | bytes 3145736 | tf_op jit(solution)/shard_map/ppermute | solution.py:9
  410.7 21.4 %copy-start.5 = (f32[256,256]{1,0:T(8,128)S(1)}, f32[256,256]{1,0:T(8,128)}, u32[]{:S(2)}) copy-start(f32[256,256]{1,0:T(8,128)} %reduce-scatter.3.cloned.1.call-done) | copy-start | bytes 786436
  412.1 18.9 %collective-permute-start.16 = (f32[1024,256]{1,0:T(8,128)S(1)}, f32[1024,256]{1,0:T(8,128)S(1)}, u32[]{:S(2)}, u32[]{:S(2)}) collective-permute-start(f32[1024,256]{1,0:T(8,128)S(1)} %bitcast_add_fusion), channel_id=1, source_target_pairs={{0,96},{4,100},{8,104},{12,108},{16,112},{20,116},{24,120},{28,124... | collective-permute-start | bytes 3145736 | tf_op jit(solution)/shard_map/ppermute | solution.py:9
  431.1 16.7 %collective-permute-start.17 = (f32[1024,256]{1,0:T(8,128)S(1)}, f32[1024,256]{1,0:T(8,128)S(1)}, u32[]{:S(2)}, u32[]{:S(2)}) collective-permute-start(f32[1024,256]{1,0:T(8,128)S(1)} %broadcast_select_fusion), channel_id=1, source_target_pairs={{0,64},{4,68},{8,72},{12,76},{16,80},{20,84},{24,88},{28,92},{32,9... | collective-permute-start | bytes 3145736 | tf_op jit(solution)/shard_map/ppermute | solution.py:9
  433.1 198.8 %copy-start.1 = (bf16[256,256]{1,0:T(8,128)(2,1)S(1)}, bf16[256,256]{1,0:T(8,128)(2,1)}, u32[]{:S(2)}) copy-start(bf16[256,256]{1,0:T(8,128)(2,1)} %param.20) | copy-start | bytes 393220
  433.2 197.2 %reduce-scatter.5.cloned.1.call-start = ((), (), s32[]{:S(2)}) async-start(), calls=%async_computation.3 | async-start | bytes 1310720 | tf_op jit(solution)/shard_map/reduce_scatter | solution.py:105
Sparse Core Ops, SparseCore 0:
  150.1 39.0 reduce-scatter.2
  433.3 163.7 all-reduce.2
  599.7 30.5 reduce-scatter.4
where the time goes:
time: 648 us; the launch traced here: 639 us
  waiting for transfers between devices  260 us (40%)
  matrix products  126 us (19%)
  blocking collectives  90.3 us (14%)
  local copies, waits for them, and re-layouts  82.2 us (13%)
  starting transfers between devices  50.2 us (8%)
  other arithmetic  15.7 us (2%)
  between operations  14.3 us (2%)
    ppermute x18, waiting for transfers between devices, passed_along(): lax.ppermute(value, axis, [(i, (i + by) % size) for i in range(size)])  124 us
    psum x1, blocking collectives, shards(): lax.psum((local_self, local_neigh, local_bias), ('blk', 'rep'))  81.5 us
    psum x1, waiting for transfers between devices, shards(): lax.psum((local_self, local_neigh, local_bias), ('blk', 'rep'))  65.9 us
    dot_general x8, local copies, waits for them, and re-layouts, spread_part(): jnp.einsum('bsji,bjf->bsif', tiles[:, distance], back_blocks, preferred_e...  53.5 us
    ppermute x18, starting transfers between devices, passed_along(): lax.ppermute(value, axis, [(i, (i + by) % size) for i in range(size)])  50.1 us
    dot_general x8, matrix products, spread_part(): jnp.einsum('bsc,bsif->cif', onehot, products, precision=lax.Precision.HIG...  49.6 us
    dot_general x8, matrix products, spread_part(): jnp.einsum('bsji,bjf->bsif', tiles[:, distance], back_blocks, preferred_e...  40.8 us
    reduce_scatter x1, waiting for transfers between devices, shards(): lax.psum_scatter(partial_value, 'rep', scatter_dimension=0, tiled=True)  38 us
  transfers between devices with their start and end apart: 21, of which 19 were waited for; matrix products, arithmetic and copies ran while one was open for 26% of the time, Pallas kernels for 0%

commit v1 on v0

v1 whole, which is shorter than its diff:
```python
import functools

import jax
import jax.numpy as jnp
from jax import lax
from jax.experimental import pallas as pl
from jax.experimental.pallas import tpu as pltpu
from jax.sharding import PartitionSpec as P

AXES = ("blk", "rep")
NB = 8
ND = 8
NS = 6
BS = 128
F = 256
VMEM = 40 * 1024 * 1024
PLAN = ((2, None), (6, None), (3, None), (7, None), (1, None), (0, None), (4, 2), (5, 6))


def index_of(y, x, zl, zh, core):
    return (((y % 4 * 4 + x % 4) * 2 + zl) * 2 + zh) * 2 + core


def places():
    for t in range(128):
        yield t, t >> 5, t >> 3 & 3, t >> 2 & 1, t >> 1 & 1, t & 1


def column_pairs(k, via):
    out = []
    for t, y, x, zl, zh, core in places():
        j, r = x * 2 + zl, 2 * zh + core
        jj = j ^ k
        if via is None:
            out.append((index_of(y - r - (jj > j), jj >> 1, jj & 1, zh ^ (k & 1), core), t))
        else:
            jn = j ^ via
            out.append((index_of(y - (jj > j) + (jj > jn), jn >> 1, jn & 1, zh, core), t))
    return out


def flip_pairs(dy=0, dx=0, dzl=0, dzh=0, dcore=0):
    return [
        (t, index_of(y ^ dy, x ^ dx, zl ^ dzl, zh ^ dzh, core ^ dcore))
        for t, y, x, zl, zh, core in places()
    ]


def send(value, pairs):
    return lax.ppermute(value, AXES, pairs)


def back(pairs):
    return [(b, a) for a, b in pairs]


def params():
    return pltpu.CompilerParams(vmem_limit_bytes=VMEM)


def forward_body(first, sel_ref, cols_ref, counts_ref, tiles_ref, shard_ref, *rest):
    out_ref = rest[-1]
    step = pl.program_id(0)
    dist = sel_ref[0]
    for inner in range(2):
        b = step * 2 + inner
        count = counts_ref[b * ND + dist]
        left, right = [], []
        for s in range(NS):
            col = cols_ref[(b * ND + dist) * NS + s]
            block = shard_ref[pl.ds(pl.multiple_of(col * BS, BS), BS), :]
            right.append(jnp.where(s < count, block, jnp.zeros((), block.dtype)))
            left.append(tiles_ref[inner, 0, s])
        summed = jnp.dot(
            jnp.concatenate(left, 1), jnp.concatenate(right, 0), preferred_element_type=jnp.float32
        )
        rows = pl.ds(pl.multiple_of(b * BS, BS), BS)
        if first:
            out_ref[rows, :] = summed
        else:
            out_ref[rows, :] = rest[0][rows, :] + summed


def forward_call(dist, cols, counts, tiles, shard, total):
    first = total is None
    whole = pl.BlockSpec((NB * BS, F), lambda i, *_: (0, 0))
    in_specs = [
        pl.BlockSpec((2, 1, NS, BS, BS), lambda i, sel, c, n: (i, sel[0], 0, 0, 0)),
        whole,
    ] + ([] if first else [whole])
    return pl.pallas_call(
        functools.partial(forward_body, first),
        out_shape=jax.ShapeDtypeStruct((NB * BS, F), jnp.float32),
        grid_spec=pltpu.PrefetchScalarGridSpec(
            num_scalar_prefetch=3, grid=(NB // 2,), in_specs=in_specs, out_specs=whole
        ),
        compiler_params=params(),
        name="forward_tiles",
    )(dist, cols, counts, tiles, shard, *([] if first else [total]))


def dense_body(
    rep_ref, own_ref, got_ref, feat_ref, cot_ref, mask_ref, inv_ref, invt_ref, ws_ref, wn_ref,
    bias_ref, act_ref, term_ref, back_ref, grad_ref, sums_ref,
):
    rep = rep_ref[0]
    zh, core = rep // 2, rep % 2
    nt = (((1,), (1,)), ((), ()))
    tn = (((0,), (0,)), ((), ()))
    grads = jnp.zeros((F, F), jnp.float32)
    sums = jnp.zeros((1, F), jnp.float32)
    for part in range(2):
        quarter = part * 2 + core
        rows = pl.ds(pl.multiple_of(quarter * 256, 256), 256)
        feat = feat_ref[rows, :]
        summed = own_ref[part].astype(jnp.float32) + got_ref[part].astype(jnp.float32)
        agg = (summed * inv_ref[rows, :]).astype(jnp.bfloat16)
        pre = (
            jnp.dot(feat, ws_ref[...], preferred_element_type=jnp.float32)
            + jnp.dot(agg, wn_ref[...], preferred_element_type=jnp.float32)
            + bias_ref[...]
        )
        sigm = jax.nn.sigmoid(pre)
        act = (pre * sigm).astype(jnp.bfloat16)
        slope = sigm * (1.0 + pre * (1.0 - sigm))
        grad_pre = (mask_ref[rows, :] * cot_ref[rows, :].astype(jnp.float32) * slope).astype(
            jnp.bfloat16
        )

        @pl.when(zh == part)
        def _():
            act_ref[...] = act
            term_ref[...] = lax.dot_general(
                grad_pre, ws_ref[...], nt, preferred_element_type=jnp.float32
            )

        back_t = lax.dot_general(wn_ref[...], grad_pre, nt, preferred_element_type=jnp.float32)
        back_ref[part] = (back_t * invt_ref[quarter]).astype(jnp.bfloat16)
        left = jnp.where(zh == 0, feat, agg)
        grads += lax.dot_general(left, grad_pre, tn, preferred_element_type=jnp.float32)
        sums += jnp.sum(grad_pre.astype(jnp.float32), axis=0, keepdims=True)
    grad_ref[...] = grads
    sums_ref[...] = sums


def dense_call(rep, own, got, feat, cot, mask, inv, inv_t, w_self, w_neigh, bias):
    vmem = pl.BlockSpec(memory_space=pltpu.VMEM)
    return pl.pallas_call(
        dense_body,
        out_shape=(
            jax.ShapeDtypeStruct((256, F), jnp.bfloat16),
            jax.ShapeDtypeStruct((256, F), jnp.float32),
            jax.ShapeDtypeStruct((2, F, 256), jnp.bfloat16),
            jax.ShapeDtypeStruct((F, F), jnp.float32),
            jax.ShapeDtypeStruct((1, F), jnp.float32),
        ),
        in_specs=[pl.BlockSpec(memory_space=pltpu.SMEM)] + [vmem] * 10,
        out_specs=(vmem,) * 5,
        compiler_params=params(),
        name="dense_rows",
    )(rep, own, got, feat, cot, mask, inv, inv_t, w_self, w_neigh, bias)


def backward_body(added, sel_ref, cols_ref, counts_ref, tiles_ref, own_ref, got_ref, *rest):
    out_ref, acc_ref = rest[-2:]
    step = pl.program_id(0)
    dist = sel_ref[0]
    core = sel_ref[1]

    @pl.when(step == 0)
    def _():
        for c in range(NB):
            if added:
                acc_ref[c] = rest[0][c].astype(jnp.float32)
            else:
                acc_ref[c] = jnp.zeros((F, BS), jnp.float32)

    mine = step % 2 == core
    part = step // 2
    message = jnp.where(mine, own_ref[part], got_ref[part])
    for inner in range(2):
        b = step * 2 + inner
        count = counts_ref[b * ND + dist]
        left = message[:, inner * BS : (inner + 1) * BS]
        for s in range(0, NS, 2):
            right = jnp.concatenate([tiles_ref[inner, 0, s], tiles_ref[inner, 0, s + 1]], 1)
            product = jnp.dot(left, right, preferred_element_type=jnp.float32)
            for k in range(2):
                col = cols_ref[(b * ND + dist) * NS + s + k]
                col = jnp.where(s + k < count, col, NB)
                acc_ref[col] += product[:, k * BS : (k + 1) * BS]

    @pl.when(step == NB // 2 - 1)
    def _():
        for c in range(NB):
            out_ref[c] = acc_ref[c].astype(jnp.bfloat16)


def backward_call(sel, cols, counts, tiles, own, got, extra):
    added = extra is not None
    whole = pl.BlockSpec((NB, F, BS), lambda i, *_: (0, 0, 0))
    message = pl.BlockSpec((2, F, 256), lambda i, *_: (0, 0, 0))
    in_specs = [
        pl.BlockSpec((2, 1, NS, BS, BS), lambda i, sel, c, n: (i, sel[0], 0, 0, 0)),
        message,
        message,
    ] + ([whole] if added else [])
    return pl.pallas_call(
        functools.partial(backward_body, added),
        out_shape=jax.ShapeDtypeStruct((NB, F, BS), jnp.bfloat16),
        grid_spec=pltpu.PrefetchScalarGridSpec(
            num_scalar_prefetch=3,
            grid=(NB // 2,),
            in_specs=in_specs,
            out_specs=whole,
            scratch_shapes=[pltpu.VMEM((NB + 1, F, BS), jnp.float32)],
        ),
        compiler_params=params(),
        name="backward_tiles",
    )(sel, cols, counts, tiles, own, got, *([extra] if added else []))


def final_body(kept_ref, got_ref, term_ref, out_ref):
    for c in range(2):
        spread = kept_ref[c] + got_ref[c].astype(jnp.float32)
        rows = slice(c * BS, (c + 1) * BS)
        out_ref[rows, :] = (term_ref[rows, :] + spread.T).astype(jnp.bfloat16)


def final_call(kept, got, term):
    return pl.pallas_call(
        final_body,
        out_shape=jax.ShapeDtypeStruct((256, F), jnp.bfloat16),
        compiler_params=params(),
        name="final_rows",
    )(kept, got, term)


def pick(pair, index):
    return lax.dynamic_index_in_dim(pair, index, 0, keepdims=False)


def summed_over(value, flips):
    value = value.astype(jnp.bfloat16)
    got = [send(value, flip_pairs(**f)).astype(jnp.float32) for f in flips]
    value = value.astype(jnp.float32)
    if len(got) == 1:
        return value + got[0]
    return (value + got[0]) + (got[1] + got[2])


def weight_grads(grads, sums, zh, core, nodes):
    halves = grads.reshape(2, F // 2, F)
    mine = pick(halves, core) + send(pick(halves, 1 - core), flip_pairs(dcore=1))
    bias = sums + send(sums, flip_pairs(dcore=1))
    high = bias.astype(jnp.bfloat16).astype(jnp.float32)
    pad = jnp.zeros((14, F), jnp.float32)
    value = jnp.concatenate([mine, high, bias - high, pad], 0)

    def split_bias(v):
        total = v[F // 2 : F // 2 + 1] + v[F // 2 + 1 : F // 2 + 2]
        hi = total.astype(jnp.bfloat16).astype(jnp.float32)
        return jnp.concatenate([v[: F // 2], hi, total - hi, pad], 0)

    value = split_bias(summed_over(value, [dict(dy=1), dict(dy=2), dict(dy=3)]))
    value = split_bias(summed_over(value, [dict(dx=1), dict(dx=2), dict(dx=3)]))
    value = summed_over(value, [dict(dzl=1)])
    bias = value[F // 2] + value[F // 2 + 1]
    half = value[: F // 2]
    other = send(half, flip_pairs(dzh=1))
    both = jnp.where(zh == 0, jnp.stack([half, other]), jnp.stack([other, half]))
    across = send(both, flip_pairs(dcore=1))
    low, top = jnp.where(core == 0, both, across), jnp.where(core == 0, across, both)
    norm = 1.0 / jnp.sqrt(jnp.float32(nodes))
    whole = jnp.concatenate([low, top], 1) * norm
    return whole[0], whole[1], bias * norm


def shards(
    features, tiles, tile_cols, counts, degree, train_mask, cotangent, w_self, w_neigh, bias_term
):
    rows = features.shape[0]
    rep = lax.axis_index("rep").astype(jnp.int32)
    zh, core = rep // 2, rep % 2
    place = (lax.axis_index("blk") % 8).astype(jnp.int32)
    cols = tile_cols.reshape(-1)
    live = counts.reshape(-1)

    def distance_of(k):
        return (place - (place ^ k)) % 8

    inv = 1.0 / degree.astype(jnp.float32)
    inv_col = inv.reshape(rows, 1)
    inv_row = inv.reshape(4, 1, 256)
    mask = train_mask.astype(jnp.float32).reshape(rows, 1)
    bias = bias_term.reshape(1, F)

    blocks = {}
    total = None
    for k, via in PLAN:
        source = features if via is None else blocks[k ^ via]
        blocks[k] = send(source, column_pairs(k, via))
    for k, _ in PLAN:
        total = forward_call(distance_of(k)[None], cols, live, tiles, blocks[k], total)

    parts = total.reshape(2, 2, 256, F)
    away = lax.dynamic_index_in_dim(parts, 1 - core, 1, keepdims=False).astype(jnp.bfloat16)
    kept = lax.dynamic_index_in_dim(parts, core, 1, keepdims=False)
    chip = (kept + send(away, flip_pairs(dcore=1)).astype(jnp.float32)).astype(jnp.bfloat16)
    other = send(chip, flip_pairs(dzh=1))

    activation, own_term, back_own, grads, sums = dense_call(
        rep[None], chip, other, features, cotangent, mask, inv_col, inv_row, w_self, w_neigh, bias
    )
    back_got = send(back_own, flip_pairs(dcore=1))

    grad_self, grad_neigh, grad_bias = weight_grads(
        grads, sums, zh, core, rows * lax.axis_size("blk")
    )

    extra = {}
    arrived = None
    for k, via in reversed(PLAN):
        sel = jnp.stack([distance_of(k), core])
        made = backward_call(sel, cols, live, tiles, back_own, back_got, extra.get(k))
        moved = send(made, back(column_pairs(k, via)))
        if via is None:
            moved = moved.astype(jnp.float32)
            arrived = moved if arrived is None else arrived + moved
        else:
            extra[k ^ via] = moved

    parts = arrived.reshape(2, 2, 2, F, BS)
    away = lax.dynamic_index_in_dim(parts, 1 - core, 1, keepdims=False).astype(jnp.bfloat16)
    kept = lax.dynamic_index_in_dim(parts, core, 1, keepdims=False)
    chip = kept + send(away, flip_pairs(dcore=1)).astype(jnp.float32)
    got = send(pick(chip, 1 - zh).astype(jnp.bfloat16), flip_pairs(dzh=1))
    grad_features = final_call(pick(chip, zh), got, own_term)
    return (activation, grad_features, grad_self, grad_neigh, grad_bias)


def solution(mesh):
    return jax.shard_map(
        shards,
        mesh=mesh,
        in_specs=(
            P("blk", None),
            P("blk", "rep", None, None, None),
            P("blk", "rep", None),
            P("blk", "rep"),
            P("blk"),
            P("blk"),
            P("blk", None),
            P(),
            P(),
            P(),
        ),
        out_specs=(P(("blk", "rep"), None), P(("blk", "rep"), None), P(), P(), P()),
        check_vma=False,
    )
```

time: 648 us -> 238 us (0.37); the launches traced: 639 us -> 237 us
  waiting for transfers between devices: 260 us -> 82.6 us
  matrix products: 126 us -> 0 us
  blocking collectives: 90.3 us -> 0 us
  local copies, waits for them, and re-layouts: 82.2 us -> 15.2 us
  Pallas kernels: 0 us -> 49 us
  starting transfers between devices: 50.2 us -> 85.1 us
  between operations: 14.3 us -> 1.22 us
  other arithmetic: 15.7 us -> 4.22 us
    dot_general x30 -> x0, matrix products: 126 us -> none  [the longest x8 49.6 us: spread_part(): jnp.einsum('bsc,bsif->cif', onehot, products, precision=lax.Precision.HIG...]
    psum x1 -> x0, blocking collectives: 81.5 us -> none  [shards(): lax.psum((local_self, local_neigh, local_bias), ('blk', 'rep'))]
    reduce_scatter x2 -> x0, waiting for transfers between devices: 69.4 us -> none  [the longest x1 38 us: shards(): lax.psum_scatter(partial_value, 'rep', scatter_dimension=0, tiled=True)]
    psum x1 -> x0, waiting for transfers between devices: 65.9 us -> none  [shards(): lax.psum((local_self, local_neigh, local_bias), ('blk', 'rep'))]
    dot_general x16 -> x0, local copies, waits for them, and re-layouts: 56.2 us -> none  [the longest x8 53.5 us: spread_part(): jnp.einsum('bsji,bjf->bsif', tiles[:, distance], back_blocks, preferred_e...]
    pallas_call x0 -> x18, Pallas kernels: none -> 49 us  [the longest x8 26.7 us: forward_call(): pl.pallas_call(functools.partial(forward_body, first), out_shape=jax.Shap...]
    ppermute x18 -> x32, waiting for transfers between devices: 124 us -> 82.6 us  [send(): return lax.ppermute(value, AXES, pairs)]
    ppermute x18 -> x32, starting transfers between devices: 50.1 us -> 85.1 us  [send(): return lax.ppermute(value, AXES, pairs)]
  transfers between devices with their start and end apart: 21 -> 32, of which waited for: 19 -> 12; matrix products, arithmetic and copies ran while one was open for 26% -> 3% of each run, Pallas kernels for 0% -> 18%
where the time goes in v1:
time: 238 us; the launch traced here: 237 us
  starting transfers between devices  85.1 us (36%)
  waiting for transfers between devices  82.6 us (35%)
  Pallas kernels  49 us (21%)
  local copies, waits for them, and re-layouts  15.2 us (6%)
  other arithmetic  4.22 us (2%)
    ppermute x32, starting transfers between devices, send(): return lax.ppermute(value, AXES, pairs)  85.1 us
    ppermute x32, waiting for transfers between devices, send(): return lax.ppermute(value, AXES, pairs)  82.6 us
    pallas_call x8, Pallas kernels, forward_call(): pl.pallas_call(functools.partial(forward_body, first), out_shape=jax.Shap...  26.7 us
    pallas_call x8, Pallas kernels, backward_call(): pl.pallas_call(functools.partial(backward_body, added), out_shape=jax.Sha...  19.8 us
    unnamed x23, local copies, waits for them, and re-layouts  12.8 us
  transfers between devices with their start and end apart: 32, of which 12 were waited for; matrix products, arithmetic and copies ran while one was open for 3% of the time, Pallas kernels for 18%

profile of v1, /device:TPU:1, one launch (start us, length us, event | category | flops | bytes accessed | tf_op | source)
XLA Modules:
  0.0 237.3 jit_solution(860098120842387456)
XLA Ops:
  0.6 3.1 %collective-permute-start.7 = (bf16[1024,256]{1,0:T(8,128)(2,1)}, bf16[1024,256]{1,0:T(8,128)(2,1)S(1)}, u32[]{:S(2)}, u32[]{:S(2)}) collective-permute-start(bf16[1024,256]{1,0:T(8,128)(2,1)} %feat_ref.1), channel_id=1, source_target_pairs={{104,0},{73,1},{42,2},{11,3},{108,4},{77,5},{46,6},{15,7},{0,8},{9... | collective-permute-start | bytes 1572872 | tf_op jit(solution)/shard_map/ppermute | solution.py:50
  3.8 3.5 %collective-permute-start.2 = (bf16[1024,256]{1,0:T(8,128)(2,1)}, bf16[1024,256]{1,0:T(8,128)(2,1)S(1)}, u32[]{:S(2)}, u32[]{:S(2)}) collective-permute-start(bf16[1024,256]{1,0:T(8,128)(2,1)} %feat_ref.1), channel_id=1, source_target_pairs={{120,0},{89,1},{58,2},{27,3},{124,4},{93,5},{62,6},{31,7},{112,8},... | collective-permute-start | bytes 1572872 | tf_op jit(solution)/shard_map/ppermute | solution.py:50
  7.3 3.6 %collective-permute-start = (bf16[1024,256]{1,0:T(8,128)(2,1)}, bf16[1024,256]{1,0:T(8,128)(2,1)S(1)}, u32[]{:S(2)}, u32[]{:S(2)}) collective-permute-start(bf16[1024,256]{1,0:T(8,128)(2,1)} %feat_ref.1), channel_id=1, source_target_pairs={{110,0},{79,1},{44,2},{13,3},{106,4},{75,5},{40,6},{9,7},{6,8},{10... | collective-permute-start | bytes 1572872 | tf_op jit(solution)/shard_map/ppermute | solution.py:50
  10.9 1.8 collective-permute-start.6
  12.7 3.2 %collective-permute-start.5 = (bf16[1024,256]{1,0:T(8,128)(2,1)}, bf16[1024,256]{1,0:T(8,128)(2,1)S(1)}, u32[]{:S(2)}, u32[]{:S(2)}) collective-permute-start(bf16[1024,256]{1,0:T(8,128)(2,1)} %feat_ref.1), channel_id=1, source_target_pairs={{102,0},{71,1},{36,2},{5,3},{2,4},{99,5},{64,6},{33,7},{110,8},{79... | collective-permute-start | bytes 1572872 | tf_op jit(solution)/shard_map/ppermute | solution.py:50
  15.9 14.2 %collective-permute-done.7.shard_ref = bf16[1024,256]{1,0:T(8,128)(2,1)S(1)} collective-permute-done((bf16[1024,256]{1,0:T(8,128)(2,1)}, bf16[1024,256]{1,0:T(8,128)(2,1)S(1)}, u32[]{:S(2)}, u32[]{:S(2)}) %collective-permute-start.7) | collective-permute-done | bytes 524320 | tf_op jit(solution)/shard_map/ppermute | solution.py:50
  30.1 0.8 copy-done.4
  30.9 1.9 collective-permute-start.4
  32.8 2.0 collective-permute-start.3
  34.8 12.0 %collective-permute-done.shard_ref = bf16[1024,256]{1,0:T(8,128)(2,1)S(1)} collective-permute-done((bf16[1024,256]{1,0:T(8,128)(2,1)}, bf16[1024,256]{1,0:T(8,128)(2,1)S(1)}, u32[]{:S(2)}, u32[]{:S(2)}) %collective-permute-start) | collective-permute-done | bytes 524320 | tf_op jit(solution)/shard_map/ppermute | solution.py:50
  46.8 6.1 %collective-permute-start.1 = (bf16[1024,256]{1,0:T(8,128)(2,1)S(1)}, bf16[1024,256]{1,0:T(8,128)(2,1)S(1)}, u32[]{:S(2)}, u32[]{:S(2)}) collective-permute-start(bf16[1024,256]{1,0:T(8,128)(2,1)S(1)} %collective-permute-done.shard_ref), channel_id=1, source_target_pairs={{120,0},{121,1},{122,2},{123,3},{124,4},{125,5},{126,6},{127,7},{1... | collective-permute-start | bytes 1572872 | tf_op jit(solution)/shard_map/ppermute | solution.py:50
  52.9 0.9 copy.15
  53.9 0.8 reshape.44.counts_ref
  54.7 4.6 %copy-done = bf16[8,8,6,128,128]{4,3,2,1,0:T(8,128)(2,1)S(1)} copy-done((bf16[8,8,6,128,128]{4,3,2,1,0:T(8,128)(2,1)S(1)}, bf16[8,8,6,128,128]{4,3,2,1,0:T(8,128)(2,1)}, u32[]{:S(2)}) %copy-start) | copy-done | bytes 12582936
  59.3 1.0 copy-done.5
  60.3 1.9 forward_tiles.8.rest_0_
  62.3 3.5 %forward_tiles.9.rest_0_ = f32[1024,256]{1,0:T(8,128)S(1)} custom-call(s32[1]{0:T(128)} %bitcast.6.sel_ref, s32[384]{0:T(512)S(1)} %reshape.43.cols_ref, s32[64]{0:T(128)S(1)} %reshape.44.counts_ref, bf16[8,8,6,128,128]{4,3,2,1,0:T(8,128)(2,1)} %tiles_ref.31, bf16[1024,256]{1,0:T(8,128)(2,1)S(1)} %collective-permute-done.2.shard_ref, ...), custom_call_target="tpu_custom_call" | custom-call | tf_op jit(solution)/shard_map/forward_tiles/pallas_call | solution.py:91
  65.8 3.5 %forward_tiles.10.rest_0_ = f32[1024,256]{1,0:T(8,128)S(1)} custom-call(s32[1]{0:T(128)} %bitcast.5.sel_ref, s32[384]{0:T(512)S(1)} %reshape.43.cols_ref, s32[64]{0:T(128)S(1)} %reshape.44.counts_ref, bf16[8,8,6,128,128]{4,3,2,1,0:T(8,128)(2,1)} %tiles_ref.31, bf16[1024,256]{1,0:T(8,128)(2,1)S(1)} %collective-permute-done.shard_ref, ...), custom_call_target="tpu_custom_call" | custom-call | tf_op jit(solution)/shard_map/forward_tiles/pallas_call | solution.py:91
  69.3 3.7 %forward_tiles.11.rest_0_ = f32[1024,256]{1,0:T(8,128)S(1)} custom-call(s32[1]{0:T(128)} %bitcast.4.sel_ref, s32[384]{0:T(512)S(1)} %reshape.43.cols_ref, s32[64]{0:T(128)S(1)} %reshape.44.counts_ref, bf16[8,8,6,128,128]{4,3,2,1,0:T(8,128)(2,1)} %tiles_ref.31, bf16[1024,256]{1,0:T(8,128)(2,1)} %collective-permute-done.6.shard_ref, ...), custom_call_target="tpu_custom_call" | custom-call | tf_op jit(solution)/shard_map/forward_tiles/pallas_call | solution.py:91
  73.0 3.5 %forward_tiles.12.rest_0_ = f32[1024,256]{1,0:T(8,128)S(1)} custom-call(s32[1]{0:T(128)} %bitcast.3.sel_ref, s32[384]{0:T(512)S(1)} %reshape.43.cols_ref, s32[64]{0:T(128)S(1)} %reshape.44.counts_ref, bf16[8,8,6,128,128]{4,3,2,1,0:T(8,128)(2,1)} %tiles_ref.31, bf16[1024,256]{1,0:T(8,128)(2,1)S(1)} %collective-permute-done.5.shard_ref, ...), custom_call_target="tpu_custom_call" | custom-call | tf_op jit(solution)/shard_map/forward_tiles/pallas_call | solution.py:91
  76.5 3.5 %forward_tiles.13.rest_0_ = f32[1024,256]{1,0:T(8,128)S(1)} custom-call(s32[1]{0:T(128)} %constant.133.clone.1.sel_ref, s32[384]{0:T(512)S(1)} %reshape.43.cols_ref, s32[64]{0:T(128)S(1)} %reshape.44.counts_ref, bf16[8,8,6,128,128]{4,3,2,1,0:T(8,128)(2,1)} %tiles_ref.31, bf16[1024,256]{1,0:T(8,128)(2,1)S(1)} %collective-permute-done.4.shard_ref, ...), custom_call_target="tpu_custom_call" | custom-call | tf_op jit(solution)/shard_map/forward_tiles/pallas_call | solution.py:91
  80.1 3.5 %forward_tiles.14.rest_0_ = f32[1024,256]{1,0:T(8,128)S(1)} custom-call(s32[1]{0:T(128)} %bitcast.2.sel_ref, s32[384]{0:T(512)S(1)} %reshape.43.cols_ref, s32[64]{0:T(128)S(1)} %reshape.44.counts_ref, bf16[8,8,6,128,128]{4,3,2,1,0:T(8,128)(2,1)} %tiles_ref.31, bf16[1024,256]{1,0:T(8,128)(2,1)S(1)} %collective-permute-done.3.shard_ref, ...), custom_call_target="tpu_custom_call" | custom-call | tf_op jit(solution)/shard_map/forward_tiles/pallas_call | solution.py:91
  83.7 3.5 %forward_tiles.15 = f32[1024,256]{1,0:T(8,128)S(1)} custom-call(s32[1]{0:T(128)} %bitcast.1.sel_ref, s32[384]{0:T(512)S(1)} %reshape.43.cols_ref, s32[64]{0:T(128)S(1)} %reshape.44.counts_ref, bf16[8,8,6,128,128]{4,3,2,1,0:T(8,128)(2,1)} %tiles_ref.31, bf16[1024,256]{1,0:T(8,128)(2,1)S(1)} %collective-permute-done.1.shard_ref, ...), custom_call_target="tpu_custom_call" | custom-call | tf_op jit(solution)/shard_map/forward_tiles/pallas_call | solution.py:91
  87.3 9.1 %collective-permute-start.8 = (bf16[2,256,256]{2,1,0:T(8,128)(2,1)S(1)}, bf16[2,256,256]{2,1,0:T(8,128)(2,1)S(1)}, u32[]{:S(2)}, u32[]{:S(2)}) collective-permute-start(bf16[2,256,256]{2,1,0:T(8,128)(2,1)S(1)} %fusion.1), channel_id=1, source_target_pairs={{0,1},{1,0},{2,3},{3,2},{4,5},{5,4},{6,7},{7,6},{8,9},{9,8},{10,11... | collective-permute-start | bytes 786440 | tf_op jit(solution)/shard_map/ppermute | solution.py:50
  96.4 1.2 collective-permute-done.8
  98.5 8.2 %collective-permute-done.9.got_ref = bf16[2,256,256]{2,1,0:T(8,128)(2,1)S(1)} collective-permute-done((bf16[2,256,256]{2,1,0:T(8,128)(2,1)S(1)}, bf16[2,256,256]{2,1,0:T(8,128)(2,1)S(1)}, u32[]{:S(2)}, u32[]{:S(2)}) %collective-permute-start.9) | collective-permute-done | bytes 262176 | tf_op jit(solution)/shard_map/ppermute | solution.py:50
  106.8 0.9 copy-done.7
  107.7 1.6 dense_rows.1
  109.2 1.2 collective-permute-start.22
  110.5 0.7 collective-permute-done.22
  111.3 0.6 collective-permute-done.21
  112.1 2.1 collective-permute-start.24
  114.2 1.8 collective-permute-start.25
  116.0 2.1 collective-permute-done.24
  118.2 1.4 collective-permute-done.25
  119.9 1.0 collective-permute-start.27
  120.9 2.9 %collective-permute-start.28 = (bf16[144,256]{1,0:T(8,128)(2,1)S(1)}, bf16[144,256]{1,0:T(8,128)(2,1)S(1)}, u32[]{:S(2)}, u32[]{:S(2)}) collective-permute-start(bf16[144,256]{1,0:T(8,128)(2,1)S(1)} %maximum_maximum_fusion.1), channel_id=1, source_target_pairs={{0,24},{1,25},{2,26},{3,27},{4,28},{5,29},{6,30},{7,31},{8,16},{9,... | collective-permute-start | bytes 221192 | tf_op jit(solution)/shard_map/ppermute | solution.py:50
  123.8 1.7 collective-permute-start.10
  125.6 0.8 collective-permute-done.28
  126.7 4.6 %copy-done.1 = bf16[8,8,6,128,128]{4,3,2,1,0:T(8,128)(2,1)S(1)} copy-done((bf16[8,8,6,128,128]{4,3,2,1,0:T(8,128)(2,1)S(1)}, bf16[8,8,6,128,128]{4,3,2,1,0:T(8,128)(2,1)}, u32[]{:S(2)}) %copy-start.1) | copy-done | bytes 12582936
  131.3 2.5 %backward_tiles.8 = bf16[8,256,128]{2,1,0:T(8,128)(2,1)S(1)} custom-call(s32[2]{0:T(128)S(1)} %pad_add_fusion.sel_ref, s32[384]{0:T(512)S(1)} %reshape.43.cols_ref, s32[64]{0:T(128)S(1)} %reshape.44.counts_ref, bf16[8,8,6,128,128]{4,3,2,1,0:T(8,128)(2,1)S(1)} %copy-done.1, bf16[2,256,256]{2,1,0:T(8,128)(2,1)S(1)} %get-tuple-element.11.own_ref, ...), custom_call_target="tpu_custom_call" | custom-call | tf_op jit(solution)/shard_map/backward_tiles/pallas_call | solution.py:208
  133.8 3.8 %collective-permute-start.11 = (bf16[8,256,128]{2,1,0:T(8,128)(2,1)S(1)}, bf16[8,256,128]{2,1,0:T(8,128)(2,1)}, u32[]{:S(2)}, u32[]{:S(2)}) collective-permute-start(bf16[8,256,128]{2,1,0:T(8,128)(2,1)S(1)} %backward_tiles.8), channel_id=1, source_target_pairs={{0,0},{1,97},{2,66},{3,35},{4,4},{5,101},{6,70},{7,39},{8,8},{9,10... | collective-permute-start | bytes 1572872 | tf_op jit(solution)/shard_map/ppermute | solution.py:50
  137.5 2.5 %backward_tiles.11 = bf16[8,256,128]{2,1,0:T(8,128)(2,1)S(1)} custom-call(s32[2]{0:T(128)S(1)} %pad_add_fusion.4.sel_ref, s32[384]{0:T(512)S(1)} %reshape.43.cols_ref, s32[64]{0:T(128)S(1)} %reshape.44.counts_ref, bf16[8,8,6,128,128]{4,3,2,1,0:T(8,128)(2,1)S(1)} %copy-done.1, bf16[2,256,256]{2,1,0:T(8,128)(2,1)S(1)} %get-tuple-element.11.own_ref, ...), custom_call_target="tpu_custom_call" | custom-call | tf_op jit(solution)/shard_map/backward_tiles/pallas_call | solution.py:208
  140.0 1.9 collective-permute-start.14
  141.9 2.5 %backward_tiles.13 = bf16[8,256,128]{2,1,0:T(8,128)(2,1)S(1)} custom-call(s32[2]{0:T(128)S(1)} %pad_add_fusion.6.sel_ref, s32[384]{0:T(512)S(1)} %reshape.43.cols_ref, s32[64]{0:T(128)S(1)} %reshape.44.counts_ref, bf16[8,8,6,128,128]{4,3,2,1,0:T(8,128)(2,1)S(1)} %copy-done.1, bf16[2,256,256]{2,1,0:T(8,128)(2,1)S(1)} %get-tuple-element.11.own_ref, ...), custom_call_target="tpu_custom_call" | custom-call | tf_op jit(solution)/shard_map/backward_tiles/pallas_call | solution.py:208
  144.8 1.1 collective-permute-start.30
  146.1 2.5 %backward_tiles.9 = bf16[8,256,128]{2,1,0:T(8,128)(2,1)S(1)} custom-call(s32[2]{0:T(128)S(1)} %pad_add_fusion.1.sel_ref, s32[384]{0:T(512)S(1)} %reshape.43.cols_ref, s32[64]{0:T(128)S(1)} %reshape.44.counts_ref, bf16[8,8,6,128,128]{4,3,2,1,0:T(8,128)(2,1)S(1)} %copy-done.1, bf16[2,256,256]{2,1,0:T(8,128)(2,1)S(1)} %get-tuple-element.11.own_ref, ...), custom_call_target="tpu_custom_call" | custom-call | tf_op jit(solution)/shard_map/backward_tiles/pallas_call | solution.py:208
  148.6 4.2 %collective-permute-start.12 = (bf16[8,256,128]{2,1,0:T(8,128)(2,1)S(1)}, bf16[8,256,128]{2,1,0:T(8,128)(2,1)}, u32[]{:S(2)}, u32[]{:S(2)}) collective-permute-start(bf16[8,256,128]{2,1,0:T(8,128)(2,1)S(1)} %backward_tiles.9), channel_id=1, source_target_pairs={{0,102},{1,71},{2,36},{3,5},{4,2},{5,99},{6,64},{7,33},{8,110},{9,... | collective-permute-start | bytes 1572872 | tf_op jit(solution)/shard_map/ppermute | solution.py:50
  152.8 2.5 %backward_tiles.10 = bf16[8,256,128]{2,1,0:T(8,128)(2,1)S(1)} custom-call(s32[2]{0:T(128)S(1)} %pad_add_fusion.2.sel_ref, s32[384]{0:T(512)S(1)} %reshape.43.cols_ref, s32[64]{0:T(128)S(1)} %reshape.44.counts_ref, bf16[8,8,6,128,128]{4,3,2,1,0:T(8,128)(2,1)S(1)} %copy-done.1, bf16[2,256,256]{2,1,0:T(8,128)(2,1)S(1)} %get-tuple-element.11.own_ref, ...), custom_call_target="tpu_custom_call" | custom-call | tf_op jit(solution)/shard_map/backward_tiles/pallas_call | solution.py:208
  155.3 2.5 %backward_tiles.15 = bf16[8,256,128]{2,1,0:T(8,128)(2,1)S(1)} custom-call(s32[2]{0:T(128)S(1)} %pad_add_fusion.7.sel_ref, s32[384]{0:T(512)S(1)} %reshape.43.cols_ref, s32[64]{0:T(128)S(1)} %reshape.44.counts_ref, bf16[8,8,6,128,128]{4,3,2,1,0:T(8,128)(2,1)S(1)} %copy-done.1, bf16[2,256,256]{2,1,0:T(8,128)(2,1)S(1)} %get-tuple-element.11.own_ref, ...), custom_call_target="tpu_custom_call" | custom-call | tf_op jit(solution)/shard_map/backward_tiles/pallas_call | solution.py:208
  157.8 1.2 collective-permute-start.13
  158.9 2.5 %backward_tiles.12 = bf16[8,256,128]{2,1,0:T(8,128)(2,1)S(1)} custom-call(s32[2]{0:T(128)S(1)} %pad_add_fusion.3.sel_ref, s32[384]{0:T(512)S(1)} %reshape.43.cols_ref, s32[64]{0:T(128)S(1)} %reshape.44.counts_ref, bf16[8,8,6,128,128]{4,3,2,1,0:T(8,128)(2,1)S(1)} %copy-done.1, bf16[2,256,256]{2,1,0:T(8,128)(2,1)S(1)} %get-tuple-element.11.own_ref, ...), custom_call_target="tpu_custom_call" | custom-call | tf_op jit(solution)/shard_map/backward_tiles/pallas_call | solution.py:208
  161.4 1.5 collective-permute-start.18
  163.0 2.5 %backward_tiles.14 = bf16[8,256,128]{2,1,0:T(8,128)(2,1)S(1)} custom-call(s32[2]{0:T(128)S(1)} %pad_add_fusion.5.sel_ref, s32[384]{0:T(512)S(1)} %reshape.43.cols_ref, s32[64]{0:T(128)S(1)} %reshape.44.counts_ref, bf16[8,8,6,128,128]{4,3,2,1,0:T(8,128)(2,1)S(1)} %copy-done.1, bf16[2,256,256]{2,1,0:T(8,128)(2,1)S(1)} %get-tuple-element.11.own_ref, ...), custom_call_target="tpu_custom_call" | custom-call | tf_op jit(solution)/shard_map/backward_tiles/pallas_call | solution.py:208
  165.5 4.1 %collective-permute-start.15 = (bf16[8,256,128]{2,1,0:T(8,128)(2,1)S(1)}, bf16[8,256,128]{2,1,0:T(8,128)(2,1)}, u32[]{:S(2)}, u32[]{:S(2)}) collective-permute-start(bf16[8,256,128]{2,1,0:T(8,128)(2,1)S(1)} %backward_tiles.12), channel_id=1, source_target_pairs={{0,110},{1,79},{2,44},{3,13},{4,106},{5,75},{6,40},{7,9},{8,6},{9,... | collective-permute-start | bytes 1572872 | tf_op jit(solution)/shard_map/ppermute | solution.py:50
  169.5 1.7 collective-permute-start.17
  171.2 0.6 fusion.5
  171.8 34.4 %collective-permute-done.12 = bf16[8,256,128]{2,1,0:T(8,128)(2,1)} collective-permute-done((bf16[8,256,128]{2,1,0:T(8,128)(2,1)S(1)}, bf16[8,256,128]{2,1,0:T(8,128)(2,1)}, u32[]{:S(2)}, u32[]{:S(2)}) %collective-permute-start.12) | collective-permute-done | bytes 524320 | tf_op jit(solution)/shard_map/ppermute | solution.py:50
  206.2 19.7 %collective-permute-start.31 = (f32[2,128,256]{2,1,0:T(8,128)S(1)}, f32[2,128,256]{2,1,0:T(8,128)S(1)}, u32[]{:S(2)}, u32[]{:S(2)}) collective-permute-start(f32[2,128,256]{2,1,0:T(8,128)S(1)} %maximum_select_fusion), channel_id=1, source_target_pairs={{0,1},{1,0},{2,3},{3,2},{4,5},{5,4},{6,7},{7,6},{8,9},{9,8},{10,11... | collective-permute-start | bytes 786440 | tf_op jit(solution)/shard_map/ppermute | solution.py:50
  225.9 2.2 convert_add_fusion
  228.4 1.4 collective-permute-done.19
  230.0 0.8 slice_bitcast_fusion
  230.9 5.6 %collective-permute-done.20.got_ref = bf16[2,256,128]{2,1,0:T(8,128)(2,1)S(1)} collective-permute-done((bf16[2,256,128]{2,1,0:T(8,128)(2,1)S(1)}, bf16[2,256,128]{2,1,0:T(8,128)(2,1)S(1)}, u32[]{:S(2)}, u32[]{:S(2)}) %collective-permute-start.20) | collective-permute-done | bytes 131104 | tf_op jit(solution)/shard_map/ppermute | solution.py:50
  236.5 0.8 final_rows.1
  (83 shorter events, 3.2 us)
Async XLA Ops:
  0.6 29.4 %collective-permute-start.7 = (bf16[1024,256]{1,0:T(8,128)(2,1)}, bf16[1024,256]{1,0:T(8,128)(2,1)S(1)}, u32[]{:S(2)}, u32[]{:S(2)}) collective-permute-start(bf16[1024,256]{1,0:T(8,128)(2,1)} %feat_ref.1), channel_id=1, source_target_pairs={{104,0},{73,1},{42,2},{11,3},{108,4},{77,5},{46,6},{15,7},{0,8},{9... | collective-permute-start | bytes 1572872 | tf_op jit(solution)/shard_map/ppermute | solution.py:50
  3.8 29.0 %collective-permute-start.2 = (bf16[1024,256]{1,0:T(8,128)(2,1)}, bf16[1024,256]{1,0:T(8,128)(2,1)S(1)}, u32[]{:S(2)}, u32[]{:S(2)}) collective-permute-start(bf16[1024,256]{1,0:T(8,128)(2,1)} %feat_ref.1), channel_id=1, source_target_pairs={{120,0},{89,1},{58,2},{27,3},{124,4},{93,5},{62,6},{31,7},{112,8},... | collective-permute-start | bytes 1572872 | tf_op jit(solution)/shard_map/ppermute | solution.py:50
  7.3 39.5 %collective-permute-start = (bf16[1024,256]{1,0:T(8,128)(2,1)}, bf16[1024,256]{1,0:T(8,128)(2,1)S(1)}, u32[]{:S(2)}, u32[]{:S(2)}) collective-permute-start(bf16[1024,256]{1,0:T(8,128)(2,1)} %feat_ref.1), channel_id=1, source_target_pairs={{110,0},{79,1},{44,2},{13,3},{106,4},{75,5},{40,6},{9,7},{6,8},{10... | collective-permute-start | bytes 1572872 | tf_op jit(solution)/shard_map/ppermute | solution.py:50
  10.9 58.4 %collective-permute-start.6 = (bf16[1024,256]{1,0:T(8,128)(2,1)}, bf16[1024,256]{1,0:T(8,128)(2,1)}, u32[]{:S(2)}, u32[]{:S(2)}) collective-permute-start(bf16[1024,256]{1,0:T(8,128)(2,1)} %feat_ref.1), channel_id=1, source_target_pairs={{126,0},{95,1},{60,2},{29,3},{122,4},{91,5},{56,6},{25,7},{118,8},... | collective-permute-start | bytes 1572872 | tf_op jit(solution)/shard_map/ppermute | solution.py:50
  12.7 60.3 %collective-permute-start.5 = (bf16[1024,256]{1,0:T(8,128)(2,1)}, bf16[1024,256]{1,0:T(8,128)(2,1)S(1)}, u32[]{:S(2)}, u32[]{:S(2)}) collective-permute-start(bf16[1024,256]{1,0:T(8,128)(2,1)} %feat_ref.1), channel_id=1, source_target_pairs={{102,0},{71,1},{36,2},{5,3},{2,4},{99,5},{64,6},{33,7},{110,8},{79... | collective-permute-start | bytes 1572872 | tf_op jit(solution)/shard_map/ppermute | solution.py:50
  30.1 0.8 copy-start.4
  30.9 45.7 %collective-permute-start.4 = (bf16[1024,256]{1,0:T(8,128)(2,1)}, bf16[1024,256]{1,0:T(8,128)(2,1)S(1)}, u32[]{:S(2)}, u32[]{:S(2)}) collective-permute-start(bf16[1024,256]{1,0:T(8,128)(2,1)} %feat_ref.1), channel_id=1, source_target_pairs={{0,0},{97,1},{66,2},{35,3},{4,4},{101,5},{70,6},{39,7},{8,8},{105,... | collective-permute-start | bytes 1572872 | tf_op jit(solution)/shard_map/ppermute | solution.py:50
  32.8 47.3 %collective-permute-start.3 = (bf16[1024,256]{1,0:T(8,128)(2,1)S(1)}, bf16[1024,256]{1,0:T(8,128)(2,1)S(1)}, u32[]{:S(2)}, u32[]{:S(2)}) collective-permute-start(bf16[1024,256]{1,0:T(8,128)(2,1)S(1)} %collective-permute-done.2.shard_ref), channel_id=1, source_target_pairs={{8,0},{9,1},{10,2},{11,3},{12,4},{13,5},{14,6},{15,7},{0,8},{1,9},... | collective-permute-start | bytes 1572872 | tf_op jit(solution)/shard_map/ppermute | solution.py:50
  46.8 36.9 %collective-permute-start.1 = (bf16[1024,256]{1,0:T(8,128)(2,1)S(1)}, bf16[1024,256]{1,0:T(8,128)(2,1)S(1)}, u32[]{:S(2)}, u32[]{:S(2)}) collective-permute-start(bf16[1024,256]{1,0:T(8,128)(2,1)S(1)} %collective-permute-done.shard_ref), channel_id=1, source_target_pairs={{120,0},{121,1},{122,2},{123,3},{124,4},{125,5},{126,6},{127,7},{1... | collective-permute-start | bytes 1572872 | tf_op jit(solution)/shard_map/ppermute | solution.py:50
  54.7 4.6 %copy-start = (bf16[8,8,6,128,128]{4,3,2,1,0:T(8,128)(2,1)S(1)}, bf16[8,8,6,128,128]{4,3,2,1,0:T(8,128)(2,1)}, u32[]{:S(2)}) copy-start(bf16[8,8,6,128,128]{4,3,2,1,0:T(8,128)(2,1)} %tiles_ref.31) | copy-start | bytes 37748740
  59.3 1.0 copy-start.5
  80.1 16.3 %copy-start.9 = (s32[1024]{0:T(1024)S(1)}, s32[1024]{0:T(1024)}, u32[]{:S(2)}) copy-start(s32[1024]{0:T(1024)} %param.14) | copy-start | bytes 12292
  83.6 14.4 %copy-start.10 = (s32[1024]{0:T(1024)S(1)}, s32[1024]{0:T(1024)}, u32[]{:S(2)}) copy-start(s32[1024]{0:T(1024)} %param.15) | copy-start | bytes 12292
  83.6 23.1 %copy-start.2 = (bf16[1024,256]{1,0:T(8,128)(2,1)S(1)}, bf16[1024,256]{1,0:T(8,128)(2,1)}, u32[]{:S(2)}) copy-start(bf16[1024,256]{1,0:T(8,128)(2,1)} %feat_ref.1) | copy-start | bytes 1572868
  83.7 23.1 %copy-start.3 = (bf16[1024,256]{1,0:T(8,128)(2,1)S(1)}, bf16[1024,256]{1,0:T(8,128)(2,1)}, u32[]{:S(2)}) copy-start(bf16[1024,256]{1,0:T(8,128)(2,1)} %cot_ref.1) | copy-start | bytes 1572868
  83.7 23.1 %copy-start.6 = (bf16[256,256]{1,0:T(8,128)(2,1)S(1)}, bf16[256,256]{1,0:T(8,128)(2,1)}, u32[]{:S(2)}) copy-start(bf16[256,256]{1,0:T(8,128)(2,1)} %ws_ref.1) | copy-start | bytes 393220
  83.7 23.1 %copy-start.8 = (f32[256]{0:T(256)S(1)}, f32[256]{0:T(256)}, u32[]{:S(2)}) copy-start(f32[256]{0:T(256)} %param.19) | copy-start | bytes 3076
  87.3 10.3 %collective-permute-start.8 = (bf16[2,256,256]{2,1,0:T(8,128)(2,1)S(1)}, bf16[2,256,256]{2,1,0:T(8,128)(2,1)S(1)}, u32[]{:S(2)}, u32[]{:S(2)}) collective-permute-start(bf16[2,256,256]{2,1,0:T(8,128)(2,1)S(1)} %fusion.1), channel_id=1, source_target_pairs={{0,1},{1,0},{2,3},{3,2},{4,5},{5,4},{6,7},{7,6},{8,9},{9,8},{10,11... | collective-permute-start | bytes 786440 | tf_op jit(solution)/shard_map/ppermute | solution.py:50
  97.6 9.1 %collective-permute-start.9 = (bf16[2,256,256]{2,1,0:T(8,128)(2,1)S(1)}, bf16[2,256,256]{2,1,0:T(8,128)(2,1)S(1)}, u32[]{:S(2)}, u32[]{:S(2)}) collective-permute-start(bf16[2,256,256]{2,1,0:T(8,128)(2,1)S(1)} %fusion.own_ref), channel_id=1, source_target_pairs={{0,2},{1,3},{2,0},{3,1},{4,6},{5,7},{6,4},{7,5},{8,10},{9,11},{10,... | collective-permute-start | bytes 786440 | tf_op jit(solution)/shard_map/ppermute | solution.py:50
  106.8 0.9 copy-start.7
  109.2 2.0 collective-permute-start.22
  110.5 1.4 collective-permute-start.21
  112.0 4.0 %collective-permute-start.23 = (bf16[144,256]{1,0:T(8,128)(2,1)S(1)}, bf16[144,256]{1,0:T(8,128)(2,1)S(1)}, u32[]{:S(2)}, u32[]{:S(2)}) collective-permute-start(bf16[144,256]{1,0:T(8,128)(2,1)S(1)} %maximum_maximum_fusion), channel_id=1, source_target_pairs={{0,32},{1,33},{2,34},{3,35},{4,36},{5,37},{6,38},{7,39},{8,40},{9,... | collective-permute-start | bytes 221192 | tf_op jit(solution)/shard_map/ppermute | solution.py:50
  112.1 6.1 %collective-permute-start.24 = (bf16[144,256]{1,0:T(8,128)(2,1)S(1)}, bf16[144,256]{1,0:T(8,128)(2,1)S(1)}, u32[]{:S(2)}, u32[]{:S(2)}) collective-permute-start(bf16[144,256]{1,0:T(8,128)(2,1)S(1)} %maximum_maximum_fusion), channel_id=1, source_target_pairs={{0,64},{1,65},{2,66},{3,67},{4,68},{5,69},{6,70},{7,71},{8,72},{9,... | collective-permute-start | bytes 221192 | tf_op jit(solution)/shard_map/ppermute | solution.py:50
  114.2 5.4 %collective-permute-start.25 = (bf16[144,256]{1,0:T(8,128)(2,1)S(1)}, bf16[144,256]{1,0:T(8,128)(2,1)S(1)}, u32[]{:S(2)}, u32[]{:S(2)}) collective-permute-start(bf16[144,256]{1,0:T(8,128)(2,1)S(1)} %maximum_maximum_fusion), channel_id=1, source_target_pairs={{0,96},{1,97},{2,98},{3,99},{4,100},{5,101},{6,102},{7,103},{8,104... | collective-permute-start | bytes 221192 | tf_op jit(solution)/shard_map/ppermute | solution.py:50
  119.8 5.8 %collective-permute-start.26 = (bf16[144,256]{1,0:T(8,128)(2,1)S(1)}, bf16[144,256]{1,0:T(8,128)(2,1)S(1)}, u32[]{:S(2)}, u32[]{:S(2)}) collective-permute-start(bf16[144,256]{1,0:T(8,128)(2,1)S(1)} %maximum_maximum_fusion.1), channel_id=1, source_target_pairs={{0,8},{1,9},{2,10},{3,11},{4,12},{5,13},{6,14},{7,15},{8,0},{9,1},... | collective-permute-start | bytes 221192 | tf_op jit(solution)/shard_map/ppermute | solution.py:50
  119.9 5.7 %collective-permute-start.27 = (bf16[144,256]{1,0:T(8,128)(2,1)S(1)}, bf16[144,256]{1,0:T(8,128)(2,1)S(1)}, u32[]{:S(2)}, u32[]{:S(2)}) collective-permute-start(bf16[144,256]{1,0:T(8,128)(2,1)S(1)} %maximum_maximum_fusion.1), channel_id=1, source_target_pairs={{0,16},{1,17},{2,18},{3,19},{4,20},{5,21},{6,22},{7,23},{8,24},{9,... | collective-permute-start | bytes 221192 | tf_op jit(solution)/shard_map/ppermute | solution.py:50
  120.9 5.5 %collective-permute-start.28 = (bf16[144,256]{1,0:T(8,128)(2,1)S(1)}, bf16[144,256]{1,0:T(8,128)(2,1)S(1)}, u32[]{:S(2)}, u32[]{:S(2)}) collective-permute-start(bf16[144,256]{1,0:T(8,128)(2,1)S(1)} %maximum_maximum_fusion.1), channel_id=1, source_target_pairs={{0,24},{1,25},{2,26},{3,27},{4,28},{5,29},{6,30},{7,31},{8,16},{9,... | collective-permute-start | bytes 221192 | tf_op jit(solution)/shard_map/ppermute | solution.py:50
  123.8 2.9 %collective-permute-start.10 = (bf16[2,256,256]{2,1,0:T(8,128)(2,1)S(1)}, bf16[2,256,256]{2,1,0:T(8,128)(2,1)S(1)}, u32[]{:S(2)}, u32[]{:S(2)}) collective-permute-start(bf16[2,256,256]{2,1,0:T(8,128)(2,1)S(1)} %get-tuple-element.11.own_ref), channel_id=1, source_target_pairs={{0,1},{1,0},{2,3},{3,2},{4,5},{5,4},{6,7},{7,6},{8,9},{9,8},{10,11... | collective-permute-start | bytes 786440 | tf_op jit(solution)/shard_map/ppermute | solution.py:50
  126.5 18.2 %collective-permute-start.29 = (bf16[144,256]{1,0:T(8,128)(2,1)S(1)}, bf16[144,256]{1,0:T(8,128)(2,1)S(1)}, u32[]{:S(2)}, u32[]{:S(2)}) collective-permute-start(bf16[144,256]{1,0:T(8,128)(2,1)S(1)} %maximum_maximum_fusion.2), channel_id=1, source_target_pairs={{0,4},{1,5},{2,6},{3,7},{4,0},{5,1},{6,2},{7,3},{8,12},{9,13},{10,... | collective-permute-start | bytes 221192 | tf_op jit(solution)/shard_map/ppermute | solution.py:50
  126.7 4.6 %copy-start.1 = (bf16[8,8,6,128,128]{4,3,2,1,0:T(8,128)(2,1)S(1)}, bf16[8,8,6,128,128]{4,3,2,1,0:T(8,128)(2,1)}, u32[]{:S(2)}) copy-start(bf16[8,8,6,128,128]{4,3,2,1,0:T(8,128)(2,1)} %tiles_ref.31) | copy-start | bytes 37748740
  133.8 35.7 %collective-permute-start.11 = (bf16[8,256,128]{2,1,0:T(8,128)(2,1)S(1)}, bf16[8,256,128]{2,1,0:T(8,128)(2,1)}, u32[]{:S(2)}, u32[]{:S(2)}) collective-permute-start(bf16[8,256,128]{2,1,0:T(8,128)(2,1)S(1)} %backward_tiles.8), channel_id=1, source_target_pairs={{0,0},{1,97},{2,66},{3,35},{4,4},{5,101},{6,70},{7,39},{8,8},{9,10... | collective-permute-start | bytes 1572872 | tf_op jit(solution)/shard_map/ppermute | solution.py:50
  140.0 17.7 %collective-permute-start.14 = (bf16[8,256,128]{2,1,0:T(8,128)(2,1)S(1)}, bf16[8,256,128]{2,1,0:T(8,128)(2,1)S(1)}, u32[]{:S(2)}, u32[]{:S(2)}) collective-permute-start(bf16[8,256,128]{2,1,0:T(8,128)(2,1)S(1)} %backward_tiles.11), channel_id=1, source_target_pairs={{0,120},{1,121},{2,122},{3,123},{4,124},{5,125},{6,126},{7,127},{8... | collective-permute-start | bytes 1572872 | tf_op jit(solution)/shard_map/ppermute | solution.py:50
  144.4 17.0 %collective-permute-start.16 = (bf16[8,256,128]{2,1,0:T(8,128)(2,1)S(1)}, bf16[8,256,128]{2,1,0:T(8,128)(2,1)S(1)}, u32[]{:S(2)}, u32[]{:S(2)}) collective-permute-start(bf16[8,256,128]{2,1,0:T(8,128)(2,1)S(1)} %backward_tiles.13), channel_id=1, source_target_pairs={{0,8},{1,9},{2,10},{3,11},{4,12},{5,13},{6,14},{7,15},{8,0},{9,1},... | collective-permute-start | bytes 1572872 | tf_op jit(solution)/shard_map/ppermute | solution.py:50
  144.8 20.6 %collective-permute-start.30 = (f32[128,256]{1,0:T(8,128)S(1)}, f32[128,256]{1,0:T(8,128)S(1)}, u32[]{:S(2)}, u32[]{:S(2)}) collective-permute-start(f32[128,256]{1,0:T(8,128)S(1)} %get-tuple-element.20), channel_id=1, source_target_pairs={{0,2},{1,3},{2,0},{3,1},{4,6},{5,7},{6,4},{7,5},{8,10},{9,11},{10,... | collective-permute-start | bytes 393224 | tf_op jit(solution)/shard_map/ppermute | solution.py:50
  148.6 57.6 %collective-permute-start.12 = (bf16[8,256,128]{2,1,0:T(8,128)(2,1)S(1)}, bf16[8,256,128]{2,1,0:T(8,128)(2,1)}, u32[]{:S(2)}, u32[]{:S(2)}) collective-permute-start(bf16[8,256,128]{2,1,0:T(8,128)(2,1)S(1)} %backward_tiles.9), channel_id=1, source_target_pairs={{0,102},{1,71},{2,36},{3,5},{4,2},{5,99},{6,64},{7,33},{8,110},{9,... | collective-permute-start | bytes 1572872 | tf_op jit(solution)/shard_map/ppermute | solution.py:50
  157.8 68.1 %collective-permute-start.13 = (bf16[8,256,128]{2,1,0:T(8,128)(2,1)S(1)}, bf16[8,256,128]{2,1,0:T(8,128)(2,1)}, u32[]{:S(2)}, u32[]{:S(2)}) collective-permute-start(bf16[8,256,128]{2,1,0:T(8,128)(2,1)S(1)} %backward_tiles.10), channel_id=1, source_target_pairs={{0,126},{1,95},{2,60},{3,29},{4,122},{5,91},{6,56},{7,25},{8,118},... | collective-permute-start | bytes 1572872 | tf_op jit(solution)/shard_map/ppermute | solution.py:50
  161.4 64.5 %collective-permute-start.18 = (bf16[8,256,128]{2,1,0:T(8,128)(2,1)S(1)}, bf16[8,256,128]{2,1,0:T(8,128)(2,1)}, u32[]{:S(2)}, u32[]{:S(2)}) collective-permute-start(bf16[8,256,128]{2,1,0:T(8,128)(2,1)S(1)} %backward_tiles.15), channel_id=1, source_target_pairs={{0,104},{1,73},{2,42},{3,11},{4,108},{5,77},{6,46},{7,15},{8,0},{9... | collective-permute-start | bytes 1572872 | tf_op jit(solution)/shard_map/ppermute | solution.py:50
  165.5 60.5 %collective-permute-start.15 = (bf16[8,256,128]{2,1,0:T(8,128)(2,1)S(1)}, bf16[8,256,128]{2,1,0:T(8,128)(2,1)}, u32[]{:S(2)}, u32[]{:S(2)}) collective-permute-start(bf16[8,256,128]{2,1,0:T(8,128)(2,1)S(1)} %backward_tiles.12), channel_id=1, source_target_pairs={{0,110},{1,79},{2,44},{3,13},{4,106},{5,75},{6,40},{7,9},{8,6},{9,... | collective-permute-start | bytes 1572872 | tf_op jit(solution)/shard_map/ppermute | solution.py:50
  169.5 56.4 %collective-permute-start.17 = (bf16[8,256,128]{2,1,0:T(8,128)(2,1)S(1)}, bf16[8,256,128]{2,1,0:T(8,128)(2,1)}, u32[]{:S(2)}, u32[]{:S(2)}) collective-permute-start(bf16[8,256,128]{2,1,0:T(8,128)(2,1)S(1)} %backward_tiles.14), channel_id=1, source_target_pairs={{0,120},{1,89},{2,58},{3,27},{4,124},{5,93},{6,62},{7,31},{8,112},... | collective-permute-start | bytes 1572872 | tf_op jit(solution)/shard_map/ppermute | solution.py:50
  206.2 22.1 %collective-permute-start.31 = (f32[2,128,256]{2,1,0:T(8,128)S(1)}, f32[2,128,256]{2,1,0:T(8,128)S(1)}, u32[]{:S(2)}, u32[]{:S(2)}) collective-permute-start(f32[2,128,256]{2,1,0:T(8,128)S(1)} %maximum_select_fusion), channel_id=1, source_target_pairs={{0,1},{1,0},{2,3},{3,2},{4,5},{5,4},{6,7},{7,6},{8,9},{9,8},{10,11... | collective-permute-start | bytes 786440 | tf_op jit(solution)/shard_map/ppermute | solution.py:50
  228.2 1.6 collective-permute-start.19
  229.9 6.5 %collective-permute-start.20 = (bf16[2,256,128]{2,1,0:T(8,128)(2,1)S(1)}, bf16[2,256,128]{2,1,0:T(8,128)(2,1)S(1)}, u32[]{:S(2)}, u32[]{:S(2)}) collective-permute-start(bf16[2,256,128]{2,1,0:T(8,128)(2,1)S(1)} %fusion.3), channel_id=1, source_target_pairs={{0,2},{1,3},{2,0},{3,1},{4,6},{5,7},{6,4},{7,5},{8,10},{9,11},{10,... | collective-permute-start | bytes 393224 | tf_op jit(solution)/shard_map/ppermute | solution.py:50

commit v2 on v1

--- a/solution.py
+++ b/solution.py
@@ -58,43 +58,68 @@
     return pltpu.CompilerParams(vmem_limit_bytes=VMEM)
 
 
+def load_tiles(tiles_ref, dist, held_ref, sems):
+    copies = [
+        pltpu.make_async_copy(tiles_ref.at[b, dist], held_ref.at[b], sems.at[b]) for b in range(NB)
+    ]
+    for copy in copies:
+        copy.start()
+    return copies
+
+
+def tile_scratch():
+    return [pltpu.VMEM((NB, NS, BS, BS), jnp.bfloat16), pltpu.SemaphoreType.DMA((NB,))]
+
+
+def tile_cost():
+    return pl.CostEstimate(
+        flops=2 * NB * NS * BS * BS * F, bytes_accessed=8 << 20, transcendentals=0
+    )
+
+
+SMEM = pl.BlockSpec(memory_space=pltpu.SMEM)
+HBM = pl.BlockSpec(memory_space=pltpu.HBM)
+WHOLE = pl.BlockSpec(memory_space=pltpu.VMEM)
+
+
 def forward_body(first, sel_ref, cols_ref, counts_ref, tiles_ref, shard_ref, *rest):
-    out_ref = rest[-1]
-    step = pl.program_id(0)
+    out_ref, held_ref, sems = rest[-3:]
     dist = sel_ref[0]
-    for inner in range(2):
-        b = step * 2 + inner
+    copies = load_tiles(tiles_ref, dist, held_ref, sems)
+    for b in range(NB):
+        copies[b].wait()
         count = counts_ref[b * ND + dist]
-        left, right = [], []
-        for s in range(NS):
-            col = cols_ref[(b * ND + dist) * NS + s]
-            block = shard_ref[pl.ds(pl.multiple_of(col * BS, BS), BS), :]
-            right.append(jnp.where(s < count, block, jnp.zeros((), block.dtype)))
-            left.append(tiles_ref[inner, 0, s])
-        summed = jnp.dot(
-            jnp.concatenate(left, 1), jnp.concatenate(right, 0), preferred_element_type=jnp.float32
-        )
-        rows = pl.ds(pl.multiple_of(b * BS, BS), BS)
-        if first:
-            out_ref[rows, :] = summed
-        else:
-            out_ref[rows, :] = rest[0][rows, :] + summed
+        rows = slice(b * BS, (b + 1) * BS)
+        out_ref[rows, :] = jnp.zeros((BS, F), jnp.float32) if first else rest[0][rows, :]
+        for s in range(0, NS, 2):
+
+            @pl.when(s < count)
+            def _():
+                left, right = [], []
+                for k in range(s, s + 2):
+                    col = cols_ref[(b * ND + dist) * NS + k]
+                    block = shard_ref[pl.ds(pl.multiple_of(col * BS, BS), BS), :]
+                    if k > s:
+                        block = jnp.where(k < count, block, jnp.zeros((), block.dtype))
+                    right.append(block)
+                    left.append(held_ref[b, k])
+                out_ref[rows, :] += jnp.dot(
+                    jnp.concatenate(left, 1),
+                    jnp.concatenate(right, 0),
+                    preferred_element_type=jnp.float32,
+                )
 
 
 def forward_call(dist, cols, counts, tiles, shard, total):
     first = total is None
-    whole = pl.BlockSpec((NB * BS, F), lambda i, *_: (0, 0))
-    in_specs = [
-        pl.BlockSpec((2, 1, NS, BS, BS), lambda i, sel, c, n: (i, sel[0], 0, 0, 0)),
-        whole,
-    ] + ([] if first else [whole])
     return pl.pallas_call(
         functools.partial(forward_body, first),
         out_shape=jax.ShapeDtypeStruct((NB * BS, F), jnp.float32),
-        grid_spec=pltpu.PrefetchScalarGridSpec(
-            num_scalar_prefetch=3, grid=(NB // 2,), in_specs=in_specs, out_specs=whole
-        ),
+        in_specs=[SMEM] * 3 + [HBM, WHOLE] + ([] if first else [WHOLE]),
+        out_specs=WHOLE,
+        scratch_shapes=tile_scratch(),
         compiler_params=params(),
+        cost_estimate=tile_cost(),
         name="forward_tiles",
     )(dist, cols, counts, tiles, shard, *([] if first else [total]))
 
@@ -161,63 +186,57 @@
     )(rep, own, got, feat, cot, mask, inv, inv_t, w_self, w_neigh, bias)
 
 
-def backward_body(added, sel_ref, cols_ref, counts_ref, tiles_ref, own_ref, got_ref, *rest):
-    out_ref, acc_ref = rest[-2:]
-    step = pl.program_id(0)
-    dist = sel_ref[0]
-    core = sel_ref[1]
-
-    @pl.when(step == 0)
-    def _():
-        for c in range(NB):
-            if added:
-                acc_ref[c] = rest[0][c].astype(jnp.float32)
-            else:
-                acc_ref[c] = jnp.zeros((F, BS), jnp.float32)
-
-    mine = step % 2 == core
-    part = step // 2
-    message = jnp.where(mine, own_ref[part], got_ref[part])
-    for inner in range(2):
-        b = step * 2 + inner
-        count = counts_ref[b * ND + dist]
-        left = message[:, inner * BS : (inner + 1) * BS]
-        for s in range(0, NS, 2):
-            right = jnp.concatenate([tiles_ref[inner, 0, s], tiles_ref[inner, 0, s + 1]], 1)
-            product = jnp.dot(left, right, preferred_element_type=jnp.float32)
-            for k in range(2):
-                col = cols_ref[(b * ND + dist) * NS + s + k]
-                col = jnp.where(s + k < count, col, NB)
-                acc_ref[col] += product[:, k * BS : (k + 1) * BS]
-
-    @pl.when(step == NB // 2 - 1)
-    def _():
-        for c in range(NB):
-            out_ref[c] = acc_ref[c].astype(jnp.bfloat16)
-
-
-def backward_call(sel, cols, counts, tiles, own, got, extra):
-    added = extra is not None
-    whole = pl.BlockSpec((NB, F, BS), lambda i, *_: (0, 0, 0))
-    message = pl.BlockSpec((2, F, 256), lambda i, *_: (0, 0, 0))
-    in_specs = [
-        pl.BlockSpec((2, 1, NS, BS, BS), lambda i, sel, c, n: (i, sel[0], 0, 0, 0)),
-        message,
-        message,
-    ] + ([whole] if added else [])
+def backward_body(
+    added, passed, sel_ref, cols_ref, counts_ref, tiles_ref, own_ref, got_ref, *rest
+):
+    acc_ref, held_ref, sems = rest[-3:]
+    out_ref = rest[added + passed]
+    dist, core = sel_ref[0], sel_ref[1]
+    copies = load_tiles(tiles_ref, dist, held_ref, sems)
+    for c in range(NB):
+        if added:
+            acc_ref[c] = rest[0][c].astype(jnp.float32)
+        else:
+            acc_ref[c] = jnp.zeros((F, BS), jnp.float32)
+    for quarter in range(NB // 2):
+        mine = core == quarter % 2
+        message = jnp.where(mine, own_ref[quarter // 2], got_ref[quarter // 2])
+        for inner in range(2):
+            b = quarter * 2 + inner
+            copies[b].wait()
+            count = counts_ref[b * ND + dist]
+            left = message[:, inner * BS : (inner + 1) * BS]
+            for s in range(0, NS, 2):
+
+                @pl.when(s < count)
+                def _():
+                    right = jnp.concatenate([held_ref[b, s], held_ref[b, s + 1]], 1)
+                    product = jnp.dot(left, right, preferred_element_type=jnp.float32)
+                    for k in range(2):
+                        col = cols_ref[(b * ND + dist) * NS + s + k]
+                        if k > 0:
+                            col = jnp.where(s + k < count, col, NB)
+                        acc_ref[col] += product[:, k * BS : (k + 1) * BS]
+
+    for c in range(NB):
+        out_ref[c] = acc_ref[c].astype(jnp.bfloat16)
+
+
+def backward_call(sel, cols, counts, tiles, own, got, extra, along):
+    added, passed = extra is not None, along is not None
+    made = jax.ShapeDtypeStruct((NB, F, BS), jnp.bfloat16)
+    hbm_along = [HBM] if passed else []
     return pl.pallas_call(
-        functools.partial(backward_body, added),
-        out_shape=jax.ShapeDtypeStruct((NB, F, BS), jnp.bfloat16),
-        grid_spec=pltpu.PrefetchScalarGridSpec(
-            num_scalar_prefetch=3,
-            grid=(NB // 2,),
-            in_specs=in_specs,
-            out_specs=whole,
-            scratch_shapes=[pltpu.VMEM((NB + 1, F, BS), jnp.float32)],
-        ),
+        functools.partial(backward_body, added, passed),
+        out_shape=(made,) + ((jax.ShapeDtypeStruct(along.shape, along.dtype),) if passed else ()),
+        in_specs=[SMEM] * 3 + [HBM, WHOLE, WHOLE] + ([WHOLE] if added else []) + hbm_along,
+        out_specs=(WHOLE,) + tuple(hbm_along),
+        scratch_shapes=[pltpu.VMEM((NB + 1, F, BS), jnp.float32)] + tile_scratch(),
+        input_output_aliases={6 + added: 1} if passed else {},
         compiler_params=params(),
+        cost_estimate=tile_cost(),
         name="backward_tiles",
-    )(sel, cols, counts, tiles, own, got, *([extra] if added else []))
+    )(sel, cols, counts, tiles, own, got, *([extra] if added else []), *([along] if passed else []))
 
 
 def final_body(kept_ref, got_ref, term_ref, out_ref):
@@ -314,21 +333,24 @@
     )
     back_got = send(back_own, flip_pairs(dcore=1))
 
-    grad_self, grad_neigh, grad_bias = weight_grads(
-        grads, sums, zh, core, rows * lax.axis_size("blk")
-    )
-
     extra = {}
     arrived = None
-    for k, via in reversed(PLAN):
+    for step, (k, via) in enumerate(reversed(PLAN)):
         sel = jnp.stack([distance_of(k), core])
-        made = backward_call(sel, cols, live, tiles, back_own, back_got, extra.get(k))
-        moved = send(made, back(column_pairs(k, via)))
+        made = backward_call(
+            sel, cols, live, tiles, back_own, back_got, extra.get(k), grads if step == 3 else None
+        )
+        if step == 3:
+            grads = made[1]
+        moved = send(made[0], back(column_pairs(k, via)))
         if via is None:
             moved = moved.astype(jnp.float32)
             arrived = moved if arrived is None else arrived + moved
         else:
             extra[k ^ via] = moved
+    grad_self, grad_neigh, grad_bias = weight_grads(
+        grads, sums, zh, core, rows * lax.axis_size("blk")
+    )
 
     parts = arrived.reshape(2, 2, 2, F, BS)
     away = lax.dynamic_index_in_dim(parts, 1 - core, 1, keepdims=False).astype(jnp.bfloat16)

time: 238 us -> 251 us (1.055)
  Pallas kernels: 49 us -> 78.6 us
  waiting for transfers between devices: 82.6 us -> 65.3 us
    pallas_call x8, Pallas kernels: 19.8 us -> 43.3 us  [backward_call(): pl.pallas_call(functools.partial(backward_body, added, passed), out_shape...]
    ppermute x32, waiting for transfers between devices: 82.6 us -> 65.3 us  [send(): return lax.ppermute(value, AXES, pairs)]
    pallas_call x8, Pallas kernels: 26.7 us -> 33 us  [forward_call(): pl.pallas_call(functools.partial(forward_body, first), out_shape=jax.Shap...]
  transfers between devices with their start and end apart: 32 -> 32, of which waited for: 12 -> 11; matrix products, arithmetic and copies ran while one was open for 3% -> 3% of each run, Pallas kernels for 18% -> 29%
where the time goes in v2:
time: 251 us; the launch traced here: 250 us
  starting transfers between devices  85.9 us (34%)
  Pallas kernels  78.6 us (31%)
  waiting for transfers between devices  65.3 us (26%)
  local copies, waits for them, and re-layouts  15.2 us (6%)
  other arithmetic  4.08 us (2%)
    ppermute x32, starting transfers between devices, send(): return lax.ppermute(value, AXES, pairs)  85.9 us
    ppermute x32, waiting for transfers between devices, send(): return lax.ppermute(value, AXES, pairs)  65.3 us
    pallas_call x8, Pallas kernels, backward_call(): pl.pallas_call(functools.partial(backward_body, added, passed), out_shape...  43.3 us
    pallas_call x8, Pallas kernels, forward_call(): pl.pallas_call(functools.partial(forward_body, first), out_shape=jax.Shap...  33 us
    unnamed x23, local copies, waits for them, and re-layouts  12.8 us
  transfers between devices with their start and end apart: 32, of which 11 were waited for; matrix products, arithmetic and copies ran while one was open for 3% of the time, Pallas kernels for 29%

profile of v2, /device:TPU:1, one launch (start us, length us, event | category | flops | bytes accessed | tf_op | source)
XLA Modules:
  0.0 250.4 jit_solution(2838003906441115228)
XLA Ops:
  0.6 3.1 %collective-permute-start.7 = (bf16[1024,256]{1,0:T(8,128)(2,1)}, bf16[1024,256]{1,0:T(8,128)(2,1)S(1)}, u32[]{:S(2)}, u32[]{:S(2)}) collective-permute-start(bf16[1024,256]{1,0:T(8,128)(2,1)} %feat_ref.1), channel_id=1, source_target_pairs={{104,0},{73,1},{42,2},{11,3},{108,4},{77,5},{46,6},{15,7},{0,8},{9... | collective-permute-start | bytes 1572872 | tf_op jit(solution)/shard_map/ppermute | solution.py:50
  3.8 3.5 %collective-permute-start.2 = (bf16[1024,256]{1,0:T(8,128)(2,1)}, bf16[1024,256]{1,0:T(8,128)(2,1)S(1)}, u32[]{:S(2)}, u32[]{:S(2)}) collective-permute-start(bf16[1024,256]{1,0:T(8,128)(2,1)} %feat_ref.1), channel_id=1, source_target_pairs={{120,0},{89,1},{58,2},{27,3},{124,4},{93,5},{62,6},{31,7},{112,8},... | collective-permute-start | bytes 1572872 | tf_op jit(solution)/shard_map/ppermute | solution.py:50
  7.3 3.6 %collective-permute-start = (bf16[1024,256]{1,0:T(8,128)(2,1)}, bf16[1024,256]{1,0:T(8,128)(2,1)S(1)}, u32[]{:S(2)}, u32[]{:S(2)}) collective-permute-start(bf16[1024,256]{1,0:T(8,128)(2,1)} %feat_ref.1), channel_id=1, source_target_pairs={{110,0},{79,1},{44,2},{13,3},{106,4},{75,5},{40,6},{9,7},{6,8},{10... | collective-permute-start | bytes 1572872 | tf_op jit(solution)/shard_map/ppermute | solution.py:50
  10.9 1.8 collective-permute-start.6
  12.7 3.2 %collective-permute-start.5 = (bf16[1024,256]{1,0:T(8,128)(2,1)}, bf16[1024,256]{1,0:T(8,128)(2,1)S(1)}, u32[]{:S(2)}, u32[]{:S(2)}) collective-permute-start(bf16[1024,256]{1,0:T(8,128)(2,1)} %feat_ref.1), channel_id=1, source_target_pairs={{102,0},{71,1},{36,2},{5,3},{2,4},{99,5},{64,6},{33,7},{110,8},{79... | collective-permute-start | bytes 1572872 | tf_op jit(solution)/shard_map/ppermute | solution.py:50
  15.9 14.2 %collective-permute-done.7.shard_ref = bf16[1024,256]{1,0:T(8,128)(2,1)S(1)} collective-permute-done((bf16[1024,256]{1,0:T(8,128)(2,1)}, bf16[1024,256]{1,0:T(8,128)(2,1)S(1)}, u32[]{:S(2)}, u32[]{:S(2)}) %collective-permute-start.7) | collective-permute-done | bytes 524320 | tf_op jit(solution)/shard_map/ppermute | solution.py:50
  30.1 0.8 copy-done.4
  30.9 1.9 collective-permute-start.4
  32.8 2.0 collective-permute-start.3
  34.8 11.9 %collective-permute-done.shard_ref = bf16[1024,256]{1,0:T(8,128)(2,1)S(1)} collective-permute-done((bf16[1024,256]{1,0:T(8,128)(2,1)}, bf16[1024,256]{1,0:T(8,128)(2,1)S(1)}, u32[]{:S(2)}, u32[]{:S(2)}) %collective-permute-start) | collective-permute-done | bytes 524320 | tf_op jit(solution)/shard_map/ppermute | solution.py:50
  46.8 6.1 %collective-permute-start.1 = (bf16[1024,256]{1,0:T(8,128)(2,1)S(1)}, bf16[1024,256]{1,0:T(8,128)(2,1)S(1)}, u32[]{:S(2)}, u32[]{:S(2)}) collective-permute-start(bf16[1024,256]{1,0:T(8,128)(2,1)S(1)} %collective-permute-done.shard_ref), channel_id=1, source_target_pairs={{120,0},{121,1},{122,2},{123,3},{124,4},{125,5},{126,6},{127,7},{1... | collective-permute-start | bytes 1572872 | tf_op jit(solution)/shard_map/ppermute | solution.py:50
  52.9 0.9 copy.16
  53.8 0.1 reshape.43.cols_ref
  53.9 0.8 reshape.44.counts_ref
  54.7 4.6 %copy-done = bf16[8,8,6,128,128]{4,3,2,1,0:T(8,128)(2,1)S(1)} copy-done((bf16[8,8,6,128,128]{4,3,2,1,0:T(8,128)(2,1)S(1)}, bf16[8,8,6,128,128]{4,3,2,1,0:T(8,128)(2,1)}, u32[]{:S(2)}) %copy-start) | copy-done | bytes 12582936
  59.3 1.0 copy-done.5
  60.3 4.5 %forward_tiles.8.rest_0_ = f32[1024,256]{1,0:T(8,128)S(1)} custom-call(s32[1]{0:T(128)} %bitcast.7.sel_ref, s32[384]{0:T(512)S(1)} %reshape.43.cols_ref, s32[64]{0:T(128)S(1)} %reshape.44.counts_ref, bf16[8,8,6,128,128]{4,3,2,1,0:T(8,128)(2,1)S(1)} %copy-done, bf16[1024,256]{1,0:T(8,128)(2,1)S(1)} %copy-done.5), custom_call_target="tpu_custom_call" | custom-call | flops 402653184 | bytes 8388608 | tf_op jit(solution)/shard_map/forward_tiles/pallas_call | solution.py:115
  64.8 3.3 %forward_tiles.9.rest_0_ = f32[1024,256]{1,0:T(8,128)S(1)} custom-call(s32[1]{0:T(128)} %bitcast.6.sel_ref, s32[384]{0:T(512)S(1)} %reshape.43.cols_ref, s32[64]{0:T(128)S(1)} %reshape.44.counts_ref, bf16[8,8,6,128,128]{4,3,2,1,0:T(8,128)(2,1)} %tiles_ref.31, bf16[1024,256]{1,0:T(8,128)(2,1)S(1)} %collective-permute-done.2.shard_ref, ...), custom_call_target="tpu_custom_call" | custom-call | flops 402653184 | bytes 8388608 | tf_op jit(solution)/shard_map/forward_tiles/pallas_call | solution.py:115
  68.1 4.2 %forward_tiles.10.rest_0_ = f32[1024,256]{1,0:T(8,128)S(1)} custom-call(s32[1]{0:T(128)} %bitcast.5.sel_ref, s32[384]{0:T(512)S(1)} %reshape.43.cols_ref, s32[64]{0:T(128)S(1)} %reshape.44.counts_ref, bf16[8,8,6,128,128]{4,3,2,1,0:T(8,128)(2,1)} %tiles_ref.31, bf16[1024,256]{1,0:T(8,128)(2,1)S(1)} %collective-permute-done.shard_ref, ...), custom_call_target="tpu_custom_call" | custom-call | flops 402653184 | bytes 8388608 | tf_op jit(solution)/shard_map/forward_tiles/pallas_call | solution.py:115
  72.3 4.6 %forward_tiles.11.rest_0_ = f32[1024,256]{1,0:T(8,128)S(1)} custom-call(s32[1]{0:T(128)} %bitcast.4.sel_ref, s32[384]{0:T(512)S(1)} %reshape.43.cols_ref, s32[64]{0:T(128)S(1)} %reshape.44.counts_ref, bf16[8,8,6,128,128]{4,3,2,1,0:T(8,128)(2,1)} %tiles_ref.31, bf16[1024,256]{1,0:T(8,128)(2,1)} %collective-permute-done.6.shard_ref, ...), custom_call_target="tpu_custom_call" | custom-call | flops 402653184 | bytes 8388608 | tf_op jit(solution)/shard_map/forward_tiles/pallas_call | solution.py:115
  76.9 4.2 %forward_tiles.12.rest_0_ = f32[1024,256]{1,0:T(8,128)S(1)} custom-call(s32[1]{0:T(128)} %bitcast.3.sel_ref, s32[384]{0:T(512)S(1)} %reshape.43.cols_ref, s32[64]{0:T(128)S(1)} %reshape.44.counts_ref, bf16[8,8,6,128,128]{4,3,2,1,0:T(8,128)(2,1)} %tiles_ref.31, bf16[1024,256]{1,0:T(8,128)(2,1)S(1)} %collective-permute-done.5.shard_ref, ...), custom_call_target="tpu_custom_call" | custom-call | flops 402653184 | bytes 8388608 | tf_op jit(solution)/shard_map/forward_tiles/pallas_call | solution.py:115
  81.2 4.2 %forward_tiles.13.rest_0_ = f32[1024,256]{1,0:T(8,128)S(1)} custom-call(s32[1]{0:T(128)} %constant.133.clone.1.sel_ref, s32[384]{0:T(512)S(1)} %reshape.43.cols_ref, s32[64]{0:T(128)S(1)} %reshape.44.counts_ref, bf16[8,8,6,128,128]{4,3,2,1,0:T(8,128)(2,1)} %tiles_ref.31, bf16[1024,256]{1,0:T(8,128)(2,1)S(1)} %collective-permute-done.4.shard_ref, ...), custom_call_target="tpu_custom_call" | custom-call | flops 402653184 | bytes 8388608 | tf_op jit(solution)/shard_map/forward_tiles/pallas_call | solution.py:115
  85.5 4.2 %forward_tiles.14.rest_0_ = f32[1024,256]{1,0:T(8,128)S(1)} custom-call(s32[1]{0:T(128)} %bitcast.2.sel_ref, s32[384]{0:T(512)S(1)} %reshape.43.cols_ref, s32[64]{0:T(128)S(1)} %reshape.44.counts_ref, bf16[8,8,6,128,128]{4,3,2,1,0:T(8,128)(2,1)} %tiles_ref.31, bf16[1024,256]{1,0:T(8,128)(2,1)S(1)} %collective-permute-done.3.shard_ref, ...), custom_call_target="tpu_custom_call" | custom-call | flops 402653184 | bytes 8388608 | tf_op jit(solution)/shard_map/forward_tiles/pallas_call | solution.py:115
  89.8 3.7 %forward_tiles.15 = f32[1024,256]{1,0:T(8,128)S(1)} custom-call(s32[1]{0:T(128)} %bitcast.1.sel_ref, s32[384]{0:T(512)S(1)} %reshape.43.cols_ref, s32[64]{0:T(128)S(1)} %reshape.44.counts_ref, bf16[8,8,6,128,128]{4,3,2,1,0:T(8,128)(2,1)} %tiles_ref.31, bf16[1024,256]{1,0:T(8,128)(2,1)S(1)} %collective-permute-done.1.shard_ref, ...), custom_call_target="tpu_custom_call" | custom-call | flops 402653184 | bytes 8388608 | tf_op jit(solution)/shard_map/forward_tiles/pallas_call | solution.py:115
  93.5 12.3 %collective-permute-start.8 = (bf16[2,256,256]{2,1,0:T(8,128)(2,1)S(1)}, bf16[2,256,256]{2,1,0:T(8,128)(2,1)S(1)}, u32[]{:S(2)}, u32[]{:S(2)}) collective-permute-start(bf16[2,256,256]{2,1,0:T(8,128)(2,1)S(1)} %fusion.1), channel_id=1, source_target_pairs={{0,1},{1,0},{2,3},{3,2},{4,5},{5,4},{6,7},{7,6},{8,9},{9,8},{10,11... | collective-permute-start | bytes 786440 | tf_op jit(solution)/shard_map/ppermute | solution.py:50
  105.9 1.2 collective-permute-done.8
  107.3 0.2 copy.19.inv_ref
  107.5 0.2 copy.18.mask_ref
  107.9 8.3 %collective-permute-done.9.got_ref = bf16[2,256,256]{2,1,0:T(8,128)(2,1)S(1)} collective-permute-done((bf16[2,256,256]{2,1,0:T(8,128)(2,1)S(1)}, bf16[2,256,256]{2,1,0:T(8,128)(2,1)S(1)}, u32[]{:S(2)}, u32[]{:S(2)}) %collective-permute-start.9) | collective-permute-done | bytes 262176 | tf_op jit(solution)/shard_map/ppermute | solution.py:50
  116.2 0.9 copy-done.7
  117.1 1.6 dense_rows.1
  118.7 1.2 collective-permute-start.10
  120.2 0.8 collective-permute-done.10.got_ref
  121.1 4.6 %copy-done.1 = bf16[8,8,6,128,128]{4,3,2,1,0:T(8,128)(2,1)S(1)} copy-done((bf16[8,8,6,128,128]{4,3,2,1,0:T(8,128)(2,1)S(1)}, bf16[8,8,6,128,128]{4,3,2,1,0:T(8,128)(2,1)}, u32[]{:S(2)}) %copy-start.1) | copy-done | bytes 12582936
  125.6 6.4 %backward_tiles.9 = (bf16[8,256,128]{2,1,0:T(8,128)(2,1)}, f32[256,256]{1,0:T(8,128)S(1)}) custom-call(s32[2]{0:T(128)S(1)} %pad_add_fusion.1.sel_ref, s32[384]{0:T(512)S(1)} %reshape.43.cols_ref, s32[64]{0:T(128)S(1)} %reshape.44.counts_ref, bf16[8,8,6,128,128]{4,3,2,1,0:T(8,128)(2,1)S(1)} %copy-done.1, ...), custom_call_target="tpu_custom_call", output_to_operand_aliasing={{1}: (6, {})} | custom-call | flops 402653184 | bytes 8388608 | tf_op jit(solution)/shard_map/backward_tiles/pallas_call | solution.py:229
  132.1 0.3 collective-permute-start.21
  132.4 1.1 collective-permute-done.21
  133.8 3.8 %collective-permute-start.25 = (bf16[144,256]{1,0:T(8,128)(2,1)S(1)}, bf16[144,256]{1,0:T(8,128)(2,1)S(1)}, u32[]{:S(2)}, u32[]{:S(2)}) collective-permute-start(bf16[144,256]{1,0:T(8,128)(2,1)S(1)} %maximum_maximum_fusion), channel_id=1, source_target_pairs={{0,96},{1,97},{2,98},{3,99},{4,100},{5,101},{6,102},{7,103},{8,104... | collective-permute-start | bytes 221192 | tf_op jit(solution)/shard_map/ppermute | solution.py:50
  137.7 1.3 collective-permute-done.24
  139.0 2.0 collective-permute-done.25
  141.4 3.8 %collective-permute-start.28 = (bf16[144,256]{1,0:T(8,128)(2,1)S(1)}, bf16[144,256]{1,0:T(8,128)(2,1)S(1)}, u32[]{:S(2)}, u32[]{:S(2)}) collective-permute-start(bf16[144,256]{1,0:T(8,128)(2,1)S(1)} %maximum_maximum_fusion.1), channel_id=1, source_target_pairs={{0,24},{1,25},{2,26},{3,27},{4,28},{5,29},{6,30},{7,31},{8,16},{9,... | collective-permute-start | bytes 221192 | tf_op jit(solution)/shard_map/ppermute | solution.py:50
  145.3 5.6 %backward_tiles.8 = bf16[8,256,128]{2,1,0:T(8,128)(2,1)S(1)} custom-call(s32[2]{0:T(128)S(1)} %pad_add_fusion.sel_ref, s32[384]{0:T(512)S(1)} %reshape.43.cols_ref, s32[64]{0:T(128)S(1)} %reshape.44.counts_ref, bf16[8,8,6,128,128]{4,3,2,1,0:T(8,128)(2,1)S(1)} %copy-done.1, bf16[2,256,256]{2,1,0:T(8,128)(2,1)S(1)} %get-tuple-element.13.own_ref, ...), custom_call_target="tpu_custom_call" | custom-call | flops 402653184 | bytes 8388608 | tf_op jit(solution)/shard_map/backward_tiles/pallas_call | solution.py:229
  150.9 3.9 %collective-permute-start.11 = (bf16[8,256,128]{2,1,0:T(8,128)(2,1)S(1)}, bf16[8,256,128]{2,1,0:T(8,128)(2,1)}, u32[]{:S(2)}, u32[]{:S(2)}) collective-permute-start(bf16[8,256,128]{2,1,0:T(8,128)(2,1)S(1)} %backward_tiles.8), channel_id=1, source_target_pairs={{0,0},{1,97},{2,66},{3,35},{4,4},{5,101},{6,70},{7,39},{8,8},{9,10... | collective-permute-start | bytes 1572872 | tf_op jit(solution)/shard_map/ppermute | solution.py:50
  154.9 0.1 add_add_fusion
  155.2 4.9 %backward_tiles.11 = bf16[8,256,128]{2,1,0:T(8,128)(2,1)S(1)} custom-call(s32[2]{0:T(128)S(1)} %pad_add_fusion.4.sel_ref, s32[384]{0:T(512)S(1)} %reshape.43.cols_ref, s32[64]{0:T(128)S(1)} %reshape.44.counts_ref, bf16[8,8,6,128,128]{4,3,2,1,0:T(8,128)(2,1)S(1)} %copy-done.1, bf16[2,256,256]{2,1,0:T(8,128)(2,1)S(1)} %get-tuple-element.13.own_ref, ...), custom_call_target="tpu_custom_call" | custom-call | flops 402653184 | bytes 8388608 | tf_op jit(solution)/shard_map/backward_tiles/pallas_call | solution.py:229
  160.2 1.2 collective-permute-start.14
  161.4 5.9 %backward_tiles.13 = bf16[8,256,128]{2,1,0:T(8,128)(2,1)S(1)} custom-call(s32[2]{0:T(128)S(1)} %pad_add_fusion.6.sel_ref, s32[384]{0:T(512)S(1)} %reshape.43.cols_ref, s32[64]{0:T(128)S(1)} %reshape.44.counts_ref, bf16[8,8,6,128,128]{4,3,2,1,0:T(8,128)(2,1)S(1)} %copy-done.1, bf16[2,256,256]{2,1,0:T(8,128)(2,1)S(1)} %get-tuple-element.13.own_ref, ...), custom_call_target="tpu_custom_call" | custom-call | flops 402653184 | bytes 8388608 | tf_op jit(solution)/shard_map/backward_tiles/pallas_call | solution.py:229
  167.5 3.3 %collective-permute-start.30 = (f32[128,256]{1,0:T(8,128)S(1)}, f32[128,256]{1,0:T(8,128)S(1)}, u32[]{:S(2)}, u32[]{:S(2)}) collective-permute-start(f32[128,256]{1,0:T(8,128)S(1)} %get-tuple-element.24), channel_id=1, source_target_pairs={{0,2},{1,3},{2,0},{3,1},{4,6},{5,7},{6,4},{7,5},{8,10},{9,11},{10,... | collective-permute-start | bytes 393224 | tf_op jit(solution)/shard_map/ppermute | solution.py:50
  170.7 5.5 %backward_tiles.10 = bf16[8,256,128]{2,1,0:T(8,128)(2,1)S(1)} custom-call(s32[2]{0:T(128)S(1)} %pad_add_fusion.2.sel_ref, s32[384]{0:T(512)S(1)} %reshape.43.cols_ref, s32[64]{0:T(128)S(1)} %reshape.44.counts_ref, bf16[8,8,6,128,128]{4,3,2,1,0:T(8,128)(2,1)S(1)} %copy-done.1, bf16[2,256,256]{2,1,0:T(8,128)(2,1)S(1)} %get-tuple-element.13.own_ref, ...), custom_call_target="tpu_custom_call" | custom-call | flops 402653184 | bytes 8388608 | tf_op jit(solution)/shard_map/backward_tiles/pallas_call | solution.py:229
  176.2 4.8 %backward_tiles.15 = bf16[8,256,128]{2,1,0:T(8,128)(2,1)S(1)} custom-call(s32[2]{0:T(128)S(1)} %pad_add_fusion.7.sel_ref, s32[384]{0:T(512)S(1)} %reshape.43.cols_ref, s32[64]{0:T(128)S(1)} %reshape.44.counts_ref, bf16[8,8,6,128,128]{4,3,2,1,0:T(8,128)(2,1)S(1)} %copy-done.1, bf16[2,256,256]{2,1,0:T(8,128)(2,1)S(1)} %get-tuple-element.13.own_ref, ...), custom_call_target="tpu_custom_call" | custom-call | flops 402653184 | bytes 8388608 | tf_op jit(solution)/shard_map/backward_tiles/pallas_call | solution.py:229
  181.0 5.0 %collective-permute-start.13 = (bf16[8,256,128]{2,1,0:T(8,128)(2,1)S(1)}, bf16[8,256,128]{2,1,0:T(8,128)(2,1)}, u32[]{:S(2)}, u32[]{:S(2)}) collective-permute-start(bf16[8,256,128]{2,1,0:T(8,128)(2,1)S(1)} %backward_tiles.10), channel_id=1, source_target_pairs={{0,126},{1,95},{2,60},{3,29},{4,122},{5,91},{6,56},{7,25},{8,118},... | collective-permute-start | bytes 1572872 | tf_op jit(solution)/shard_map/ppermute | solution.py:50
  186.0 5.6 %backward_tiles.12 = bf16[8,256,128]{2,1,0:T(8,128)(2,1)S(1)} custom-call(s32[2]{0:T(128)S(1)} %pad_add_fusion.3.sel_ref, s32[384]{0:T(512)S(1)} %reshape.43.cols_ref, s32[64]{0:T(128)S(1)} %reshape.44.counts_ref, bf16[8,8,6,128,128]{4,3,2,1,0:T(8,128)(2,1)S(1)} %copy-done.1, bf16[2,256,256]{2,1,0:T(8,128)(2,1)S(1)} %get-tuple-element.13.own_ref, ...), custom_call_target="tpu_custom_call" | custom-call | flops 402653184 | bytes 8388608 | tf_op jit(solution)/shard_map/backward_tiles/pallas_call | solution.py:229
  191.7 1.2 collective-permute-start.18
  192.9 4.6 %backward_tiles.14 = bf16[8,256,128]{2,1,0:T(8,128)(2,1)S(1)} custom-call(s32[2]{0:T(128)S(1)} %pad_add_fusion.5.sel_ref, s32[384]{0:T(512)S(1)} %reshape.43.cols_ref, s32[64]{0:T(128)S(1)} %reshape.44.counts_ref, bf16[8,8,6,128,128]{4,3,2,1,0:T(8,128)(2,1)S(1)} %copy-done.1, bf16[2,256,256]{2,1,0:T(8,128)(2,1)S(1)} %get-tuple-element.13.own_ref, ...), custom_call_target="tpu_custom_call" | custom-call | flops 402653184 | bytes 8388608 | tf_op jit(solution)/shard_map/backward_tiles/pallas_call | solution.py:229
  197.5 3.6 %collective-permute-start.15 = (bf16[8,256,128]{2,1,0:T(8,128)(2,1)S(1)}, bf16[8,256,128]{2,1,0:T(8,128)(2,1)S(1)}, u32[]{:S(2)}, u32[]{:S(2)}) collective-permute-start(bf16[8,256,128]{2,1,0:T(8,128)(2,1)S(1)} %backward_tiles.12), channel_id=1, source_target_pairs={{0,110},{1,79},{2,44},{3,13},{4,106},{5,75},{6,40},{7,9},{8,6},{9,... | collective-permute-start | bytes 1572872 | tf_op jit(solution)/shard_map/ppermute | solution.py:50
  201.0 0.6 fusion.5
  201.6 5.2 %collective-permute-start.31 = (f32[2,128,256]{2,1,0:T(8,128)S(1)}, f32[2,128,256]{2,1,0:T(8,128)S(1)}, u32[]{:S(2)}, u32[]{:S(2)}) collective-permute-start(f32[2,128,256]{2,1,0:T(8,128)S(1)} %maximum_select_fusion), channel_id=1, source_target_pairs={{0,1},{1,0},{2,3},{3,2},{4,5},{5,4},{6,7},{7,6},{8,9},{9,8},{10,11... | collective-permute-start | bytes 786440 | tf_op jit(solution)/shard_map/ppermute | solution.py:50
  206.9 17.9 %collective-permute-done.15 = bf16[8,256,128]{2,1,0:T(8,128)(2,1)S(1)} collective-permute-done((bf16[8,256,128]{2,1,0:T(8,128)(2,1)S(1)}, bf16[8,256,128]{2,1,0:T(8,128)(2,1)S(1)}, u32[]{:S(2)}, u32[]{:S(2)}) %collective-permute-start.15) | collective-permute-done | bytes 524320 | tf_op jit(solution)/shard_map/ppermute | solution.py:50
  224.8 2.1 convert_add_fusion
  226.9 15.1 %collective-permute-start.19 = (bf16[2,2,256,128]{3,2,1,0:T(8,128)(2,1)S(1)}, bf16[2,2,256,128]{3,2,1,0:T(8,128)(2,1)S(1)}, u32[]{:S(2)}, u32[]{:S(2)}) collective-permute-start(bf16[2,2,256,128]{3,2,1,0:T(8,128)(2,1)S(1)} %fusion.2), channel_id=1, source_target_pairs={{0,1},{1,0},{2,3},{3,2},{4,5},{5,4},{6,7},{7,6},{8,9},{9,8},{10,11... | collective-permute-start | bytes 786440 | tf_op jit(solution)/shard_map/ppermute | solution.py:50
  242.1 1.1 collective-permute-done.19
  243.4 0.8 slice_bitcast_fusion
  244.2 5.4 %collective-permute-done.20.got_ref = bf16[2,256,128]{2,1,0:T(8,128)(2,1)S(1)} collective-permute-done((bf16[2,256,128]{2,1,0:T(8,128)(2,1)S(1)}, bf16[2,256,128]{2,1,0:T(8,128)(2,1)S(1)}, u32[]{:S(2)}, u32[]{:S(2)}) %collective-permute-start.20) | collective-permute-done | bytes 131104 | tf_op jit(solution)/shard_map/ppermute | solution.py:50
  249.6 0.8 final_rows.1
  (83 shorter events, 2.5 us)
Async XLA Ops:
  0.6 29.4 %collective-permute-start.7 = (bf16[1024,256]{1,0:T(8,128)(2,1)}, bf16[1024,256]{1,0:T(8,128)(2,1)S(1)}, u32[]{:S(2)}, u32[]{:S(2)}) collective-permute-start(bf16[1024,256]{1,0:T(8,128)(2,1)} %feat_ref.1), channel_id=1, source_target_pairs={{104,0},{73,1},{42,2},{11,3},{108,4},{77,5},{46,6},{15,7},{0,8},{9... | collective-permute-start | bytes 1572872 | tf_op jit(solution)/shard_map/ppermute | solution.py:50
  3.8 29.1 %collective-permute-start.2 = (bf16[1024,256]{1,0:T(8,128)(2,1)}, bf16[1024,256]{1,0:T(8,128)(2,1)S(1)}, u32[]{:S(2)}, u32[]{:S(2)}) collective-permute-start(bf16[1024,256]{1,0:T(8,128)(2,1)} %feat_ref.1), channel_id=1, source_target_pairs={{120,0},{89,1},{58,2},{27,3},{124,4},{93,5},{62,6},{31,7},{112,8},... | collective-permute-start | bytes 1572872 | tf_op jit(solution)/shard_map/ppermute | solution.py:50
  7.3 39.5 %collective-permute-start = (bf16[1024,256]{1,0:T(8,128)(2,1)}, bf16[1024,256]{1,0:T(8,128)(2,1)S(1)}, u32[]{:S(2)}, u32[]{:S(2)}) collective-permute-start(bf16[1024,256]{1,0:T(8,128)(2,1)} %feat_ref.1), channel_id=1, source_target_pairs={{110,0},{79,1},{44,2},{13,3},{106,4},{75,5},{40,6},{9,7},{6,8},{10... | collective-permute-start | bytes 1572872 | tf_op jit(solution)/shard_map/ppermute | solution.py:50
  10.9 61.5 %collective-permute-start.6 = (bf16[1024,256]{1,0:T(8,128)(2,1)}, bf16[1024,256]{1,0:T(8,128)(2,1)}, u32[]{:S(2)}, u32[]{:S(2)}) collective-permute-start(bf16[1024,256]{1,0:T(8,128)(2,1)} %feat_ref.1), channel_id=1, source_target_pairs={{126,0},{95,1},{60,2},{29,3},{122,4},{91,5},{56,6},{25,7},{118,8},... | collective-permute-start | bytes 1572872 | tf_op jit(solution)/shard_map/ppermute | solution.py:50
  12.7 64.2 %collective-permute-start.5 = (bf16[1024,256]{1,0:T(8,128)(2,1)}, bf16[1024,256]{1,0:T(8,128)(2,1)S(1)}, u32[]{:S(2)}, u32[]{:S(2)}) collective-permute-start(bf16[1024,256]{1,0:T(8,128)(2,1)} %feat_ref.1), channel_id=1, source_target_pairs={{102,0},{71,1},{36,2},{5,3},{2,4},{99,5},{64,6},{33,7},{110,8},{79... | collective-permute-start | bytes 1572872 | tf_op jit(solution)/shard_map/ppermute | solution.py:50
  30.1 0.8 copy-start.4
  30.9 50.3 %collective-permute-start.4 = (bf16[1024,256]{1,0:T(8,128)(2,1)}, bf16[1024,256]{1,0:T(8,128)(2,1)S(1)}, u32[]{:S(2)}, u32[]{:S(2)}) collective-permute-start(bf16[1024,256]{1,0:T(8,128)(2,1)} %feat_ref.1), channel_id=1, source_target_pairs={{0,0},{97,1},{66,2},{35,3},{4,4},{101,5},{70,6},{39,7},{8,8},{105,... | collective-permute-start | bytes 1572872 | tf_op jit(solution)/shard_map/ppermute | solution.py:50
  32.8 52.6 %collective-permute-start.3 = (bf16[1024,256]{1,0:T(8,128)(2,1)S(1)}, bf16[1024,256]{1,0:T(8,128)(2,1)S(1)}, u32[]{:S(2)}, u32[]{:S(2)}) collective-permute-start(bf16[1024,256]{1,0:T(8,128)(2,1)S(1)} %collective-permute-done.2.shard_ref), channel_id=1, source_target_pairs={{8,0},{9,1},{10,2},{11,3},{12,4},{13,5},{14,6},{15,7},{0,8},{1,9},... | collective-permute-start | bytes 1572872 | tf_op jit(solution)/shard_map/ppermute | solution.py:50
  46.8 43.0 %collective-permute-start.1 = (bf16[1024,256]{1,0:T(8,128)(2,1)S(1)}, bf16[1024,256]{1,0:T(8,128)(2,1)S(1)}, u32[]{:S(2)}, u32[]{:S(2)}) collective-permute-start(bf16[1024,256]{1,0:T(8,128)(2,1)S(1)} %collective-permute-done.shard_ref), channel_id=1, source_target_pairs={{120,0},{121,1},{122,2},{123,3},{124,4},{125,5},{126,6},{127,7},{1... | collective-permute-start | bytes 1572872 | tf_op jit(solution)/shard_map/ppermute | solution.py:50
  54.7 4.6 %copy-start = (bf16[8,8,6,128,128]{4,3,2,1,0:T(8,128)(2,1)S(1)}, bf16[8,8,6,128,128]{4,3,2,1,0:T(8,128)(2,1)}, u32[]{:S(2)}) copy-start(bf16[8,8,6,128,128]{4,3,2,1,0:T(8,128)(2,1)} %tiles_ref.31) | copy-start | bytes 37748740
  59.3 1.0 copy-start.5
  85.4 20.4 %copy-start.9 = (s32[1024]{0:T(1024)S(1)}, s32[1024]{0:T(1024)}, u32[]{:S(2)}) copy-start(s32[1024]{0:T(1024)} %param.14) | copy-start | bytes 12292
  89.7 17.8 %copy-start.10 = (s32[1024]{0:T(1024)S(1)}, s32[1024]{0:T(1024)}, u32[]{:S(2)}) copy-start(s32[1024]{0:T(1024)} %param.15) | copy-start | bytes 12292
  89.7 26.5 %copy-start.2 = (bf16[1024,256]{1,0:T(8,128)(2,1)S(1)}, bf16[1024,256]{1,0:T(8,128)(2,1)}, u32[]{:S(2)}) copy-start(bf16[1024,256]{1,0:T(8,128)(2,1)} %feat_ref.1) | copy-start | bytes 1572868
  89.7 26.5 %copy-start.3 = (bf16[1024,256]{1,0:T(8,128)(2,1)S(1)}, bf16[1024,256]{1,0:T(8,128)(2,1)}, u32[]{:S(2)}) copy-start(bf16[1024,256]{1,0:T(8,128)(2,1)} %cot_ref.1) | copy-start | bytes 1572868
  89.7 26.5 %copy-start.6 = (bf16[256,256]{1,0:T(8,128)(2,1)S(1)}, bf16[256,256]{1,0:T(8,128)(2,1)}, u32[]{:S(2)}) copy-start(bf16[256,256]{1,0:T(8,128)(2,1)} %ws_ref.1) | copy-start | bytes 393220
  89.8 26.5 %copy-start.8 = (f32[256]{0:T(256)S(1)}, f32[256]{0:T(256)}, u32[]{:S(2)}) copy-start(f32[256]{0:T(256)} %param.19) | copy-start | bytes 3076
  93.5 13.5 %collective-permute-start.8 = (bf16[2,256,256]{2,1,0:T(8,128)(2,1)S(1)}, bf16[2,256,256]{2,1,0:T(8,128)(2,1)S(1)}, u32[]{:S(2)}, u32[]{:S(2)}) collective-permute-start(bf16[2,256,256]{2,1,0:T(8,128)(2,1)S(1)} %fusion.1), channel_id=1, source_target_pairs={{0,1},{1,0},{2,3},{3,2},{4,5},{5,4},{6,7},{7,6},{8,9},{9,8},{10,11... | collective-permute-start | bytes 786440 | tf_op jit(solution)/shard_map/ppermute | solution.py:50
  107.1 9.1 %collective-permute-start.9 = (bf16[2,256,256]{2,1,0:T(8,128)(2,1)S(1)}, bf16[2,256,256]{2,1,0:T(8,128)(2,1)S(1)}, u32[]{:S(2)}, u32[]{:S(2)}) collective-permute-start(bf16[2,256,256]{2,1,0:T(8,128)(2,1)S(1)} %fusion.own_ref), channel_id=1, source_target_pairs={{0,2},{1,3},{2,0},{3,1},{4,6},{5,7},{6,4},{7,5},{8,10},{9,11},{10,... | collective-permute-start | bytes 786440 | tf_op jit(solution)/shard_map/ppermute | solution.py:50
  116.2 0.9 copy-start.7
  118.7 2.4 collective-permute-start.10
  120.2 12.2 %collective-permute-start.22 = (f32[1,256]{1,0:T(1,128)S(1)}, f32[1,256]{1,0:T(1,128)S(1)}, u32[]{:S(2)}, u32[]{:S(2)}) collective-permute-start(f32[1,256]{1,0:T(1,128)S(1)} %get-tuple-element.18), channel_id=1, source_target_pairs={{0,1},{1,0},{2,3},{3,2},{4,5},{5,4},{6,7},{7,6},{8,9},{9,8},{10,11... | collective-permute-start | bytes 3080 | tf_op jit(solution)/shard_map/ppermute | solution.py:50
  121.1 4.6 %copy-start.1 = (bf16[8,8,6,128,128]{4,3,2,1,0:T(8,128)(2,1)S(1)}, bf16[8,8,6,128,128]{4,3,2,1,0:T(8,128)(2,1)}, u32[]{:S(2)}) copy-start(bf16[8,8,6,128,128]{4,3,2,1,0:T(8,128)(2,1)} %tiles_ref.31) | copy-start | bytes 37748740
  132.1 1.4 collective-permute-start.21
  133.7 4.0 %collective-permute-start.23 = (bf16[144,256]{1,0:T(8,128)(2,1)S(1)}, bf16[144,256]{1,0:T(8,128)(2,1)S(1)}, u32[]{:S(2)}, u32[]{:S(2)}) collective-permute-start(bf16[144,256]{1,0:T(8,128)(2,1)S(1)} %maximum_maximum_fusion), channel_id=1, source_target_pairs={{0,32},{1,33},{2,34},{3,35},{4,36},{5,37},{6,38},{7,39},{8,40},{9,... | collective-permute-start | bytes 221192 | tf_op jit(solution)/shard_map/ppermute | solution.py:50
  133.7 5.3 %collective-permute-start.24 = (bf16[144,256]{1,0:T(8,128)(2,1)S(1)}, bf16[144,256]{1,0:T(8,128)(2,1)S(1)}, u32[]{:S(2)}, u32[]{:S(2)}) collective-permute-start(bf16[144,256]{1,0:T(8,128)(2,1)S(1)} %maximum_maximum_fusion), channel_id=1, source_target_pairs={{0,64},{1,65},{2,66},{3,67},{4,68},{5,69},{6,70},{7,71},{8,72},{9,... | collective-permute-start | bytes 221192 | tf_op jit(solution)/shard_map/ppermute | solution.py:50
  133.8 7.2 %collective-permute-start.25 = (bf16[144,256]{1,0:T(8,128)(2,1)S(1)}, bf16[144,256]{1,0:T(8,128)(2,1)S(1)}, u32[]{:S(2)}, u32[]{:S(2)}) collective-permute-start(bf16[144,256]{1,0:T(8,128)(2,1)S(1)} %maximum_maximum_fusion), channel_id=1, source_target_pairs={{0,96},{1,97},{2,98},{3,99},{4,100},{5,101},{6,102},{7,103},{8,104... | collective-permute-start | bytes 221192 | tf_op jit(solution)/shard_map/ppermute | solution.py:50
  141.3 13.6 %collective-permute-start.26 = (bf16[144,256]{1,0:T(8,128)(2,1)S(1)}, bf16[144,256]{1,0:T(8,128)(2,1)S(1)}, u32[]{:S(2)}, u32[]{:S(2)}) collective-permute-start(bf16[144,256]{1,0:T(8,128)(2,1)S(1)} %maximum_maximum_fusion.1), channel_id=1, source_target_pairs={{0,8},{1,9},{2,10},{3,11},{4,12},{5,13},{6,14},{7,15},{8,0},{9,1},... | collective-permute-start | bytes 221192 | tf_op jit(solution)/shard_map/ppermute | solution.py:50
  141.3 13.5 %collective-permute-start.27 = (bf16[144,256]{1,0:T(8,128)(2,1)S(1)}, bf16[144,256]{1,0:T(8,128)(2,1)S(1)}, u32[]{:S(2)}, u32[]{:S(2)}) collective-permute-start(bf16[144,256]{1,0:T(8,128)(2,1)S(1)} %maximum_maximum_fusion.1), channel_id=1, source_target_pairs={{0,16},{1,17},{2,18},{3,19},{4,20},{5,21},{6,22},{7,23},{8,24},{9,... | collective-permute-start | bytes 221192 | tf_op jit(solution)/shard_map/ppermute | solution.py:50
  141.4 13.5 %collective-permute-start.28 = (bf16[144,256]{1,0:T(8,128)(2,1)S(1)}, bf16[144,256]{1,0:T(8,128)(2,1)S(1)}, u32[]{:S(2)}, u32[]{:S(2)}) collective-permute-start(bf16[144,256]{1,0:T(8,128)(2,1)S(1)} %maximum_maximum_fusion.1), channel_id=1, source_target_pairs={{0,24},{1,25},{2,26},{3,27},{4,28},{5,29},{6,30},{7,31},{8,16},{9,... | collective-permute-start | bytes 221192 | tf_op jit(solution)/shard_map/ppermute | solution.py:50
  150.9 50.1 %collective-permute-start.11 = (bf16[8,256,128]{2,1,0:T(8,128)(2,1)S(1)}, bf16[8,256,128]{2,1,0:T(8,128)(2,1)}, u32[]{:S(2)}, u32[]{:S(2)}) collective-permute-start(bf16[8,256,128]{2,1,0:T(8,128)(2,1)S(1)} %backward_tiles.8), channel_id=1, source_target_pairs={{0,0},{1,97},{2,66},{3,35},{4,4},{5,101},{6,70},{7,39},{8,8},{9,10... | collective-permute-start | bytes 1572872 | tf_op jit(solution)/shard_map/ppermute | solution.py:50
  154.8 46.8 %collective-permute-start.12 = (bf16[8,256,128]{2,1,0:T(8,128)(2,1)}, bf16[8,256,128]{2,1,0:T(8,128)(2,1)}, u32[]{:S(2)}, u32[]{:S(2)}) collective-permute-start(bf16[8,256,128]{2,1,0:T(8,128)(2,1)} %get-tuple-element.15), channel_id=1, source_target_pairs={{0,102},{1,71},{2,36},{3,5},{4,2},{5,99},{6,64},{7,33},{8,110},{9,... | collective-permute-start | bytes 1572872 | tf_op jit(solution)/shard_map/ppermute | solution.py:50
  155.1 12.2 %collective-permute-start.29 = (bf16[144,256]{1,0:T(8,128)(2,1)S(1)}, bf16[144,256]{1,0:T(8,128)(2,1)S(1)}, u32[]{:S(2)}, u32[]{:S(2)}) collective-permute-start(bf16[144,256]{1,0:T(8,128)(2,1)S(1)} %maximum_maximum_fusion.2), channel_id=1, source_target_pairs={{0,4},{1,5},{2,6},{3,7},{4,0},{5,1},{6,2},{7,3},{8,12},{9,13},{10,... | collective-permute-start | bytes 221192 | tf_op jit(solution)/shard_map/ppermute | solution.py:50
  160.2 20.8 %collective-permute-start.14 = (bf16[8,256,128]{2,1,0:T(8,128)(2,1)S(1)}, bf16[8,256,128]{2,1,0:T(8,128)(2,1)S(1)}, u32[]{:S(2)}, u32[]{:S(2)}) collective-permute-start(bf16[8,256,128]{2,1,0:T(8,128)(2,1)S(1)} %backward_tiles.11), channel_id=1, source_target_pairs={{0,120},{1,121},{2,122},{3,123},{4,124},{5,125},{6,126},{7,127},{8... | collective-permute-start | bytes 1572872 | tf_op jit(solution)/shard_map/ppermute | solution.py:50
  167.3 24.4 %collective-permute-start.16 = (bf16[8,256,128]{2,1,0:T(8,128)(2,1)S(1)}, bf16[8,256,128]{2,1,0:T(8,128)(2,1)S(1)}, u32[]{:S(2)}, u32[]{:S(2)}) collective-permute-start(bf16[8,256,128]{2,1,0:T(8,128)(2,1)S(1)} %backward_tiles.13), channel_id=1, source_target_pairs={{0,8},{1,9},{2,10},{3,11},{4,12},{5,13},{6,14},{7,15},{8,0},{9,1},... | collective-permute-start | bytes 1572872 | tf_op jit(solution)/shard_map/ppermute | solution.py:50
  167.5 30.0 %collective-permute-start.30 = (f32[128,256]{1,0:T(8,128)S(1)}, f32[128,256]{1,0:T(8,128)S(1)}, u32[]{:S(2)}, u32[]{:S(2)}) collective-permute-start(f32[128,256]{1,0:T(8,128)S(1)} %get-tuple-element.24), channel_id=1, source_target_pairs={{0,2},{1,3},{2,0},{3,1},{4,6},{5,7},{6,4},{7,5},{8,10},{9,11},{10,... | collective-permute-start | bytes 393224 | tf_op jit(solution)/shard_map/ppermute | solution.py:50
  181.0 25.9 %collective-permute-start.13 = (bf16[8,256,128]{2,1,0:T(8,128)(2,1)S(1)}, bf16[8,256,128]{2,1,0:T(8,128)(2,1)}, u32[]{:S(2)}, u32[]{:S(2)}) collective-permute-start(bf16[8,256,128]{2,1,0:T(8,128)(2,1)S(1)} %backward_tiles.10), channel_id=1, source_target_pairs={{0,126},{1,95},{2,60},{3,29},{4,122},{5,91},{6,56},{7,25},{8,118},... | collective-permute-start | bytes 1572872 | tf_op jit(solution)/shard_map/ppermute | solution.py:50
  191.7 15.2 %collective-permute-start.18 = (bf16[8,256,128]{2,1,0:T(8,128)(2,1)S(1)}, bf16[8,256,128]{2,1,0:T(8,128)(2,1)}, u32[]{:S(2)}, u32[]{:S(2)}) collective-permute-start(bf16[8,256,128]{2,1,0:T(8,128)(2,1)S(1)} %backward_tiles.15), channel_id=1, source_target_pairs={{0,104},{1,73},{2,42},{3,11},{4,108},{5,77},{6,46},{7,15},{8,0},{9... | collective-permute-start | bytes 1572872 | tf_op jit(solution)/shard_map/ppermute | solution.py:50
  197.5 27.3 %collective-permute-start.15 = (bf16[8,256,128]{2,1,0:T(8,128)(2,1)S(1)}, bf16[8,256,128]{2,1,0:T(8,128)(2,1)S(1)}, u32[]{:S(2)}, u32[]{:S(2)}) collective-permute-start(bf16[8,256,128]{2,1,0:T(8,128)(2,1)S(1)} %backward_tiles.12), channel_id=1, source_target_pairs={{0,110},{1,79},{2,44},{3,13},{4,106},{5,75},{6,40},{7,9},{8,6},{9,... | collective-permute-start | bytes 1572872 | tf_op jit(solution)/shard_map/ppermute | solution.py:50
  201.0 23.8 %collective-permute-start.17 = (bf16[8,256,128]{2,1,0:T(8,128)(2,1)S(1)}, bf16[8,256,128]{2,1,0:T(8,128)(2,1)}, u32[]{:S(2)}, u32[]{:S(2)}) collective-permute-start(bf16[8,256,128]{2,1,0:T(8,128)(2,1)S(1)} %backward_tiles.14), channel_id=1, source_target_pairs={{0,120},{1,89},{2,58},{3,27},{4,124},{5,93},{6,62},{7,31},{8,112},... | collective-permute-start | bytes 1572872 | tf_op jit(solution)/shard_map/ppermute | solution.py:50
  201.6 40.4 %collective-permute-start.31 = (f32[2,128,256]{2,1,0:T(8,128)S(1)}, f32[2,128,256]{2,1,0:T(8,128)S(1)}, u32[]{:S(2)}, u32[]{:S(2)}) collective-permute-start(f32[2,128,256]{2,1,0:T(8,128)S(1)} %maximum_select_fusion), channel_id=1, source_target_pairs={{0,1},{1,0},{2,3},{3,2},{4,5},{5,4},{6,7},{7,6},{8,9},{9,8},{10,11... | collective-permute-start | bytes 786440 | tf_op jit(solution)/shard_map/ppermute | solution.py:50
  226.9 16.2 %collective-permute-start.19 = (bf16[2,2,256,128]{3,2,1,0:T(8,128)(2,1)S(1)}, bf16[2,2,256,128]{3,2,1,0:T(8,128)(2,1)S(1)}, u32[]{:S(2)}, u32[]{:S(2)}) collective-permute-start(bf16[2,2,256,128]{3,2,1,0:T(8,128)(2,1)S(1)} %fusion.2), channel_id=1, source_target_pairs={{0,1},{1,0},{2,3},{3,2},{4,5},{5,4},{6,7},{7,6},{8,9},{9,8},{10,11... | collective-permute-start | bytes 786440 | tf_op jit(solution)/shard_map/ppermute | solution.py:50
  243.3 6.3 %collective-permute-start.20 = (bf16[2,256,128]{2,1,0:T(8,128)(2,1)S(1)}, bf16[2,256,128]{2,1,0:T(8,128)(2,1)S(1)}, u32[]{:S(2)}, u32[]{:S(2)}) collective-permute-start(bf16[2,256,128]{2,1,0:T(8,128)(2,1)S(1)} %fusion.3), channel_id=1, source_target_pairs={{0,2},{1,3},{2,0},{3,1},{4,6},{5,7},{6,4},{7,5},{8,10},{9,11},{10,... | collective-permute-start | bytes 393224 | tf_op jit(solution)/shard_map/ppermute | solution.py:50

commit v3 on v2

--- a/solution.py
+++ b/solution.py
@@ -13,8 +13,10 @@
 NS = 6
 BS = 128
 F = 256
-VMEM = 40 * 1024 * 1024
-PLAN = ((2, None), (6, None), (3, None), (7, None), (1, None), (0, None), (4, 2), (5, 6))
+VMEM = 53 * 1024 * 1024
+BACK_PLAN = (
+    (5, 6), (4, 2), (2, None), (7, None), (1, None), (0, None), (6, None), (3, None)
+)
 
 
 def index_of(y, x, zl, zh, core):
@@ -71,9 +73,9 @@
     return [pltpu.VMEM((NB, NS, BS, BS), jnp.bfloat16), pltpu.SemaphoreType.DMA((NB,))]
 
 
-def tile_cost():
+def tile_cost(times=1):
     return pl.CostEstimate(
-        flops=2 * NB * NS * BS * BS * F, bytes_accessed=8 << 20, transcendentals=0
+        flops=2 * NB * NS * BS * BS * F * times, bytes_accessed=(8 << 20) * times, transcendentals=0
     )
 
 
@@ -82,46 +84,42 @@
 WHOLE = pl.BlockSpec(memory_space=pltpu.VMEM)
 
 
-def forward_body(first, sel_ref, cols_ref, counts_ref, tiles_ref, shard_ref, *rest):
-    out_ref, held_ref, sems = rest[-3:]
+def forward_body(first, passed, sel_ref, cols_ref, counts_ref, tiles_ref, shard_ref, *rest):
+    held_ref, sems = rest[-2:]
+    out_ref = rest[(not first) + passed]
     dist = sel_ref[0]
     copies = load_tiles(tiles_ref, dist, held_ref, sems)
     for b in range(NB):
         copies[b].wait()
         count = counts_ref[b * ND + dist]
         rows = slice(b * BS, (b + 1) * BS)
-        out_ref[rows, :] = jnp.zeros((BS, F), jnp.float32) if first else rest[0][rows, :]
-        for s in range(0, NS, 2):
-
-            @pl.when(s < count)
-            def _():
-                left, right = [], []
-                for k in range(s, s + 2):
-                    col = cols_ref[(b * ND + dist) * NS + k]
-                    block = shard_ref[pl.ds(pl.multiple_of(col * BS, BS), BS), :]
-                    if k > s:
-                        block = jnp.where(k < count, block, jnp.zeros((), block.dtype))
-                    right.append(block)
-                    left.append(held_ref[b, k])
-                out_ref[rows, :] += jnp.dot(
-                    jnp.concatenate(left, 1),
-                    jnp.concatenate(right, 0),
-                    preferred_element_type=jnp.float32,
-                )
-
-
-def forward_call(dist, cols, counts, tiles, shard, total):
-    first = total is None
+        left, right = [], []
+        for s in range(NS):
+            col = cols_ref[(b * ND + dist) * NS + s]
+            block = shard_ref[pl.ds(pl.multiple_of(col * BS, BS), BS), :]
+            right.append(jnp.where(s < count, block, jnp.zeros((), block.dtype)))
+            left.append(held_ref[b, s])
+        summed = jnp.dot(
+            jnp.concatenate(left, 1), jnp.concatenate(right, 0), preferred_element_type=jnp.float32
+        )
+        out_ref[rows, :] = summed if first else rest[0][rows, :] + summed
+
+
+def forward_call(dist, cols, counts, tiles, shard, total, along=None):
+    first, passed = total is None, along is not None
+    made = jax.ShapeDtypeStruct((NB * BS, F), jnp.float32)
+    hbm_along = [HBM] if passed else []
     return pl.pallas_call(
-        functools.partial(forward_body, first),
-        out_shape=jax.ShapeDtypeStruct((NB * BS, F), jnp.float32),
-        in_specs=[SMEM] * 3 + [HBM, WHOLE] + ([] if first else [WHOLE]),
-        out_specs=WHOLE,
+        functools.partial(forward_body, first, passed),
+        out_shape=(made,) + ((jax.ShapeDtypeStruct(along.shape, along.dtype),) if passed else ()),
+        in_specs=[SMEM] * 3 + [HBM, WHOLE] + ([] if first else [WHOLE]) + hbm_along,
+        out_specs=(WHOLE,) + tuple(hbm_along),
         scratch_shapes=tile_scratch(),
+        input_output_aliases={5 + (not first): 1} if passed else {},
         compiler_params=params(),
         cost_estimate=tile_cost(),
         name="forward_tiles",
-    )(dist, cols, counts, tiles, shard, *([] if first else [total]))
+    )(dist, cols, counts, tiles, shard, *([] if first else [total]), *([along] if passed else []))
 
 
 def dense_body(
@@ -207,16 +205,12 @@
             count = counts_ref[b * ND + dist]
             left = message[:, inner * BS : (inner + 1) * BS]
             for s in range(0, NS, 2):
-
-                @pl.when(s < count)
-                def _():
-                    right = jnp.concatenate([held_ref[b, s], held_ref[b, s + 1]], 1)
-                    product = jnp.dot(left, right, preferred_element_type=jnp.float32)
-                    for k in range(2):
-                        col = cols_ref[(b * ND + dist) * NS + s + k]
-                        if k > 0:
-                            col = jnp.where(s + k < count, col, NB)
-                        acc_ref[col] += product[:, k * BS : (k + 1) * BS]
+                right = jnp.concatenate([held_ref[b, s], held_ref[b, s + 1]], 1)
+                product = jnp.dot(left, right, preferred_element_type=jnp.float32)
+                for k in range(2):
+                    col = cols_ref[(b * ND + dist) * NS + s + k]
+                    col = jnp.where(s + k < count, col, NB)
+                    acc_ref[col] += product[:, k * BS : (k + 1) * BS]
 
     for c in range(NB):
         out_ref[c] = acc_ref[c].astype(jnp.bfloat16)
@@ -234,7 +228,7 @@
         scratch_shapes=[pltpu.VMEM((NB + 1, F, BS), jnp.float32)] + tile_scratch(),
         input_output_aliases={6 + added: 1} if passed else {},
         compiler_params=params(),
-        cost_estimate=tile_cost(),
+        cost_estimate=tile_cost(8),
         name="backward_tiles",
     )(sel, cols, counts, tiles, own, got, *([extra] if added else []), *([along] if passed else []))
 
@@ -316,11 +310,27 @@
 
     blocks = {}
     total = None
-    for k, via in PLAN:
-        source = features if via is None else blocks[k ^ via]
-        blocks[k] = send(source, column_pairs(k, via))
-    for k, _ in PLAN:
-        total = forward_call(distance_of(k)[None], cols, live, tiles, blocks[k], total)
+
+    def fetch(k, via):
+        blocks[k] = send(features if via is None else blocks[k ^ via], column_pairs(k, via))
+
+    def consume(k, along=None):
+        nonlocal total
+        made = forward_call(
+            distance_of(k)[None], cols, live, tiles, blocks[k], total, blocks.get(along)
+        )
+        total = made[0]
+        if along is not None:
+            blocks[along] = made[1]
+
+    for k in (2, 6, 3, 7, 1, 0):
+        fetch(k, None)
+    consume(2, along=6)
+    fetch(4, 2)
+    consume(6, along=3)
+    fetch(5, 6)
+    for k in (3, 7, 1, 0, 4, 5):
+        consume(k)
 
     parts = total.reshape(2, 2, 256, F)
     away = lax.dynamic_index_in_dim(parts, 1 - core, 1, keepdims=False).astype(jnp.bfloat16)
@@ -335,12 +345,11 @@
 
     extra = {}
     arrived = None
-    for step, (k, via) in enumerate(reversed(PLAN)):
+    for k, via in BACK_PLAN:
         sel = jnp.stack([distance_of(k), core])
-        made = backward_call(
-            sel, cols, live, tiles, back_own, back_got, extra.get(k), grads if step == 3 else None
-        )
-        if step == 3:
+        along = grads if k == 5 else None
+        made = backward_call(sel, cols, live, tiles, back_own, back_got, extra.get(k), along)
+        if along is not None:
             grads = made[1]
         moved = send(made[0], back(column_pairs(k, via)))
         if via is None:

time: 251 us -> 241 us (0.960)
  local copies, waits for them, and re-layouts: 15.2 us -> 7.66 us
  Pallas kernels: 78.6 us -> 85.9 us
  waiting for transfers between devices: 65.3 us -> 58.6 us
  starting transfers between devices: 85.9 us -> 81 us
    unnamed x23 -> x29, local copies, waits for them, and re-layouts: 12.8 us -> 2.56 us
    pallas_call x8, Pallas kernels: 33 us -> 42.2 us  [forward_call(): pl.pallas_call(functools.partial(forward_body, first, passed), out_shape=...]
    ppermute x32, waiting for transfers between devices: 65.3 us -> 58.6 us  [send(): return lax.ppermute(value, AXES, pairs)]
    ppermute x32, starting transfers between devices: 85.9 us -> 81 us  [send(): return lax.ppermute(value, AXES, pairs)]
    pallas_call x8, Pallas kernels: 43.3 us -> 39.3 us  [backward_call(): pl.pallas_call(functools.partial(backward_body, added, passed), out_shape...]
  transfers between devices with their start and end apart: 32 -> 32, of which waited for: 11 -> 11; matrix products, arithmetic and copies ran while one was open for 3% -> 4% of each run, Pallas kernels for 29% -> 30%
where the time goes in v3:
time: 241 us; the launch traced here: 239 us
  Pallas kernels  85.9 us (36%)
  starting transfers between devices  81 us (34%)
  waiting for transfers between devices  58.6 us (24%)
  local copies, waits for them, and re-layouts  7.66 us (3%)
  other arithmetic  4.92 us (2%)
    ppermute x32, starting transfers between devices, send(): return lax.ppermute(value, AXES, pairs)  81 us
    ppermute x32, waiting for transfers between devices, send(): return lax.ppermute(value, AXES, pairs)  58.6 us
    pallas_call x8, Pallas kernels, forward_call(): pl.pallas_call(functools.partial(forward_body, first, passed), out_shape=...  42.2 us
    pallas_call x8, Pallas kernels, backward_call(): pl.pallas_call(functools.partial(backward_body, added, passed), out_shape...  39.3 us
  transfers between devices with their start and end apart: 32, of which 11 were waited for; matrix products, arithmetic and copies ran while one was open for 4% of the time, Pallas kernels for 30%

profile of v3, /device:TPU:1, one launch (start us, length us, event | category | flops | bytes accessed | tf_op | source)
XLA Modules:
  0.0 239.3 jit_solution(7845391619273750679)
XLA Ops:
  0.6 3.1 %collective-permute-start = (bf16[1024,256]{1,0:T(8,128)(2,1)}, bf16[1024,256]{1,0:T(8,128)(2,1)S(1)}, u32[]{:S(2)}, u32[]{:S(2)}) collective-permute-start(bf16[1024,256]{1,0:T(8,128)(2,1)} %feat_ref.1), channel_id=1, source_target_pairs={{104,0},{73,1},{42,2},{11,3},{108,4},{77,5},{46,6},{15,7},{0,8},{9... | collective-permute-start | bytes 1572872 | tf_op jit(solution)/shard_map/ppermute | solution.py:52
  3.8 3.5 %collective-permute-start.1 = (bf16[1024,256]{1,0:T(8,128)(2,1)}, bf16[1024,256]{1,0:T(8,128)(2,1)S(1)}, u32[]{:S(2)}, u32[]{:S(2)}) collective-permute-start(bf16[1024,256]{1,0:T(8,128)(2,1)} %feat_ref.1), channel_id=1, source_target_pairs={{120,0},{89,1},{58,2},{27,3},{124,4},{93,5},{62,6},{31,7},{112,8},... | collective-permute-start | bytes 1572872 | tf_op jit(solution)/shard_map/ppermute | solution.py:52
  7.3 3.6 %collective-permute-start.2 = (bf16[1024,256]{1,0:T(8,128)(2,1)}, bf16[1024,256]{1,0:T(8,128)(2,1)S(1)}, u32[]{:S(2)}, u32[]{:S(2)}) collective-permute-start(bf16[1024,256]{1,0:T(8,128)(2,1)} %feat_ref.1), channel_id=1, source_target_pairs={{110,0},{79,1},{44,2},{13,3},{106,4},{75,5},{40,6},{9,7},{6,8},{10... | collective-permute-start | bytes 1572872 | tf_op jit(solution)/shard_map/ppermute | solution.py:52
  10.9 1.8 collective-permute-start.7
  12.7 3.2 %collective-permute-start.6 = (bf16[1024,256]{1,0:T(8,128)(2,1)}, bf16[1024,256]{1,0:T(8,128)(2,1)S(1)}, u32[]{:S(2)}, u32[]{:S(2)}) collective-permute-start(bf16[1024,256]{1,0:T(8,128)(2,1)} %feat_ref.1), channel_id=1, source_target_pairs={{102,0},{71,1},{36,2},{5,3},{2,4},{99,5},{64,6},{33,7},{110,8},{79... | collective-permute-start | bytes 1572872 | tf_op jit(solution)/shard_map/ppermute | solution.py:52
  15.9 0.9 copy.18
  16.9 0.8 reshape.44.counts_ref
  17.7 12.4 %collective-permute-done.shard_ref = bf16[1024,256]{1,0:T(8,128)(2,1)S(1)} collective-permute-done((bf16[1024,256]{1,0:T(8,128)(2,1)}, bf16[1024,256]{1,0:T(8,128)(2,1)S(1)}, u32[]{:S(2)}, u32[]{:S(2)}) %collective-permute-start) | collective-permute-done | bytes 524320 | tf_op jit(solution)/shard_map/ppermute | solution.py:52
  30.1 1.9 collective-permute-start.5
  32.0 5.1 %forward_tiles.8 = (f32[1024,256]{1,0:T(8,128)}, bf16[1024,256]{1,0:T(8,128)(2,1)S(1)}) custom-call(s32[1]{0:T(128)} %bitcast.3.sel_ref, s32[384]{0:T(512)S(1)} %reshape.43.cols_ref, s32[64]{0:T(128)S(1)} %reshape.44.counts_ref, bf16[8,8,6,128,128]{4,3,2,1,0:T(8,128)(2,1)} %tiles_ref.31, ...), custom_call_target="tpu_custom_call", output_to_operand_aliasing={{1}: (5, {})} | custom-call | flops 402653184 | bytes 8388608 | tf_op jit(solution)/shard_map/forward_tiles/pallas_call | solution.py:112
  37.1 2.0 collective-permute-start.4
  39.1 7.7 %collective-permute-done.2.rest_1_ = bf16[1024,256]{1,0:T(8,128)(2,1)S(1)} collective-permute-done((bf16[1024,256]{1,0:T(8,128)(2,1)}, bf16[1024,256]{1,0:T(8,128)(2,1)S(1)}, u32[]{:S(2)}, u32[]{:S(2)}) %collective-permute-start.2) | collective-permute-done | bytes 524320 | tf_op jit(solution)/shard_map/ppermute | solution.py:52
  46.8 5.4 %forward_tiles.9 = (f32[1024,256]{1,0:T(8,128)}, bf16[1024,256]{1,0:T(8,128)(2,1)S(1)}) custom-call(s32[1]{0:T(128)} %bitcast.2.sel_ref, s32[384]{0:T(512)S(1)} %reshape.43.cols_ref, s32[64]{0:T(128)S(1)} %reshape.44.counts_ref, bf16[8,8,6,128,128]{4,3,2,1,0:T(8,128)(2,1)} %tiles_ref.31, bf16[1024,256]{1,0:T(8,128)(2,1)} %copy-done, ...), custom_call_target="tpu_custom_call", output_to_operand_aliasing={{1}: (6, {})} | custom-call | flops 402653184 | bytes 8388608 | tf_op jit(solution)/shard_map/forward_tiles/pallas_call | solution.py:112
  52.2 6.2 %collective-permute-start.3 = (bf16[1024,256]{1,0:T(8,128)(2,1)S(1)}, bf16[1024,256]{1,0:T(8,128)(2,1)S(1)}, u32[]{:S(2)}, u32[]{:S(2)}) collective-permute-start(bf16[1024,256]{1,0:T(8,128)(2,1)S(1)} %get-tuple-element.18.shard_ref), channel_id=1, source_target_pairs={{120,0},{121,1},{122,2},{123,3},{124,4},{125,5},{126,6},{127,7},{1... | collective-permute-start | bytes 1572872 | tf_op jit(solution)/shard_map/ppermute | solution.py:52
  58.6 5.3 %forward_tiles.10.rest_0_ = f32[1024,256]{1,0:T(8,128)} custom-call(s32[1]{0:T(128)} %bitcast.7.sel_ref, s32[384]{0:T(512)S(1)} %reshape.43.cols_ref, s32[64]{0:T(128)S(1)} %reshape.44.counts_ref, bf16[8,8,6,128,128]{4,3,2,1,0:T(8,128)(2,1)} %tiles_ref.31, bf16[1024,256]{1,0:T(8,128)(2,1)S(1)} %get-tuple-element.18.shard_ref, ...), custom_call_target="tpu_custom_call" | custom-call | flops 402653184 | bytes 8388608 | tf_op jit(solution)/shard_map/forward_tiles/pallas_call | solution.py:112
  63.9 5.2 %forward_tiles.11.rest_0_ = f32[1024,256]{1,0:T(8,128)} custom-call(s32[1]{0:T(128)} %bitcast.6.sel_ref, s32[384]{0:T(512)S(1)} %reshape.43.cols_ref, s32[64]{0:T(128)S(1)} %reshape.44.counts_ref, bf16[8,8,6,128,128]{4,3,2,1,0:T(8,128)(2,1)} %tiles_ref.31, bf16[1024,256]{1,0:T(8,128)(2,1)S(1)} %collective-permute-done.7.shard_ref, ...), custom_call_target="tpu_custom_call" | custom-call | flops 402653184 | bytes 8388608 | tf_op jit(solution)/shard_map/forward_tiles/pallas_call | solution.py:112
  69.2 5.3 %forward_tiles.12.rest_0_ = f32[1024,256]{1,0:T(8,128)} custom-call(s32[1]{0:T(128)} %bitcast.5.sel_ref, s32[384]{0:T(512)S(1)} %reshape.43.cols_ref, s32[64]{0:T(128)S(1)} %reshape.44.counts_ref, bf16[8,8,6,128,128]{4,3,2,1,0:T(8,128)(2,1)} %tiles_ref.31, bf16[1024,256]{1,0:T(8,128)(2,1)S(1)} %collective-permute-done.6.shard_ref, ...), custom_call_target="tpu_custom_call" | custom-call | flops 402653184 | bytes 8388608 | tf_op jit(solution)/shard_map/forward_tiles/pallas_call | solution.py:112
  74.5 5.2 %forward_tiles.13.rest_0_ = f32[1024,256]{1,0:T(8,128)} custom-call(s32[1]{0:T(128)} %constant.135.clone.1.sel_ref, s32[384]{0:T(512)S(1)} %reshape.43.cols_ref, s32[64]{0:T(128)S(1)} %reshape.44.counts_ref, bf16[8,8,6,128,128]{4,3,2,1,0:T(8,128)(2,1)} %tiles_ref.31, bf16[1024,256]{1,0:T(8,128)(2,1)S(1)} %collective-permute-done.5.shard_ref, ...), custom_call_target="tpu_custom_call" | custom-call | flops 402653184 | bytes 8388608 | tf_op jit(solution)/shard_map/forward_tiles/pallas_call | solution.py:112
  79.8 5.3 %forward_tiles.14.rest_0_ = f32[1024,256]{1,0:T(8,128)} custom-call(s32[1]{0:T(128)} %bitcast.4.sel_ref, s32[384]{0:T(512)S(1)} %reshape.43.cols_ref, s32[64]{0:T(128)S(1)} %reshape.44.counts_ref, bf16[8,8,6,128,128]{4,3,2,1,0:T(8,128)(2,1)} %tiles_ref.31, bf16[1024,256]{1,0:T(8,128)(2,1)S(1)} %collective-permute-done.4.shard_ref, ...), custom_call_target="tpu_custom_call" | custom-call | flops 402653184 | bytes 8388608 | tf_op jit(solution)/shard_map/forward_tiles/pallas_call | solution.py:112
  85.1 5.3 %forward_tiles.15 = f32[1024,256]{1,0:T(8,128)} custom-call(s32[1]{0:T(128)} %bitcast.1.sel_ref, s32[384]{0:T(512)S(1)} %reshape.43.cols_ref, s32[64]{0:T(128)S(1)} %reshape.44.counts_ref, bf16[8,8,6,128,128]{4,3,2,1,0:T(8,128)(2,1)} %tiles_ref.31, bf16[1024,256]{1,0:T(8,128)(2,1)S(1)} %collective-permute-done.3.shard_ref, f32[1024,256]{1,0:T(8,128)} %forward_tiles.14.rest_0_), custom_call_target="tpu_custom_call" | custom-call | flops 402653184 | bytes 8388608 | tf_op jit(solution)/shard_map/forward_tiles/pallas_call | solution.py:112
  90.5 1.1 fusion.1
  91.5 9.1 %collective-permute-start.8 = (bf16[2,256,256]{2,1,0:T(8,128)(2,1)S(1)}, bf16[2,256,256]{2,1,0:T(8,128)(2,1)S(1)}, u32[]{:S(2)}, u32[]{:S(2)}) collective-permute-start(bf16[2,256,256]{2,1,0:T(8,128)(2,1)S(1)} %fusion.1), channel_id=1, source_target_pairs={{0,1},{1,0},{2,3},{3,2},{4,5},{5,4},{6,7},{7,6},{8,9},{9,8},{10,11... | collective-permute-start | bytes 786440 | tf_op jit(solution)/shard_map/ppermute | solution.py:52
  100.8 1.1 collective-permute-done.8
  101.8 1.1 fusion.own_ref
  102.9 0.3 collective-permute-start.9
  103.3 1.0 copy.21.inv_ref
  104.3 1.0 copy.20.mask_ref
  105.5 6.7 %collective-permute-done.9.got_ref = bf16[2,256,256]{2,1,0:T(8,128)(2,1)S(1)} collective-permute-done((bf16[2,256,256]{2,1,0:T(8,128)(2,1)S(1)}, bf16[2,256,256]{2,1,0:T(8,128)(2,1)S(1)}, u32[]{:S(2)}, u32[]{:S(2)}) %collective-permute-start.9) | collective-permute-done | bytes 262176 | tf_op jit(solution)/shard_map/ppermute | solution.py:52
  112.2 0.7 copy-done.10
  112.9 3.6 %dense_rows.1 = (bf16[256,256]{1,0:T(8,128)(2,1)}, f32[256,256]{1,0:T(8,128)S(1)}, bf16[2,256,256]{2,1,0:T(8,128)(2,1)S(1)}, f32[256,256]{1,0:T(8,128)}, f32[1,256]{1,0:T(1,128)S(1)}) custom-call(s32[1]{0:T(128)} %bitcast.rep_ref, bf16[2,256,256]{2,1,0:T(8,128)(2,1)} %copy-done.5, bf16[2,256,256]{2,1,0:T(8,128)(2,1)} %copy-done.10, ...), custom_call_target="tpu_custom_call" | custom-call | tf_op jit(solution)/shard_map/dense_rows/pallas_call | solution.py:171
  116.5 1.2 collective-permute-start.10
  117.9 1.0 collective-permute-done.22
  118.9 0.9 copy-done.1
  119.9 4.8 %backward_tiles.14 = (bf16[8,256,128]{2,1,0:T(8,128)(2,1)}, f32[256,256]{1,0:T(8,128)S(1)}) custom-call(s32[2]{0:T(128)S(1)} %pad_add_fusion.7.sel_ref, s32[384]{0:T(512)S(1)} %reshape.43.cols_ref, s32[64]{0:T(128)S(1)} %reshape.44.counts_ref, bf16[8,8,6,128,128]{4,3,2,1,0:T(8,128)(2,1)} %tiles_ref.31, ...), custom_call_target="tpu_custom_call", output_to_operand_aliasing={{1}: (6, {})} | custom-call | flops 3221225472 | bytes 67108864 | tf_op jit(solution)/shard_map/backward_tiles/pallas_call | solution.py:223
  124.7 0.5 collective-permute-start.21
  125.1 4.8 %backward_tiles.8 = bf16[8,256,128]{2,1,0:T(8,128)(2,1)} custom-call(s32[2]{0:T(128)S(1)} %pad_add_fusion.sel_ref, s32[384]{0:T(512)S(1)} %reshape.43.cols_ref, s32[64]{0:T(128)S(1)} %reshape.44.counts_ref, bf16[8,8,6,128,128]{4,3,2,1,0:T(8,128)(2,1)} %tiles_ref.31, bf16[2,256,256]{2,1,0:T(8,128)(2,1)S(1)} %get-tuple-element.21.own_ref, ...), custom_call_target="tpu_custom_call" | custom-call | flops 3221225472 | bytes 67108864 | tf_op jit(solution)/shard_map/backward_tiles/pallas_call | solution.py:223
  130.0 4.8 %backward_tiles.9 = bf16[8,256,128]{2,1,0:T(8,128)(2,1)} custom-call(s32[2]{0:T(128)S(1)} %pad_add_fusion.1.sel_ref, s32[384]{0:T(512)S(1)} %reshape.43.cols_ref, s32[64]{0:T(128)S(1)} %reshape.44.counts_ref, bf16[8,8,6,128,128]{4,3,2,1,0:T(8,128)(2,1)} %tiles_ref.31, bf16[2,256,256]{2,1,0:T(8,128)(2,1)S(1)} %get-tuple-element.21.own_ref, ...), custom_call_target="tpu_custom_call" | custom-call | flops 3221225472 | bytes 67108864 | tf_op jit(solution)/shard_map/backward_tiles/pallas_call | solution.py:223
  134.9 0.7 collective-permute-start.12
  135.8 1.4 collective-permute-start.24
  137.2 2.4 %collective-permute-start.25 = (bf16[144,256]{1,0:T(8,128)(2,1)S(1)}, bf16[144,256]{1,0:T(8,128)(2,1)S(1)}, u32[]{:S(2)}, u32[]{:S(2)}) collective-permute-start(bf16[144,256]{1,0:T(8,128)(2,1)S(1)} %maximum_maximum_fusion), channel_id=1, source_target_pairs={{0,96},{1,97},{2,98},{3,99},{4,100},{5,101},{6,102},{7,103},{8,104... | collective-permute-start | bytes 221192 | tf_op jit(solution)/shard_map/ppermute | solution.py:52
  139.6 4.8 %backward_tiles.10 = bf16[8,256,128]{2,1,0:T(8,128)(2,1)} custom-call(s32[2]{0:T(128)S(1)} %pad_add_fusion.2.sel_ref, s32[384]{0:T(512)S(1)} %reshape.43.cols_ref, s32[64]{0:T(128)S(1)} %reshape.44.counts_ref, bf16[8,8,6,128,128]{4,3,2,1,0:T(8,128)(2,1)} %tiles_ref.31, bf16[2,256,256]{2,1,0:T(8,128)(2,1)S(1)} %get-tuple-element.21.own_ref, ...), custom_call_target="tpu_custom_call" | custom-call | flops 3221225472 | bytes 67108864 | tf_op jit(solution)/shard_map/backward_tiles/pallas_call | solution.py:223
  144.5 3.4 %collective-permute-done.23 = bf16[144,256]{1,0:T(8,128)(2,1)S(1)} collective-permute-done((bf16[144,256]{1,0:T(8,128)(2,1)S(1)}, bf16[144,256]{1,0:T(8,128)(2,1)S(1)}, u32[]{:S(2)}, u32[]{:S(2)}) %collective-permute-start.23) | collective-permute-done | bytes 73760 | tf_op jit(solution)/shard_map/ppermute | solution.py:52
  148.1 2.0 collective-permute-start.26
  150.1 9.0 %collective-permute-start.27 = (bf16[144,256]{1,0:T(8,128)(2,1)S(1)}, bf16[144,256]{1,0:T(8,128)(2,1)S(1)}, u32[]{:S(2)}, u32[]{:S(2)}) collective-permute-start(bf16[144,256]{1,0:T(8,128)(2,1)S(1)} %maximum_maximum_fusion.1), channel_id=1, source_target_pairs={{0,16},{1,17},{2,18},{3,19},{4,20},{5,21},{6,22},{7,23},{8,24},{9,... | collective-permute-start | bytes 221192 | tf_op jit(solution)/shard_map/ppermute | solution.py:52
  159.0 4.8 %backward_tiles.12 = bf16[8,256,128]{2,1,0:T(8,128)(2,1)} custom-call(s32[2]{0:T(128)S(1)} %pad_add_fusion.5.sel_ref, s32[384]{0:T(512)S(1)} %reshape.43.cols_ref, s32[64]{0:T(128)S(1)} %reshape.44.counts_ref, bf16[8,8,6,128,128]{4,3,2,1,0:T(8,128)(2,1)} %tiles_ref.31, bf16[2,256,256]{2,1,0:T(8,128)(2,1)S(1)} %get-tuple-element.21.own_ref, ...), custom_call_target="tpu_custom_call" | custom-call | flops 3221225472 | bytes 67108864 | tf_op jit(solution)/shard_map/backward_tiles/pallas_call | solution.py:223
  163.8 2.9 %collective-permute-start.13 = (bf16[8,256,128]{2,1,0:T(8,128)(2,1)S(1)}, bf16[8,256,128]{2,1,0:T(8,128)(2,1)}, u32[]{:S(2)}, u32[]{:S(2)}) collective-permute-start(bf16[8,256,128]{2,1,0:T(8,128)(2,1)S(1)} %copy-done.7), channel_id=1, source_target_pairs={{0,102},{1,71},{2,36},{3,5},{4,2},{5,99},{6,64},{7,33},{8,110},{9,... | collective-permute-start | bytes 1572872 | tf_op jit(solution)/shard_map/ppermute | solution.py:52
  167.1 4.8 %backward_tiles.11 = bf16[8,256,128]{2,1,0:T(8,128)(2,1)} custom-call(s32[2]{0:T(128)S(1)} %pad_add_fusion.3.sel_ref, s32[384]{0:T(512)S(1)} %reshape.43.cols_ref, s32[64]{0:T(128)S(1)} %reshape.44.counts_ref, bf16[8,8,6,128,128]{4,3,2,1,0:T(8,128)(2,1)} %tiles_ref.31, bf16[2,256,256]{2,1,0:T(8,128)(2,1)S(1)} %get-tuple-element.21.own_ref, ...), custom_call_target="tpu_custom_call" | custom-call | flops 3221225472 | bytes 67108864 | tf_op jit(solution)/shard_map/backward_tiles/pallas_call | solution.py:223
  171.9 3.3 %collective-permute-start.17 = (bf16[8,256,128]{2,1,0:T(8,128)(2,1)S(1)}, bf16[8,256,128]{2,1,0:T(8,128)(2,1)S(1)}, u32[]{:S(2)}, u32[]{:S(2)}) collective-permute-start(bf16[8,256,128]{2,1,0:T(8,128)(2,1)S(1)} %copy-done.13), channel_id=1, source_target_pairs={{0,120},{1,121},{2,122},{3,123},{4,124},{5,125},{6,126},{7,127},{8... | collective-permute-start | bytes 1572872 | tf_op jit(solution)/shard_map/ppermute | solution.py:52
  175.3 4.4 %collective-permute-done.15.rest_0_ = bf16[8,256,128]{2,1,0:T(8,128)(2,1)S(1)} collective-permute-done((bf16[8,256,128]{2,1,0:T(8,128)(2,1)}, bf16[8,256,128]{2,1,0:T(8,128)(2,1)S(1)}, u32[]{:S(2)}, u32[]{:S(2)}) %collective-permute-start.15) | collective-permute-done | bytes 524320 | tf_op jit(solution)/shard_map/ppermute | solution.py:52
  179.7 2.4 collective-permute-start.14
  182.2 5.3 %backward_tiles.13 = bf16[8,256,128]{2,1,0:T(8,128)(2,1)} custom-call(s32[2]{0:T(128)S(1)} %pad_add_fusion.4.sel_ref, s32[384]{0:T(512)S(1)} %reshape.43.cols_ref, s32[64]{0:T(128)S(1)} %reshape.44.counts_ref, bf16[8,8,6,128,128]{4,3,2,1,0:T(8,128)(2,1)} %tiles_ref.31, bf16[2,256,256]{2,1,0:T(8,128)(2,1)S(1)} %get-tuple-element.21.own_ref, ...), custom_call_target="tpu_custom_call" | custom-call | flops 3221225472 | bytes 67108864 | tf_op jit(solution)/shard_map/backward_tiles/pallas_call | solution.py:223
  187.4 4.9 %collective-permute-start.30 = (f32[128,256]{1,0:T(8,128)S(1)}, f32[128,256]{1,0:T(8,128)S(1)}, u32[]{:S(2)}, u32[]{:S(2)}) collective-permute-start(f32[128,256]{1,0:T(8,128)S(1)} %get-tuple-element.32), channel_id=1, source_target_pairs={{0,2},{1,3},{2,0},{3,1},{4,6},{5,7},{6,4},{7,5},{8,10},{9,11},{10,... | collective-permute-start | bytes 393224 | tf_op jit(solution)/shard_map/ppermute | solution.py:52
  192.3 5.3 %backward_tiles.15 = bf16[8,256,128]{2,1,0:T(8,128)(2,1)} custom-call(s32[2]{0:T(128)S(1)} %pad_add_fusion.6.sel_ref, s32[384]{0:T(512)S(1)} %reshape.43.cols_ref, s32[64]{0:T(128)S(1)} %reshape.44.counts_ref, bf16[8,8,6,128,128]{4,3,2,1,0:T(8,128)(2,1)} %tiles_ref.31, bf16[2,256,256]{2,1,0:T(8,128)(2,1)S(1)} %get-tuple-element.21.own_ref, ...), custom_call_target="tpu_custom_call" | custom-call | flops 3221225472 | bytes 67108864 | tf_op jit(solution)/shard_map/backward_tiles/pallas_call | solution.py:223
  197.6 2.3 collective-permute-start.16
  200.0 0.6 fusion.5
  200.6 4.2 %collective-permute-start.31 = (f32[2,128,256]{2,1,0:T(8,128)S(1)}, f32[2,128,256]{2,1,0:T(8,128)S(1)}, u32[]{:S(2)}, u32[]{:S(2)}) collective-permute-start(f32[2,128,256]{2,1,0:T(8,128)S(1)} %maximum_select_fusion), channel_id=1, source_target_pairs={{0,1},{1,0},{2,3},{3,2},{4,5},{5,4},{6,7},{7,6},{8,9},{9,8},{10,11... | collective-permute-start | bytes 786440 | tf_op jit(solution)/shard_map/ppermute | solution.py:52
  204.8 8.1 %collective-permute-done.16 = bf16[8,256,128]{2,1,0:T(8,128)(2,1)} collective-permute-done((bf16[8,256,128]{2,1,0:T(8,128)(2,1)}, bf16[8,256,128]{2,1,0:T(8,128)(2,1)}, u32[]{:S(2)}, u32[]{:S(2)}) %collective-permute-start.16) | collective-permute-done | bytes 524320 | tf_op jit(solution)/shard_map/ppermute | solution.py:52
  212.9 7.3 %collective-permute-done.18 = bf16[8,256,128]{2,1,0:T(8,128)(2,1)} collective-permute-done((bf16[8,256,128]{2,1,0:T(8,128)(2,1)}, bf16[8,256,128]{2,1,0:T(8,128)(2,1)}, u32[]{:S(2)}, u32[]{:S(2)}) %collective-permute-start.18) | collective-permute-done | bytes 524320 | tf_op jit(solution)/shard_map/ppermute | solution.py:52
  220.2 1.9 convert_add_fusion
  222.2 8.7 %collective-permute-start.19 = (bf16[2,2,256,128]{3,2,1,0:T(8,128)(2,1)S(1)}, bf16[2,2,256,128]{3,2,1,0:T(8,128)(2,1)S(1)}, u32[]{:S(2)}, u32[]{:S(2)}) collective-permute-start(bf16[2,2,256,128]{3,2,1,0:T(8,128)(2,1)S(1)} %fusion.2), channel_id=1, source_target_pairs={{0,1},{1,0},{2,3},{3,2},{4,5},{5,4},{6,7},{7,6},{8,9},{9,8},{10,11... | collective-permute-start | bytes 786440 | tf_op jit(solution)/shard_map/ppermute | solution.py:52
  231.0 1.1 collective-permute-done.19
  232.3 0.8 slice_bitcast_fusion
  233.1 5.4 %collective-permute-done.20.got_ref = bf16[2,256,128]{2,1,0:T(8,128)(2,1)S(1)} collective-permute-done((bf16[2,256,128]{2,1,0:T(8,128)(2,1)S(1)}, bf16[2,256,128]{2,1,0:T(8,128)(2,1)S(1)}, u32[]{:S(2)}, u32[]{:S(2)}) %collective-permute-start.20) | collective-permute-done | bytes 131104 | tf_op jit(solution)/shard_map/ppermute | solution.py:52
  238.5 0.8 final_rows.1
  (89 shorter events, 2.2 us)
Async XLA Ops:
  0.6 29.4 %collective-permute-start = (bf16[1024,256]{1,0:T(8,128)(2,1)}, bf16[1024,256]{1,0:T(8,128)(2,1)S(1)}, u32[]{:S(2)}, u32[]{:S(2)}) collective-permute-start(bf16[1024,256]{1,0:T(8,128)(2,1)} %feat_ref.1), channel_id=1, source_target_pairs={{104,0},{73,1},{42,2},{11,3},{108,4},{77,5},{46,6},{15,7},{0,8},{9... | collective-permute-start | bytes 1572872 | tf_op jit(solution)/shard_map/ppermute | solution.py:52
  3.8 28.2 %collective-permute-start.1 = (bf16[1024,256]{1,0:T(8,128)(2,1)}, bf16[1024,256]{1,0:T(8,128)(2,1)S(1)}, u32[]{:S(2)}, u32[]{:S(2)}) collective-permute-start(bf16[1024,256]{1,0:T(8,128)(2,1)} %feat_ref.1), channel_id=1, source_target_pairs={{120,0},{89,1},{58,2},{27,3},{124,4},{93,5},{62,6},{31,7},{112,8},... | collective-permute-start | bytes 1572872 | tf_op jit(solution)/shard_map/ppermute | solution.py:52
  7.3 39.5 %collective-permute-start.2 = (bf16[1024,256]{1,0:T(8,128)(2,1)}, bf16[1024,256]{1,0:T(8,128)(2,1)S(1)}, u32[]{:S(2)}, u32[]{:S(2)}) collective-permute-start(bf16[1024,256]{1,0:T(8,128)(2,1)} %feat_ref.1), channel_id=1, source_target_pairs={{110,0},{79,1},{44,2},{13,3},{106,4},{75,5},{40,6},{9,7},{6,8},{10... | collective-permute-start | bytes 1572872 | tf_op jit(solution)/shard_map/ppermute | solution.py:52
  10.9 53.1 %collective-permute-start.7 = (bf16[1024,256]{1,0:T(8,128)(2,1)}, bf16[1024,256]{1,0:T(8,128)(2,1)S(1)}, u32[]{:S(2)}, u32[]{:S(2)}) collective-permute-start(bf16[1024,256]{1,0:T(8,128)(2,1)} %feat_ref.1), channel_id=1, source_target_pairs={{126,0},{95,1},{60,2},{29,3},{122,4},{91,5},{56,6},{25,7},{118,8},... | collective-permute-start | bytes 1572872 | tf_op jit(solution)/shard_map/ppermute | solution.py:52
  12.7 56.5 %collective-permute-start.6 = (bf16[1024,256]{1,0:T(8,128)(2,1)}, bf16[1024,256]{1,0:T(8,128)(2,1)S(1)}, u32[]{:S(2)}, u32[]{:S(2)}) collective-permute-start(bf16[1024,256]{1,0:T(8,128)(2,1)} %feat_ref.1), channel_id=1, source_target_pairs={{102,0},{71,1},{36,2},{5,3},{2,4},{99,5},{64,6},{33,7},{110,8},{79... | collective-permute-start | bytes 1572872 | tf_op jit(solution)/shard_map/ppermute | solution.py:52
  30.1 1.9 copy-start.6
  30.1 44.4 %collective-permute-start.5 = (bf16[1024,256]{1,0:T(8,128)(2,1)}, bf16[1024,256]{1,0:T(8,128)(2,1)S(1)}, u32[]{:S(2)}, u32[]{:S(2)}) collective-permute-start(bf16[1024,256]{1,0:T(8,128)(2,1)} %feat_ref.1), channel_id=1, source_target_pairs={{0,0},{97,1},{66,2},{35,3},{4,4},{101,5},{70,6},{39,7},{8,8},{105,... | collective-permute-start | bytes 1572872 | tf_op jit(solution)/shard_map/ppermute | solution.py:52
  37.1 9.7 %copy-start = (bf16[1024,256]{1,0:T(8,128)(2,1)}, bf16[1024,256]{1,0:T(8,128)(2,1)S(1)}, u32[]{:S(2)}) copy-start(bf16[1024,256]{1,0:T(8,128)(2,1)S(1)} %get-tuple-element.16.shard_ref) | copy-start | bytes 1572868
  37.1 42.7 %collective-permute-start.4 = (bf16[1024,256]{1,0:T(8,128)(2,1)S(1)}, bf16[1024,256]{1,0:T(8,128)(2,1)S(1)}, u32[]{:S(2)}, u32[]{:S(2)}) collective-permute-start(bf16[1024,256]{1,0:T(8,128)(2,1)S(1)} %get-tuple-element.16.shard_ref), channel_id=1, source_target_pairs={{8,0},{9,1},{10,2},{11,3},{12,4},{13,5},{14,6},{15,7},{0,8},{1,9},... | collective-permute-start | bytes 1572872 | tf_op jit(solution)/shard_map/ppermute | solution.py:52
  52.2 32.9 %collective-permute-start.3 = (bf16[1024,256]{1,0:T(8,128)(2,1)S(1)}, bf16[1024,256]{1,0:T(8,128)(2,1)S(1)}, u32[]{:S(2)}, u32[]{:S(2)}) collective-permute-start(bf16[1024,256]{1,0:T(8,128)(2,1)S(1)} %get-tuple-element.18.shard_ref), channel_id=1, source_target_pairs={{120,0},{121,1},{122,2},{123,3},{124,4},{125,5},{126,6},{127,7},{1... | collective-permute-start | bytes 1572872 | tf_op jit(solution)/shard_map/ppermute | solution.py:52
  79.8 21.0 %copy-start.11 = (s32[1024]{0:T(1024)S(1)}, s32[1024]{0:T(1024)}, u32[]{:S(2)}) copy-start(s32[1024]{0:T(1024)} %param.14) | copy-start | bytes 12292
  79.8 24.6 %copy-start.12 = (s32[1024]{0:T(1024)S(1)}, s32[1024]{0:T(1024)}, u32[]{:S(2)}) copy-start(s32[1024]{0:T(1024)} %param.15) | copy-start | bytes 12292
  85.1 27.9 %copy-start.2 = (bf16[256,256]{1,0:T(8,128)(2,1)S(1)}, bf16[256,256]{1,0:T(8,128)(2,1)}, u32[]{:S(2)}) copy-start(bf16[256,256]{1,0:T(8,128)(2,1)} %ws_ref.1) | copy-start | bytes 393220
  85.1 27.8 %copy-start.3 = (bf16[256,256]{1,0:T(8,128)(2,1)S(1)}, bf16[256,256]{1,0:T(8,128)(2,1)}, u32[]{:S(2)}) copy-start(bf16[256,256]{1,0:T(8,128)(2,1)} %wn_ref.1) | copy-start | bytes 393220
  85.1 27.8 %copy-start.4 = (f32[256]{0:T(256)S(1)}, f32[256]{0:T(256)}, u32[]{:S(2)}) copy-start(f32[256]{0:T(256)} %param.19) | copy-start | bytes 3076
  91.5 10.3 %collective-permute-start.8 = (bf16[2,256,256]{2,1,0:T(8,128)(2,1)S(1)}, bf16[2,256,256]{2,1,0:T(8,128)(2,1)S(1)}, u32[]{:S(2)}, u32[]{:S(2)}) collective-permute-start(bf16[2,256,256]{2,1,0:T(8,128)(2,1)S(1)} %fusion.1), channel_id=1, source_target_pairs={{0,1},{1,0},{2,3},{3,2},{4,5},{5,4},{6,7},{7,6},{8,9},{9,8},{10,11... | collective-permute-start | bytes 786440 | tf_op jit(solution)/shard_map/ppermute | solution.py:52
  102.9 9.3 %copy-start.5 = (bf16[2,256,256]{2,1,0:T(8,128)(2,1)}, bf16[2,256,256]{2,1,0:T(8,128)(2,1)S(1)}, u32[]{:S(2)}) copy-start(bf16[2,256,256]{2,1,0:T(8,128)(2,1)S(1)} %fusion.own_ref) | copy-start | bytes 786436
  102.9 9.3 %collective-permute-start.9 = (bf16[2,256,256]{2,1,0:T(8,128)(2,1)S(1)}, bf16[2,256,256]{2,1,0:T(8,128)(2,1)S(1)}, u32[]{:S(2)}, u32[]{:S(2)}) collective-permute-start(bf16[2,256,256]{2,1,0:T(8,128)(2,1)S(1)} %fusion.own_ref), channel_id=1, source_target_pairs={{0,2},{1,3},{2,0},{3,1},{4,6},{5,7},{6,4},{7,5},{8,10},{9,11},{10,... | collective-permute-start | bytes 786440 | tf_op jit(solution)/shard_map/ppermute | solution.py:52
  112.2 0.7 copy-start.10
  116.5 2.4 collective-permute-start.10
  117.7 1.2 collective-permute-start.22
  118.9 1.0 copy-start.1
  124.7 10.9 %collective-permute-start.21 = (f32[128,256]{1,0:T(8,128)S(1)}, f32[128,256]{1,0:T(8,128)S(1)}, u32[]{:S(2)}, u32[]{:S(2)}) collective-permute-start(f32[128,256]{1,0:T(8,128)S(1)} %dynamic-slice_bitcast_fusion.1), channel_id=1, source_target_pairs={{0,1},{1,0},{2,3},{3,2},{4,5},{5,4},{6,7},{7,6},{8,9},{9,8},{10,11... | collective-permute-start | bytes 393224 | tf_op jit(solution)/shard_map/ppermute | solution.py:52
  130.0 70.0 %collective-permute-start.11 = (bf16[8,256,128]{2,1,0:T(8,128)(2,1)}, bf16[8,256,128]{2,1,0:T(8,128)(2,1)S(1)}, u32[]{:S(2)}, u32[]{:S(2)}) collective-permute-start(bf16[8,256,128]{2,1,0:T(8,128)(2,1)} %backward_tiles.8), channel_id=1, source_target_pairs={{0,104},{1,73},{2,42},{3,11},{4,108},{5,77},{6,46},{7,15},{8,0},{9... | collective-permute-start | bytes 1572872 | tf_op jit(solution)/shard_map/ppermute | solution.py:52
  134.9 65.7 %collective-permute-start.12 = (bf16[8,256,128]{2,1,0:T(8,128)(2,1)}, bf16[8,256,128]{2,1,0:T(8,128)(2,1)S(1)}, u32[]{:S(2)}, u32[]{:S(2)}) collective-permute-start(bf16[8,256,128]{2,1,0:T(8,128)(2,1)} %backward_tiles.9), channel_id=1, source_target_pairs={{0,126},{1,95},{2,60},{3,29},{4,122},{5,91},{6,56},{7,25},{8,118},... | collective-permute-start | bytes 1572872 | tf_op jit(solution)/shard_map/ppermute | solution.py:52
  135.7 12.1 %collective-permute-start.23 = (bf16[144,256]{1,0:T(8,128)(2,1)S(1)}, bf16[144,256]{1,0:T(8,128)(2,1)S(1)}, u32[]{:S(2)}, u32[]{:S(2)}) collective-permute-start(bf16[144,256]{1,0:T(8,128)(2,1)S(1)} %maximum_maximum_fusion), channel_id=1, source_target_pairs={{0,32},{1,33},{2,34},{3,35},{4,36},{5,37},{6,38},{7,39},{8,40},{9,... | collective-permute-start | bytes 221192 | tf_op jit(solution)/shard_map/ppermute | solution.py:52
  135.8 12.1 %collective-permute-start.24 = (bf16[144,256]{1,0:T(8,128)(2,1)S(1)}, bf16[144,256]{1,0:T(8,128)(2,1)S(1)}, u32[]{:S(2)}, u32[]{:S(2)}) collective-permute-start(bf16[144,256]{1,0:T(8,128)(2,1)S(1)} %maximum_maximum_fusion), channel_id=1, source_target_pairs={{0,64},{1,65},{2,66},{3,67},{4,68},{5,69},{6,70},{7,71},{8,72},{9,... | collective-permute-start | bytes 221192 | tf_op jit(solution)/shard_map/ppermute | solution.py:52
  137.2 10.6 %collective-permute-start.25 = (bf16[144,256]{1,0:T(8,128)(2,1)S(1)}, bf16[144,256]{1,0:T(8,128)(2,1)S(1)}, u32[]{:S(2)}, u32[]{:S(2)}) collective-permute-start(bf16[144,256]{1,0:T(8,128)(2,1)S(1)} %maximum_maximum_fusion), channel_id=1, source_target_pairs={{0,96},{1,97},{2,98},{3,99},{4,100},{5,101},{6,102},{7,103},{8,104... | collective-permute-start | bytes 221192 | tf_op jit(solution)/shard_map/ppermute | solution.py:52
  144.4 19.4 %copy-start.7 = (bf16[8,256,128]{2,1,0:T(8,128)(2,1)S(1)}, bf16[8,256,128]{2,1,0:T(8,128)(2,1)}, u32[]{:S(2)}) copy-start(bf16[8,256,128]{2,1,0:T(8,128)(2,1)} %backward_tiles.10) | copy-start | bytes 1572868
  148.1 23.8 %copy-start.13 = (bf16[8,256,128]{2,1,0:T(8,128)(2,1)S(1)}, bf16[8,256,128]{2,1,0:T(8,128)(2,1)}, u32[]{:S(2)}) copy-start(bf16[8,256,128]{2,1,0:T(8,128)(2,1)} %get-tuple-element.23) | copy-start | bytes 1572868
  148.1 15.7 %collective-permute-start.26 = (bf16[144,256]{1,0:T(8,128)(2,1)S(1)}, bf16[144,256]{1,0:T(8,128)(2,1)S(1)}, u32[]{:S(2)}, u32[]{:S(2)}) collective-permute-start(bf16[144,256]{1,0:T(8,128)(2,1)S(1)} %maximum_maximum_fusion.1), channel_id=1, source_target_pairs={{0,8},{1,9},{2,10},{3,11},{4,12},{5,13},{6,14},{7,15},{8,0},{9,1},... | collective-permute-start | bytes 221192 | tf_op jit(solution)/shard_map/ppermute | solution.py:52
  150.1 16.7 %collective-permute-start.27 = (bf16[144,256]{1,0:T(8,128)(2,1)S(1)}, bf16[144,256]{1,0:T(8,128)(2,1)S(1)}, u32[]{:S(2)}, u32[]{:S(2)}) collective-permute-start(bf16[144,256]{1,0:T(8,128)(2,1)S(1)} %maximum_maximum_fusion.1), channel_id=1, source_target_pairs={{0,16},{1,17},{2,18},{3,19},{4,20},{5,21},{6,22},{7,23},{8,24},{9,... | collective-permute-start | bytes 221192 | tf_op jit(solution)/shard_map/ppermute | solution.py:52
  159.0 7.7 %collective-permute-start.28 = (bf16[144,256]{1,0:T(8,128)(2,1)S(1)}, bf16[144,256]{1,0:T(8,128)(2,1)S(1)}, u32[]{:S(2)}, u32[]{:S(2)}) collective-permute-start(bf16[144,256]{1,0:T(8,128)(2,1)S(1)} %maximum_maximum_fusion.1), channel_id=1, source_target_pairs={{0,24},{1,25},{2,26},{3,27},{4,28},{5,29},{6,30},{7,31},{8,16},{9,... | collective-permute-start | bytes 221192 | tf_op jit(solution)/shard_map/ppermute | solution.py:52
  163.8 40.9 %collective-permute-start.13 = (bf16[8,256,128]{2,1,0:T(8,128)(2,1)S(1)}, bf16[8,256,128]{2,1,0:T(8,128)(2,1)}, u32[]{:S(2)}, u32[]{:S(2)}) collective-permute-start(bf16[8,256,128]{2,1,0:T(8,128)(2,1)S(1)} %copy-done.7), channel_id=1, source_target_pairs={{0,102},{1,71},{2,36},{3,5},{4,2},{5,99},{6,64},{7,33},{8,110},{9,... | collective-permute-start | bytes 1572872 | tf_op jit(solution)/shard_map/ppermute | solution.py:52
  166.8 13.0 %collective-permute-start.15 = (bf16[8,256,128]{2,1,0:T(8,128)(2,1)}, bf16[8,256,128]{2,1,0:T(8,128)(2,1)S(1)}, u32[]{:S(2)}, u32[]{:S(2)}) collective-permute-start(bf16[8,256,128]{2,1,0:T(8,128)(2,1)} %backward_tiles.12), channel_id=1, source_target_pairs={{0,8},{1,9},{2,10},{3,11},{4,12},{5,13},{6,14},{7,15},{8,0},{9,1},... | collective-permute-start | bytes 1572872 | tf_op jit(solution)/shard_map/ppermute | solution.py:52
  167.0 4.9 %collective-permute-start.29 = (bf16[144,256]{1,0:T(8,128)(2,1)S(1)}, bf16[144,256]{1,0:T(8,128)(2,1)S(1)}, u32[]{:S(2)}, u32[]{:S(2)}) collective-permute-start(bf16[144,256]{1,0:T(8,128)(2,1)S(1)} %maximum_maximum_fusion.2), channel_id=1, source_target_pairs={{0,4},{1,5},{2,6},{3,7},{4,0},{5,1},{6,2},{7,3},{8,12},{9,13},{10,... | collective-permute-start | bytes 221192 | tf_op jit(solution)/shard_map/ppermute | solution.py:52
  171.9 15.5 %collective-permute-start.17 = (bf16[8,256,128]{2,1,0:T(8,128)(2,1)S(1)}, bf16[8,256,128]{2,1,0:T(8,128)(2,1)S(1)}, u32[]{:S(2)}, u32[]{:S(2)}) collective-permute-start(bf16[8,256,128]{2,1,0:T(8,128)(2,1)S(1)} %copy-done.13), channel_id=1, source_target_pairs={{0,120},{1,121},{2,122},{3,123},{4,124},{5,125},{6,126},{7,127},{8... | collective-permute-start | bytes 1572872 | tf_op jit(solution)/shard_map/ppermute | solution.py:52
  179.7 2.4 %copy-start.8 = (bf16[8,256,128]{2,1,0:T(8,128)(2,1)}, bf16[8,256,128]{2,1,0:T(8,128)(2,1)S(1)}, u32[]{:S(2)}) copy-start(bf16[8,256,128]{2,1,0:T(8,128)(2,1)S(1)} %collective-permute-done.15.rest_0_) | copy-start | bytes 1572868
  179.7 25.0 %collective-permute-start.14 = (bf16[8,256,128]{2,1,0:T(8,128)(2,1)}, bf16[8,256,128]{2,1,0:T(8,128)(2,1)}, u32[]{:S(2)}, u32[]{:S(2)}) collective-permute-start(bf16[8,256,128]{2,1,0:T(8,128)(2,1)} %backward_tiles.11), channel_id=1, source_target_pairs={{0,0},{1,97},{2,66},{3,35},{4,4},{5,101},{6,70},{7,39},{8,8},{9,10... | collective-permute-start | bytes 1572872 | tf_op jit(solution)/shard_map/ppermute | solution.py:52
  187.4 4.9 %copy-start.9 = (bf16[8,256,128]{2,1,0:T(8,128)(2,1)}, bf16[8,256,128]{2,1,0:T(8,128)(2,1)S(1)}, u32[]{:S(2)}) copy-start(bf16[8,256,128]{2,1,0:T(8,128)(2,1)S(1)} %collective-permute-done.17.rest_0_) | copy-start | bytes 1572868
  187.4 10.2 %collective-permute-start.30 = (f32[128,256]{1,0:T(8,128)S(1)}, f32[128,256]{1,0:T(8,128)S(1)}, u32[]{:S(2)}, u32[]{:S(2)}) collective-permute-start(f32[128,256]{1,0:T(8,128)S(1)} %get-tuple-element.32), channel_id=1, source_target_pairs={{0,2},{1,3},{2,0},{3,1},{4,6},{5,7},{6,4},{7,5},{8,10},{9,11},{10,... | collective-permute-start | bytes 393224 | tf_op jit(solution)/shard_map/ppermute | solution.py:52
  197.6 15.3 %collective-permute-start.16 = (bf16[8,256,128]{2,1,0:T(8,128)(2,1)}, bf16[8,256,128]{2,1,0:T(8,128)(2,1)}, u32[]{:S(2)}, u32[]{:S(2)}) collective-permute-start(bf16[8,256,128]{2,1,0:T(8,128)(2,1)} %backward_tiles.13), channel_id=1, source_target_pairs={{0,120},{1,89},{2,58},{3,27},{4,124},{5,93},{6,62},{7,31},{8,112},... | collective-permute-start | bytes 1572872 | tf_op jit(solution)/shard_map/ppermute | solution.py:52
  200.0 20.3 %collective-permute-start.18 = (bf16[8,256,128]{2,1,0:T(8,128)(2,1)}, bf16[8,256,128]{2,1,0:T(8,128)(2,1)}, u32[]{:S(2)}, u32[]{:S(2)}) collective-permute-start(bf16[8,256,128]{2,1,0:T(8,128)(2,1)} %backward_tiles.15), channel_id=1, source_target_pairs={{0,110},{1,79},{2,44},{3,13},{4,106},{5,75},{6,40},{7,9},{8,6},{9,... | collective-permute-start | bytes 1572872 | tf_op jit(solution)/shard_map/ppermute | solution.py:52
  200.6 30.4 %collective-permute-start.31 = (f32[2,128,256]{2,1,0:T(8,128)S(1)}, f32[2,128,256]{2,1,0:T(8,128)S(1)}, u32[]{:S(2)}, u32[]{:S(2)}) collective-permute-start(f32[2,128,256]{2,1,0:T(8,128)S(1)} %maximum_select_fusion), channel_id=1, source_target_pairs={{0,1},{1,0},{2,3},{3,2},{4,5},{5,4},{6,7},{7,6},{8,9},{9,8},{10,11... | collective-permute-start | bytes 786440 | tf_op jit(solution)/shard_map/ppermute | solution.py:52
  222.2 9.9 %collective-permute-start.19 = (bf16[2,2,256,128]{3,2,1,0:T(8,128)(2,1)S(1)}, bf16[2,2,256,128]{3,2,1,0:T(8,128)(2,1)S(1)}, u32[]{:S(2)}, u32[]{:S(2)}) collective-permute-start(bf16[2,2,256,128]{3,2,1,0:T(8,128)(2,1)S(1)} %fusion.2), channel_id=1, source_target_pairs={{0,1},{1,0},{2,3},{3,2},{4,5},{5,4},{6,7},{7,6},{8,9},{9,8},{10,11... | collective-permute-start | bytes 786440 | tf_op jit(solution)/shard_map/ppermute | solution.py:52
  232.2 6.3 %collective-permute-start.20 = (bf16[2,256,128]{2,1,0:T(8,128)(2,1)S(1)}, bf16[2,256,128]{2,1,0:T(8,128)(2,1)S(1)}, u32[]{:S(2)}, u32[]{:S(2)}) collective-permute-start(bf16[2,256,128]{2,1,0:T(8,128)(2,1)S(1)} %fusion.3), channel_id=1, source_target_pairs={{0,2},{1,3},{2,0},{3,1},{4,6},{5,7},{6,4},{7,5},{8,10},{9,11},{10,... | collective-permute-start | bytes 393224 | tf_op jit(solution)/shard_map/ppermute | solution.py:52

commit v4 on v1

--- a/solution.py
+++ b/solution.py
@@ -13,8 +13,11 @@
 NS = 6
 BS = 128
 F = 256
-VMEM = 40 * 1024 * 1024
-PLAN = ((2, None), (6, None), (3, None), (7, None), (1, None), (0, None), (4, 2), (5, 6))
+VMEM = 53 * 1024 * 1024
+PLAN = {6: None, 2: None, 1: None, 4: 2, 7: None, 3: None, 0: None, 5: 1}
+CROSS = {1: 0x7776, 3: 0xDFFF, 7: 0xDFEF}
+GROUPS = ((6, 2, 1), (4, 7, 3), (0,), (5,))
+BACK = ((5, ()), (2, (5,)), (1, (2,)), (4, (1,)), (7, (4,)), (3, (7,)), (0, (3,)), (6, (0,)))
 
 
 def index_of(y, x, zl, zh, core):
@@ -26,13 +29,15 @@
         yield t, t >> 5, t >> 3 & 3, t >> 2 & 1, t >> 1 & 1, t & 1
 
 
-def column_pairs(k, via):
+def column_pairs(k):
+    via = PLAN[k]
     out = []
     for t, y, x, zl, zh, core in places():
         j, r = x * 2 + zl, 2 * zh + core
         jj = j ^ k
         if via is None:
-            out.append((index_of(y - r - (jj > j), jj >> 1, jj & 1, zh ^ (k & 1), core), t))
+            flip = CROSS[k] >> (jj * 2 + core) & 1 if k & 1 else 0
+            out.append((index_of(y - r - (jj > j), jj >> 1, jj & 1, zh ^ flip, core), t))
         else:
             jn = j ^ via
             out.append((index_of(y - (jj > j) + (jj > jn), jn >> 1, jn & 1, zh, core), t))
@@ -50,53 +55,116 @@
     return lax.ppermute(value, AXES, pairs)
 
 
-def back(pairs):
-    return [(b, a) for a, b in pairs]
-
-
-def params():
-    return pltpu.CompilerParams(vmem_limit_bytes=VMEM)
-
-
-def forward_body(first, sel_ref, cols_ref, counts_ref, tiles_ref, shard_ref, *rest):
-    out_ref = rest[-1]
-    step = pl.program_id(0)
-    dist = sel_ref[0]
-    for inner in range(2):
-        b = step * 2 + inner
+def params(limit=VMEM):
+    return pltpu.CompilerParams(vmem_limit_bytes=limit)
+
+
+SMEM = pl.BlockSpec(memory_space=pltpu.SMEM)
+HBM = pl.BlockSpec(memory_space=pltpu.HBM)
+UNREAD = pl.BlockSpec(memory_space=pl.ANY)
+WHOLE = pl.BlockSpec(memory_space=pltpu.VMEM)
+
+
+def tile_cost(n):
+    return pl.CostEstimate(
+        flops=2 * NB * NS * BS * BS * F * n, bytes_accessed=(8 << 20) * n, transcendentals=0
+    )
+
+
+def forward_body(n, first, last, sel_ref, cols_ref, counts_ref, tiles_ref, *rest):
+    shards = rest[:n]
+    before = None if first else rest[n]
+    outs = rest[n + (not first) : -3]
+    total_ref, held_ref, sems = rest[-3:]
+    i, half = pl.program_id(0), pl.program_id(1)
+    dist = sel_ref[i]
+
+    def fetch(k):
+        return pltpu.make_async_copy(shards[k], held_ref.at[k % 2], sems.at[k % 2])
+
+    @pl.when((i == 0) & (half == 0))
+    def _():
+        fetch(0).start()
+
+    for k in range(n):
+
+        @pl.when((i == k) & (half == 0))
+        def _():
+            fetch(k).wait()
+            if k + 1 < n:
+                fetch(k + 1).start()
+
+    def block_row(inner, carry):
+        b = half * 4 + inner
         count = counts_ref[b * ND + dist]
         left, right = [], []
         for s in range(NS):
             col = cols_ref[(b * ND + dist) * NS + s]
-            block = shard_ref[pl.ds(pl.multiple_of(col * BS, BS), BS), :]
+            block = held_ref[i % 2, pl.ds(pl.multiple_of(col * BS, BS), BS), :]
             right.append(jnp.where(s < count, block, jnp.zeros((), block.dtype)))
             left.append(tiles_ref[inner, 0, s])
         summed = jnp.dot(
             jnp.concatenate(left, 1), jnp.concatenate(right, 0), preferred_element_type=jnp.float32
         )
         rows = pl.ds(pl.multiple_of(b * BS, BS), BS)
-        if first:
-            out_ref[rows, :] = summed
+
+        @pl.when(i == 0)
+        def _():
+            total_ref[rows, :] = summed if first else before[rows, :] + summed
+
+        @pl.when(i > 0)
+        def _():
+            total_ref[rows, :] += summed
+
+        return carry
+
+    lax.fori_loop(0, 4, block_row, 0, unroll=2)
+
+    @pl.when((i == n - 1) & (half == 1))
+    def _():
+        if last:
+            core = sel_ref[n]
+            for part in range(2):
+                keep = pl.multiple_of((part * 2 + core) * 256, 256)
+                away = pl.multiple_of((part * 2 + 1 - core) * 256, 256)
+                outs[0][part] = total_ref[pl.ds(keep, 256), :]
+                outs[1][part] = total_ref[pl.ds(away, 256), :].astype(jnp.bfloat16)
         else:
-            out_ref[rows, :] = rest[0][rows, :] + summed
-
-
-def forward_call(dist, cols, counts, tiles, shard, total):
-    first = total is None
-    whole = pl.BlockSpec((NB * BS, F), lambda i, *_: (0, 0))
-    in_specs = [
-        pl.BlockSpec((2, 1, NS, BS, BS), lambda i, sel, c, n: (i, sel[0], 0, 0, 0)),
-        whole,
-    ] + ([] if first else [whole])
+            outs[0][...] = total_ref[...]
+
+
+def forward_call(sel, cols, counts, tiles, shards, before, last):
+    n, first = len(shards), before is None
+
+    def full(shape):
+        return pl.BlockSpec(shape, lambda *_: (0,) * len(shape))
+
+    if last:
+        out_shape = (
+            jax.ShapeDtypeStruct((2, 256, F), jnp.float32),
+            jax.ShapeDtypeStruct((2, 256, F), jnp.bfloat16),
+        )
+    else:
+        out_shape = (jax.ShapeDtypeStruct((NB * BS, F), jnp.float32),)
+    tile_spec = pl.BlockSpec((4, 1, NS, BS, BS), lambda i, h, sel, c, m: (h, sel[i], 0, 0, 0))
     return pl.pallas_call(
-        functools.partial(forward_body, first),
-        out_shape=jax.ShapeDtypeStruct((NB * BS, F), jnp.float32),
+        functools.partial(forward_body, n, first, last),
+        out_shape=out_shape,
         grid_spec=pltpu.PrefetchScalarGridSpec(
-            num_scalar_prefetch=3, grid=(NB // 2,), in_specs=in_specs, out_specs=whole
+            num_scalar_prefetch=3,
+            grid=(n, 2),
+            in_specs=[tile_spec] + [HBM] * n + ([] if first else [full((NB * BS, F))]),
+            out_specs=tuple(full(o.shape) for o in out_shape),
+            scratch_shapes=[
+                pltpu.VMEM((NB * BS, F), jnp.float32),
+                pltpu.VMEM((2, NB * BS, F), jnp.bfloat16),
+                pltpu.SemaphoreType.DMA((2,)),
+            ],
         ),
         compiler_params=params(),
+        cost_estimate=tile_cost(n),
         name="forward_tiles",
-    )(dist, cols, counts, tiles, shard, *([] if first else [total]))
+    )(sel, cols, counts, tiles, *shards, *([] if first else [before]))
 
 
 def dense_body(
@@ -156,7 +224,7 @@
         ),
         in_specs=[pl.BlockSpec(memory_space=pltpu.SMEM)] + [vmem] * 10,
         out_specs=(vmem,) * 5,
-        compiler_params=params(),
+        compiler_params=params(16 << 20),
         name="dense_rows",
     )(rep, own, got, feat, cot, mask, inv, inv_t, w_self, w_neigh, bias)
 
@@ -164,8 +232,7 @@
 def backward_body(added, sel_ref, cols_ref, counts_ref, tiles_ref, own_ref, got_ref, *rest):
     out_ref, acc_ref = rest[-2:]
     step = pl.program_id(0)
-    dist = sel_ref[0]
-    core = sel_ref[1]
+    dist, core = sel_ref[0], sel_ref[1]
 
     @pl.when(step == 0)
     def _():
@@ -175,9 +242,7 @@
             else:
                 acc_ref[c] = jnp.zeros((F, BS), jnp.float32)
 
-    mine = step % 2 == core
-    part = step // 2
-    message = jnp.where(mine, own_ref[part], got_ref[part])
+    message = jnp.where(step % 2 == core, own_ref[step // 2], got_ref[step // 2])
     for inner in range(2):
         b = step * 2 + inner
         count = counts_ref[b * ND + dist]
@@ -196,28 +261,59 @@
             out_ref[c] = acc_ref[c].astype(jnp.bfloat16)
 
 
-def backward_call(sel, cols, counts, tiles, own, got, extra):
+def backward_call(sel, cols, counts, tiles, own, got, extra, after):
     added = extra is not None
     whole = pl.BlockSpec((NB, F, BS), lambda i, *_: (0, 0, 0))
     message = pl.BlockSpec((2, F, 256), lambda i, *_: (0, 0, 0))
-    in_specs = [
-        pl.BlockSpec((2, 1, NS, BS, BS), lambda i, sel, c, n: (i, sel[0], 0, 0, 0)),
-        message,
-        message,
-    ] + ([whole] if added else [])
+    tile_spec = pl.BlockSpec((2, 1, NS, BS, BS), lambda i, sel, c, n: (i, sel[0], 0, 0, 0))
     return pl.pallas_call(
         functools.partial(backward_body, added),
         out_shape=jax.ShapeDtypeStruct((NB, F, BS), jnp.bfloat16),
         grid_spec=pltpu.PrefetchScalarGridSpec(
             num_scalar_prefetch=3,
             grid=(NB // 2,),
-            in_specs=in_specs,
+            in_specs=[tile_spec, message, message]
+            + ([whole] if added else [])
+            + [UNREAD] * len(after),
             out_specs=whole,
             scratch_shapes=[pltpu.VMEM((NB + 1, F, BS), jnp.float32)],
         ),
         compiler_params=params(),
+        cost_estimate=tile_cost(1),
         name="backward_tiles",
-    )(sel, cols, counts, tiles, own, got, *([extra] if added else []))
+    )(sel, cols, counts, tiles, own, got, *([extra] if added else []), *after)
+
+
+def split_body(core_ref, along_ref, *rest):
+    arrived, (_, keep_ref, away_ref) = rest[:-3], rest[-3:]
+    core = core_ref[0]
+    for part in range(2):
+        for c in range(2):
+            keep = (part * 2 + core) * 2 + c
+            away = (part * 2 + 1 - core) * 2 + c
+            kept = arrived[0][keep].astype(jnp.float32)
+            sent = arrived[0][away].astype(jnp.float32)
+            for ref in arrived[1:]:
+                kept += ref[keep].astype(jnp.float32)
+                sent += ref[away].astype(jnp.float32)
+            keep_ref[part, c] = kept
+            away_ref[part, c] = sent.astype(jnp.bfloat16)
+
+
+def split_call(core, arrived, along):
+    return pl.pallas_call(
+        split_body,
+        out_shape=(
+            jax.ShapeDtypeStruct(along.shape, along.dtype),
+            jax.ShapeDtypeStruct((2, 2, F, BS), jnp.float32),
+            jax.ShapeDtypeStruct((2, 2, F, BS), jnp.bfloat16),
+        ),
+        in_specs=[SMEM, UNREAD] + [WHOLE] * len(arrived),
+        out_specs=(UNREAD, WHOLE, WHOLE),
+        input_output_aliases={1: 0},
+        compiler_params=params(16 << 20),
+        name="split_products",
+    )(core, along, *arrived)
 
 
 def final_body(kept_ref, got_ref, term_ref, out_ref):
@@ -231,7 +327,7 @@
     return pl.pallas_call(
         final_body,
         out_shape=jax.ShapeDtypeStruct((256, F), jnp.bfloat16),
-        compiler_params=params(),
+        compiler_params=params(16 << 20),
         name="final_rows",
     )(kept, got, term)
 
@@ -296,16 +392,16 @@
     bias = bias_term.reshape(1, F)
 
     blocks = {}
-    total = None
-    for k, via in PLAN:
-        source = features if via is None else blocks[k ^ via]
-        blocks[k] = send(source, column_pairs(k, via))
-    for k, _ in PLAN:
-        total = forward_call(distance_of(k)[None], cols, live, tiles, blocks[k], total)
-
-    parts = total.reshape(2, 2, 256, F)
-    away = lax.dynamic_index_in_dim(parts, 1 - core, 1, keepdims=False).astype(jnp.bfloat16)
-    kept = lax.dynamic_index_in_dim(parts, core, 1, keepdims=False)
+    for k, via in PLAN.items():
+        blocks[k] = send(features if via is None else blocks[k ^ via], column_pairs(k))
+    made = (None,)
+    for group in GROUPS:
+        last = group is GROUPS[-1]
+        sel = jnp.stack([distance_of(k) for k in group] + [core])
+        shards = [blocks[k] for k in group]
+        made = forward_call(sel, cols, live, tiles, shards, made[0], last)
+
+    kept, away = made
     chip = (kept + send(away, flip_pairs(dcore=1)).astype(jnp.float32)).astype(jnp.bfloat16)
     other = send(chip, flip_pairs(dzh=1))
 
@@ -314,25 +410,22 @@
     )
     back_got = send(back_own, flip_pairs(dcore=1))
 
+    arrived, extra, products = {}, {}, {}
+    for k, after in BACK:
+        sel = jnp.stack([distance_of(k), core])
+        products[k] = backward_call(
+            sel, cols, live, tiles, back_own, back_got, extra.get(k), [products[a] for a in after]
+        )
+        moved = send(products[k], [(b, a) for a, b in column_pairs(k)])
+        if PLAN[k] is None:
+            arrived[k] = moved
+        else:
+            extra[k ^ PLAN[k]] = moved
+    grads, kept, away = split_call(core[None], list(arrived.values()), grads)
     grad_self, grad_neigh, grad_bias = weight_grads(
         grads, sums, zh, core, rows * lax.axis_size("blk")
     )
 
-    extra = {}
-    arrived = None
-    for k, via in reversed(PLAN):
-        sel = jnp.stack([distance_of(k), core])
-        made = backward_call(sel, cols, live, tiles, back_own, back_got, extra.get(k))
-        moved = send(made, back(column_pairs(k, via)))
-        if via is None:
-            moved = moved.astype(jnp.float32)
-            arrived = moved if arrived is None else arrived + moved
-        else:
-            extra[k ^ via] = moved
-
-    parts = arrived.reshape(2, 2, 2, F, BS)
-    away = lax.dynamic_index_in_dim(parts, 1 - core, 1, keepdims=False).astype(jnp.bfloat16)
-    kept = lax.dynamic_index_in_dim(parts, core, 1, keepdims=False)
     chip = kept + send(away, flip_pairs(dcore=1)).astype(jnp.float32)
     got = send(pick(chip, 1 - zh).astype(jnp.bfloat16), flip_pairs(dzh=1))
     grad_features = final_call(pick(chip, zh), got, own_term)

time: 238 us -> 249 us (1.046)
  Pallas kernels: 49 us -> 69.4 us
  starting transfers between devices: 85.1 us -> 76.6 us
  waiting for transfers between devices: 82.6 us -> 89.5 us
  local copies, waits for them, and re-layouts: 15.2 us -> 9.14 us
    pallas_call x8, Pallas kernels: 19.8 us -> 38.4 us  [backward_call(): pl.pallas_call(functools.partial(backward_body, added), out_shape=jax.Sha...]
    ppermute x32, starting transfers between devices: 85.1 us -> 76.6 us  [send(): return lax.ppermute(value, AXES, pairs)]
    ppermute x32, waiting for transfers between devices: 82.6 us -> 89.5 us  [send(): return lax.ppermute(value, AXES, pairs)]
    unnamed x23 -> x37, local copies, waits for them, and re-layouts: 12.8 us -> 6.79 us
    pallas_call x8 -> x5, Pallas kernels: 26.7 us -> 28.7 us  [the longest x4 28.2 us: forward_call(): pl.pallas_call(functools.partial(forward_body, n, first, last), out_shape...]
  transfers between devices with their start and end apart: 32 -> 32, of which waited for: 12 -> 16; matrix products, arithmetic and copies ran while one was open for 3% -> 2% of each run, Pallas kernels for 18% -> 22%
where the time goes in v4:
time: 249 us; the launch traced here: 248 us
  waiting for transfers between devices  89.5 us (36%)
  starting transfers between devices  76.6 us (31%)
  Pallas kernels  69.4 us (28%)
  local copies, waits for them, and re-layouts  9.14 us (4%)
    ppermute x32, waiting for transfers between devices, send(): return lax.ppermute(value, AXES, pairs)  89.5 us
    ppermute x32, starting transfers between devices, send(): return lax.ppermute(value, AXES, pairs)  76.6 us
    pallas_call x8, Pallas kernels, backward_call(): pl.pallas_call(functools.partial(backward_body, added), out_shape=jax.Sha...  38.4 us
    pallas_call x4, Pallas kernels, forward_call(): pl.pallas_call(functools.partial(forward_body, n, first, last), out_shape...  28.2 us
    unnamed x37, local copies, waits for them, and re-layouts  6.79 us
  transfers between devices with their start and end apart: 32, of which 16 were waited for; matrix products, arithmetic and copies ran while one was open for 2% of the time, Pallas kernels for 22%

profile of v4, /device:TPU:1, one launch (start us, length us, event | category | flops | bytes accessed | tf_op | source)
XLA Modules:
  0.0 247.9 jit_solution(7228473016161457183)
XLA Ops:
  0.6 4.4 %collective-permute-start = (bf16[1024,256]{1,0:T(8,128)(2,1)}, bf16[1024,256]{1,0:T(8,128)(2,1)S(1)}, u32[]{:S(2)}, u32[]{:S(2)}) collective-permute-start(bf16[1024,256]{1,0:T(8,128)(2,1)} %feat_ref.1), channel_id=1, source_target_pairs={{120,0},{89,1},{58,2},{27,3},{124,4},{93,5},{62,6},{31,7},{112,8},... | collective-permute-start | bytes 1572872 | tf_op jit(solution)/shard_map/ppermute | solution.py:55
  5.0 1.0 collective-permute-start.6
  6.0 20.0 %collective-permute-done.rest_0_ = bf16[1024,256]{1,0:T(8,128)(2,1)S(1)} collective-permute-done((bf16[1024,256]{1,0:T(8,128)(2,1)}, bf16[1024,256]{1,0:T(8,128)(2,1)S(1)}, u32[]{:S(2)}, u32[]{:S(2)}) %collective-permute-start) | collective-permute-done | bytes 524320 | tf_op jit(solution)/shard_map/ppermute | solution.py:55
  26.0 1.7 collective-permute-start.7
  27.7 1.6 collective-permute-start.4
  29.3 5.2 %collective-permute-start.5 = (bf16[1024,256]{1,0:T(8,128)(2,1)}, bf16[1024,256]{1,0:T(8,128)(2,1)S(1)}, u32[]{:S(2)}, u32[]{:S(2)}) collective-permute-start(bf16[1024,256]{1,0:T(8,128)(2,1)} %feat_ref.1), channel_id=1, source_target_pairs={{110,0},{79,1},{44,2},{13,3},{106,4},{75,5},{40,6},{9,7},{6,8},{10... | collective-permute-start | bytes 1572872 | tf_op jit(solution)/shard_map/ppermute | solution.py:55
  34.6 1.9 collective-permute-start.3
  36.5 7.3 %collective-permute-done.1.rest_0_ = bf16[1024,256]{1,0:T(8,128)(2,1)S(1)} collective-permute-done((bf16[1024,256]{1,0:T(8,128)(2,1)S(1)}, bf16[1024,256]{1,0:T(8,128)(2,1)S(1)}, u32[]{:S(2)}, u32[]{:S(2)}) %collective-permute-start.1) | collective-permute-done | bytes 524320 | tf_op jit(solution)/shard_map/ppermute | solution.py:55
  43.8 2.4 collective-permute-start.2
  46.3 0.9 copy.16
  47.3 0.8 reshape.36.counts_ref
  48.2 5.5 %collective-permute-done.7.rest_2_ = bf16[1024,256]{1,0:T(8,128)(2,1)} collective-permute-done((bf16[1024,256]{1,0:T(8,128)(2,1)}, bf16[1024,256]{1,0:T(8,128)(2,1)}, u32[]{:S(2)}, u32[]{:S(2)}) %collective-permute-start.7) | collective-permute-done | bytes 524320 | tf_op jit(solution)/shard_map/ppermute | solution.py:55
  53.7 9.6 %forward_tiles.4.rest_3_ = f32[1024,256]{1,0:T(8,128)} custom-call(s32[4]{0:T(128)S(1)} %add_add_fusion.3.sel_ref, s32[384]{0:T(512)S(1)} %reshape.35.cols_ref, s32[64]{0:T(128)S(1)} %reshape.36.counts_ref, bf16[8,8,6,128,128]{4,3,2,1,0:T(8,128)(2,1)} %tiles_ref.23, bf16[1024,256]{1,0:T(8,128)(2,1)S(1)} %collective-permute-done.rest_0_, ...), custom_call_target="tpu_custom_call" | custom-call | flops 1207959552 | bytes 25165824 | tf_op jit(solution)/shard_map/forward_tiles/pallas_call | solution.py:150
  63.3 0.8 copy-done.12
  64.1 0.8 copy-done.13
  64.8 9.9 %forward_tiles.5.rest_1_ = f32[1024,256]{1,0:T(8,128)} custom-call(s32[4]{0:T(128)S(1)} %add_add_fusion.2.sel_ref, s32[384]{0:T(512)S(1)} %reshape.35.cols_ref, s32[64]{0:T(128)S(1)} %reshape.36.counts_ref, bf16[8,8,6,128,128]{4,3,2,1,0:T(8,128)(2,1)} %tiles_ref.23, bf16[1024,256]{1,0:T(8,128)(2,1)S(1)} %collective-permute-done.1.rest_0_, ...), custom_call_target="tpu_custom_call" | custom-call | flops 1207959552 | bytes 25165824 | tf_op jit(solution)/shard_map/forward_tiles/pallas_call | solution.py:150
  74.8 4.4 %forward_tiles.6.rest_1_ = f32[1024,256]{1,0:T(8,128)} custom-call(s32[2]{0:T(128)S(1)} %pad_add_fusion.1.sel_ref, s32[384]{0:T(512)S(1)} %reshape.35.cols_ref, s32[64]{0:T(128)S(1)} %reshape.36.counts_ref, bf16[8,8,6,128,128]{4,3,2,1,0:T(8,128)(2,1)} %tiles_ref.23, bf16[1024,256]{1,0:T(8,128)(2,1)S(1)} %collective-permute-done.3.rest_0_, ...), custom_call_target="tpu_custom_call" | custom-call | flops 402653184 | bytes 8388608 | tf_op jit(solution)/shard_map/forward_tiles/pallas_call | solution.py:150
  79.2 4.4 %forward_tiles.7 = (f32[2,256,256]{2,1,0:T(8,128)S(1)}, bf16[2,256,256]{2,1,0:T(8,128)(2,1)S(1)}) custom-call(s32[2]{0:T(128)S(1)} %pad_add_fusion.sel_ref, s32[384]{0:T(512)S(1)} %reshape.35.cols_ref, s32[64]{0:T(128)S(1)} %reshape.36.counts_ref, bf16[8,8,6,128,128]{4,3,2,1,0:T(8,128)(2,1)} %tiles_ref.23, bf16[1024,256]{1,0:T(8,128)(2,1)} %collective-permute-done.2.rest_0_, ...), custom_call_target="tpu_custom_call" | custom-call | flops 402653184 | bytes 8388608 | tf_op jit(solution)/shard_map/forward_tiles/pallas_call | solution.py:150
  83.6 7.6 %collective-permute-start.8 = (bf16[2,256,256]{2,1,0:T(8,128)(2,1)S(1)}, bf16[2,256,256]{2,1,0:T(8,128)(2,1)S(1)}, u32[]{:S(2)}, u32[]{:S(2)}) collective-permute-start(bf16[2,256,256]{2,1,0:T(8,128)(2,1)S(1)} %get-tuple-element.16), channel_id=1, source_target_pairs={{0,1},{1,0},{2,3},{3,2},{4,5},{5,4},{6,7},{7,6},{8,9},{9,8},{10,11... | collective-permute-start | bytes 786440 | tf_op jit(solution)/shard_map/ppermute | solution.py:55
  91.2 1.2 collective-permute-done.8
  93.0 8.5 %collective-permute-done.9.got_ref = bf16[2,256,256]{2,1,0:T(8,128)(2,1)S(1)} collective-permute-done((bf16[2,256,256]{2,1,0:T(8,128)(2,1)S(1)}, bf16[2,256,256]{2,1,0:T(8,128)(2,1)S(1)}, u32[]{:S(2)}, u32[]{:S(2)}) %collective-permute-start.9) | collective-permute-done | bytes 262176 | tf_op jit(solution)/shard_map/ppermute | solution.py:55
  101.6 1.6 dense_rows.1
  103.1 0.7 copy-done.4
  103.8 1.2 collective-permute-start.10
  105.1 1.2 collective-permute-done.10.got_ref
  106.2 4.8 %backward_tiles.8.rest_0_ = bf16[8,256,128]{2,1,0:T(8,128)(2,1)} custom-call(s32[2]{0:T(128)S(1)} %pad_add_fusion.sel_ref, s32[384]{0:T(512)S(1)} %reshape.35.cols_ref, s32[64]{0:T(128)S(1)} %reshape.36.counts_ref, bf16[8,8,6,128,128]{4,3,2,1,0:T(8,128)(2,1)} %tiles_ref.23, bf16[2,256,256]{2,1,0:T(8,128)(2,1)S(1)} %get-tuple-element.19.own_ref, ...), custom_call_target="tpu_custom_call" | custom-call | flops 402653184 | bytes 8388608 | tf_op jit(solution)/shard_map/backward_tiles/pallas_call | solution.py:269
  111.0 3.8 %collective-permute-start.13 = (bf16[8,256,128]{2,1,0:T(8,128)(2,1)}, bf16[8,256,128]{2,1,0:T(8,128)(2,1)S(1)}, u32[]{:S(2)}, u32[]{:S(2)}) collective-permute-start(bf16[8,256,128]{2,1,0:T(8,128)(2,1)} %backward_tiles.8.rest_0_), channel_id=1, source_target_pairs={{0,4},{1,5},{2,6},{3,7},{4,0},{5,1},{6,2},{7,3},{8,12},{9,13},{10,... | collective-permute-start | bytes 1572872 | tf_op jit(solution)/shard_map/ppermute | solution.py:55
  115.0 4.8 %backward_tiles.9.rest_0_ = bf16[8,256,128]{2,1,0:T(8,128)(2,1)} custom-call(s32[2]{0:T(128)S(1)} %pad_add_fusion.2.sel_ref, s32[384]{0:T(512)S(1)} %reshape.35.cols_ref, s32[64]{0:T(128)S(1)} %reshape.36.counts_ref, bf16[8,8,6,128,128]{4,3,2,1,0:T(8,128)(2,1)} %tiles_ref.23, bf16[2,256,256]{2,1,0:T(8,128)(2,1)S(1)} %get-tuple-element.19.own_ref, ...), custom_call_target="tpu_custom_call" | custom-call | flops 402653184 | bytes 8388608 | tf_op jit(solution)/shard_map/backward_tiles/pallas_call | solution.py:269
  119.8 4.7 %backward_tiles.10.rest_1_ = bf16[8,256,128]{2,1,0:T(8,128)(2,1)} custom-call(s32[2]{0:T(128)S(1)} %pad_add_fusion.3.sel_ref, s32[384]{0:T(512)S(1)} %reshape.35.cols_ref, s32[64]{0:T(128)S(1)} %reshape.36.counts_ref, bf16[8,8,6,128,128]{4,3,2,1,0:T(8,128)(2,1)} %tiles_ref.23, bf16[2,256,256]{2,1,0:T(8,128)(2,1)S(1)} %get-tuple-element.19.own_ref, ...), custom_call_target="tpu_custom_call" | custom-call | flops 402653184 | bytes 8388608 | tf_op jit(solution)/shard_map/backward_tiles/pallas_call | solution.py:269
  124.5 2.5 collective-permute-done.13.rest_0_
  127.0 0.8 copy-done.15
  127.8 4.9 %backward_tiles.11.rest_0_ = bf16[8,256,128]{2,1,0:T(8,128)(2,1)} custom-call(s32[2]{0:T(128)S(1)} %pad_add_fusion.5.sel_ref, s32[384]{0:T(512)S(1)} %reshape.35.cols_ref, s32[64]{0:T(128)S(1)} %reshape.36.counts_ref, bf16[8,8,6,128,128]{4,3,2,1,0:T(8,128)(2,1)} %tiles_ref.23, bf16[2,256,256]{2,1,0:T(8,128)(2,1)S(1)} %get-tuple-element.19.own_ref, ...), custom_call_target="tpu_custom_call" | custom-call | flops 402653184 | bytes 8388608 | tf_op jit(solution)/shard_map/backward_tiles/pallas_call | solution.py:269
  132.7 2.4 collective-permute-start.17
  135.1 2.4 collective-permute-start.12
  137.8 1.1 collective-permute-start.11
  138.9 4.8 %backward_tiles.12.rest_0_ = bf16[8,256,128]{2,1,0:T(8,128)(2,1)} custom-call(s32[2]{0:T(128)S(1)} %pad_add_fusion.4.sel_ref, s32[384]{0:T(512)S(1)} %reshape.35.cols_ref, s32[64]{0:T(128)S(1)} %reshape.36.counts_ref, bf16[8,8,6,128,128]{4,3,2,1,0:T(8,128)(2,1)} %tiles_ref.23, bf16[2,256,256]{2,1,0:T(8,128)(2,1)S(1)} %get-tuple-element.19.own_ref, ...), custom_call_target="tpu_custom_call" | custom-call | flops 402653184 | bytes 8388608 | tf_op jit(solution)/shard_map/backward_tiles/pallas_call | solution.py:269
  143.7 10.6 %collective-permute-start.14 = (bf16[8,256,128]{2,1,0:T(8,128)(2,1)}, bf16[8,256,128]{2,1,0:T(8,128)(2,1)S(1)}, u32[]{:S(2)}, u32[]{:S(2)}) collective-permute-start(bf16[8,256,128]{2,1,0:T(8,128)(2,1)} %backward_tiles.12.rest_0_), channel_id=1, source_target_pairs={{0,126},{1,95},{2,60},{3,29},{4,122},{5,89},{6,56},{7,27},{8,118},... | collective-permute-start | bytes 1572872 | tf_op jit(solution)/shard_map/ppermute | solution.py:55
  154.3 4.7 %backward_tiles.13.rest_0_ = bf16[8,256,128]{2,1,0:T(8,128)(2,1)} custom-call(s32[2]{0:T(128)S(1)} %pad_add_fusion.6.sel_ref, s32[384]{0:T(512)S(1)} %reshape.35.cols_ref, s32[64]{0:T(128)S(1)} %reshape.36.counts_ref, bf16[8,8,6,128,128]{4,3,2,1,0:T(8,128)(2,1)} %tiles_ref.23, bf16[2,256,256]{2,1,0:T(8,128)(2,1)S(1)} %get-tuple-element.19.own_ref, ...), custom_call_target="tpu_custom_call" | custom-call | flops 402653184 | bytes 8388608 | tf_op jit(solution)/shard_map/backward_tiles/pallas_call | solution.py:269
  159.0 4.7 %backward_tiles.14.rest_1_ = bf16[8,256,128]{2,1,0:T(8,128)(2,1)} custom-call(s32[2]{0:T(128)S(1)} %pad_add_fusion.1.sel_ref, s32[384]{0:T(512)S(1)} %reshape.35.cols_ref, s32[64]{0:T(128)S(1)} %reshape.36.counts_ref, bf16[8,8,6,128,128]{4,3,2,1,0:T(8,128)(2,1)} %tiles_ref.23, bf16[2,256,256]{2,1,0:T(8,128)(2,1)S(1)} %get-tuple-element.19.own_ref, ...), custom_call_target="tpu_custom_call" | custom-call | flops 402653184 | bytes 8388608 | tf_op jit(solution)/shard_map/backward_tiles/pallas_call | solution.py:269
  163.8 4.2 %collective-permute-start.16 = (bf16[8,256,128]{2,1,0:T(8,128)(2,1)}, bf16[8,256,128]{2,1,0:T(8,128)(2,1)S(1)}, u32[]{:S(2)}, u32[]{:S(2)}) collective-permute-start(bf16[8,256,128]{2,1,0:T(8,128)(2,1)} %backward_tiles.14.rest_1_), channel_id=1, source_target_pairs={{0,0},{1,97},{2,66},{3,35},{4,4},{5,101},{6,70},{7,39},{8,8},{9,10... | collective-permute-start | bytes 1572872 | tf_op jit(solution)/shard_map/ppermute | solution.py:55
  168.0 4.9 %backward_tiles.15 = bf16[8,256,128]{2,1,0:T(8,128)(2,1)} custom-call(s32[2]{0:T(128)S(1)} %pad_add_fusion.7.sel_ref, s32[384]{0:T(512)S(1)} %reshape.35.cols_ref, s32[64]{0:T(128)S(1)} %reshape.36.counts_ref, bf16[8,8,6,128,128]{4,3,2,1,0:T(8,128)(2,1)} %tiles_ref.23, bf16[2,256,256]{2,1,0:T(8,128)(2,1)S(1)} %get-tuple-element.19.own_ref, ...), custom_call_target="tpu_custom_call" | custom-call | flops 402653184 | bytes 8388608 | tf_op jit(solution)/shard_map/backward_tiles/pallas_call | solution.py:269
  173.0 18.9 %collective-permute-done.12.rest_1_ = bf16[8,256,128]{2,1,0:T(8,128)(2,1)S(1)} collective-permute-done((bf16[8,256,128]{2,1,0:T(8,128)(2,1)S(1)}, bf16[8,256,128]{2,1,0:T(8,128)(2,1)S(1)}, u32[]{:S(2)}, u32[]{:S(2)}) %collective-permute-start.12) | collective-permute-done | bytes 524320 | tf_op jit(solution)/shard_map/ppermute | solution.py:55
  192.0 4.1 %collective-permute-start.22 = (f32[1,256]{1,0:T(1,128)S(1)}, f32[1,256]{1,0:T(1,128)S(1)}, u32[]{:S(2)}, u32[]{:S(2)}) collective-permute-start(f32[1,256]{1,0:T(1,128)S(1)} %get-tuple-element.24), channel_id=1, source_target_pairs={{0,1},{1,0},{2,3},{3,2},{4,5},{5,4},{6,7},{7,6},{8,9},{9,8},{10,11... | collective-permute-start | bytes 3080 | tf_op jit(solution)/shard_map/ppermute | solution.py:55
  196.1 11.6 %collective-permute-done.18.rest_5_ = bf16[8,256,128]{2,1,0:T(8,128)(2,1)S(1)} collective-permute-done((bf16[8,256,128]{2,1,0:T(8,128)(2,1)}, bf16[8,256,128]{2,1,0:T(8,128)(2,1)S(1)}, u32[]{:S(2)}, u32[]{:S(2)}) %collective-permute-start.18) | collective-permute-done | bytes 524320 | tf_op jit(solution)/shard_map/ppermute | solution.py:55
  207.7 0.8 copy-done.2
  208.5 1.0 copy-done.3
  210.1 1.3 collective-permute-done.21
  212.0 2.6 %collective-permute-start.24 = (bf16[144,256]{1,0:T(8,128)(2,1)S(1)}, bf16[144,256]{1,0:T(8,128)(2,1)S(1)}, u32[]{:S(2)}, u32[]{:S(2)}) collective-permute-start(bf16[144,256]{1,0:T(8,128)(2,1)S(1)} %maximum_maximum_fusion), channel_id=1, source_target_pairs={{0,64},{1,65},{2,66},{3,67},{4,68},{5,69},{6,70},{7,71},{8,72},{9,... | collective-permute-start | bytes 221192 | tf_op jit(solution)/shard_map/ppermute | solution.py:55
  214.6 0.9 collective-permute-start.25
  215.5 2.4 collective-permute-done.24
  217.9 1.6 collective-permute-done.25
  220.2 3.9 %collective-permute-start.27 = (bf16[144,256]{1,0:T(8,128)(2,1)S(1)}, bf16[144,256]{1,0:T(8,128)(2,1)S(1)}, u32[]{:S(2)}, u32[]{:S(2)}) collective-permute-start(bf16[144,256]{1,0:T(8,128)(2,1)S(1)} %maximum_maximum_fusion.1), channel_id=1, source_target_pairs={{0,16},{1,17},{2,18},{3,19},{4,20},{5,21},{6,22},{7,23},{8,24},{9,... | collective-permute-start | bytes 221192 | tf_op jit(solution)/shard_map/ppermute | solution.py:55
  224.2 2.5 %collective-permute-done.27 = bf16[144,256]{1,0:T(8,128)(2,1)S(1)} collective-permute-done((bf16[144,256]{1,0:T(8,128)(2,1)S(1)}, bf16[144,256]{1,0:T(8,128)(2,1)S(1)}, u32[]{:S(2)}, u32[]{:S(2)}) %collective-permute-start.27) | collective-permute-done | bytes 73760 | tf_op jit(solution)/shard_map/ppermute | solution.py:55
  226.7 2.7 %collective-permute-done.28 = bf16[144,256]{1,0:T(8,128)(2,1)S(1)} collective-permute-done((bf16[144,256]{1,0:T(8,128)(2,1)S(1)}, bf16[144,256]{1,0:T(8,128)(2,1)S(1)}, u32[]{:S(2)}, u32[]{:S(2)}) %collective-permute-start.28) | collective-permute-done | bytes 73760 | tf_op jit(solution)/shard_map/ppermute | solution.py:55
  229.7 2.6 %collective-permute-start.19 = (bf16[2,2,256,128]{3,2,1,0:T(8,128)(2,1)}, bf16[2,2,256,128]{3,2,1,0:T(8,128)(2,1)S(1)}, u32[]{:S(2)}, u32[]{:S(2)}) collective-permute-start(bf16[2,2,256,128]{3,2,1,0:T(8,128)(2,1)} %copy-done.9), channel_id=1, source_target_pairs={{0,1},{1,0},{2,3},{3,2},{4,5},{5,4},{6,7},{7,6},{8,9},{9,8},{10,11... | collective-permute-start | bytes 786440 | tf_op jit(solution)/shard_map/ppermute | solution.py:55
  232.3 0.6 collective-permute-done.29
  233.0 3.9 %collective-permute-start.30 = (f32[128,256]{1,0:T(8,128)S(1)}, f32[128,256]{1,0:T(8,128)S(1)}, u32[]{:S(2)}, u32[]{:S(2)}) collective-permute-start(f32[128,256]{1,0:T(8,128)S(1)} %get-tuple-element.30), channel_id=1, source_target_pairs={{0,2},{1,3},{2,0},{3,1},{4,6},{5,7},{6,4},{7,5},{8,10},{9,11},{10,... | collective-permute-start | bytes 393224 | tf_op jit(solution)/shard_map/ppermute | solution.py:55
  237.0 1.2 collective-permute-start.20
  238.3 1.8 collective-permute-done.30
  240.1 4.6 %collective-permute-start.31 = (f32[2,128,256]{2,1,0:T(8,128)S(1)}, f32[2,128,256]{2,1,0:T(8,128)S(1)}, u32[]{:S(2)}, u32[]{:S(2)}) collective-permute-start(f32[2,128,256]{2,1,0:T(8,128)S(1)} %maximum_select_fusion), channel_id=1, source_target_pairs={{0,1},{1,0},{2,3},{3,2},{4,5},{5,4},{6,7},{7,6},{8,9},{9,8},{10,11... | collective-permute-start | bytes 786440 | tf_op jit(solution)/shard_map/ppermute | solution.py:55
  244.7 0.6 fusion.2
  245.2 0.9 copy-done.5
  246.2 0.8 final_rows.1
  247.1 0.8 slice_bitcast_fusion
  (93 shorter events, 4.1 us)
Async XLA Ops:
  0.6 25.4 %collective-permute-start = (bf16[1024,256]{1,0:T(8,128)(2,1)}, bf16[1024,256]{1,0:T(8,128)(2,1)S(1)}, u32[]{:S(2)}, u32[]{:S(2)}) collective-permute-start(bf16[1024,256]{1,0:T(8,128)(2,1)} %feat_ref.1), channel_id=1, source_target_pairs={{120,0},{89,1},{58,2},{27,3},{124,4},{93,5},{62,6},{31,7},{112,8},... | collective-permute-start | bytes 1572872 | tf_op jit(solution)/shard_map/ppermute | solution.py:55
  5.0 29.6 %collective-permute-start.6 = (bf16[1024,256]{1,0:T(8,128)(2,1)}, bf16[1024,256]{1,0:T(8,128)(2,1)S(1)}, u32[]{:S(2)}, u32[]{:S(2)}) collective-permute-start(bf16[1024,256]{1,0:T(8,128)(2,1)} %feat_ref.1), channel_id=1, source_target_pairs={{104,0},{73,1},{42,2},{11,3},{108,4},{77,5},{46,6},{15,7},{0,8},{9... | collective-permute-start | bytes 1572872 | tf_op jit(solution)/shard_map/ppermute | solution.py:55
  26.0 17.8 %collective-permute-start.1 = (bf16[1024,256]{1,0:T(8,128)(2,1)S(1)}, bf16[1024,256]{1,0:T(8,128)(2,1)S(1)}, u32[]{:S(2)}, u32[]{:S(2)}) collective-permute-start(bf16[1024,256]{1,0:T(8,128)(2,1)S(1)} %collective-permute-done.rest_0_), channel_id=1, source_target_pairs={{8,0},{9,1},{10,2},{11,3},{12,4},{13,5},{14,6},{15,7},{0,8},{1,9},... | collective-permute-start | bytes 1572872 | tf_op jit(solution)/shard_map/ppermute | solution.py:55
  26.0 27.7 %collective-permute-start.7 = (bf16[1024,256]{1,0:T(8,128)(2,1)}, bf16[1024,256]{1,0:T(8,128)(2,1)}, u32[]{:S(2)}, u32[]{:S(2)}) collective-permute-start(bf16[1024,256]{1,0:T(8,128)(2,1)} %feat_ref.1), channel_id=1, source_target_pairs={{102,0},{69,1},{36,2},{7,3},{0,4},{99,5},{66,6},{33,7},{110,8},{77... | collective-permute-start | bytes 1572872 | tf_op jit(solution)/shard_map/ppermute | solution.py:55
  27.7 35.6 %collective-permute-start.4 = (bf16[1024,256]{1,0:T(8,128)(2,1)}, bf16[1024,256]{1,0:T(8,128)(2,1)S(1)}, u32[]{:S(2)}, u32[]{:S(2)}) collective-permute-start(bf16[1024,256]{1,0:T(8,128)(2,1)} %feat_ref.1), channel_id=1, source_target_pairs={{126,0},{95,1},{60,2},{29,3},{122,4},{89,5},{56,6},{27,7},{118,8},... | collective-permute-start | bytes 1572872 | tf_op jit(solution)/shard_map/ppermute | solution.py:55
  29.3 34.0 %collective-permute-start.5 = (bf16[1024,256]{1,0:T(8,128)(2,1)}, bf16[1024,256]{1,0:T(8,128)(2,1)S(1)}, u32[]{:S(2)}, u32[]{:S(2)}) collective-permute-start(bf16[1024,256]{1,0:T(8,128)(2,1)} %feat_ref.1), channel_id=1, source_target_pairs={{110,0},{79,1},{44,2},{13,3},{106,4},{75,5},{40,6},{9,7},{6,8},{10... | collective-permute-start | bytes 1572872 | tf_op jit(solution)/shard_map/ppermute | solution.py:55
  34.6 19.1 %copy-start.11 = (bf16[1024,256]{1,0:T(8,128)(2,1)}, bf16[1024,256]{1,0:T(8,128)(2,1)S(1)}, u32[]{:S(2)}) copy-start(bf16[1024,256]{1,0:T(8,128)(2,1)S(1)} %collective-permute-done.6.rest_1_) | copy-start | bytes 1572868
  34.6 40.2 %collective-permute-start.3 = (bf16[1024,256]{1,0:T(8,128)(2,1)}, bf16[1024,256]{1,0:T(8,128)(2,1)S(1)}, u32[]{:S(2)}, u32[]{:S(2)}) collective-permute-start(bf16[1024,256]{1,0:T(8,128)(2,1)} %feat_ref.1), channel_id=1, source_target_pairs={{0,0},{97,1},{66,2},{35,3},{4,4},{101,5},{70,6},{39,7},{8,8},{105,... | collective-permute-start | bytes 1572872 | tf_op jit(solution)/shard_map/ppermute | solution.py:55
  43.8 35.4 %collective-permute-start.2 = (bf16[1024,256]{1,0:T(8,128)(2,1)S(1)}, bf16[1024,256]{1,0:T(8,128)(2,1)}, u32[]{:S(2)}, u32[]{:S(2)}) collective-permute-start(bf16[1024,256]{1,0:T(8,128)(2,1)S(1)} %collective-permute-done.1.rest_0_), channel_id=1, source_target_pairs={{4,0},{5,1},{6,2},{7,3},{0,4},{1,5},{2,6},{3,7},{12,8},{13,9},{14,... | collective-permute-start | bytes 1572872 | tf_op jit(solution)/shard_map/ppermute | solution.py:55
  63.3 0.8 copy-start.12
  64.1 0.8 copy-start.13
  74.7 17.8 %copy-start.16 = (s32[1024]{0:T(1024)S(1)}, s32[1024]{0:T(1024)}, u32[]{:S(2)}) copy-start(s32[1024]{0:T(1024)} %param.14) | copy-start | bytes 12292
  74.7 18.1 %copy-start.17 = (s32[1024]{0:T(1024)S(1)}, s32[1024]{0:T(1024)}, u32[]{:S(2)}) copy-start(s32[1024]{0:T(1024)} %param.15) | copy-start | bytes 12292
  74.7 26.8 %copy-start = (bf16[1024,256]{1,0:T(8,128)(2,1)S(1)}, bf16[1024,256]{1,0:T(8,128)(2,1)}, u32[]{:S(2)}) copy-start(bf16[1024,256]{1,0:T(8,128)(2,1)} %feat_ref.1) | copy-start | bytes 1572868
  74.7 26.8 %copy-start.1 = (bf16[1024,256]{1,0:T(8,128)(2,1)S(1)}, bf16[1024,256]{1,0:T(8,128)(2,1)}, u32[]{:S(2)}) copy-start(bf16[1024,256]{1,0:T(8,128)(2,1)} %cot_ref.1) | copy-start | bytes 1572868
  74.7 26.8 %copy-start.6 = (bf16[256,256]{1,0:T(8,128)(2,1)S(1)}, bf16[256,256]{1,0:T(8,128)(2,1)}, u32[]{:S(2)}) copy-start(bf16[256,256]{1,0:T(8,128)(2,1)} %ws_ref.1) | copy-start | bytes 393220
  74.8 26.8 %copy-start.7 = (bf16[256,256]{1,0:T(8,128)(2,1)S(1)}, bf16[256,256]{1,0:T(8,128)(2,1)}, u32[]{:S(2)}) copy-start(bf16[256,256]{1,0:T(8,128)(2,1)} %wn_ref.1) | copy-start | bytes 393220
  74.8 26.8 %copy-start.8 = (f32[256]{0:T(256)S(1)}, f32[256]{0:T(256)}, u32[]{:S(2)}) copy-start(f32[256]{0:T(256)} %param.19) | copy-start | bytes 3076
  83.6 8.7 %collective-permute-start.8 = (bf16[2,256,256]{2,1,0:T(8,128)(2,1)S(1)}, bf16[2,256,256]{2,1,0:T(8,128)(2,1)S(1)}, u32[]{:S(2)}, u32[]{:S(2)}) collective-permute-start(bf16[2,256,256]{2,1,0:T(8,128)(2,1)S(1)} %get-tuple-element.16), channel_id=1, source_target_pairs={{0,1},{1,0},{2,3},{3,2},{4,5},{5,4},{6,7},{7,6},{8,9},{9,8},{10,11... | collective-permute-start | bytes 786440 | tf_op jit(solution)/shard_map/ppermute | solution.py:55
  92.4 9.1 %collective-permute-start.9 = (bf16[2,256,256]{2,1,0:T(8,128)(2,1)S(1)}, bf16[2,256,256]{2,1,0:T(8,128)(2,1)S(1)}, u32[]{:S(2)}, u32[]{:S(2)}) collective-permute-start(bf16[2,256,256]{2,1,0:T(8,128)(2,1)S(1)} %add_convert_fusion.own_ref), channel_id=1, source_target_pairs={{0,2},{1,3},{2,0},{3,1},{4,6},{5,7},{6,4},{7,5},{8,10},{9,11},{10,... | collective-permute-start | bytes 786440 | tf_op jit(solution)/shard_map/ppermute | solution.py:55
  103.1 0.7 copy-start.4
  103.8 2.4 collective-permute-start.10
  111.0 16.0 %collective-permute-start.13 = (bf16[8,256,128]{2,1,0:T(8,128)(2,1)}, bf16[8,256,128]{2,1,0:T(8,128)(2,1)S(1)}, u32[]{:S(2)}, u32[]{:S(2)}) collective-permute-start(bf16[8,256,128]{2,1,0:T(8,128)(2,1)} %backward_tiles.8.rest_0_), channel_id=1, source_target_pairs={{0,4},{1,5},{2,6},{3,7},{4,0},{5,1},{6,2},{7,3},{8,12},{9,13},{10,... | collective-permute-start | bytes 1572872 | tf_op jit(solution)/shard_map/ppermute | solution.py:55
  124.5 10.6 %copy-start.10 = (bf16[8,256,128]{2,1,0:T(8,128)(2,1)S(1)}, bf16[8,256,128]{2,1,0:T(8,128)(2,1)}, u32[]{:S(2)}) copy-start(bf16[8,256,128]{2,1,0:T(8,128)(2,1)} %backward_tiles.10.rest_1_) | copy-start | bytes 1572868
  127.0 0.8 copy-start.15
  132.7 31.0 %collective-permute-start.17 = (bf16[8,256,128]{2,1,0:T(8,128)(2,1)}, bf16[8,256,128]{2,1,0:T(8,128)(2,1)S(1)}, u32[]{:S(2)}, u32[]{:S(2)}) collective-permute-start(bf16[8,256,128]{2,1,0:T(8,128)(2,1)} %backward_tiles.11.rest_0_), channel_id=1, source_target_pairs={{0,8},{1,9},{2,10},{3,11},{4,12},{5,13},{6,14},{7,15},{8,0},{9,1},... | collective-permute-start | bytes 1572872 | tf_op jit(solution)/shard_map/ppermute | solution.py:55
  135.1 56.8 %collective-permute-start.12 = (bf16[8,256,128]{2,1,0:T(8,128)(2,1)S(1)}, bf16[8,256,128]{2,1,0:T(8,128)(2,1)S(1)}, u32[]{:S(2)}, u32[]{:S(2)}) collective-permute-start(bf16[8,256,128]{2,1,0:T(8,128)(2,1)S(1)} %copy-done.10), channel_id=1, source_target_pairs={{0,102},{1,69},{2,36},{3,7},{4,0},{5,99},{6,66},{7,33},{8,110},{9,... | collective-permute-start | bytes 1572872 | tf_op jit(solution)/shard_map/ppermute | solution.py:55
  137.8 54.2 %collective-permute-start.11 = (bf16[8,256,128]{2,1,0:T(8,128)(2,1)}, bf16[8,256,128]{2,1,0:T(8,128)(2,1)S(1)}, u32[]{:S(2)}, u32[]{:S(2)}) collective-permute-start(bf16[8,256,128]{2,1,0:T(8,128)(2,1)} %backward_tiles.9.rest_0_), channel_id=1, source_target_pairs={{0,104},{1,73},{2,42},{3,11},{4,108},{5,77},{6,46},{7,15},{8,0},{9... | collective-permute-start | bytes 1572872 | tf_op jit(solution)/shard_map/ppermute | solution.py:55
  143.7 52.4 %collective-permute-start.14 = (bf16[8,256,128]{2,1,0:T(8,128)(2,1)}, bf16[8,256,128]{2,1,0:T(8,128)(2,1)S(1)}, u32[]{:S(2)}, u32[]{:S(2)}) collective-permute-start(bf16[8,256,128]{2,1,0:T(8,128)(2,1)} %backward_tiles.12.rest_0_), channel_id=1, source_target_pairs={{0,126},{1,95},{2,60},{3,29},{4,122},{5,89},{6,56},{7,27},{8,118},... | collective-permute-start | bytes 1572872 | tf_op jit(solution)/shard_map/ppermute | solution.py:55
  159.0 37.1 %collective-permute-start.15 = (bf16[8,256,128]{2,1,0:T(8,128)(2,1)}, bf16[8,256,128]{2,1,0:T(8,128)(2,1)S(1)}, u32[]{:S(2)}, u32[]{:S(2)}) collective-permute-start(bf16[8,256,128]{2,1,0:T(8,128)(2,1)} %backward_tiles.13.rest_0_), channel_id=1, source_target_pairs={{0,110},{1,79},{2,44},{3,13},{4,106},{5,75},{6,40},{7,9},{8,6},{9,... | collective-permute-start | bytes 1572872 | tf_op jit(solution)/shard_map/ppermute | solution.py:55
  163.8 4.2 %copy-start.14 = (bf16[8,256,128]{2,1,0:T(8,128)(2,1)}, bf16[8,256,128]{2,1,0:T(8,128)(2,1)S(1)}, u32[]{:S(2)}) copy-start(bf16[8,256,128]{2,1,0:T(8,128)(2,1)S(1)} %collective-permute-done.17.rest_0_) | copy-start | bytes 1572868
  163.8 32.3 %collective-permute-start.16 = (bf16[8,256,128]{2,1,0:T(8,128)(2,1)}, bf16[8,256,128]{2,1,0:T(8,128)(2,1)S(1)}, u32[]{:S(2)}, u32[]{:S(2)}) collective-permute-start(bf16[8,256,128]{2,1,0:T(8,128)(2,1)} %backward_tiles.14.rest_1_), channel_id=1, source_target_pairs={{0,0},{1,97},{2,66},{3,35},{4,4},{5,101},{6,70},{7,39},{8,8},{9,10... | collective-permute-start | bytes 1572872 | tf_op jit(solution)/shard_map/ppermute | solution.py:55
  191.9 15.8 %collective-permute-start.18 = (bf16[8,256,128]{2,1,0:T(8,128)(2,1)}, bf16[8,256,128]{2,1,0:T(8,128)(2,1)S(1)}, u32[]{:S(2)}, u32[]{:S(2)}) collective-permute-start(bf16[8,256,128]{2,1,0:T(8,128)(2,1)} %backward_tiles.15), channel_id=1, source_target_pairs={{0,120},{1,89},{2,58},{3,27},{4,124},{5,93},{6,62},{7,31},{8,112},... | collective-permute-start | bytes 1572872 | tf_op jit(solution)/shard_map/ppermute | solution.py:55
  192.0 18.1 %collective-permute-start.22 = (f32[1,256]{1,0:T(1,128)S(1)}, f32[1,256]{1,0:T(1,128)S(1)}, u32[]{:S(2)}, u32[]{:S(2)}) collective-permute-start(f32[1,256]{1,0:T(1,128)S(1)} %get-tuple-element.24), channel_id=1, source_target_pairs={{0,1},{1,0},{2,3},{3,2},{4,5},{5,4},{6,7},{7,6},{8,9},{9,8},{10,11... | collective-permute-start | bytes 3080 | tf_op jit(solution)/shard_map/ppermute | solution.py:55
  207.7 0.8 copy-start.2
  208.5 1.0 copy-start.3
  209.9 1.5 copy-start.9
  210.0 1.4 collective-permute-start.21
  211.5 3.9 %collective-permute-start.23 = (bf16[144,256]{1,0:T(8,128)(2,1)S(1)}, bf16[144,256]{1,0:T(8,128)(2,1)S(1)}, u32[]{:S(2)}, u32[]{:S(2)}) collective-permute-start(bf16[144,256]{1,0:T(8,128)(2,1)S(1)} %maximum_maximum_fusion), channel_id=1, source_target_pairs={{0,32},{1,33},{2,34},{3,35},{4,36},{5,37},{6,38},{7,39},{8,40},{9,... | collective-permute-start | bytes 221192 | tf_op jit(solution)/shard_map/ppermute | solution.py:55
  212.0 5.9 %collective-permute-start.24 = (bf16[144,256]{1,0:T(8,128)(2,1)S(1)}, bf16[144,256]{1,0:T(8,128)(2,1)S(1)}, u32[]{:S(2)}, u32[]{:S(2)}) collective-permute-start(bf16[144,256]{1,0:T(8,128)(2,1)S(1)} %maximum_maximum_fusion), channel_id=1, source_target_pairs={{0,64},{1,65},{2,66},{3,67},{4,68},{5,69},{6,70},{7,71},{8,72},{9,... | collective-permute-start | bytes 221192 | tf_op jit(solution)/shard_map/ppermute | solution.py:55
  214.6 4.9 %collective-permute-start.25 = (bf16[144,256]{1,0:T(8,128)(2,1)S(1)}, bf16[144,256]{1,0:T(8,128)(2,1)S(1)}, u32[]{:S(2)}, u32[]{:S(2)}) collective-permute-start(bf16[144,256]{1,0:T(8,128)(2,1)S(1)} %maximum_maximum_fusion), channel_id=1, source_target_pairs={{0,96},{1,97},{2,98},{3,99},{4,100},{5,101},{6,102},{7,103},{8,104... | collective-permute-start | bytes 221192 | tf_op jit(solution)/shard_map/ppermute | solution.py:55
  219.7 4.4 %collective-permute-start.26 = (bf16[144,256]{1,0:T(8,128)(2,1)S(1)}, bf16[144,256]{1,0:T(8,128)(2,1)S(1)}, u32[]{:S(2)}, u32[]{:S(2)}) collective-permute-start(bf16[144,256]{1,0:T(8,128)(2,1)S(1)} %maximum_maximum_fusion.1), channel_id=1, source_target_pairs={{0,8},{1,9},{2,10},{3,11},{4,12},{5,13},{6,14},{7,15},{8,0},{9,1},... | collective-permute-start | bytes 221192 | tf_op jit(solution)/shard_map/ppermute | solution.py:55
  220.2 6.5 %collective-permute-start.27 = (bf16[144,256]{1,0:T(8,128)(2,1)S(1)}, bf16[144,256]{1,0:T(8,128)(2,1)S(1)}, u32[]{:S(2)}, u32[]{:S(2)}) collective-permute-start(bf16[144,256]{1,0:T(8,128)(2,1)S(1)} %maximum_maximum_fusion.1), channel_id=1, source_target_pairs={{0,16},{1,17},{2,18},{3,19},{4,20},{5,21},{6,22},{7,23},{8,24},{9,... | collective-permute-start | bytes 221192 | tf_op jit(solution)/shard_map/ppermute | solution.py:55
  224.2 5.2 %collective-permute-start.28 = (bf16[144,256]{1,0:T(8,128)(2,1)S(1)}, bf16[144,256]{1,0:T(8,128)(2,1)S(1)}, u32[]{:S(2)}, u32[]{:S(2)}) collective-permute-start(bf16[144,256]{1,0:T(8,128)(2,1)S(1)} %maximum_maximum_fusion.1), channel_id=1, source_target_pairs={{0,24},{1,25},{2,26},{3,27},{4,28},{5,29},{6,30},{7,31},{8,16},{9,... | collective-permute-start | bytes 221192 | tf_op jit(solution)/shard_map/ppermute | solution.py:55
  229.6 3.3 %collective-permute-start.29 = (bf16[144,256]{1,0:T(8,128)(2,1)S(1)}, bf16[144,256]{1,0:T(8,128)(2,1)S(1)}, u32[]{:S(2)}, u32[]{:S(2)}) collective-permute-start(bf16[144,256]{1,0:T(8,128)(2,1)S(1)} %maximum_maximum_fusion.2), channel_id=1, source_target_pairs={{0,4},{1,5},{2,6},{3,7},{4,0},{5,1},{6,2},{7,3},{8,12},{9,13},{10,... | collective-permute-start | bytes 221192 | tf_op jit(solution)/shard_map/ppermute | solution.py:55
  229.7 7.2 %collective-permute-start.19 = (bf16[2,2,256,128]{3,2,1,0:T(8,128)(2,1)}, bf16[2,2,256,128]{3,2,1,0:T(8,128)(2,1)S(1)}, u32[]{:S(2)}, u32[]{:S(2)}) collective-permute-start(bf16[2,2,256,128]{3,2,1,0:T(8,128)(2,1)} %copy-done.9), channel_id=1, source_target_pairs={{0,1},{1,0},{2,3},{3,2},{4,5},{5,4},{6,7},{7,6},{8,9},{9,8},{10,11... | collective-permute-start | bytes 786440 | tf_op jit(solution)/shard_map/ppermute | solution.py:55
  233.0 7.0 %collective-permute-start.30 = (f32[128,256]{1,0:T(8,128)S(1)}, f32[128,256]{1,0:T(8,128)S(1)}, u32[]{:S(2)}, u32[]{:S(2)}) collective-permute-start(f32[128,256]{1,0:T(8,128)S(1)} %get-tuple-element.30), channel_id=1, source_target_pairs={{0,2},{1,3},{2,0},{3,1},{4,6},{5,7},{6,4},{7,5},{8,10},{9,11},{10,... | collective-permute-start | bytes 393224 | tf_op jit(solution)/shard_map/ppermute | solution.py:55
  237.0 8.2 %collective-permute-start.20 = (bf16[2,256,128]{2,1,0:T(8,128)(2,1)S(1)}, bf16[2,256,128]{2,1,0:T(8,128)(2,1)S(1)}, u32[]{:S(2)}, u32[]{:S(2)}) collective-permute-start(bf16[2,256,128]{2,1,0:T(8,128)(2,1)S(1)} %fusion), channel_id=1, source_target_pairs={{0,2},{1,3},{2,0},{3,1},{4,6},{5,7},{6,4},{7,5},{8,10},{9,11},{10,... | collective-permute-start | bytes 393224 | tf_op jit(solution)/shard_map/ppermute | solution.py:55
  240.1 6.9 %collective-permute-start.31 = (f32[2,128,256]{2,1,0:T(8,128)S(1)}, f32[2,128,256]{2,1,0:T(8,128)S(1)}, u32[]{:S(2)}, u32[]{:S(2)}) collective-permute-start(f32[2,128,256]{2,1,0:T(8,128)S(1)} %maximum_select_fusion), channel_id=1, source_target_pairs={{0,1},{1,0},{2,3},{3,2},{4,5},{5,4},{6,7},{7,6},{8,9},{9,8},{10,11... | collective-permute-start | bytes 786440 | tf_op jit(solution)/shard_map/ppermute | solution.py:55
  245.2 1.0 copy-start.5

commit v5 on v4

v5 whole, which is shorter than its diff:
```python
import functools

import jax
import jax.numpy as jnp
from jax import lax
from jax.experimental import pallas as pl
from jax.experimental.pallas import tpu as pltpu
from jax.sharding import PartitionSpec as P

AXES = ("blk", "rep")
NB = 8
ND = 8
NS = 6
BS = 128
F = 256
VMEM = 16 * 1024 * 1024
ASSEMBLE_VMEM = 40 * 1024 * 1024
PLAN = {6: None, 3: None, 1: None, 2: None, 0: None, 7: 1, 4: 2, 5: 6}
CROSS = {1: 0x7666, 3: 0x5FDB}
GROUPS = ((6, 3, 1, 2, 0), (7, 4, 5))
HELD = ((6, (1,)), (3, (2, 0)))
BACK = ((7, ()), (4, ()), (5, ()), (2, ()), (1, ()), (0, ()), (6, (2,)), (3, (1,)))
MADE = (6, 3)
EARLY = (0,)


def index_of(y, x, zl, zh, core):
    return (((y % 4 * 4 + x % 4) * 2 + zl) * 2 + zh) * 2 + core


def places():
    for t in range(128):
        yield t, t >> 5, t >> 3 & 3, t >> 2 & 1, t >> 1 & 1, t & 1


def column_pairs(k):
    via = PLAN[k]
    out = []
    for t, y, x, zl, zh, core in places():
        j, r = x * 2 + zl, 2 * zh + core
        jj = j ^ k
        if via is None:
            flip = CROSS[k] >> (jj * 2 + core) & 1 if k & 1 else 0
            out.append((index_of(y - r - (jj > j), jj >> 1, jj & 1, zh ^ flip, core), t))
        else:
            jn = j ^ via
            out.append((index_of(y - (jj > j) + (jj > jn), jn >> 1, jn & 1, zh, core), t))
    return out


def flip_pairs(dy=0, dx=0, dzl=0, dzh=0, dcore=0):
    return [
        (t, index_of(y ^ dy, x ^ dx, zl ^ dzl, zh ^ dzh, core ^ dcore))
        for t, y, x, zl, zh, core in places()
    ]


def send(value, pairs):
    return lax.ppermute(value, AXES, pairs)


def params(limit=VMEM):
    return pltpu.CompilerParams(vmem_limit_bytes=limit)


SMEM = pl.BlockSpec(memory_space=pltpu.SMEM)
HBM = pl.BlockSpec(memory_space=pltpu.HBM)
UNREAD = pl.BlockSpec(memory_space=pl.ANY)
WHOLE = pl.BlockSpec(memory_space=pltpu.VMEM)


def matmul_cost(n):
    return pl.CostEstimate(
        flops=2 * NB * NB * BS * BS * F * n, bytes_accessed=(3 << 20) * n, transcendentals=0
    )


def assemble_body(n, sel_ref, cols_ref, counts_ref, tiles_ref, *rest):
    outs, (held_ref, sems) = rest[:n], rest[n:]

    def fetch(k):
        dist, slot = sel_ref[k], k % 2
        return pltpu.make_async_copy(tiles_ref.at[:, dist], held_ref.at[slot], sems.at[slot])

    fetch(0).start()
    for k in range(n):
        fetch(k).wait()
        if k + 1 < n:
            fetch(k + 1).start()
        dist, out_ref, slot = sel_ref[k], outs[k], k % 2

        def block_row(b, carry):
            count = counts_ref[b * ND + dist]
            rows = pl.ds(pl.multiple_of(b * BS, BS), BS)
            cols = [cols_ref[(b * ND + dist) * NS + s] for s in range(NS)]
            cols = [jnp.where(s < count, cols[s], NB) for s in range(NS)]
            tiles = [held_ref[slot, b, s] for s in range(NS)]
            zero = jnp.zeros((BS, BS), jnp.bfloat16)
            for c in range(NB):
                parts = [jnp.where(cols[s] == c, tiles[s], zero) for s in range(NS)]
                pairs = [parts[s] + parts[s + 1] for s in range(0, NS, 2)]
                out_ref[c, rows, :] = pairs[0] + pairs[1] + pairs[2]
            return carry

        lax.fori_loop(0, NB, block_row, 0)


def assemble_call(sel, cols, counts, tiles):
    n = sel.shape[0]
    return pl.pallas_call(
        functools.partial(assemble_body, n),
        out_shape=(jax.ShapeDtypeStruct((NB, NB * BS, BS), jnp.bfloat16),) * n,
        in_specs=[SMEM] * 3 + [HBM],
        out_specs=(WHOLE,) * n,
        scratch_shapes=[
            pltpu.VMEM((2, NB, NS, BS, BS), jnp.bfloat16),
            pltpu.SemaphoreType.DMA((2,)),
        ],
        compiler_params=params(ASSEMBLE_VMEM),
        cost_estimate=matmul_cost(n),
        name="assemble_adjacency",
    )(sel, cols, counts, tiles)


def wide(adj_ref):
    return jnp.concatenate([adj_ref[c] for c in range(NB)], 1)


def forward_body(n, first, last, core_ref, *refs):
    adjacency, shards, rest = refs[:n], refs[n : 2 * n], refs[2 * n :]
    outs = rest[-3:-1] if last else rest[-2:-1]
    total_ref = rest[-1]
    for k in range(n):
        product = jnp.dot(wide(adjacency[k]), shards[k][...], preferred_element_type=jnp.float32)
        if k > 0:
            total_ref[...] += product
        else:
            total_ref[...] = product if first else rest[0][...] + product
    if last:
        core = core_ref[0]
        for part in range(2):
            keep = pl.multiple_of((part * 2 + core) * 256, 256)
            away = pl.multiple_of((part * 2 + 1 - core) * 256, 256)
            outs[0][part] = total_ref[pl.ds(keep, 256), :]
            outs[1][part] = total_ref[pl.ds(away, 256), :].astype(jnp.bfloat16)
    else:
        outs[0][...] = total_ref[...]


def forward_call(core, adjacency, shards, before, last, after):
    n, first = len(shards), before is None
    if last:
        out_shape = (
            jax.ShapeDtypeStruct((2, 256, F), jnp.float32),
            jax.ShapeDtypeStruct((2, 256, F), jnp.bfloat16),
        )
    else:
        out_shape = (jax.ShapeDtypeStruct((NB * BS, F), jnp.float32),)
    return pl.pallas_call(
        functools.partial(forward_body, n, first, last),
        out_shape=out_shape,
        in_specs=[SMEM] + [WHOLE] * (2 * n + (not first)) + [UNREAD] * len(after),
        out_specs=(WHOLE,) * len(out_shape),
        scratch_shapes=[pltpu.VMEM((NB * BS, F), jnp.float32)],
        compiler_params=params(),
        cost_estimate=matmul_cost(n),
        name="forward_product",
    )(core, *adjacency, *shards, *([] if first else [before]), *after)


def dense_body(
    rep_ref, own_ref, got_ref, feat_ref, cot_ref, mask_ref, inv_ref, invt_ref, ws_ref, wn_ref,
    bias_ref, act_ref, term_ref, back_ref, grad_ref, sums_ref,
):
    rep = rep_ref[0]
    zh, core = rep // 2, rep % 2
    nt = (((1,), (1,)), ((), ()))
    tn = (((0,), (0,)), ((), ()))
    grads = jnp.zeros((F, F), jnp.float32)
    sums = jnp.zeros((1, F), jnp.float32)
    for part in range(2):
        quarter = part * 2 + core
        rows = pl.ds(pl.multiple_of(quarter * 256, 256), 256)
        feat = feat_ref[rows, :]
        summed = own_ref[part].astype(jnp.float32) + got_ref[part].astype(jnp.float32)
        agg = (summed * inv_ref[rows, :]).astype(jnp.bfloat16)
        pre = (
            jnp.dot(feat, ws_ref[...], preferred_element_type=jnp.float32)
            + jnp.dot(agg, wn_ref[...], preferred_element_type=jnp.float32)
            + bias_ref[...]
        )
        sigm = jax.nn.sigmoid(pre)
        act = (pre * sigm).astype(jnp.bfloat16)
        slope = sigm * (1.0 + pre * (1.0 - sigm))
        grad_pre = (mask_ref[rows, :] * cot_ref[rows, :].astype(jnp.float32) * slope).astype(
            jnp.bfloat16
        )

        @pl.when(zh == part)
        def _():
            act_ref[...] = act
            term_ref[...] = lax.dot_general(
                grad_pre, ws_ref[...], nt, preferred_element_type=jnp.float32
            )

        back_t = lax.dot_general(wn_ref[...], grad_pre, nt, preferred_element_type=jnp.float32)
        back_ref[part] = (back_t * invt_ref[quarter]).astype(jnp.bfloat16)
        left = jnp.where(zh == 0, feat, agg)
        grads += lax.dot_general(left, grad_pre, tn, preferred_element_type=jnp.float32)
        sums += jnp.sum(grad_pre.astype(jnp.float32), axis=0, keepdims=True)
    grad_ref[...] = grads
    sums_ref[...] = sums


def dense_call(rep, own, got, feat, cot, mask, inv, inv_t, w_self, w_neigh, bias):
    vmem = pl.BlockSpec(memory_space=pltpu.VMEM)
    return pl.pallas_call(
        dense_body,
        out_shape=(
            jax.ShapeDtypeStruct((256, F), jnp.bfloat16),
            jax.ShapeDtypeStruct((256, F), jnp.float32),
            jax.ShapeDtypeStruct((2, F, 256), jnp.bfloat16),
            jax.ShapeDtypeStruct((F, F), jnp.float32),
            jax.ShapeDtypeStruct((1, F), jnp.float32),
        ),
        in_specs=[pl.BlockSpec(memory_space=pltpu.SMEM)] + [vmem] * 10,
        out_specs=(vmem,) * 5,
        compiler_params=params(16 << 20),
        name="dense_rows",
    )(rep, own, got, feat, cot, mask, inv, inv_t, w_self, w_neigh, bias)


def backward_body(added, core_ref, adj_ref, own_ref, got_ref, *rest):
    out_ref = rest[-1]
    core = core_ref[0]
    message = []
    for quarter in range(4):
        mine = core == quarter % 2
        message.append(jnp.where(mine, own_ref[quarter // 2], got_ref[quarter // 2]))
    product = jnp.dot(
        jnp.concatenate(message, 1), wide(adj_ref), preferred_element_type=jnp.float32
    )
    for c in range(NB):
        part = product[:, c * BS : (c + 1) * BS]
        for ref in rest[:added]:
            part += ref[c].astype(jnp.float32)
        out_ref[c] = part.astype(jnp.bfloat16)


def backward_call(core, adjacency, own, got, extra, after):
    added = len(extra)
    return pl.pallas_call(
        functools.partial(backward_body, added),
        out_shape=jax.ShapeDtypeStruct((NB, F, BS), jnp.bfloat16),
        in_specs=[SMEM] + [WHOLE] * (3 + added) + [UNREAD] * len(after),
        out_specs=WHOLE,
        compiler_params=params(),
        cost_estimate=matmul_cost(1),
        name="backward_product",
    )(core, adjacency, own, got, *extra, *after)


def split_body(core_ref, *rest):
    arrived, (keep_ref, away_ref) = rest[:-2], rest[-2:]
    core = core_ref[0]
    for part in range(2):
        for c in range(2):
            keep = (part * 2 + core) * 2 + c
            away = (part * 2 + 1 - core) * 2 + c
            kept = arrived[0][keep].astype(jnp.float32)
            sent = arrived[0][away].astype(jnp.float32)
            for ref in arrived[1:]:
                kept += ref[keep].astype(jnp.float32)
                sent += ref[away].astype(jnp.float32)
            keep_ref[part, c] = kept
            away_ref[part, c] = sent.astype(jnp.bfloat16)


def split_call(core, arrived):
    return pl.pallas_call(
        split_body,
        out_shape=(
            jax.ShapeDtypeStruct((2, 2, F, BS), jnp.float32),
            jax.ShapeDtypeStruct((2, 2, F, BS), jnp.bfloat16),
        ),
        in_specs=[SMEM] + [WHOLE] * len(arrived),
        out_specs=(WHOLE, WHOLE),
        compiler_params=params(16 << 20),
        name="split_products",
    )(core, *arrived)


def hold_body(*refs):
    pass


def hold_call(along, after):
    return pl.pallas_call(
        hold_body,
        out_shape=jax.ShapeDtypeStruct(along.shape, along.dtype),
        in_specs=[UNREAD] * (1 + len(after)),
        out_specs=UNREAD,
        input_output_aliases={0: 0},
        name="hold",
    )(along, *after)


def final_body(kept_ref, got_ref, term_ref, out_ref):
    for c in range(2):
        spread = kept_ref[c] + got_ref[c].astype(jnp.float32)
        rows = slice(c * BS, (c + 1) * BS)
        out_ref[rows, :] = (term_ref[rows, :] + spread.T).astype(jnp.bfloat16)


def final_call(kept, got, term):
    return pl.pallas_call(
        final_body,
        out_shape=jax.ShapeDtypeStruct((256, F), jnp.bfloat16),
        compiler_params=params(16 << 20),
        name="final_rows",
    )(kept, got, term)


def pick(pair, index):
    return lax.dynamic_index_in_dim(pair, index, 0, keepdims=False)


def weight_grads(grads, sums, zh, core, nodes):
    halves = grads.reshape(2, F // 2, F)
    mine = pick(halves, core) + send(pick(halves, 1 - core), flip_pairs(dcore=1))
    count = lax.axis_size("blk")
    share = F // 2 // count
    bias = sums + send(sums, flip_pairs(dcore=1))
    high = bias.astype(jnp.bfloat16)
    low = (bias - high.astype(jnp.float32)).astype(jnp.bfloat16)
    bias_rows = jnp.broadcast_to(jnp.concatenate([high, low], 0)[None], (count, 2, F))
    rows = mine.astype(jnp.bfloat16).reshape(count, share, F)
    parts = lax.all_to_all(jnp.concatenate([rows, bias_rows], 1), "blk", 0, 0)
    total = jnp.sum(parts.astype(jnp.float32), axis=0)
    bias = total[share] + total[share + 1]
    spread = jnp.broadcast_to(total[None, :share], (count, share, F))
    half = lax.all_to_all(spread, "blk", 0, 0).reshape(F // 2, F)
    other = send(half, flip_pairs(dzh=1))
    both = jnp.where(zh == 0, jnp.stack([half, other]), jnp.stack([other, half]))
    across = send(both, flip_pairs(dcore=1))
    low, top = jnp.where(core == 0, both, across), jnp.where(core == 0, across, both)
    norm = 1.0 / jnp.sqrt(jnp.float32(nodes))
    whole = jnp.concatenate([low, top], 1) * norm
    return whole[0], whole[1], bias * norm


def shards(
    features, tiles, tile_cols, counts, degree, train_mask, cotangent, w_self, w_neigh, bias_term
):
    rows = features.shape[0]
    rep = lax.axis_index("rep").astype(jnp.int32)
    zh, core = rep // 2, rep % 2
    place = (lax.axis_index("blk") % 8).astype(jnp.int32)
    cols = tile_cols.reshape(-1)
    live = counts.reshape(-1)

    def distance_of(k):
        return (place - (place ^ k)) % 8

    inv = 1.0 / degree.astype(jnp.float32)
    inv_col = inv.reshape(rows, 1)
    inv_row = inv.reshape(4, 1, 256)
    mask = train_mask.astype(jnp.float32).reshape(rows, 1)
    bias = bias_term.reshape(1, F)

    order = list(PLAN)
    sel = jnp.stack([distance_of(k) for k in order])
    adjacency = dict(zip(order, assemble_call(sel, cols, live, tiles)))
    blocks, held = {}, []
    for k, via in PLAN.items():
        if via is None:
            blocks[k] = send(features, column_pairs(k))
    for k, after in HELD:
        blocks[k] = hold_call(blocks[k], [adjacency[k]] + [blocks[a] for a in after])
        held.append(blocks[k])
    for k, via in PLAN.items():
        if via is not None:
            blocks[k] = send(blocks[k ^ via], column_pairs(k))
    made = (None,)
    for group in GROUPS:
        made = forward_call(
            core[None],
            [adjacency[k] for k in group],
            [blocks[k] for k in group],
            made[0],
            group is GROUPS[-1],
            held if group is GROUPS[0] else [],
        )

    kept, away = made
    chip = (kept + send(away, flip_pairs(dcore=1)).astype(jnp.float32)).astype(jnp.bfloat16)
    other = send(chip, flip_pairs(dzh=1))

    activation, own_term, back_own, grads, sums = dense_call(
        rep[None], chip, other, features, cotangent, mask, inv_col, inv_row, w_self, w_neigh, bias
    )
    back_got = send(back_own, flip_pairs(dcore=1))

    arrived, extra, products = {}, {}, {}
    for k, after in BACK:
        products[k] = backward_call(
            core[None],
            adjacency[k],
            back_own,
            back_got,
            extra.get(k, []),
            [arrived[a] for a in after],
        )
        moved = send(products[k], [(b, a) for a, b in column_pairs(k)])
        if PLAN[k] is None:
            arrived[k] = moved
        else:
            extra.setdefault(k ^ PLAN[k], []).append(moved)
    waited = [products[k] for k in MADE] + [arrived[k] for k in EARLY]
    grad_self, grad_neigh, grad_bias = weight_grads(
        grads, sums, zh, core, rows * lax.axis_size("blk")
    )

    kept, away = split_call(core[None], list(arrived.values()))
    chip = kept + send(away, flip_pairs(dcore=1)).astype(jnp.float32)
    got = send(pick(chip, 1 - zh).astype(jnp.bfloat16), flip_pairs(dzh=1))
    grad_features = final_call(pick(chip, zh), got, own_term)
    return (activation, grad_features, grad_self, grad_neigh, grad_bias)


def solution(mesh):
    return jax.shard_map(
        shards,
        mesh=mesh,
        in_specs=(
            P("blk", None),
            P("blk", "rep", None, None, None),
            P("blk", "rep", None),
            P("blk", "rep"),
            P("blk"),
            P("blk"),
            P("blk", None),
            P(),
            P(),
            P(),
        ),
        out_specs=(P(("blk", "rep"), None), P(("blk", "rep"), None), P(), P(), P()),
        check_vma=False,
    )
```

time: 249 us -> 193 us (0.78)
  waiting for transfers between devices: 89.5 us -> 19.3 us
  Pallas kernels: 69.4 us -> 44.9 us
  local copies, waits for them, and re-layouts: 9.14 us -> 29.8 us
  blocking collectives: 0 us -> 20.3 us
    ppermute x32 -> x25, waiting for transfers between devices: 89.5 us -> 19.3 us  [send(): return lax.ppermute(value, AXES, pairs)]
    pallas_call x8, Pallas kernels: 38.4 us -> 14.5 us  [backward_call(): pl.pallas_call(functools.partial(backward_body, added), out_shape=jax.Sha...]
    pallas_call x4 -> x2, Pallas kernels: 28.2 us -> 7.1 us  [forward_call(): pl.pallas_call(functools.partial(forward_body, n, first, last), out_shape...]
    pallas_call x1 -> x4, Pallas kernels: 0.43 us -> 21 us  [the longest x1 19.3 us: assemble_call(): pl.pallas_call(functools.partial(assemble_body, n), out_shape=(jax.ShapeD...]
    all_to_all x0 -> x1, blocking collectives: none -> 20.3 us  [weight_grads(): parts = lax.all_to_all(jnp.concatenate([rows, bias_rows], 1), 'blk', 0, 0)]
    unnamed x37 -> x79, local copies, waits for them, and re-layouts: 6.79 us -> 25.9 us
    ppermute x32 -> x25, starting transfers between devices: 76.6 us -> 64.4 us  [send(): return lax.ppermute(value, AXES, pairs)]
    all_to_all x0 -> x1, starting transfers between devices: none -> 11.1 us  [weight_grads(): half = lax.all_to_all(spread, 'blk', 0, 0).reshape(F // 2, F)]
  transfers between devices with their start and end apart: 32 -> 26, of which waited for: 16 -> 8; matrix products, arithmetic and copies ran while one was open for 2% -> 3% of each run, Pallas kernels for 22% -> 21%
where the time goes in v5:
time: 193 us; the launch traced here: 192 us
  starting transfers between devices  75.5 us (39%)
  Pallas kernels  44.9 us (23%)
  local copies, waits for them, and re-layouts  29.8 us (15%)
  blocking collectives  20.3 us (11%)
  waiting for transfers between devices  19.3 us (10%)
    ppermute x25, starting transfers between devices, send(): return lax.ppermute(value, AXES, pairs)  64.4 us
    unnamed x79, local copies, waits for them, and re-layouts  25.9 us
    all_to_all x1, blocking collectives, weight_grads(): parts = lax.all_to_all(jnp.concatenate([rows, bias_rows], 1), 'blk', 0, 0)  20.3 us
    pallas_call x1, Pallas kernels, assemble_call(): pl.pallas_call(functools.partial(assemble_body, n), out_shape=(jax.ShapeD...  19.3 us
    ppermute x25, waiting for transfers between devices, send(): return lax.ppermute(value, AXES, pairs)  19.3 us
    pallas_call x8, Pallas kernels, backward_call(): pl.pallas_call(functools.partial(backward_body, added), out_shape=jax.Sha...  14.5 us
    all_to_all x1, starting transfers between devices, weight_grads(): half = lax.all_to_all(spread, 'blk', 0, 0).reshape(F // 2, F)  11.1 us
    pallas_call x2, Pallas kernels, forward_call(): pl.pallas_call(functools.partial(forward_body, n, first, last), out_shape...  7.1 us
  transfers between devices with their start and end apart: 26, of which 8 were waited for; matrix products, arithmetic and copies ran while one was open for 3% of the time, Pallas kernels for 21%

profile of v5, /device:TPU:1, one launch (start us, length us, event | category | flops | bytes accessed | tf_op | source)
XLA Modules:
  0.0 191.9 jit_solution(1066431743941631524)
XLA Ops:
  0.6 3.1 %collective-permute-start.5 = (bf16[1024,256]{1,0:T(8,128)(2,1)}, bf16[1024,256]{1,0:T(8,128)(2,1)S(1)}, u32[]{:S(2)}, u32[]{:S(2)}) collective-permute-start(bf16[1024,256]{1,0:T(8,128)(2,1)} %feat_ref.1), channel_id=1, source_target_pairs={{104,0},{73,1},{42,2},{11,3},{108,4},{77,5},{46,6},{15,7},{0,8},{9... | collective-permute-start | bytes 1572872 | tf_op jit(solution)/shard_map/ppermute | solution.py:59
  3.8 3.2 %collective-permute-start.6 = (bf16[1024,256]{1,0:T(8,128)(2,1)}, bf16[1024,256]{1,0:T(8,128)(2,1)S(1)}, u32[]{:S(2)}, u32[]{:S(2)}) collective-permute-start(bf16[1024,256]{1,0:T(8,128)(2,1)} %feat_ref.1), channel_id=1, source_target_pairs={{0,0},{97,1},{66,2},{35,3},{4,4},{101,5},{70,6},{39,7},{8,8},{105,... | collective-permute-start | bytes 1572872 | tf_op jit(solution)/shard_map/ppermute | solution.py:59
  7.0 4.4 %collective-permute-start.4 = (bf16[1024,256]{1,0:T(8,128)(2,1)}, bf16[1024,256]{1,0:T(8,128)(2,1)S(1)}, u32[]{:S(2)}, u32[]{:S(2)}) collective-permute-start(bf16[1024,256]{1,0:T(8,128)(2,1)} %feat_ref.1), channel_id=1, source_target_pairs={{110,0},{79,1},{44,2},{13,3},{106,4},{73,5},{40,6},{11,7},{4,8},{1... | collective-permute-start | bytes 1572872 | tf_op jit(solution)/shard_map/ppermute | solution.py:59
  11.4 1.1 collective-permute-start.1
  12.5 2.4 %collective-permute-start = (bf16[1024,256]{1,0:T(8,128)(2,1)}, bf16[1024,256]{1,0:T(8,128)(2,1)S(1)}, u32[]{:S(2)}, u32[]{:S(2)}) collective-permute-start(bf16[1024,256]{1,0:T(8,128)(2,1)} %feat_ref.1), channel_id=1, source_target_pairs={{120,0},{89,1},{58,2},{27,3},{124,4},{93,5},{62,6},{31,7},{112,8},... | collective-permute-start | bytes 1572872 | tf_op jit(solution)/shard_map/ppermute | solution.py:59
  14.9 0.9 copy.17
  15.9 0.8 reshape.44.counts_ref
  16.7 19.3 %assemble_adjacency.1 = (bf16[8,1024,128]{2,1,0:T(8,128)(2,1)S(1)}, bf16[8,1024,128]{2,1,0:T(8,128)(2,1)S(1)}, bf16[8,1024,128]{2,1,0:T(8,128)(2,1)S(1)}, bf16[8...) custom-call(s32[8]{0:T(128)S(1)} %stack.42.sel_ref, ...), custom_call_target="tpu_custom_call" | custom-call | flops 4294967296 | bytes 25165824 | tf_op jit(solution)/shard_map/assemble_adjacency/pallas_call | solution.py:110
  36.0 1.3 copy-done
  37.3 1.3 copy-done.2
  38.7 1.3 copy-done.5
  40.0 1.3 copy-done.12
  41.3 1.4 copy-done.15
  42.7 1.3 copy-done.18
  45.2 2.3 %collective-permute-start.7 = (bf16[1024,256]{1,0:T(8,128)(2,1)}, bf16[1024,256]{1,0:T(8,128)(2,1)}, u32[]{:S(2)}, u32[]{:S(2)}) collective-permute-start(bf16[1024,256]{1,0:T(8,128)(2,1)} %hold.3.refs_6_.refs_11_), channel_id=1, source_target_pairs={{120,0},{121,1},{122,2},{123,3},{124,4},{125,5},{126,6},{127,7},{1... | collective-permute-start | bytes 1572872 | tf_op jit(solution)/shard_map/ppermute | solution.py:59
  47.5 0.8 copy-done.21
  48.9 1.6 copy-done.3
  50.5 1.6 copy-done.13
  52.1 1.6 copy-done.16
  53.7 1.6 copy-done.19
  55.3 1.0 copy-done.22
  56.3 1.0 copy-done.27
  57.4 1.0 copy-done.29
  58.4 4.0 %forward_product.2.refs_6_ = f32[1024,256]{1,0:T(8,128)S(1)} custom-call(s32[1]{0:T(128)} %bitcast.1.core_ref, bf16[8,1024,128]{2,1,0:T(8,128)(2,1)S(1)} %copy-done.1, bf16[8,1024,128]{2,1,0:T(8,128)(2,1)S(1)} %copy-done.3, bf16[8,1024,128]{2,1,0:T(8,128)(2,1)S(1)} %copy-done.19, bf16[8,1024,128]{2,1,0:T(8,128)(2,1)S(1)} %copy-done.16, ...), custom_call_target="tpu_custom_call" | custom-call | flops 2684354560 | bytes 15728640 | tf_op jit(solution)/shard_map/forward_product/pallas_call | solution.py:159
  62.6 3.1 %forward_product.3 = (f32[2,256,256]{2,1,0:T(8,128)S(1)}, bf16[2,256,256]{2,1,0:T(8,128)(2,1)S(1)}) custom-call(s32[1]{0:T(128)} %bitcast.1.core_ref, bf16[8,1024,128]{2,1,0:T(8,128)(2,1)S(1)} %copy-done.6, bf16[8,1024,128]{2,1,0:T(8,128)(2,1)S(1)} %copy-done.8, bf16[8,1024,128]{2,1,0:T(8,128)(2,1)S(1)} %copy-done.10, ...), custom_call_target="tpu_custom_call" | custom-call | flops 1610612736 | bytes 9437184 | tf_op jit(solution)/shard_map/forward_product/pallas_call | solution.py:159
  65.6 2.7 %collective-permute-start.8 = (bf16[2,256,256]{2,1,0:T(8,128)(2,1)S(1)}, bf16[2,256,256]{2,1,0:T(8,128)(2,1)S(1)}, u32[]{:S(2)}, u32[]{:S(2)}) collective-permute-start(bf16[2,256,256]{2,1,0:T(8,128)(2,1)S(1)} %get-tuple-element.31), channel_id=1, source_target_pairs={{0,1},{1,0},{2,3},{3,2},{4,5},{5,4},{6,7},{7,6},{8,9},{9,8},{10,11... | collective-permute-start | bytes 786440 | tf_op jit(solution)/shard_map/ppermute | solution.py:59
  68.4 1.2 collective-permute-done.8
  69.6 4.8 %collective-permute-start.9 = (bf16[2,256,256]{2,1,0:T(8,128)(2,1)S(1)}, bf16[2,256,256]{2,1,0:T(8,128)(2,1)S(1)}, u32[]{:S(2)}, u32[]{:S(2)}) collective-permute-start(bf16[2,256,256]{2,1,0:T(8,128)(2,1)S(1)} %add_convert_fusion.own_ref), channel_id=1, source_target_pairs={{0,2},{1,3},{2,0},{3,1},{4,6},{5,7},{6,4},{7,5},{8,10},{9,11},{10,... | collective-permute-start | bytes 786440 | tf_op jit(solution)/shard_map/ppermute | solution.py:59
  74.6 1.0 copy.18.mask_ref
  75.7 5.1 %collective-permute-done.9.got_ref = bf16[2,256,256]{2,1,0:T(8,128)(2,1)S(1)} collective-permute-done((bf16[2,256,256]{2,1,0:T(8,128)(2,1)S(1)}, bf16[2,256,256]{2,1,0:T(8,128)(2,1)S(1)}, u32[]{:S(2)}, u32[]{:S(2)}) %collective-permute-start.9) | collective-permute-done | bytes 262176 | tf_op jit(solution)/shard_map/ppermute | solution.py:59
  80.8 1.0 copy-done.25
  81.8 1.0 copy-done.30
  82.8 1.0 copy-done.31
  83.9 0.9 copy-done.35
  84.8 1.6 dense_rows.1
  86.3 0.9 collective-permute-start.22
  88.1 1.0 collective-permute-done.10.got_ref
  89.0 1.5 backward_product.14
  90.6 3.3 %collective-permute-start.17 = (bf16[8,256,128]{2,1,0:T(8,128)(2,1)}, bf16[8,256,128]{2,1,0:T(8,128)(2,1)}, u32[]{:S(2)}, u32[]{:S(2)}) collective-permute-start(bf16[8,256,128]{2,1,0:T(8,128)(2,1)} %backward_product.14), channel_id=1, source_target_pairs={{0,120},{1,121},{2,122},{3,123},{4,124},{5,125},{6,126},{7,127},{8... | collective-permute-start | bytes 1572872 | tf_op jit(solution)/shard_map/ppermute | solution.py:59
  93.9 1.5 backward_product.9
  95.4 1.5 backward_product.12
  97.3 1.5 backward_product.11
  98.8 3.4 %collective-permute-start.14 = (bf16[8,256,128]{2,1,0:T(8,128)(2,1)}, bf16[8,256,128]{2,1,0:T(8,128)(2,1)}, u32[]{:S(2)}, u32[]{:S(2)}) collective-permute-start(bf16[8,256,128]{2,1,0:T(8,128)(2,1)} %backward_product.11), channel_id=1, source_target_pairs={{0,4},{1,5},{2,6},{3,7},{4,0},{5,1},{6,2},{7,3},{8,12},{9,13},{10,... | collective-permute-start | bytes 1572872 | tf_op jit(solution)/shard_map/ppermute | solution.py:59
  102.3 1.5 backward_product.8
  103.8 1.9 %collective-permute-start.11 = (bf16[8,256,128]{2,1,0:T(8,128)(2,1)}, bf16[8,256,128]{2,1,0:T(8,128)(2,1)}, u32[]{:S(2)}, u32[]{:S(2)}) collective-permute-start(bf16[8,256,128]{2,1,0:T(8,128)(2,1)} %backward_product.8), channel_id=1, source_target_pairs={{0,104},{1,73},{2,42},{3,11},{4,108},{5,77},{6,46},{7,15},{8,0},{9... | collective-permute-start | bytes 1572872 | tf_op jit(solution)/shard_map/ppermute | solution.py:59
  105.9 20.3 %all_to_all.10 = bf16[32,6,256]{2,1,0:T(8,128)(2,1)S(1)} all-to-all(bf16[32,6,256]{2,1,0:T(8,128)(2,1)S(1)} %pad_maximum_fusion), channel_id=1, replica_groups=mesh['blk'=32,'rep'=4] {'blk'}, dimensions={0} | all-to-all | bytes 196608 | tf_op jit(solution)/shard_map/all_to_all | solution.py:338
  126.9 11.1 %all-to-all-start.1 = ((f32[32,4,256]{2,1,0:T(4,128)}), f32[32,4,256]{2,1,0:T(4,128)S(1)}, u32[]{:S(2)}, u32[]{:S(2)}) async-start(f32[32,4,256]{2,1,0:T(4,128)} %broadcast_in_dim.11), calls=%async_computation.1 | async-start | bytes 262144 | tf_op jit(solution)/shard_map/all_to_all | solution.py:342
  138.1 1.6 copy-done.14
  139.6 1.5 backward_product.10
  141.2 4.4 %collective-permute-start.13 = (bf16[8,256,128]{2,1,0:T(8,128)(2,1)}, bf16[8,256,128]{2,1,0:T(8,128)(2,1)}, u32[]{:S(2)}, u32[]{:S(2)}) collective-permute-start(bf16[8,256,128]{2,1,0:T(8,128)(2,1)} %backward_product.10), channel_id=1, source_target_pairs={{0,0},{1,97},{2,66},{3,35},{4,4},{5,101},{6,70},{7,39},{8,8},{9,10... | collective-permute-start | bytes 1572872 | tf_op jit(solution)/shard_map/ppermute | solution.py:59
  145.6 2.6 %backward_product.15 = bf16[8,256,128]{2,1,0:T(8,128)(2,1)} custom-call(s32[1]{0:T(128)} %bitcast.1.core_ref, bf16[8,1024,128]{2,1,0:T(8,128)(2,1)S(1)} %copy-done.4, bf16[2,256,256]{2,1,0:T(8,128)(2,1)S(1)} %get-tuple-element.33.own_ref, bf16[2,256,256]{2,1,0:T(8,128)(2,1)S(1)} %collective-permute-done.10.got_ref, ...), custom_call_target="tpu_custom_call" | custom-call | flops 536870912 | bytes 3145728 | tf_op jit(solution)/shard_map/backward_product/pallas_call | solution.py:252
  148.1 2.4 %collective-permute-start.18 = (bf16[8,256,128]{2,1,0:T(8,128)(2,1)}, bf16[8,256,128]{2,1,0:T(8,128)(2,1)}, u32[]{:S(2)}, u32[]{:S(2)}) collective-permute-start(bf16[8,256,128]{2,1,0:T(8,128)(2,1)} %backward_product.15), channel_id=1, source_target_pairs={{0,110},{1,79},{2,44},{3,13},{4,106},{5,73},{6,40},{7,11},{8,4},{9... | collective-permute-start | bytes 1572872 | tf_op jit(solution)/shard_map/ppermute | solution.py:59
  150.6 2.7 %backward_product.13 = bf16[8,256,128]{2,1,0:T(8,128)(2,1)} custom-call(s32[1]{0:T(128)} %bitcast.1.core_ref, bf16[8,1024,128]{2,1,0:T(8,128)(2,1)S(1)} %copy-done.1, bf16[2,256,256]{2,1,0:T(8,128)(2,1)S(1)} %get-tuple-element.33.own_ref, bf16[2,256,256]{2,1,0:T(8,128)(2,1)S(1)} %collective-permute-done.10.got_ref, ...), custom_call_target="tpu_custom_call" | custom-call | flops 536870912 | bytes 3145728 | tf_op jit(solution)/shard_map/backward_product/pallas_call | solution.py:252
  153.3 2.0 %collective-permute-start.16 = (bf16[8,256,128]{2,1,0:T(8,128)(2,1)}, bf16[8,256,128]{2,1,0:T(8,128)(2,1)S(1)}, u32[]{:S(2)}, u32[]{:S(2)}) collective-permute-start(bf16[8,256,128]{2,1,0:T(8,128)(2,1)} %backward_product.13), channel_id=1, source_target_pairs={{0,120},{1,89},{2,58},{3,27},{4,124},{5,93},{6,62},{7,31},{8,112},... | collective-permute-start | bytes 1572872 | tf_op jit(solution)/shard_map/ppermute | solution.py:59
  155.6 6.5 %collective-permute-done.23 = f32[128,256]{1,0:T(8,128)S(1)} collective-permute-done((f32[128,256]{1,0:T(8,128)S(1)}, f32[128,256]{1,0:T(8,128)S(1)}, u32[]{:S(2)}, u32[]{:S(2)}) %collective-permute-start.23) | collective-permute-done | bytes 131104 | tf_op jit(solution)/shard_map/ppermute | solution.py:59
  162.1 4.4 %collective-permute-start.24 = (f32[2,128,256]{2,1,0:T(8,128)S(1)}, f32[2,128,256]{2,1,0:T(8,128)S(1)}, u32[]{:S(2)}, u32[]{:S(2)}) collective-permute-start(f32[2,128,256]{2,1,0:T(8,128)S(1)} %maximum_select_fusion), channel_id=1, source_target_pairs={{0,1},{1,0},{2,3},{3,2},{4,5},{5,4},{6,7},{7,6},{8,9},{9,8},{10,11... | collective-permute-start | bytes 786440 | tf_op jit(solution)/shard_map/ppermute | solution.py:59
  167.1 1.6 collective-permute-done.16.rest_3_
  168.7 1.7 split_products.1
  170.3 8.9 %collective-permute-start.19 = (bf16[2,2,256,128]{3,2,1,0:T(8,128)(2,1)S(1)}, bf16[2,2,256,128]{3,2,1,0:T(8,128)(2,1)S(1)}, u32[]{:S(2)}, u32[]{:S(2)}) collective-permute-start(bf16[2,2,256,128]{3,2,1,0:T(8,128)(2,1)S(1)} %get-tuple-element.35), channel_id=1, source_target_pairs={{0,1},{1,0},{2,3},{3,2},{4,5},{5,4},{6,7},{7,6},{8,9},{9,8},{10,11... | collective-permute-start | bytes 786440 | tf_op jit(solution)/shard_map/ppermute | solution.py:59
  179.3 1.1 collective-permute-done.19
  180.5 7.0 %collective-permute-start.20 = (bf16[2,256,128]{2,1,0:T(8,128)(2,1)S(1)}, bf16[2,256,128]{2,1,0:T(8,128)(2,1)S(1)}, u32[]{:S(2)}, u32[]{:S(2)}) collective-permute-start(bf16[2,256,128]{2,1,0:T(8,128)(2,1)S(1)} %fusion), channel_id=1, source_target_pairs={{0,2},{1,3},{2,0},{3,1},{4,6},{5,7},{6,4},{7,5},{8,10},{9,11},{10,... | collective-permute-start | bytes 393224 | tf_op jit(solution)/shard_map/ppermute | solution.py:59
  187.5 0.8 slice_bitcast_fusion
  188.3 2.7 %collective-permute-done.20.got_ref = bf16[2,256,128]{2,1,0:T(8,128)(2,1)S(1)} collective-permute-done((bf16[2,256,128]{2,1,0:T(8,128)(2,1)S(1)}, bf16[2,256,128]{2,1,0:T(8,128)(2,1)S(1)}, u32[]{:S(2)}, u32[]{:S(2)}) %collective-permute-start.20) | collective-permute-done | bytes 131104 | tf_op jit(solution)/shard_map/ppermute | solution.py:59
  191.1 0.8 final_rows.1
  (112 shorter events, 5.4 us)
Async XLA Ops:
  0.6 43.3 %collective-permute-start.5 = (bf16[1024,256]{1,0:T(8,128)(2,1)}, bf16[1024,256]{1,0:T(8,128)(2,1)S(1)}, u32[]{:S(2)}, u32[]{:S(2)}) collective-permute-start(bf16[1024,256]{1,0:T(8,128)(2,1)} %feat_ref.1), channel_id=1, source_target_pairs={{104,0},{73,1},{42,2},{11,3},{108,4},{77,5},{46,6},{15,7},{0,8},{9... | collective-permute-start | bytes 1572872 | tf_op jit(solution)/shard_map/ppermute | solution.py:59
  3.8 40.2 %collective-permute-start.6 = (bf16[1024,256]{1,0:T(8,128)(2,1)}, bf16[1024,256]{1,0:T(8,128)(2,1)S(1)}, u32[]{:S(2)}, u32[]{:S(2)}) collective-permute-start(bf16[1024,256]{1,0:T(8,128)(2,1)} %feat_ref.1), channel_id=1, source_target_pairs={{0,0},{97,1},{66,2},{35,3},{4,4},{101,5},{70,6},{39,7},{8,8},{105,... | collective-permute-start | bytes 1572872 | tf_op jit(solution)/shard_map/ppermute | solution.py:59
  7.0 37.0 %collective-permute-start.4 = (bf16[1024,256]{1,0:T(8,128)(2,1)}, bf16[1024,256]{1,0:T(8,128)(2,1)S(1)}, u32[]{:S(2)}, u32[]{:S(2)}) collective-permute-start(bf16[1024,256]{1,0:T(8,128)(2,1)} %feat_ref.1), channel_id=1, source_target_pairs={{110,0},{79,1},{44,2},{13,3},{106,4},{73,5},{40,6},{11,7},{4,8},{1... | collective-permute-start | bytes 1572872 | tf_op jit(solution)/shard_map/ppermute | solution.py:59
  11.4 36.1 %collective-permute-start.1 = (bf16[1024,256]{1,0:T(8,128)(2,1)}, bf16[1024,256]{1,0:T(8,128)(2,1)}, u32[]{:S(2)}, u32[]{:S(2)}) collective-permute-start(bf16[1024,256]{1,0:T(8,128)(2,1)} %feat_ref.1), channel_id=1, source_target_pairs={{102,0},{69,1},{36,2},{7,3},{0,4},{99,5},{66,6},{33,7},{110,8},{77... | collective-permute-start | bytes 1572872 | tf_op jit(solution)/shard_map/ppermute | solution.py:59
  12.5 35.0 %collective-permute-start = (bf16[1024,256]{1,0:T(8,128)(2,1)}, bf16[1024,256]{1,0:T(8,128)(2,1)S(1)}, u32[]{:S(2)}, u32[]{:S(2)}) collective-permute-start(bf16[1024,256]{1,0:T(8,128)(2,1)} %feat_ref.1), channel_id=1, source_target_pairs={{120,0},{89,1},{58,2},{27,3},{124,4},{93,5},{62,6},{31,7},{112,8},... | collective-permute-start | bytes 1572872 | tf_op jit(solution)/shard_map/ppermute | solution.py:59
  36.0 1.3 copy-start
  37.3 1.3 copy-start.2
  38.6 1.3 copy-start.5
  40.0 1.3 copy-start.12
  41.3 1.4 copy-start.15
  42.7 1.3 copy-start.18
  44.0 0.8 copy-start.26
  44.0 1.0 copy-start.28
  44.0 1.2 copy-start.23
  45.2 3.7 %copy-start.1 = (bf16[8,1024,128]{2,1,0:T(8,128)(2,1)S(1)}, bf16[8,1024,128]{2,1,0:T(8,128)(2,1)}, u32[]{:S(2)}) copy-start(bf16[8,1024,128]{2,1,0:T(8,128)(2,1)} %copy-done) | copy-start | bytes 6291460
  45.2 3.7 %copy-start.24 = (bf16[1024,256]{1,0:T(8,128)(2,1)S(1)}, bf16[1024,256]{1,0:T(8,128)(2,1)}, u32[]{:S(2)}) copy-start(bf16[1024,256]{1,0:T(8,128)(2,1)} %hold.3.refs_6_.refs_11_) | copy-start | bytes 1572868
  45.2 17.3 %collective-permute-start.7 = (bf16[1024,256]{1,0:T(8,128)(2,1)}, bf16[1024,256]{1,0:T(8,128)(2,1)}, u32[]{:S(2)}, u32[]{:S(2)}) collective-permute-start(bf16[1024,256]{1,0:T(8,128)(2,1)} %hold.3.refs_6_.refs_11_), channel_id=1, source_target_pairs={{120,0},{121,1},{122,2},{123,3},{124,4},{125,5},{126,6},{127,7},{1... | collective-permute-start | bytes 1572872 | tf_op jit(solution)/shard_map/ppermute | solution.py:59
  48.3 14.2 %collective-permute-start.2 = (bf16[1024,256]{1,0:T(8,128)(2,1)}, bf16[1024,256]{1,0:T(8,128)(2,1)S(1)}, u32[]{:S(2)}, u32[]{:S(2)}) collective-permute-start(bf16[1024,256]{1,0:T(8,128)(2,1)} %hold.2.refs_5_.refs_10_), channel_id=1, source_target_pairs={{4,0},{5,1},{6,2},{7,3},{0,4},{1,5},{2,6},{3,7},{12,8},{13,9},{14,... | collective-permute-start | bytes 1572872 | tf_op jit(solution)/shard_map/ppermute | solution.py:59
  48.9 13.6 %collective-permute-start.3 = (bf16[1024,256]{1,0:T(8,128)(2,1)}, bf16[1024,256]{1,0:T(8,128)(2,1)}, u32[]{:S(2)}, u32[]{:S(2)}) collective-permute-start(bf16[1024,256]{1,0:T(8,128)(2,1)} %hold.2.refs_5_.refs_10_), channel_id=1, source_target_pairs={{8,0},{9,1},{10,2},{11,3},{12,4},{13,5},{14,6},{15,7},{0,8},{1,9},... | collective-permute-start | bytes 1572872 | tf_op jit(solution)/shard_map/ppermute | solution.py:59
  48.9 1.6 copy-start.3
  50.5 1.6 copy-start.13
  52.1 1.6 copy-start.16
  53.7 1.6 copy-start.19
  55.3 1.0 copy-start.22
  56.3 1.0 copy-start.27
  57.4 1.0 copy-start.29
  58.4 4.1 %copy-start.6 = (bf16[8,1024,128]{2,1,0:T(8,128)(2,1)S(1)}, bf16[8,1024,128]{2,1,0:T(8,128)(2,1)}, u32[]{:S(2)}) copy-start(bf16[8,1024,128]{2,1,0:T(8,128)(2,1)} %copy-done.5) | copy-start | bytes 6291460
  58.4 4.1 %copy-start.8 = (bf16[8,1024,128]{2,1,0:T(8,128)(2,1)S(1)}, bf16[8,1024,128]{2,1,0:T(8,128)(2,1)}, u32[]{:S(2)}) copy-start(bf16[8,1024,128]{2,1,0:T(8,128)(2,1)} %get-tuple-element.23.refs_1_.adj_ref) | copy-start | bytes 6291460
  58.4 4.1 %copy-start.10 = (bf16[8,1024,128]{2,1,0:T(8,128)(2,1)S(1)}, bf16[8,1024,128]{2,1,0:T(8,128)(2,1)}, u32[]{:S(2)}) copy-start(bf16[8,1024,128]{2,1,0:T(8,128)(2,1)} %get-tuple-element.24.refs_2_.adj_ref) | copy-start | bytes 6291460
  62.5 11.8 %copy-start.37 = (s32[1024]{0:T(1024)S(1)}, s32[1024]{0:T(1024)}, u32[]{:S(2)}) copy-start(s32[1024]{0:T(1024)} %param.14) | copy-start | bytes 12292
  62.5 12.1 %copy-start.38 = (s32[1024]{0:T(1024)S(1)}, s32[1024]{0:T(1024)}, u32[]{:S(2)}) copy-start(s32[1024]{0:T(1024)} %param.15) | copy-start | bytes 12292
  65.6 15.1 %copy-start.34 = (bf16[256,256]{1,0:T(8,128)(2,1)S(1)}, bf16[256,256]{1,0:T(8,128)(2,1)}, u32[]{:S(2)}) copy-start(bf16[256,256]{1,0:T(8,128)(2,1)} %ws_ref.1) | copy-start | bytes 393220
  65.6 15.1 %copy-start.36 = (f32[256]{0:T(256)S(1)}, f32[256]{0:T(256)}, u32[]{:S(2)}) copy-start(f32[256]{0:T(256)} %param.19) | copy-start | bytes 3076
  65.6 3.9 %collective-permute-start.8 = (bf16[2,256,256]{2,1,0:T(8,128)(2,1)S(1)}, bf16[2,256,256]{2,1,0:T(8,128)(2,1)S(1)}, u32[]{:S(2)}, u32[]{:S(2)}) collective-permute-start(bf16[2,256,256]{2,1,0:T(8,128)(2,1)S(1)} %get-tuple-element.31), channel_id=1, source_target_pairs={{0,1},{1,0},{2,3},{3,2},{4,5},{5,4},{6,7},{7,6},{8,9},{9,8},{10,11... | collective-permute-start | bytes 786440 | tf_op jit(solution)/shard_map/ppermute | solution.py:59
  69.6 11.1 %collective-permute-start.9 = (bf16[2,256,256]{2,1,0:T(8,128)(2,1)S(1)}, bf16[2,256,256]{2,1,0:T(8,128)(2,1)S(1)}, u32[]{:S(2)}, u32[]{:S(2)}) collective-permute-start(bf16[2,256,256]{2,1,0:T(8,128)(2,1)S(1)} %add_convert_fusion.own_ref), channel_id=1, source_target_pairs={{0,2},{1,3},{2,0},{3,1},{4,6},{5,7},{6,4},{7,5},{8,10},{9,11},{10,... | collective-permute-start | bytes 786440 | tf_op jit(solution)/shard_map/ppermute | solution.py:59
  75.7 13.4 %copy-start.11 = (bf16[8,1024,128]{2,1,0:T(8,128)(2,1)S(1)}, bf16[8,1024,128]{2,1,0:T(8,128)(2,1)}, u32[]{:S(2)}) copy-start(bf16[8,1024,128]{2,1,0:T(8,128)(2,1)} %get-tuple-element.24.refs_2_.adj_ref) | copy-start | bytes 6291460
  80.8 1.0 copy-start.25
  81.8 1.0 copy-start.30
  82.8 1.0 copy-start.31
  83.9 0.9 copy-start.35
  86.3 1.7 copy-start.32
  86.3 7.5 %copy-start.20 = (bf16[8,1024,128]{2,1,0:T(8,128)(2,1)S(1)}, bf16[8,1024,128]{2,1,0:T(8,128)(2,1)}, u32[]{:S(2)}) copy-start(bf16[8,1024,128]{2,1,0:T(8,128)(2,1)} %copy-done.18) | copy-start | bytes 6291460
  86.3 1.7 collective-permute-start.22
  87.2 16.6 %collective-permute-start.21 = (f32[128,256]{1,0:T(8,128)S(1)}, f32[128,256]{1,0:T(8,128)S(1)}, u32[]{:S(2)}, u32[]{:S(2)}) collective-permute-start(f32[128,256]{1,0:T(8,128)S(1)} %dynamic-slice_bitcast_fusion.1), channel_id=1, source_target_pairs={{0,1},{1,0},{2,3},{3,2},{4,5},{5,4},{6,7},{7,6},{8,9},{9,8},{10,11... | collective-permute-start | bytes 393224 | tf_op jit(solution)/shard_map/ppermute | solution.py:59
  87.3 1.7 collective-permute-start.10
  90.6 4.8 %copy-start.9 = (bf16[8,1024,128]{2,1,0:T(8,128)(2,1)S(1)}, bf16[8,1024,128]{2,1,0:T(8,128)(2,1)}, u32[]{:S(2)}) copy-start(bf16[8,1024,128]{2,1,0:T(8,128)(2,1)} %get-tuple-element.23.refs_1_.adj_ref) | copy-start | bytes 6291460
  90.6 50.6 %collective-permute-start.17 = (bf16[8,256,128]{2,1,0:T(8,128)(2,1)}, bf16[8,256,128]{2,1,0:T(8,128)(2,1)}, u32[]{:S(2)}, u32[]{:S(2)}) collective-permute-start(bf16[8,256,128]{2,1,0:T(8,128)(2,1)} %backward_product.14), channel_id=1, source_target_pairs={{0,120},{1,121},{2,122},{3,123},{4,124},{5,125},{6,126},{7,127},{8... | collective-permute-start | bytes 1572872 | tf_op jit(solution)/shard_map/ppermute | solution.py:59
  95.4 1.9 %copy-start.7 = (bf16[8,1024,128]{2,1,0:T(8,128)(2,1)S(1)}, bf16[8,1024,128]{2,1,0:T(8,128)(2,1)}, u32[]{:S(2)}) copy-start(bf16[8,1024,128]{2,1,0:T(8,128)(2,1)} %copy-done.5) | copy-start | bytes 6291460
  95.4 50.2 %collective-permute-start.12 = (bf16[8,256,128]{2,1,0:T(8,128)(2,1)}, bf16[8,256,128]{2,1,0:T(8,128)(2,1)S(1)}, u32[]{:S(2)}, u32[]{:S(2)}) collective-permute-start(bf16[8,256,128]{2,1,0:T(8,128)(2,1)} %backward_product.9), channel_id=1, source_target_pairs={{0,102},{1,69},{2,36},{3,7},{4,0},{5,99},{6,66},{7,33},{8,110},{9,... | collective-permute-start | bytes 1572872 | tf_op jit(solution)/shard_map/ppermute | solution.py:59
  96.9 5.3 %copy-start.17 = (bf16[8,1024,128]{2,1,0:T(8,128)(2,1)S(1)}, bf16[8,1024,128]{2,1,0:T(8,128)(2,1)}, u32[]{:S(2)}) copy-start(bf16[8,1024,128]{2,1,0:T(8,128)(2,1)} %copy-done.15) | copy-start | bytes 6291460
  96.9 53.6 %collective-permute-start.15 = (bf16[8,256,128]{2,1,0:T(8,128)(2,1)}, bf16[8,256,128]{2,1,0:T(8,128)(2,1)}, u32[]{:S(2)}, u32[]{:S(2)}) collective-permute-start(bf16[8,256,128]{2,1,0:T(8,128)(2,1)} %backward_product.12), channel_id=1, source_target_pairs={{0,8},{1,9},{2,10},{3,11},{4,12},{5,13},{6,14},{7,15},{8,0},{9,1},... | collective-permute-start | bytes 1572872 | tf_op jit(solution)/shard_map/ppermute | solution.py:59
  98.8 51.7 %collective-permute-start.14 = (bf16[8,256,128]{2,1,0:T(8,128)(2,1)}, bf16[8,256,128]{2,1,0:T(8,128)(2,1)}, u32[]{:S(2)}, u32[]{:S(2)}) collective-permute-start(bf16[8,256,128]{2,1,0:T(8,128)(2,1)} %backward_product.11), channel_id=1, source_target_pairs={{0,4},{1,5},{2,6},{3,7},{4,0},{5,1},{6,2},{7,3},{8,12},{9,13},{10,... | collective-permute-start | bytes 1572872 | tf_op jit(solution)/shard_map/ppermute | solution.py:59
  103.8 46.8 %collective-permute-start.11 = (bf16[8,256,128]{2,1,0:T(8,128)(2,1)}, bf16[8,256,128]{2,1,0:T(8,128)(2,1)}, u32[]{:S(2)}, u32[]{:S(2)}) collective-permute-start(bf16[8,256,128]{2,1,0:T(8,128)(2,1)} %backward_product.8), channel_id=1, source_target_pairs={{0,104},{1,73},{2,42},{3,11},{4,108},{5,77},{6,46},{7,15},{8,0},{9... | collective-permute-start | bytes 1572872 | tf_op jit(solution)/shard_map/ppermute | solution.py:59
  126.9 28.4 %all-to-all-start.1 = ((f32[32,4,256]{2,1,0:T(4,128)}), f32[32,4,256]{2,1,0:T(4,128)S(1)}, u32[]{:S(2)}, u32[]{:S(2)}) async-start(f32[32,4,256]{2,1,0:T(4,128)} %broadcast_in_dim.11), calls=%async_computation.1 | async-start | bytes 262144 | tf_op jit(solution)/shard_map/all_to_all | solution.py:342
  138.0 1.6 copy-start.14
  139.6 5.9 %copy-start.4 = (bf16[8,1024,128]{2,1,0:T(8,128)(2,1)S(1)}, bf16[8,1024,128]{2,1,0:T(8,128)(2,1)}, u32[]{:S(2)}) copy-start(bf16[8,1024,128]{2,1,0:T(8,128)(2,1)} %copy-done.2) | copy-start | bytes 6291460
  141.2 25.9 %collective-permute-start.13 = (bf16[8,256,128]{2,1,0:T(8,128)(2,1)}, bf16[8,256,128]{2,1,0:T(8,128)(2,1)}, u32[]{:S(2)}, u32[]{:S(2)}) collective-permute-start(bf16[8,256,128]{2,1,0:T(8,128)(2,1)} %backward_product.10), channel_id=1, source_target_pairs={{0,0},{1,97},{2,66},{3,35},{4,4},{5,101},{6,70},{7,39},{8,8},{9,10... | collective-permute-start | bytes 1572872 | tf_op jit(solution)/shard_map/ppermute | solution.py:59
  148.1 19.0 %collective-permute-start.18 = (bf16[8,256,128]{2,1,0:T(8,128)(2,1)}, bf16[8,256,128]{2,1,0:T(8,128)(2,1)}, u32[]{:S(2)}, u32[]{:S(2)}) collective-permute-start(bf16[8,256,128]{2,1,0:T(8,128)(2,1)} %backward_product.15), channel_id=1, source_target_pairs={{0,110},{1,79},{2,44},{3,13},{4,106},{5,73},{6,40},{7,11},{8,4},{9... | collective-permute-start | bytes 1572872 | tf_op jit(solution)/shard_map/ppermute | solution.py:59
  153.3 15.3 %collective-permute-start.16 = (bf16[8,256,128]{2,1,0:T(8,128)(2,1)}, bf16[8,256,128]{2,1,0:T(8,128)(2,1)S(1)}, u32[]{:S(2)}, u32[]{:S(2)}) collective-permute-start(bf16[8,256,128]{2,1,0:T(8,128)(2,1)} %backward_product.13), channel_id=1, source_target_pairs={{0,120},{1,89},{2,58},{3,27},{4,124},{5,93},{6,62},{7,31},{8,112},... | collective-permute-start | bytes 1572872 | tf_op jit(solution)/shard_map/ppermute | solution.py:59
  155.4 6.6 %collective-permute-start.23 = (f32[128,256]{1,0:T(8,128)S(1)}, f32[128,256]{1,0:T(8,128)S(1)}, u32[]{:S(2)}, u32[]{:S(2)}) collective-permute-start(f32[128,256]{1,0:T(8,128)S(1)} %reshape.51), channel_id=1, source_target_pairs={{0,2},{1,3},{2,0},{3,1},{4,6},{5,7},{6,4},{7,5},{8,10},{9,11},{10,... | collective-permute-start | bytes 393224 | tf_op jit(solution)/shard_map/ppermute | solution.py:59
  162.1 17.1 %collective-permute-start.24 = (f32[2,128,256]{2,1,0:T(8,128)S(1)}, f32[2,128,256]{2,1,0:T(8,128)S(1)}, u32[]{:S(2)}, u32[]{:S(2)}) collective-permute-start(f32[2,128,256]{2,1,0:T(8,128)S(1)} %maximum_select_fusion), channel_id=1, source_target_pairs={{0,1},{1,0},{2,3},{3,2},{4,5},{5,4},{6,7},{7,6},{8,9},{9,8},{10,11... | collective-permute-start | bytes 786440 | tf_op jit(solution)/shard_map/ppermute | solution.py:59
  170.3 10.1 %collective-permute-start.19 = (bf16[2,2,256,128]{3,2,1,0:T(8,128)(2,1)S(1)}, bf16[2,2,256,128]{3,2,1,0:T(8,128)(2,1)S(1)}, u32[]{:S(2)}, u32[]{:S(2)}) collective-permute-start(bf16[2,2,256,128]{3,2,1,0:T(8,128)(2,1)S(1)} %get-tuple-element.35), channel_id=1, source_target_pairs={{0,1},{1,0},{2,3},{3,2},{4,5},{5,4},{6,7},{7,6},{8,9},{9,8},{10,11... | collective-permute-start | bytes 786440 | tf_op jit(solution)/shard_map/ppermute | solution.py:59
  179.3 11.8 %copy-start.33 = (f32[256,256]{1,0:T(8,128)S(1)}, f32[256,256]{1,0:T(8,128)}, u32[]{:S(2)}) copy-start(f32[256,256]{1,0:T(8,128)} %copy-done.32) | copy-start | bytes 786436
  180.5 10.6 %collective-permute-start.20 = (bf16[2,256,128]{2,1,0:T(8,128)(2,1)S(1)}, bf16[2,256,128]{2,1,0:T(8,128)(2,1)S(1)}, u32[]{:S(2)}, u32[]{:S(2)}) collective-permute-start(bf16[2,256,128]{2,1,0:T(8,128)(2,1)S(1)} %fusion), channel_id=1, source_target_pairs={{0,2},{1,3},{2,0},{3,1},{4,6},{5,7},{6,4},{7,5},{8,10},{9,11},{10,... | collective-permute-start | bytes 393224 | tf_op jit(solution)/shard_map/ppermute | solution.py:59
  (1 other events, 0.8 us)

commit v6 on v5

v6 whole, which is shorter than its diff:
```python
import functools

import jax
import jax.numpy as jnp
from jax import lax
from jax.experimental import pallas as pl
from jax.experimental.pallas import tpu as pltpu
from jax.sharding import PartitionSpec as P

AXES = ("blk", "rep")
NB = 8
ND = 8
NS = 6
BS = 128
F = 256
VMEM = 50 * 1024 * 1024
SMALL = 16 * 1024 * 1024
PLAN = {6: None, 3: None, 1: None, 2: None, 0: None, 7: 1, 4: 2, 5: 6}
CROSS = {1: 0x7666, 3: 0x5FDB}
BACK_PLAN = {6: None, 2: None, 1: None, 0: None, 3: 1, 7: 1, 4: 2, 5: 2}
BACK_CROSS = {1: 0xAAAA}
GROUPS = ((6, 3, 1, 2, 0), (7, 4, 5))
HELD = ((6, (1,)), (3, (2, 0)))
BACK = ((5, 3, 4), (1, 0), (7,), (2,), (6,))
LATER = (7, 1)


def index_of(y, x, zl, zh, core):
    return (((y % 4 * 4 + x % 4) * 2 + zl) * 2 + zh) * 2 + core


def places():
    for t in range(128):
        yield t, t >> 5, t >> 3 & 3, t >> 2 & 1, t >> 1 & 1, t & 1


def column_pairs(k, plan, cross):
    via = plan[k]
    out = []
    for t, y, x, zl, zh, core in places():
        j, r = x * 2 + zl, 2 * zh + core
        jj = j ^ k
        if via is None:
            flip = cross[k] >> (jj * 2 + core) & 1 if k & 1 else 0
            out.append((index_of(y - r - (jj > j), jj >> 1, jj & 1, zh ^ flip, core), t))
        else:
            jn = j ^ via
            out.append((index_of(y - (jj > j) + (jj > jn), jn >> 1, jn & 1, zh, core), t))
    return out


def flip_pairs(dy=0, dx=0, dzl=0, dzh=0, dcore=0):
    return [
        (t, index_of(y ^ dy, x ^ dx, zl ^ dzl, zh ^ dzh, core ^ dcore))
        for t, y, x, zl, zh, core in places()
    ]


def send(value, pairs):
    return lax.ppermute(value, AXES, pairs)


def params(limit=VMEM):
    return pltpu.CompilerParams(vmem_limit_bytes=limit)


SMEM = pl.BlockSpec(memory_space=pltpu.SMEM)
HBM = pl.BlockSpec(memory_space=pltpu.HBM)
UNREAD = pl.BlockSpec(memory_space=pl.ANY)
WHOLE = pl.BlockSpec(memory_space=pltpu.VMEM)


def matmul_cost(n):
    return pl.CostEstimate(
        flops=2 * NB * NB * BS * BS * F * n, bytes_accessed=(3 << 20) * n, transcendentals=0
    )


def assemble_body(n, sel_ref, cols_ref, counts_ref, tiles_ref, out_ref, held_ref, made_ref, sems):
    def fetch(k):
        dist, slot = sel_ref[k], k % 2
        return pltpu.make_async_copy(tiles_ref.at[:, dist], held_ref.at[slot], sems.at[0, slot])

    def store(k):
        return pltpu.make_async_copy(made_ref.at[k % 2], out_ref.at[k], sems.at[1, k % 2])

    fetch(0).start()
    for k in range(n):
        fetch(k).wait()
        if k + 1 < n:
            fetch(k + 1).start()
        if k > 1:
            store(k - 2).wait()
        dist, slot = sel_ref[k], k % 2

        def block_row(b, carry):
            count = counts_ref[b * ND + dist]
            rows = pl.ds(pl.multiple_of(b * BS, BS), BS)
            cols = [cols_ref[(b * ND + dist) * NS + s] for s in range(NS)]
            cols = [jnp.where(s < count, cols[s], NB) for s in range(NS)]
            tiles = [held_ref[slot, b, s] for s in range(NS)]
            zero = jnp.zeros((BS, BS), jnp.bfloat16)
            for c in range(NB):
                parts = [jnp.where(cols[s] == c, tiles[s], zero) for s in range(NS)]
                pairs = [parts[s] + parts[s + 1] for s in range(0, NS, 2)]
                made_ref[slot, c, rows, :] = pairs[0] + pairs[1] + pairs[2]
            return carry

        lax.fori_loop(0, NB, block_row, 0)
        store(k).start()
    store(n - 2).wait()
    store(n - 1).wait()


def assemble_call(sel, cols, counts, tiles):
    n = sel.shape[0]
    return pl.pallas_call(
        functools.partial(assemble_body, n),
        out_shape=jax.ShapeDtypeStruct((n, NB, NB * BS, BS), jnp.bfloat16),
        in_specs=[SMEM] * 3 + [HBM],
        out_specs=HBM,
        scratch_shapes=[
            pltpu.VMEM((2, NB, NS, BS, BS), jnp.bfloat16),
            pltpu.VMEM((2, NB, NB * BS, BS), jnp.bfloat16),
            pltpu.SemaphoreType.DMA((2, 2)),
        ],
        compiler_params=params(),
        cost_estimate=matmul_cost(n),
        name="assemble_adjacency",
    )(sel, cols, counts, tiles)


def copies_of(adj_ref, places, held_ref, sems):
    copies = [
        pltpu.make_async_copy(adj_ref.at[place], held_ref.at[k], sems.at[k])
        for k, place in enumerate(places)
    ]
    for copy in copies:
        copy.start()
    return copies


def copy_scratch(n):
    return [
        pltpu.VMEM((n, NB, NB * BS, BS), jnp.bfloat16),
        pltpu.SemaphoreType.DMA((n,)),
    ]


def wide(ref, k):
    return jnp.concatenate([ref[k, c] for c in range(NB)], 1)


def forward_body(n, start, first, last, core_ref, adj_ref, *refs):
    shards, rest = refs[:n], refs[n:]
    total_ref, held_ref, sems = rest[-3:]
    outs = rest[-5:-3] if last else rest[-4:-3]
    copies = copies_of(adj_ref, range(start, start + n), held_ref, sems)
    for k in range(n):
        copies[k].wait()
        product = jnp.dot(wide(held_ref, k), shards[k][...], preferred_element_type=jnp.float32)
        if k > 0:
            total_ref[...] += product
        else:
            total_ref[...] = product if first else rest[0][...] + product
    if last:
        core = core_ref[0]
        for part in range(2):
            keep = pl.multiple_of((part * 2 + core) * 256, 256)
            away = pl.multiple_of((part * 2 + 1 - core) * 256, 256)
            outs[0][part] = total_ref[pl.ds(keep, 256), :]
            outs[1][part] = total_ref[pl.ds(away, 256), :].astype(jnp.bfloat16)
    else:
        outs[0][...] = total_ref[...]


def forward_call(core, adjacency, start, shards, before, last, after):
    n, first = len(shards), before is None
    if last:
        out_shape = (
            jax.ShapeDtypeStruct((2, 256, F), jnp.float32),
            jax.ShapeDtypeStruct((2, 256, F), jnp.bfloat16),
        )
    else:
        out_shape = (jax.ShapeDtypeStruct((NB * BS, F), jnp.float32),)
    return pl.pallas_call(
        functools.partial(forward_body, n, start, first, last),
        out_shape=out_shape,
        in_specs=[SMEM, HBM] + [WHOLE] * (n + (not first)) + [UNREAD] * len(after),
        out_specs=(WHOLE,) * len(out_shape),
        scratch_shapes=[pltpu.VMEM((NB * BS, F), jnp.float32)] + copy_scratch(n),
        compiler_params=params(),
        cost_estimate=matmul_cost(n),
        name="forward_product",
    )(core, adjacency, *shards, *([] if first else [before]), *after)


def dense_body(
    rep_ref, own_ref, got_ref, feat_ref, cot_ref, inv_ref, ws_ref, wn_ref, bias_ref,
    act_ref, term_ref, back_ref, grad_ref,
):
    zh = rep_ref[0] // 2
    nt = (((1,), (1,)), ((), ()))
    tn = (((0,), (0,)), ((), ()))
    grads = jnp.zeros((F, F), jnp.float32)
    sums = jnp.zeros((1, F), jnp.float32)
    for part in range(2):
        feat = feat_ref[part]
        inv = inv_ref[part]
        summed = own_ref[part].astype(jnp.float32) + got_ref[part].astype(jnp.float32)
        agg = (summed * jnp.broadcast_to(inv, (256, 256)).T).astype(jnp.bfloat16)
        pre = (
            jnp.dot(feat, ws_ref[...], preferred_element_type=jnp.float32)
            + jnp.dot(agg, wn_ref[...], preferred_element_type=jnp.float32)
            + bias_ref[...]
        )
        sigm = jax.nn.sigmoid(pre)
        act = (pre * sigm).astype(jnp.bfloat16)
        slope = sigm * (1.0 + pre * (1.0 - sigm))
        grad_pre = (cot_ref[part].astype(jnp.float32) * slope).astype(jnp.bfloat16)

        @pl.when(zh == part)
        def _():
            act_ref[...] = act
            term_ref[...] = lax.dot_general(
                grad_pre, ws_ref[...], nt, preferred_element_type=jnp.float32
            )

        back_t = lax.dot_general(wn_ref[...], grad_pre, nt, preferred_element_type=jnp.float32)
        back_ref[part] = (back_t * inv).astype(jnp.bfloat16)
        left = jnp.where(zh == 0, feat, agg)
        grads += lax.dot_general(left, grad_pre, tn, preferred_element_type=jnp.float32)
        sums += jnp.sum(grad_pre.astype(jnp.float32), axis=0, keepdims=True)
    grad_ref[:F, :] = grads
    grad_ref[F:, :] = jnp.broadcast_to(sums, (8, F))


def dense_call(rep, own, got, feat, cot, inv, w_self, w_neigh, bias):
    return pl.pallas_call(
        dense_body,
        out_shape=(
            jax.ShapeDtypeStruct((256, F), jnp.bfloat16),
            jax.ShapeDtypeStruct((256, F), jnp.float32),
            jax.ShapeDtypeStruct((2, F, 256), jnp.bfloat16),
            jax.ShapeDtypeStruct((F + 8, F), jnp.float32),
        ),
        in_specs=[SMEM] + [WHOLE] * 8,
        out_specs=(WHOLE,) * 4,
        compiler_params=params(SMALL),
        name="dense_rows",
    )(rep, own, got, feat, cot, inv, w_self, w_neigh, bias)


def backward_body(places, added, core_ref, adj_ref, own_ref, got_ref, *rest):
    n = len(places)
    held_ref, sems = rest[-2:]
    outs = rest[-2 - n : -2]
    copies = copies_of(adj_ref, places, held_ref, sems)
    core = core_ref[0]
    message = []
    for quarter in range(4):
        mine = core == quarter % 2
        message.append(jnp.where(mine, own_ref[quarter // 2], got_ref[quarter // 2]))
    message = jnp.concatenate(message, 1)
    for k in range(n):
        copies[k].wait()
        product = jnp.dot(message, wide(held_ref, k), preferred_element_type=jnp.float32)
        for c in range(NB):
            part = product[:, c * BS : (c + 1) * BS]
            for ref in rest[:added]:
                part += ref[c].astype(jnp.float32)
            outs[k][c] = part.astype(jnp.bfloat16)


def backward_call(core, adjacency, places, own, got, extra, after):
    n, added = len(places), len(extra)
    return pl.pallas_call(
        functools.partial(backward_body, tuple(places), added),
        out_shape=(jax.ShapeDtypeStruct((NB, F, BS), jnp.bfloat16),) * n,
        in_specs=[SMEM, HBM] + [WHOLE] * (2 + added) + [UNREAD] * len(after),
        out_specs=(WHOLE,) * n,
        scratch_shapes=copy_scratch(n),
        compiler_params=params(),
        cost_estimate=matmul_cost(n),
        name="backward_product",
    )(core, adjacency, own, got, *extra, *after)


def split_body(core_ref, *rest):
    arrived, (keep_ref, away_ref) = rest[:-2], rest[-2:]
    core = core_ref[0]
    for part in range(2):
        for c in range(2):
            keep = (part * 2 + core) * 2 + c
            away = (part * 2 + 1 - core) * 2 + c
            kept = arrived[0][keep].astype(jnp.float32)
            sent = arrived[0][away].astype(jnp.float32)
            for ref in arrived[1:]:
                kept += ref[keep].astype(jnp.float32)
                sent += ref[away].astype(jnp.float32)
            keep_ref[part, c] = kept
            away_ref[part, c] = sent.astype(jnp.bfloat16)


def split_call(core, arrived):
    return pl.pallas_call(
        split_body,
        out_shape=(
            jax.ShapeDtypeStruct((2, 2, F, BS), jnp.float32),
            jax.ShapeDtypeStruct((2, 2, F, BS), jnp.bfloat16),
        ),
        in_specs=[SMEM] + [WHOLE] * len(arrived),
        out_specs=(WHOLE, WHOLE),
        compiler_params=params(SMALL),
        name="split_products",
    )(core, *arrived)


def hold_body(*refs):
    pass


def hold_call(along, after):
    return pl.pallas_call(
        hold_body,
        out_shape=jax.ShapeDtypeStruct(along.shape, along.dtype),
        in_specs=[UNREAD] * (1 + len(after)),
        out_specs=UNREAD,
        input_output_aliases={0: 0},
        name="hold",
    )(along, *after)


def final_body(kept_ref, got_ref, term_ref, out_ref):
    for c in range(2):
        spread = kept_ref[c] + got_ref[c].astype(jnp.float32)
        rows = slice(c * BS, (c + 1) * BS)
        out_ref[rows, :] = (term_ref[rows, :] + spread.T).astype(jnp.bfloat16)


def final_call(kept, got, term):
    return pl.pallas_call(
        final_body,
        out_shape=jax.ShapeDtypeStruct((256, F), jnp.bfloat16),
        compiler_params=params(SMALL),
        name="final_rows",
    )(kept, got, term)


def pick(pair, index):
    return lax.dynamic_index_in_dim(pair, index, 0, keepdims=False)


def weight_shares(grads, core):
    halves, sums = grads[:F].reshape(2, F // 2, F), grads[F:]
    away = jnp.concatenate([pick(halves, 1 - core), sums], 0)
    mine = jnp.concatenate([pick(halves, core), sums], 0) + send(away, flip_pairs(dcore=1))
    count = lax.axis_size("blk")
    bias = mine[F // 2 : F // 2 + 1]
    high = bias.astype(jnp.bfloat16)
    low = (bias - high.astype(jnp.float32)).astype(jnp.bfloat16)
    bias_rows = jnp.broadcast_to(jnp.concatenate([high, low], 0)[None], (count, 2, F))
    rows = mine[: F // 2].astype(jnp.bfloat16).reshape(count, F // 2 // count, F)
    return lax.all_to_all(jnp.concatenate([rows, bias_rows], 1), "blk", 0, 0)


def weight_grads(parts, zh, core, nodes):
    count, share = parts.shape[0], parts.shape[1] - 2
    total = jnp.sum(parts.astype(jnp.float32), axis=0)
    bias = total[share] + total[share + 1]
    spread = jnp.broadcast_to(total[None, :share], (count, share, F))
    half = lax.all_to_all(spread, "blk", 0, 0).reshape(F // 2, F)
    other = send(half, flip_pairs(dzh=1))
    both = jnp.where(zh == 0, jnp.stack([half, other]), jnp.stack([other, half]))
    across = send(both, flip_pairs(dcore=1))
    low, top = jnp.where(core == 0, both, across), jnp.where(core == 0, across, both)
    norm = 1.0 / jnp.sqrt(jnp.float32(nodes))
    whole = jnp.concatenate([low, top], 1) * norm
    return whole[0], whole[1], bias * norm


def shards(
    features, tiles, tile_cols, counts, degree, train_mask, cotangent, w_self, w_neigh, bias_term
):
    rows = features.shape[0]
    rep = lax.axis_index("rep").astype(jnp.int32)
    zh, core = rep // 2, rep % 2
    place = (lax.axis_index("blk") % 8).astype(jnp.int32)
    cols = tile_cols.reshape(-1)
    live = counts.reshape(-1)

    def distance_of(k):
        return (place - (place ^ k)) % 8

    def own_rows(value):
        value = value.reshape((2, 2, rows // 4) + value.shape[1:])
        return lax.dynamic_index_in_dim(value, core, 1, keepdims=False)

    inv = own_rows(1.0 / degree.astype(jnp.float32))[:, None, :]
    feat = own_rows(features)
    cot = own_rows(cotangent) * own_rows(train_mask).astype(jnp.bfloat16)[:, :, None]
    bias = bias_term.reshape(1, F)

    order = list(PLAN)
    sel = jnp.stack([distance_of(k) for k in order])
    adjacency = assemble_call(sel, cols, live, tiles)
    blocks, held = {}, []
    for k, via in PLAN.items():
        if via is None:
            blocks[k] = send(features, column_pairs(k, PLAN, CROSS))
    for k, after in HELD:
        blocks[k] = hold_call(blocks[k], [adjacency] + [blocks[a] for a in after])
        held.append(blocks[k])
    for k, via in PLAN.items():
        if via is not None:
            blocks[k] = send(blocks[k ^ via], column_pairs(k, PLAN, CROSS))
    made = (None,)
    for group in GROUPS:
        made = forward_call(
            core[None],
            adjacency,
            order.index(group[0]),
            [blocks[k] for k in group],
            made[0],
            group is GROUPS[-1],
            held if group is GROUPS[0] else [],
        )

    kept, away = made
    chip = (kept + send(away, flip_pairs(dcore=1)).astype(jnp.float32)).astype(jnp.bfloat16)
    other = send(chip, flip_pairs(dzh=1))

    activation, own_term, back_own, grads = dense_call(
        rep[None], chip, other, feat, cot, inv, w_self, w_neigh, bias
    )
    back_got = send(back_own, flip_pairs(dcore=1))

    parts = weight_shares(grads, core)
    arrived, extra = {}, {}
    for group in BACK:
        made = backward_call(
            core[None],
            adjacency,
            [order.index(k) for k in group],
            back_own,
            back_got,
            extra.get(group[0], []),
            [parts] if group[0] in LATER else [],
        )
        for k, product in zip(group, made):
            pairs = column_pairs(k, BACK_PLAN, BACK_CROSS)
            moved = send(product, [(b, a) for a, b in pairs])
            if BACK_PLAN[k] is None:
                arrived[k] = moved
            else:
                extra.setdefault(k ^ BACK_PLAN[k], []).append(moved)
    kept, away = split_call(core[None], list(arrived.values()))
    chip = kept + send(away, flip_pairs(dcore=1)).astype(jnp.float32)
    got = send(pick(chip, 1 - zh).astype(jnp.bfloat16), flip_pairs(dzh=1))
    grad_features = final_call(pick(chip, zh), got, own_term)
    grad_self, grad_neigh, grad_bias = weight_grads(
        parts, zh, core, rows * lax.axis_size("blk")
    )
    return (activation, grad_features, grad_self, grad_neigh, grad_bias)


def solution(mesh):
    return jax.shard_map(
        shards,
        mesh=mesh,
        in_specs=(
            P("blk", None),
            P("blk", "rep", None, None, None),
            P("blk", "rep", None),
            P("blk", "rep"),
            P("blk"),
            P("blk"),
            P("blk", None),
            P(),
            P(),
            P(),
        ),
        out_specs=(P(("blk", "rep"), None), P(("blk", "rep"), None), P(), P(), P()),
        check_vma=False,
    )
```

time: 193 us -> 178 us (0.922); the launches traced: 192 us -> 175 us
  waiting for transfers between devices: 19.3 us -> 40 us
  blocking collectives: 20.3 us -> 0 us
  local copies, waits for them, and re-layouts: 29.8 us -> 10.8 us
  starting transfers between devices: 75.5 us -> 68.8 us
  Pallas kernels: 44.9 us -> 50.5 us
  other arithmetic: 0.94 us -> 3.66 us
    all_to_all x1 -> x0, blocking collectives: 20.3 us -> none  [weight_grads(): parts = lax.all_to_all(jnp.concatenate([rows, bias_rows], 1), 'blk', 0, 0)]
    unnamed x79 -> x38, local copies, waits for them, and re-layouts: 25.9 us -> 8.06 us
    ppermute x25 -> x24, waiting for transfers between devices: 19.3 us -> 32.2 us  [send(): return lax.ppermute(value, AXES, pairs)]
    all_to_all x0 -> x1, waiting for transfers between devices: none -> 7.82 us  [weight_shares(): return lax.all_to_all(jnp.concatenate([rows, bias_rows], 1), 'blk', 0, 0)]
    pallas_call x11 -> x8, Pallas kernels: 40.9 us -> 47.9 us  [the longest x1 19.2 us: assemble_call(): pl.pallas_call(functools.partial(assemble_body, n), out_shape=jax.ShapeDt...]
    ppermute x25 -> x24, starting transfers between devices: 64.4 us -> 58.5 us  [send(): return lax.ppermute(value, AXES, pairs)]
    all_to_all x1, starting transfers between devices: 11.1 us -> 6.35 us  [weight_grads(): half = lax.all_to_all(spread, 'blk', 0, 0).reshape(F // 2, F)]
    all_to_all x0 -> x1, starting transfers between devices: none -> 3.86 us  [weight_shares(): return lax.all_to_all(jnp.concatenate([rows, bias_rows], 1), 'blk', 0, 0)]
  transfers between devices with their start and end apart: 26 -> 26, of which waited for: 8 -> 12; matrix products, arithmetic and copies ran while one was open for 3% -> 4% of each run, Pallas kernels for 21% -> 22%
where the time goes in v6:
time: 178 us; the launch traced here: 175 us
  starting transfers between devices  68.8 us (39%)
  Pallas kernels  50.5 us (28%)
  waiting for transfers between devices  40 us (22%)
  local copies, waits for them, and re-layouts  10.8 us (6%)
  other arithmetic  3.66 us (2%)
    ppermute x24, starting transfers between devices, send(): return lax.ppermute(value, AXES, pairs)  58.5 us
    ppermute x24, waiting for transfers between devices, send(): return lax.ppermute(value, AXES, pairs)  32.2 us
    pallas_call x1, Pallas kernels, assemble_call(): pl.pallas_call(functools.partial(assemble_body, n), out_shape=jax.ShapeDt...  19.2 us
    pallas_call x5, Pallas kernels, backward_call(): pl.pallas_call(functools.partial(backward_body, tuple(places), added), ou...  17 us
    pallas_call x2, Pallas kernels, forward_call(): pl.pallas_call(functools.partial(forward_body, n, start, first, last), ou...  11.7 us
    unnamed x38, local copies, waits for them, and re-layouts  8.06 us
    all_to_all x1, waiting for transfers between devices, weight_shares(): return lax.all_to_all(jnp.concatenate([rows, bias_rows], 1), 'blk', 0, 0)  7.82 us
    all_to_all x1, starting transfers between devices, weight_grads(): half = lax.all_to_all(spread, 'blk', 0, 0).reshape(F // 2, F)  6.35 us
  transfers between devices with their start and end apart: 26, of which 12 were waited for; matrix products, arithmetic and copies ran while one was open for 4% of the time, Pallas kernels for 22%

profile of v6, /device:TPU:1, one launch (start us, length us, event | category | flops | bytes accessed | tf_op | source)
XLA Modules:
  0.0 174.9 jit_solution(14863849754475967550)
XLA Ops:
  0.6 3.1 %collective-permute-start.5 = (bf16[1024,256]{1,0:T(8,128)(2,1)}, bf16[1024,256]{1,0:T(8,128)(2,1)S(1)}, u32[]{:S(2)}, u32[]{:S(2)}) collective-permute-start(bf16[1024,256]{1,0:T(8,128)(2,1)} %param.10), channel_id=1, source_target_pairs={{104,0},{73,1},{42,2},{11,3},{108,4},{77,5},{46,6},{15,7},{0,8},{9... | collective-permute-start | bytes 1572872 | tf_op jit(solution)/shard_map/ppermute | solution.py:60
  3.8 3.2 %collective-permute-start.6 = (bf16[1024,256]{1,0:T(8,128)(2,1)}, bf16[1024,256]{1,0:T(8,128)(2,1)S(1)}, u32[]{:S(2)}, u32[]{:S(2)}) collective-permute-start(bf16[1024,256]{1,0:T(8,128)(2,1)} %param.10), channel_id=1, source_target_pairs={{0,0},{97,1},{66,2},{35,3},{4,4},{101,5},{70,6},{39,7},{8,8},{105,... | collective-permute-start | bytes 1572872 | tf_op jit(solution)/shard_map/ppermute | solution.py:60
  7.0 4.4 %collective-permute-start.4 = (bf16[1024,256]{1,0:T(8,128)(2,1)}, bf16[1024,256]{1,0:T(8,128)(2,1)S(1)}, u32[]{:S(2)}, u32[]{:S(2)}) collective-permute-start(bf16[1024,256]{1,0:T(8,128)(2,1)} %param.10), channel_id=1, source_target_pairs={{110,0},{79,1},{44,2},{13,3},{106,4},{73,5},{40,6},{11,7},{4,8},{1... | collective-permute-start | bytes 1572872 | tf_op jit(solution)/shard_map/ppermute | solution.py:60
  11.4 1.1 collective-permute-start.1
  12.5 2.4 %collective-permute-start = (bf16[1024,256]{1,0:T(8,128)(2,1)}, bf16[1024,256]{1,0:T(8,128)(2,1)S(1)}, u32[]{:S(2)}, u32[]{:S(2)}) collective-permute-start(bf16[1024,256]{1,0:T(8,128)(2,1)} %param.10), channel_id=1, source_target_pairs={{120,0},{89,1},{58,2},{27,3},{124,4},{93,5},{62,6},{31,7},{112,8},... | collective-permute-start | bytes 1572872 | tf_op jit(solution)/shard_map/ppermute | solution.py:60
  14.9 0.9 copy.22
  15.7 0.1 reshape.52.cols_ref
  15.9 0.8 reshape.53.counts_ref
  16.6 0.1 stack.42.sel_ref
  16.7 19.2 %assemble_adjacency.1.refs_1_.adj_ref = bf16[8,8,1024,128]{3,2,1,0:T(8,128)(2,1)} custom-call(s32[8]{0:T(128)S(1)} %stack.42.sel_ref, s32[384]{0:T(512)S(1)} %reshape.52.cols_ref, s32[64]{0:T(128)S(1)} %reshape.53.counts_ref, bf16[8,8,6,128,128]{4,3,2,1,0:T(8,128)(2,1)} %tiles_ref.1), custom_call_target="tpu_custom_call" | custom-call | flops 4294967296 | bytes 25165824 | tf_op jit(solution)/shard_map/assemble_adjacency/pallas_call | solution.py:117
  35.9 4.3 %collective-permute-done.6.refs_3_.refs_4_ = bf16[1024,256]{1,0:T(8,128)(2,1)S(1)} collective-permute-done((bf16[1024,256]{1,0:T(8,128)(2,1)}, bf16[1024,256]{1,0:T(8,128)(2,1)S(1)}, u32[]{:S(2)}, u32[]{:S(2)}) %collective-permute-start.6) | collective-permute-done | bytes 524320 | tf_op jit(solution)/shard_map/ppermute | solution.py:60
  40.3 0.8 copy-done.6
  41.1 0.8 copy-done.2
  41.9 0.8 copy-done.8
  42.7 0.8 copy-done
  43.5 1.1 copy-done.1
  44.6 1.0 copy-done.9
  45.7 7.0 %forward_product.2.refs_3_ = f32[1024,256]{1,0:T(8,128)S(1)} custom-call(s32[1]{0:T(128)} %bitcast.1.core_ref, bf16[8,8,1024,128]{3,2,1,0:T(8,128)(2,1)} %assemble_adjacency.1.refs_1_.adj_ref, bf16[1024,256]{1,0:T(8,128)(2,1)S(1)} %copy-done.1, bf16[1024,256]{1,0:T(8,128)(2,1)S(1)} %copy-done.3, bf16[1024,256]{1,0:T(8,128)(2,1)S(1)} %copy-done.9, ...), custom_call_target="tpu_custom_call" | custom-call | flops 2684354560 | bytes 15728640 | tf_op jit(solution)/shard_map/forward_product/pallas_call | solution.py:186
  52.7 5.7 %collective-permute-done.7.refs_2_ = bf16[1024,256]{1,0:T(8,128)(2,1)S(1)} collective-permute-done((bf16[1024,256]{1,0:T(8,128)(2,1)}, bf16[1024,256]{1,0:T(8,128)(2,1)S(1)}, u32[]{:S(2)}, u32[]{:S(2)}) %collective-permute-start.7) | collective-permute-done | bytes 524320 | tf_op jit(solution)/shard_map/ppermute | solution.py:60
  58.3 4.8 %forward_product.3 = (f32[2,256,256]{2,1,0:T(8,128)S(1)}, bf16[2,256,256]{2,1,0:T(8,128)(2,1)S(1)}) custom-call(s32[1]{0:T(128)} %bitcast.1.core_ref, bf16[8,8,1024,128]{3,2,1,0:T(8,128)(2,1)} %assemble_adjacency.1.refs_1_.adj_ref, bf16[1024,256]{1,0:T(8,128)(2,1)S(1)} %collective-permute-done.2.refs_0_, ...), custom_call_target="tpu_custom_call" | custom-call | flops 1610612736 | bytes 9437184 | tf_op jit(solution)/shard_map/forward_product/pallas_call | solution.py:186
  63.1 0.1 collective-permute-start.8
  63.4 1.4 collective-permute-done.8
  64.8 9.2 %collective-permute-start.9 = (bf16[2,256,256]{2,1,0:T(8,128)(2,1)S(1)}, bf16[2,256,256]{2,1,0:T(8,128)(2,1)S(1)}, u32[]{:S(2)}, u32[]{:S(2)}) collective-permute-start(bf16[2,256,256]{2,1,0:T(8,128)(2,1)S(1)} %add_convert_fusion.own_ref), channel_id=1, source_target_pairs={{0,2},{1,3},{2,0},{3,1},{4,6},{5,7},{6,4},{7,5},{8,10},{9,11},{10,... | collective-permute-start | bytes 786440 | tf_op jit(solution)/shard_map/ppermute | solution.py:60
  74.1 1.1 bitcast_multiply_fusion.cot_ref
  75.2 5.3 %collective-permute-done.9.got_ref = bf16[2,256,256]{2,1,0:T(8,128)(2,1)S(1)} collective-permute-done((bf16[2,256,256]{2,1,0:T(8,128)(2,1)S(1)}, bf16[2,256,256]{2,1,0:T(8,128)(2,1)S(1)}, u32[]{:S(2)}, u32[]{:S(2)}) %collective-permute-start.9) | collective-permute-done | bytes 262176 | tf_op jit(solution)/shard_map/ppermute | solution.py:60
  80.5 1.6 dense_rows.1
  82.1 1.0 collective-permute-start.11
  83.1 0.3 collective-permute-start.10
  83.3 0.7 collective-permute-done.11
  84.1 0.5 collective-permute-done.10.got_ref
  84.6 4.6 %backward_product.6 = (bf16[8,256,128]{2,1,0:T(8,128)(2,1)S(1)}, bf16[8,256,128]{2,1,0:T(8,128)(2,1)}, bf16[8,256,128]{2,1,0:T(8,128)(2,1)}) custom-call(s32[1]{0:T(128)} %bitcast.1.core_ref, bf16[8,8,1024,128]{3,2,1,0:T(8,128)(2,1)} %assemble_adjacency.1.refs_1_.adj_ref, bf16[2,256,256]{2,1,0:T(8,128)(2,1)S(1)} %get-tuple-element.21.own_ref, ...), custom_call_target="tpu_custom_call" | custom-call | flops 1610612736 | bytes 9437184 | tf_op jit(solution)/shard_map/backward_product/pallas_call | solution.py:277
  89.2 0.1 collective-permute-start.17
  89.3 0.7 pad_maximum_fusion.2
  90.0 3.9 %all-to-all-start = ((bf16[32,6,256]{2,1,0:T(8,128)(2,1)}), bf16[32,6,256]{2,1,0:T(8,128)(2,1)S(1)}, u32[]{:S(2)}, u32[]{:S(2)}) async-start(bf16[32,6,256]{2,1,0:T(8,128)(2,1)} %pad_maximum_fusion.2), calls=%async_computation | async-start | bytes 262144 | tf_op jit(solution)/shard_map/all_to_all | solution.py:364
  93.9 1.3 collective-permute-start.16
  95.2 1.1 collective-permute-start.14
  96.3 7.8 %all-to-all-done.rest_0_.rest_1_ = bf16[32,6,256]{2,1,0:T(8,128)(2,1)S(1)} async-done(((bf16[32,6,256]{2,1,0:T(8,128)(2,1)}), bf16[32,6,256]{2,1,0:T(8,128)(2,1)S(1)}, u32[]{:S(2)}, u32[]{:S(2)}) %all-to-all-start) | async-done | bytes 98336 | tf_op jit(solution)/shard_map/all_to_all | solution.py:364
  104.1 3.1 %backward_product.8 = bf16[8,256,128]{2,1,0:T(8,128)(2,1)} custom-call(s32[1]{0:T(128)} %bitcast.1.core_ref, bf16[8,8,1024,128]{3,2,1,0:T(8,128)(2,1)} %assemble_adjacency.1.refs_1_.adj_ref, bf16[2,256,256]{2,1,0:T(8,128)(2,1)S(1)} %get-tuple-element.21.own_ref, bf16[2,256,256]{2,1,0:T(8,128)(2,1)S(1)} %collective-permute-done.10.got_ref, ...), custom_call_target="tpu_custom_call" | custom-call | flops 536870912 | bytes 3145728 | tf_op jit(solution)/shard_map/backward_product/pallas_call | solution.py:277
  107.2 0.9 collective-permute-start.18
  108.1 0.7 broadcast_in_dim.11
  108.8 6.4 %all-to-all-start.1 = ((f32[32,4,256]{2,1,0:T(4,128)}), f32[32,4,256]{2,1,0:T(4,128)S(1)}, u32[]{:S(2)}, u32[]{:S(2)}) async-start(f32[32,4,256]{2,1,0:T(4,128)} %broadcast_in_dim.11), calls=%async_computation.1 | async-start | bytes 262144 | tf_op jit(solution)/shard_map/all_to_all | solution.py:372
  115.2 3.8 %backward_product.5 = (bf16[8,256,128]{2,1,0:T(8,128)(2,1)}, bf16[8,256,128]{2,1,0:T(8,128)(2,1)}) custom-call(s32[1]{0:T(128)} %bitcast.1.core_ref, bf16[8,8,1024,128]{3,2,1,0:T(8,128)(2,1)} %assemble_adjacency.1.refs_1_.adj_ref, bf16[2,256,256]{2,1,0:T(8,128)(2,1)S(1)} %get-tuple-element.21.own_ref, ...), custom_call_target="tpu_custom_call" | custom-call | flops 1073741824 | bytes 6291456 | tf_op jit(solution)/shard_map/backward_product/pallas_call | solution.py:277
  119.0 5.5 %collective-permute-start.12 = (bf16[8,256,128]{2,1,0:T(8,128)(2,1)}, bf16[8,256,128]{2,1,0:T(8,128)(2,1)S(1)}, u32[]{:S(2)}, u32[]{:S(2)}) collective-permute-start(bf16[8,256,128]{2,1,0:T(8,128)(2,1)} %get-tuple-element.23), channel_id=1, source_target_pairs={{0,100},{1,71},{2,38},{3,5},{4,0},{5,99},{6,66},{7,33},{8,108},{9,... | collective-permute-start | bytes 1572872 | tf_op jit(solution)/shard_map/ppermute | solution.py:60
  124.5 2.8 %collective-permute-start.13 = (bf16[8,256,128]{2,1,0:T(8,128)(2,1)}, bf16[8,256,128]{2,1,0:T(8,128)(2,1)S(1)}, u32[]{:S(2)}, u32[]{:S(2)}) collective-permute-start(bf16[8,256,128]{2,1,0:T(8,128)(2,1)} %get-tuple-element.24), channel_id=1, source_target_pairs={{0,0},{1,97},{2,66},{3,35},{4,4},{5,101},{6,70},{7,39},{8,8},{9,10... | collective-permute-start | bytes 1572872 | tf_op jit(solution)/shard_map/ppermute | solution.py:60
  127.3 3.1 %backward_product.7 = bf16[8,256,128]{2,1,0:T(8,128)(2,1)} custom-call(s32[1]{0:T(128)} %bitcast.1.core_ref, bf16[8,8,1024,128]{3,2,1,0:T(8,128)(2,1)} %assemble_adjacency.1.refs_1_.adj_ref, bf16[2,256,256]{2,1,0:T(8,128)(2,1)S(1)} %get-tuple-element.21.own_ref, bf16[2,256,256]{2,1,0:T(8,128)(2,1)S(1)} %collective-permute-done.10.got_ref, ...), custom_call_target="tpu_custom_call" | custom-call | flops 536870912 | bytes 3145728 | tf_op jit(solution)/shard_map/backward_product/pallas_call | solution.py:277
  130.5 2.2 %collective-permute-start.15 = (bf16[8,256,128]{2,1,0:T(8,128)(2,1)}, bf16[8,256,128]{2,1,0:T(8,128)(2,1)S(1)}, u32[]{:S(2)}, u32[]{:S(2)}) collective-permute-start(bf16[8,256,128]{2,1,0:T(8,128)(2,1)} %backward_product.7), channel_id=1, source_target_pairs={{0,104},{1,73},{2,42},{3,11},{4,108},{5,77},{6,46},{7,15},{8,0},{9... | collective-permute-start | bytes 1572872 | tf_op jit(solution)/shard_map/ppermute | solution.py:60
  132.7 0.8 copy-done.10
  133.5 1.0 copy-done.11
  134.5 2.3 %backward_product.9 = bf16[8,256,128]{2,1,0:T(8,128)(2,1)S(1)} custom-call(s32[1]{0:T(128)} %bitcast.1.core_ref, bf16[8,8,1024,128]{3,2,1,0:T(8,128)(2,1)} %assemble_adjacency.1.refs_1_.adj_ref, bf16[2,256,256]{2,1,0:T(8,128)(2,1)S(1)} %get-tuple-element.21.own_ref, bf16[2,256,256]{2,1,0:T(8,128)(2,1)S(1)} %collective-permute-done.10.got_ref, ...), custom_call_target="tpu_custom_call" | custom-call | flops 536870912 | bytes 3145728 | tf_op jit(solution)/shard_map/backward_product/pallas_call | solution.py:277
  136.9 2.7 %collective-permute-start.19 = (bf16[8,256,128]{2,1,0:T(8,128)(2,1)S(1)}, bf16[8,256,128]{2,1,0:T(8,128)(2,1)S(1)}, u32[]{:S(2)}, u32[]{:S(2)}) collective-permute-start(bf16[8,256,128]{2,1,0:T(8,128)(2,1)S(1)} %backward_product.9), channel_id=1, source_target_pairs={{0,120},{1,89},{2,58},{3,27},{4,124},{5,93},{6,62},{7,31},{8,112},... | collective-permute-start | bytes 1572872 | tf_op jit(solution)/shard_map/ppermute | solution.py:60
  139.6 0.1 collective-permute-start.22
  139.8 5.2 %collective-permute-done.22 = f32[128,256]{1,0:T(8,128)S(1)} collective-permute-done((f32[128,256]{1,0:T(8,128)S(1)}, f32[128,256]{1,0:T(8,128)S(1)}, u32[]{:S(2)}, u32[]{:S(2)}) %collective-permute-start.22) | collective-permute-done | bytes 131104 | tf_op jit(solution)/shard_map/ppermute | solution.py:60
  145.1 2.6 %collective-permute-start.23 = (f32[2,128,256]{2,1,0:T(8,128)S(1)}, f32[2,128,256]{2,1,0:T(8,128)}, u32[]{:S(2)}, u32[]{:S(2)}) collective-permute-start(f32[2,128,256]{2,1,0:T(8,128)S(1)} %maximum_select_fusion), channel_id=1, source_target_pairs={{0,1},{1,0},{2,3},{3,2},{4,5},{5,4},{6,7},{7,6},{8,9},{9,8},{10,11... | collective-permute-start | bytes 786440 | tf_op jit(solution)/shard_map/ppermute | solution.py:60
  147.7 0.6 fusion.2
  148.2 2.9 %collective-permute-done.12.rest_0_ = bf16[8,256,128]{2,1,0:T(8,128)(2,1)S(1)} collective-permute-done((bf16[8,256,128]{2,1,0:T(8,128)(2,1)}, bf16[8,256,128]{2,1,0:T(8,128)(2,1)S(1)}, u32[]{:S(2)}, u32[]{:S(2)}) %collective-permute-start.12) | collective-permute-done | bytes 524320 | tf_op jit(solution)/shard_map/ppermute | solution.py:60
  151.1 3.0 %collective-permute-done.13.rest_1_ = bf16[8,256,128]{2,1,0:T(8,128)(2,1)S(1)} collective-permute-done((bf16[8,256,128]{2,1,0:T(8,128)(2,1)}, bf16[8,256,128]{2,1,0:T(8,128)(2,1)S(1)}, u32[]{:S(2)}, u32[]{:S(2)}) %collective-permute-start.13) | collective-permute-done | bytes 524320 | tf_op jit(solution)/shard_map/ppermute | solution.py:60
  154.1 0.2 split_products.1
  154.4 0.1 collective-permute-start.20
  154.5 1.0 broadcast_select_fusion.1
  155.5 0.5 collective-permute-done.20
  156.1 14.4 %collective-permute-start.21 = (bf16[2,256,128]{2,1,0:T(8,128)(2,1)S(1)}, bf16[2,256,128]{2,1,0:T(8,128)(2,1)S(1)}, u32[]{:S(2)}, u32[]{:S(2)}) collective-permute-start(bf16[2,256,128]{2,1,0:T(8,128)(2,1)S(1)} %fusion.1), channel_id=1, source_target_pairs={{0,2},{1,3},{2,0},{3,1},{4,6},{5,7},{6,4},{7,5},{8,10},{9,11},{10,... | collective-permute-start | bytes 393224 | tf_op jit(solution)/shard_map/ppermute | solution.py:60
  170.5 0.8 slice_bitcast_fusion
  171.3 2.7 %collective-permute-done.21.got_ref = bf16[2,256,128]{2,1,0:T(8,128)(2,1)S(1)} collective-permute-done((bf16[2,256,128]{2,1,0:T(8,128)(2,1)S(1)}, bf16[2,256,128]{2,1,0:T(8,128)(2,1)S(1)}, u32[]{:S(2)}, u32[]{:S(2)}) %collective-permute-start.21) | collective-permute-done | bytes 131104 | tf_op jit(solution)/shard_map/ppermute | solution.py:60
  174.1 0.8 final_rows.1
  (75 shorter events, 0.7 us)
Async XLA Ops:
  0.6 35.3 %collective-permute-start.5 = (bf16[1024,256]{1,0:T(8,128)(2,1)}, bf16[1024,256]{1,0:T(8,128)(2,1)S(1)}, u32[]{:S(2)}, u32[]{:S(2)}) collective-permute-start(bf16[1024,256]{1,0:T(8,128)(2,1)} %param.10), channel_id=1, source_target_pairs={{104,0},{73,1},{42,2},{11,3},{108,4},{77,5},{46,6},{15,7},{0,8},{9... | collective-permute-start | bytes 1572872 | tf_op jit(solution)/shard_map/ppermute | solution.py:60
  3.8 36.5 %collective-permute-start.6 = (bf16[1024,256]{1,0:T(8,128)(2,1)}, bf16[1024,256]{1,0:T(8,128)(2,1)S(1)}, u32[]{:S(2)}, u32[]{:S(2)}) collective-permute-start(bf16[1024,256]{1,0:T(8,128)(2,1)} %param.10), channel_id=1, source_target_pairs={{0,0},{97,1},{66,2},{35,3},{4,4},{101,5},{70,6},{39,7},{8,8},{105,... | collective-permute-start | bytes 1572872 | tf_op jit(solution)/shard_map/ppermute | solution.py:60
  7.0 33.3 %collective-permute-start.4 = (bf16[1024,256]{1,0:T(8,128)(2,1)}, bf16[1024,256]{1,0:T(8,128)(2,1)S(1)}, u32[]{:S(2)}, u32[]{:S(2)}) collective-permute-start(bf16[1024,256]{1,0:T(8,128)(2,1)} %param.10), channel_id=1, source_target_pairs={{110,0},{79,1},{44,2},{13,3},{106,4},{73,5},{40,6},{11,7},{4,8},{1... | collective-permute-start | bytes 1572872 | tf_op jit(solution)/shard_map/ppermute | solution.py:60
  11.4 30.5 %collective-permute-start.1 = (bf16[1024,256]{1,0:T(8,128)(2,1)}, bf16[1024,256]{1,0:T(8,128)(2,1)S(1)}, u32[]{:S(2)}, u32[]{:S(2)}) collective-permute-start(bf16[1024,256]{1,0:T(8,128)(2,1)} %param.10), channel_id=1, source_target_pairs={{102,0},{69,1},{36,2},{7,3},{0,4},{99,5},{66,6},{33,7},{110,8},{77... | collective-permute-start | bytes 1572872 | tf_op jit(solution)/shard_map/ppermute | solution.py:60
  12.5 29.4 %collective-permute-start = (bf16[1024,256]{1,0:T(8,128)(2,1)}, bf16[1024,256]{1,0:T(8,128)(2,1)S(1)}, u32[]{:S(2)}, u32[]{:S(2)}) collective-permute-start(bf16[1024,256]{1,0:T(8,128)(2,1)} %param.10), channel_id=1, source_target_pairs={{120,0},{89,1},{58,2},{27,3},{124,4},{93,5},{62,6},{31,7},{112,8},... | collective-permute-start | bytes 1572872 | tf_op jit(solution)/shard_map/ppermute | solution.py:60
  35.9 4.3 %copy-start.4 = (bf16[1024,256]{1,0:T(8,128)(2,1)}, bf16[1024,256]{1,0:T(8,128)(2,1)S(1)}, u32[]{:S(2)}) copy-start(bf16[1024,256]{1,0:T(8,128)(2,1)S(1)} %collective-permute-done.5.refs_2_.refs_3_) | copy-start | bytes 1572868
  40.2 0.8 copy-start.6
  41.1 0.8 copy-start.2
  41.9 1.7 copy-start.3
  41.9 1.7 copy-start.5
  41.9 1.7 copy-start.7
  41.9 16.5 %collective-permute-start.7 = (bf16[1024,256]{1,0:T(8,128)(2,1)}, bf16[1024,256]{1,0:T(8,128)(2,1)S(1)}, u32[]{:S(2)}, u32[]{:S(2)}) collective-permute-start(bf16[1024,256]{1,0:T(8,128)(2,1)} %hold.3.refs_1_.refs_6_), channel_id=1, source_target_pairs={{120,0},{121,1},{122,2},{123,3},{124,4},{125,5},{126,6},{127,7},{1... | collective-permute-start | bytes 1572872 | tf_op jit(solution)/shard_map/ppermute | solution.py:60
  41.9 0.8 copy-start.8
  42.7 0.8 copy-start
  43.5 14.8 %collective-permute-start.2 = (bf16[1024,256]{1,0:T(8,128)(2,1)}, bf16[1024,256]{1,0:T(8,128)(2,1)S(1)}, u32[]{:S(2)}, u32[]{:S(2)}) collective-permute-start(bf16[1024,256]{1,0:T(8,128)(2,1)} %hold.2.refs_0_.refs_5_), channel_id=1, source_target_pairs={{4,0},{5,1},{6,2},{7,3},{0,4},{1,5},{2,6},{3,7},{12,8},{13,9},{14,... | collective-permute-start | bytes 1572872 | tf_op jit(solution)/shard_map/ppermute | solution.py:60
  43.5 14.8 %collective-permute-start.3 = (bf16[1024,256]{1,0:T(8,128)(2,1)}, bf16[1024,256]{1,0:T(8,128)(2,1)S(1)}, u32[]{:S(2)}, u32[]{:S(2)}) collective-permute-start(bf16[1024,256]{1,0:T(8,128)(2,1)} %hold.2.refs_0_.refs_5_), channel_id=1, source_target_pairs={{8,0},{9,1},{10,2},{11,3},{12,4},{13,5},{14,6},{15,7},{0,8},{1,9},... | collective-permute-start | bytes 1572872 | tf_op jit(solution)/shard_map/ppermute | solution.py:60
  43.5 1.1 copy-start.1
  44.6 1.0 copy-start.9
  45.7 17.6 %copy-start.16 = (s32[1024]{0:T(1024)S(1)}, s32[1024]{0:T(1024)}, u32[]{:S(2)}) copy-start(s32[1024]{0:T(1024)} %param.14) | copy-start | bytes 12292
  45.7 17.6 %copy-start.17 = (s32[1024]{0:T(1024)S(1)}, s32[1024]{0:T(1024)}, u32[]{:S(2)}) copy-start(s32[1024]{0:T(1024)} %param.15) | copy-start | bytes 12292
  45.7 34.8 %copy-start.12 = (bf16[256,256]{1,0:T(8,128)(2,1)S(1)}, bf16[256,256]{1,0:T(8,128)(2,1)}, u32[]{:S(2)}) copy-start(bf16[256,256]{1,0:T(8,128)(2,1)} %ws_ref.1) | copy-start | bytes 393220
  45.7 34.8 %copy-start.14 = (f32[256]{0:T(256)S(1)}, f32[256]{0:T(256)}, u32[]{:S(2)}) copy-start(f32[256]{0:T(256)} %param.19) | copy-start | bytes 3076
  52.6 10.7 %copy-start.15 = (bf16[1024,256]{1,0:T(8,128)(2,1)S(1)}, bf16[1024,256]{1,0:T(8,128)(2,1)}, u32[]{:S(2)}) copy-start(bf16[1024,256]{1,0:T(8,128)(2,1)} %param.10) | copy-start | bytes 1572868
  52.6 27.8 %copy-start.13 = (bf16[256,256]{1,0:T(8,128)(2,1)S(1)}, bf16[256,256]{1,0:T(8,128)(2,1)}, u32[]{:S(2)}) copy-start(bf16[256,256]{1,0:T(8,128)(2,1)} %wn_ref.1) | copy-start | bytes 393220
  63.1 1.6 collective-permute-start.8
  64.8 15.6 %collective-permute-start.9 = (bf16[2,256,256]{2,1,0:T(8,128)(2,1)S(1)}, bf16[2,256,256]{2,1,0:T(8,128)(2,1)S(1)}, u32[]{:S(2)}, u32[]{:S(2)}) collective-permute-start(bf16[2,256,256]{2,1,0:T(8,128)(2,1)S(1)} %add_convert_fusion.own_ref), channel_id=1, source_target_pairs={{0,2},{1,3},{2,0},{3,1},{4,6},{5,7},{6,4},{7,5},{8,10},{9,11},{10,... | collective-permute-start | bytes 786440 | tf_op jit(solution)/shard_map/ppermute | solution.py:60
  82.1 2.0 %collective-permute-start.11 = (f32[136,256]{1,0:T(8,128)S(1)}, f32[136,256]{1,0:T(8,128)S(1)}, u32[]{:S(2)}, u32[]{:S(2)}) collective-permute-start(f32[136,256]{1,0:T(8,128)S(1)} %pad_maximum_fusion), channel_id=1, source_target_pairs={{0,1},{1,0},{2,3},{3,2},{4,5},{5,4},{6,7},{7,6},{8,9},{9,8},{10,11... | collective-permute-start | bytes 417800 | tf_op jit(solution)/shard_map/ppermute | solution.py:60
  83.1 1.5 collective-permute-start.10
  89.2 15.0 %collective-permute-start.17 = (bf16[8,256,128]{2,1,0:T(8,128)(2,1)S(1)}, bf16[8,256,128]{2,1,0:T(8,128)(2,1)S(1)}, u32[]{:S(2)}, u32[]{:S(2)}) collective-permute-start(bf16[8,256,128]{2,1,0:T(8,128)(2,1)S(1)} %get-tuple-element.27), channel_id=1, source_target_pairs={{0,8},{1,9},{2,10},{3,11},{4,12},{5,13},{6,14},{7,15},{8,0},{9,1},... | collective-permute-start | bytes 1572872 | tf_op jit(solution)/shard_map/ppermute | solution.py:60
  90.0 14.1 %all-to-all-start = ((bf16[32,6,256]{2,1,0:T(8,128)(2,1)}), bf16[32,6,256]{2,1,0:T(8,128)(2,1)S(1)}, u32[]{:S(2)}, u32[]{:S(2)}) async-start(bf16[32,6,256]{2,1,0:T(8,128)(2,1)} %pad_maximum_fusion.2), calls=%async_computation | async-start | bytes 262144 | tf_op jit(solution)/shard_map/all_to_all | solution.py:364
  93.9 38.8 %collective-permute-start.16 = (bf16[8,256,128]{2,1,0:T(8,128)(2,1)}, bf16[8,256,128]{2,1,0:T(8,128)(2,1)S(1)}, u32[]{:S(2)}, u32[]{:S(2)}) collective-permute-start(bf16[8,256,128]{2,1,0:T(8,128)(2,1)} %get-tuple-element.26), channel_id=1, source_target_pairs={{0,8},{1,9},{2,10},{3,11},{4,12},{5,13},{6,14},{7,15},{8,0},{9,1},... | collective-permute-start | bytes 1572872 | tf_op jit(solution)/shard_map/ppermute | solution.py:60
  95.2 32.1 %collective-permute-start.14 = (bf16[8,256,128]{2,1,0:T(8,128)(2,1)}, bf16[8,256,128]{2,1,0:T(8,128)(2,1)S(1)}, u32[]{:S(2)}, u32[]{:S(2)}) collective-permute-start(bf16[8,256,128]{2,1,0:T(8,128)(2,1)} %get-tuple-element.25), channel_id=1, source_target_pairs={{0,4},{1,5},{2,6},{3,7},{4,0},{5,1},{6,2},{7,3},{8,12},{9,13},{10,... | collective-permute-start | bytes 1572872 | tf_op jit(solution)/shard_map/ppermute | solution.py:60
  107.2 25.4 %collective-permute-start.18 = (bf16[8,256,128]{2,1,0:T(8,128)(2,1)}, bf16[8,256,128]{2,1,0:T(8,128)(2,1)S(1)}, u32[]{:S(2)}, u32[]{:S(2)}) collective-permute-start(bf16[8,256,128]{2,1,0:T(8,128)(2,1)} %backward_product.8), channel_id=1, source_target_pairs={{0,4},{1,5},{2,6},{3,7},{4,0},{5,1},{6,2},{7,3},{8,12},{9,13},{10,... | collective-permute-start | bytes 1572872 | tf_op jit(solution)/shard_map/ppermute | solution.py:60
  108.8 30.8 %all-to-all-start.1 = ((f32[32,4,256]{2,1,0:T(4,128)}), f32[32,4,256]{2,1,0:T(4,128)S(1)}, u32[]{:S(2)}, u32[]{:S(2)}) async-start(f32[32,4,256]{2,1,0:T(4,128)} %broadcast_in_dim.11), calls=%async_computation.1 | async-start | bytes 262144 | tf_op jit(solution)/shard_map/all_to_all | solution.py:372
  119.0 32.1 %collective-permute-start.12 = (bf16[8,256,128]{2,1,0:T(8,128)(2,1)}, bf16[8,256,128]{2,1,0:T(8,128)(2,1)S(1)}, u32[]{:S(2)}, u32[]{:S(2)}) collective-permute-start(bf16[8,256,128]{2,1,0:T(8,128)(2,1)} %get-tuple-element.23), channel_id=1, source_target_pairs={{0,100},{1,71},{2,38},{3,5},{4,0},{5,99},{6,66},{7,33},{8,108},{9,... | collective-permute-start | bytes 1572872 | tf_op jit(solution)/shard_map/ppermute | solution.py:60
  124.5 29.6 %collective-permute-start.13 = (bf16[8,256,128]{2,1,0:T(8,128)(2,1)}, bf16[8,256,128]{2,1,0:T(8,128)(2,1)S(1)}, u32[]{:S(2)}, u32[]{:S(2)}) collective-permute-start(bf16[8,256,128]{2,1,0:T(8,128)(2,1)} %get-tuple-element.24), channel_id=1, source_target_pairs={{0,0},{1,97},{2,66},{3,35},{4,4},{5,101},{6,70},{7,39},{8,8},{9,10... | collective-permute-start | bytes 1572872 | tf_op jit(solution)/shard_map/ppermute | solution.py:60
  130.5 23.7 %collective-permute-start.15 = (bf16[8,256,128]{2,1,0:T(8,128)(2,1)}, bf16[8,256,128]{2,1,0:T(8,128)(2,1)S(1)}, u32[]{:S(2)}, u32[]{:S(2)}) collective-permute-start(bf16[8,256,128]{2,1,0:T(8,128)(2,1)} %backward_product.7), channel_id=1, source_target_pairs={{0,104},{1,73},{2,42},{3,11},{4,108},{5,77},{6,46},{7,15},{8,0},{9... | collective-permute-start | bytes 1572872 | tf_op jit(solution)/shard_map/ppermute | solution.py:60
  132.7 0.8 copy-start.10
  133.5 1.0 copy-start.11
  136.9 17.3 %collective-permute-start.19 = (bf16[8,256,128]{2,1,0:T(8,128)(2,1)S(1)}, bf16[8,256,128]{2,1,0:T(8,128)(2,1)S(1)}, u32[]{:S(2)}, u32[]{:S(2)}) collective-permute-start(bf16[8,256,128]{2,1,0:T(8,128)(2,1)S(1)} %backward_product.9), channel_id=1, source_target_pairs={{0,120},{1,89},{2,58},{3,27},{4,124},{5,93},{6,62},{7,31},{8,112},... | collective-permute-start | bytes 1572872 | tf_op jit(solution)/shard_map/ppermute | solution.py:60
  139.6 5.4 %collective-permute-start.22 = (f32[128,256]{1,0:T(8,128)S(1)}, f32[128,256]{1,0:T(8,128)S(1)}, u32[]{:S(2)}, u32[]{:S(2)}) collective-permute-start(f32[128,256]{1,0:T(8,128)S(1)} %reshape.61), channel_id=1, source_target_pairs={{0,2},{1,3},{2,0},{3,1},{4,6},{5,7},{6,4},{7,5},{8,10},{9,11},{10,... | collective-permute-start | bytes 393224 | tf_op jit(solution)/shard_map/ppermute | solution.py:60
  145.1 9.4 %collective-permute-start.23 = (f32[2,128,256]{2,1,0:T(8,128)S(1)}, f32[2,128,256]{2,1,0:T(8,128)}, u32[]{:S(2)}, u32[]{:S(2)}) collective-permute-start(f32[2,128,256]{2,1,0:T(8,128)S(1)} %maximum_select_fusion), channel_id=1, source_target_pairs={{0,1},{1,0},{2,3},{3,2},{4,5},{5,4},{6,7},{7,6},{8,9},{9,8},{10,11... | collective-permute-start | bytes 786440 | tf_op jit(solution)/shard_map/ppermute | solution.py:60
  154.4 1.6 collective-permute-start.20
  156.1 18.0 %collective-permute-start.21 = (bf16[2,256,128]{2,1,0:T(8,128)(2,1)S(1)}, bf16[2,256,128]{2,1,0:T(8,128)(2,1)S(1)}, u32[]{:S(2)}, u32[]{:S(2)}) collective-permute-start(bf16[2,256,128]{2,1,0:T(8,128)(2,1)S(1)} %fusion.1), channel_id=1, source_target_pairs={{0,2},{1,3},{2,0},{3,1},{4,6},{5,7},{6,4},{7,5},{8,10},{9,11},{10,... | collective-permute-start | bytes 393224 | tf_op jit(solution)/shard_map/ppermute | solution.py:60

commit v7 on v6

--- a/solution.py
+++ b/solution.py
@@ -17,12 +17,12 @@
 SMALL = 16 * 1024 * 1024
 PLAN = {6: None, 3: None, 1: None, 2: None, 0: None, 7: 1, 4: 2, 5: 6}
 CROSS = {1: 0x7666, 3: 0x5FDB}
-BACK_PLAN = {6: None, 2: None, 1: None, 0: None, 3: 1, 7: 1, 4: 2, 5: 2}
+BACK_PLAN = {6: None, 1: None, 0: None, 2: 2, 3: 1, 7: 1, 4: 2, 5: 2}
 BACK_CROSS = {1: 0xAAAA}
 GROUPS = ((6, 3, 1, 2, 0), (7, 4, 5))
 HELD = ((6, (1,)), (3, (2, 0)))
-BACK = ((5, 3, 4), (1, 0), (7,), (2,), (6,))
-LATER = (7, 1)
+BACK = ((5, 3, 4, 1), (7,), (2,), (6,), (0,))
+LATER = (7,)
 
 
 def index_of(y, x, zl, zh, core):

time: 178 us -> 166 us (0.933); the launches traced: 175 us -> 165 us
  starting transfers between devices: 68.8 us -> 63.6 us
  waiting for transfers between devices: 40 us -> 36.1 us
    ppermute x24, waiting for transfers between devices: 32.2 us -> 28.1 us  [send(): return lax.ppermute(value, AXES, pairs)]
    ppermute x24, starting transfers between devices: 58.5 us -> 55.3 us  [send(): return lax.ppermute(value, AXES, pairs)]
    unnamed x38, local copies, waits for them, and re-layouts: 8.06 us -> 5.44 us
    all_to_all x1, starting transfers between devices: 6.35 us -> 4.23 us  [weight_grads(): half = lax.all_to_all(spread, 'blk', 0, 0).reshape(F // 2, F)]
  transfers between devices with their start and end apart: 26 -> 26, of which waited for: 12 -> 11; matrix products, arithmetic and copies ran while one was open for 4% -> 6% of each run, Pallas kernels for 22% -> 23%
where the time goes in v7:
time: 166 us; the launch traced here: 165 us
  starting transfers between devices  63.6 us (38%)
  Pallas kernels  50.4 us (30%)
  waiting for transfers between devices  36.1 us (22%)
  local copies, waits for them, and re-layouts  9.79 us (6%)
  other arithmetic  4.48 us (3%)
    ppermute x24, starting transfers between devices, send(): return lax.ppermute(value, AXES, pairs)  55.3 us
    ppermute x24, waiting for transfers between devices, send(): return lax.ppermute(value, AXES, pairs)  28.1 us
    pallas_call x1, Pallas kernels, assemble_call(): pl.pallas_call(functools.partial(assemble_body, n), out_shape=jax.ShapeDt...  19.2 us
    pallas_call x5, Pallas kernels, backward_call(): pl.pallas_call(functools.partial(backward_body, tuple(places), added), ou...  15.9 us
    pallas_call x2, Pallas kernels, forward_call(): pl.pallas_call(functools.partial(forward_body, n, start, first, last), ou...  12.8 us
    all_to_all x1, waiting for transfers between devices, weight_shares(): return lax.all_to_all(jnp.concatenate([rows, bias_rows], 1), 'blk', 0, 0)  7.91 us
    unnamed x38, local copies, waits for them, and re-layouts  5.44 us
    all_to_all x1, starting transfers between devices, weight_grads(): half = lax.all_to_all(spread, 'blk', 0, 0).reshape(F // 2, F)  4.23 us
  transfers between devices with their start and end apart: 26, of which 11 were waited for; matrix products, arithmetic and copies ran while one was open for 6% of the time, Pallas kernels for 23%

profile of v7, /device:TPU:1, one launch (start us, length us, event | category | flops | bytes accessed | tf_op | source)
XLA Modules:
  0.0 165.4 jit_solution(13373811891072397751)
XLA Ops:
  0.6 3.1 %collective-permute-start.5 = (bf16[1024,256]{1,0:T(8,128)(2,1)}, bf16[1024,256]{1,0:T(8,128)(2,1)S(1)}, u32[]{:S(2)}, u32[]{:S(2)}) collective-permute-start(bf16[1024,256]{1,0:T(8,128)(2,1)} %param.10), channel_id=1, source_target_pairs={{104,0},{73,1},{42,2},{11,3},{108,4},{77,5},{46,6},{15,7},{0,8},{9... | collective-permute-start | bytes 1572872 | tf_op jit(solution)/shard_map/ppermute | solution.py:60
  3.8 5.2 %collective-permute-start.4 = (bf16[1024,256]{1,0:T(8,128)(2,1)}, bf16[1024,256]{1,0:T(8,128)(2,1)S(1)}, u32[]{:S(2)}, u32[]{:S(2)}) collective-permute-start(bf16[1024,256]{1,0:T(8,128)(2,1)} %param.10), channel_id=1, source_target_pairs={{110,0},{79,1},{44,2},{13,3},{106,4},{73,5},{40,6},{11,7},{4,8},{1... | collective-permute-start | bytes 1572872 | tf_op jit(solution)/shard_map/ppermute | solution.py:60
  8.9 1.9 %collective-permute-start.6 = (bf16[1024,256]{1,0:T(8,128)(2,1)}, bf16[1024,256]{1,0:T(8,128)(2,1)S(1)}, u32[]{:S(2)}, u32[]{:S(2)}) collective-permute-start(bf16[1024,256]{1,0:T(8,128)(2,1)} %param.10), channel_id=1, source_target_pairs={{0,0},{97,1},{66,2},{35,3},{4,4},{101,5},{70,6},{39,7},{8,8},{105,... | collective-permute-start | bytes 1572872 | tf_op jit(solution)/shard_map/ppermute | solution.py:60
  10.8 1.3 collective-permute-start.1
  12.1 2.7 %collective-permute-start = (bf16[1024,256]{1,0:T(8,128)(2,1)}, bf16[1024,256]{1,0:T(8,128)(2,1)S(1)}, u32[]{:S(2)}, u32[]{:S(2)}) collective-permute-start(bf16[1024,256]{1,0:T(8,128)(2,1)} %param.10), channel_id=1, source_target_pairs={{120,0},{89,1},{58,2},{27,3},{124,4},{93,5},{62,6},{31,7},{112,8},... | collective-permute-start | bytes 1572872 | tf_op jit(solution)/shard_map/ppermute | solution.py:60
  14.9 0.8 reshape.53.counts_ref
  15.6 0.9 copy.22
  16.5 0.1 reshape.52.cols_ref
  16.7 0.1 stack.42.sel_ref
  16.8 19.2 %assemble_adjacency.1.refs_1_.adj_ref = bf16[8,8,1024,128]{3,2,1,0:T(8,128)(2,1)} custom-call(s32[8]{0:T(128)S(1)} %stack.42.sel_ref, s32[384]{0:T(512)S(1)} %reshape.52.cols_ref, s32[64]{0:T(128)S(1)} %reshape.53.counts_ref, bf16[8,8,6,128,128]{4,3,2,1,0:T(8,128)(2,1)} %tiles_ref.1), custom_call_target="tpu_custom_call" | custom-call | flops 4294967296 | bytes 25165824 | tf_op jit(solution)/shard_map/assemble_adjacency/pallas_call | solution.py:117
  36.0 4.2 %collective-permute-done.6.refs_3_.refs_4_ = bf16[1024,256]{1,0:T(8,128)(2,1)S(1)} collective-permute-done((bf16[1024,256]{1,0:T(8,128)(2,1)}, bf16[1024,256]{1,0:T(8,128)(2,1)S(1)}, u32[]{:S(2)}, u32[]{:S(2)}) %collective-permute-start.6) | collective-permute-done | bytes 524320 | tf_op jit(solution)/shard_map/ppermute | solution.py:60
  40.3 0.8 copy-done.6
  41.1 0.6 collective-permute-done.1.refs_2_
  41.7 0.8 copy-done.8
  42.5 0.8 copy-done.2
  43.3 1.0 collective-permute-start.2
  44.4 1.1 copy-done.3
  45.4 1.0 copy-done.9
  46.5 7.0 %forward_product.2.refs_3_ = f32[1024,256]{1,0:T(8,128)S(1)} custom-call(s32[1]{0:T(128)} %bitcast.1.core_ref, bf16[8,8,1024,128]{3,2,1,0:T(8,128)(2,1)} %assemble_adjacency.1.refs_1_.adj_ref, bf16[1024,256]{1,0:T(8,128)(2,1)S(1)} %copy-done.3, bf16[1024,256]{1,0:T(8,128)(2,1)S(1)} %copy-done.1, bf16[1024,256]{1,0:T(8,128)(2,1)S(1)} %copy-done.9, ...), custom_call_target="tpu_custom_call" | custom-call | flops 2684354560 | bytes 15728640 | tf_op jit(solution)/shard_map/forward_product/pallas_call | solution.py:186
  53.5 4.3 %collective-permute-done.7.refs_2_ = bf16[1024,256]{1,0:T(8,128)(2,1)S(1)} collective-permute-done((bf16[1024,256]{1,0:T(8,128)(2,1)}, bf16[1024,256]{1,0:T(8,128)(2,1)S(1)}, u32[]{:S(2)}, u32[]{:S(2)}) %collective-permute-start.7) | collective-permute-done | bytes 524320 | tf_op jit(solution)/shard_map/ppermute | solution.py:60
  57.8 5.8 %forward_product.3 = (f32[2,256,256]{2,1,0:T(8,128)S(1)}, bf16[2,256,256]{2,1,0:T(8,128)(2,1)S(1)}) custom-call(s32[1]{0:T(128)} %bitcast.1.core_ref, bf16[8,8,1024,128]{3,2,1,0:T(8,128)(2,1)} %assemble_adjacency.1.refs_1_.adj_ref, bf16[1024,256]{1,0:T(8,128)(2,1)} %collective-permute-done.2.refs_0_, bf16[1024,256]{1,0:T(8,128)(2,1)S(1)} %collective-permute-done.3.refs_1_, ...), custom_call_target="tpu_custom_call" | custom-call | flops 1610612736 | bytes 9437184 | tf_op jit(solution)/shard_map/forward_product/pallas_call | solution.py:186
  63.6 0.4 collective-permute-start.8
  64.1 1.1 collective-permute-done.8
  65.3 0.1 add_convert_fusion.own_ref
  65.3 7.7 %collective-permute-start.9 = (bf16[2,256,256]{2,1,0:T(8,128)(2,1)S(1)}, bf16[2,256,256]{2,1,0:T(8,128)(2,1)S(1)}, u32[]{:S(2)}, u32[]{:S(2)}) collective-permute-start(bf16[2,256,256]{2,1,0:T(8,128)(2,1)S(1)} %add_convert_fusion.own_ref), channel_id=1, source_target_pairs={{0,2},{1,3},{2,0},{3,1},{4,6},{5,7},{6,4},{7,5},{8,10},{9,11},{10,... | collective-permute-start | bytes 786440 | tf_op jit(solution)/shard_map/ppermute | solution.py:60
  73.0 0.1 bitcast_multiply_fusion.cot_ref
  73.2 6.2 %collective-permute-done.9.got_ref = bf16[2,256,256]{2,1,0:T(8,128)(2,1)S(1)} collective-permute-done((bf16[2,256,256]{2,1,0:T(8,128)(2,1)S(1)}, bf16[2,256,256]{2,1,0:T(8,128)(2,1)S(1)}, u32[]{:S(2)}, u32[]{:S(2)}) %collective-permute-start.9) | collective-permute-done | bytes 262176 | tf_op jit(solution)/shard_map/ppermute | solution.py:60
  79.4 1.6 dense_rows.1
  81.0 1.0 collective-permute-start.14
  82.0 0.3 collective-permute-start.10
  82.3 0.7 collective-permute-done.14
  83.1 0.5 collective-permute-done.10.got_ref
  83.5 4.7 %backward_product.5 = (bf16[8,256,128]{2,1,0:T(8,128)(2,1)S(1)}, bf16[8,256,128]{2,1,0:T(8,128)(2,1)}, bf16[8,256,128]{2,1,0:T(8,128)(2,1)}, bf16[8,256,128]{2,1,0:T(8,128)(2,1)S(1)}) custom-call(s32[1]{0:T(128)} %bitcast.1.core_ref, bf16[8,8,1024,128]{3,2,1,0:T(8,128)(2,1)} %assemble_adjacency.1.refs_1_.adj_ref, ...), custom_call_target="tpu_custom_call" | custom-call | flops 2147483648 | bytes 12582912 | tf_op jit(solution)/shard_map/backward_product/pallas_call | solution.py:277
  88.3 1.5 collective-permute-start.13
  89.8 0.8 collective-permute-start.17
  90.7 0.7 pad_maximum_fusion.2
  91.4 4.0 %all-to-all-start = ((bf16[32,6,256]{2,1,0:T(8,128)(2,1)}), bf16[32,6,256]{2,1,0:T(8,128)(2,1)S(1)}, u32[]{:S(2)}, u32[]{:S(2)}) async-start(bf16[32,6,256]{2,1,0:T(8,128)(2,1)} %pad_maximum_fusion.2), calls=%async_computation | async-start | bytes 262144 | tf_op jit(solution)/shard_map/all_to_all | solution.py:364
  95.5 1.3 collective-permute-start.12
  96.8 7.9 %all-to-all-done.rest_1_ = bf16[32,6,256]{2,1,0:T(8,128)(2,1)S(1)} async-done(((bf16[32,6,256]{2,1,0:T(8,128)(2,1)}), bf16[32,6,256]{2,1,0:T(8,128)(2,1)S(1)}, u32[]{:S(2)}, u32[]{:S(2)}) %all-to-all-start) | async-done | bytes 98336 | tf_op jit(solution)/shard_map/all_to_all | solution.py:364
  104.7 2.3 %backward_product.6 = bf16[8,256,128]{2,1,0:T(8,128)(2,1)S(1)} custom-call(s32[1]{0:T(128)} %bitcast.1.core_ref, bf16[8,8,1024,128]{3,2,1,0:T(8,128)(2,1)} %assemble_adjacency.1.refs_1_.adj_ref, bf16[2,256,256]{2,1,0:T(8,128)(2,1)S(1)} %get-tuple-element.20.own_ref, bf16[2,256,256]{2,1,0:T(8,128)(2,1)S(1)} %collective-permute-done.10.got_ref, ...), custom_call_target="tpu_custom_call" | custom-call | flops 536870912 | bytes 3145728 | tf_op jit(solution)/shard_map/backward_product/pallas_call | solution.py:277
  107.0 1.2 collective-permute-start.15
  108.2 3.1 %backward_product.8 = bf16[8,256,128]{2,1,0:T(8,128)(2,1)} custom-call(s32[1]{0:T(128)} %bitcast.1.core_ref, bf16[8,8,1024,128]{3,2,1,0:T(8,128)(2,1)} %assemble_adjacency.1.refs_1_.adj_ref, bf16[2,256,256]{2,1,0:T(8,128)(2,1)S(1)} %get-tuple-element.20.own_ref, bf16[2,256,256]{2,1,0:T(8,128)(2,1)S(1)} %collective-permute-done.10.got_ref, ...), custom_call_target="tpu_custom_call" | custom-call | flops 536870912 | bytes 3145728 | tf_op jit(solution)/shard_map/backward_product/pallas_call | solution.py:277
  111.3 1.6 collective-permute-start.18
  113.0 0.7 broadcast_in_dim.11
  113.7 4.2 %all-to-all-start.1 = ((f32[32,4,256]{2,1,0:T(4,128)}), f32[32,4,256]{2,1,0:T(4,128)S(1)}, u32[]{:S(2)}, u32[]{:S(2)}) async-start(f32[32,4,256]{2,1,0:T(4,128)} %broadcast_in_dim.11), calls=%async_computation.1 | async-start | bytes 262144 | tf_op jit(solution)/shard_map/all_to_all | solution.py:372
  117.9 5.7 %collective-permute-start.11 = (bf16[8,256,128]{2,1,0:T(8,128)(2,1)S(1)}, bf16[8,256,128]{2,1,0:T(8,128)(2,1)S(1)}, u32[]{:S(2)}, u32[]{:S(2)}) collective-permute-start(bf16[8,256,128]{2,1,0:T(8,128)(2,1)S(1)} %get-tuple-element.21), channel_id=1, source_target_pairs={{0,100},{1,71},{2,38},{3,5},{4,0},{5,99},{6,66},{7,33},{8,108},{9,... | collective-permute-start | bytes 1572872 | tf_op jit(solution)/shard_map/ppermute | solution.py:60
  123.6 2.3 %backward_product.7 = bf16[8,256,128]{2,1,0:T(8,128)(2,1)S(1)} custom-call(s32[1]{0:T(128)} %bitcast.1.core_ref, bf16[8,8,1024,128]{3,2,1,0:T(8,128)(2,1)} %assemble_adjacency.1.refs_1_.adj_ref, bf16[2,256,256]{2,1,0:T(8,128)(2,1)S(1)} %get-tuple-element.20.own_ref, bf16[2,256,256]{2,1,0:T(8,128)(2,1)S(1)} %collective-permute-done.10.got_ref, ...), custom_call_target="tpu_custom_call" | custom-call | flops 536870912 | bytes 3145728 | tf_op jit(solution)/shard_map/backward_product/pallas_call | solution.py:277
  126.0 2.4 %collective-permute-start.16 = (bf16[8,256,128]{2,1,0:T(8,128)(2,1)S(1)}, bf16[8,256,128]{2,1,0:T(8,128)(2,1)S(1)}, u32[]{:S(2)}, u32[]{:S(2)}) collective-permute-start(bf16[8,256,128]{2,1,0:T(8,128)(2,1)S(1)} %backward_product.7), channel_id=1, source_target_pairs={{0,120},{1,89},{2,58},{3,27},{4,124},{5,93},{6,62},{7,31},{8,112},... | collective-permute-start | bytes 1572872 | tf_op jit(solution)/shard_map/ppermute | solution.py:60
  128.4 3.4 %backward_product.9 = bf16[8,256,128]{2,1,0:T(8,128)(2,1)S(1)} custom-call(s32[1]{0:T(128)} %bitcast.1.core_ref, bf16[8,8,1024,128]{3,2,1,0:T(8,128)(2,1)} %assemble_adjacency.1.refs_1_.adj_ref, bf16[2,256,256]{2,1,0:T(8,128)(2,1)S(1)} %get-tuple-element.20.own_ref, bf16[2,256,256]{2,1,0:T(8,128)(2,1)S(1)} %collective-permute-done.10.got_ref, ...), custom_call_target="tpu_custom_call" | custom-call | flops 536870912 | bytes 3145728 | tf_op jit(solution)/shard_map/backward_product/pallas_call | solution.py:277
  131.8 4.4 %collective-permute-start.19 = (bf16[8,256,128]{2,1,0:T(8,128)(2,1)S(1)}, bf16[8,256,128]{2,1,0:T(8,128)(2,1)S(1)}, u32[]{:S(2)}, u32[]{:S(2)}) collective-permute-start(bf16[8,256,128]{2,1,0:T(8,128)(2,1)S(1)} %backward_product.9), channel_id=1, source_target_pairs={{0,0},{1,97},{2,66},{3,35},{4,4},{5,101},{6,70},{7,39},{8,8},{9,10... | collective-permute-start | bytes 1572872 | tf_op jit(solution)/shard_map/ppermute | solution.py:60
  136.2 0.7 reshape.61
  136.9 0.9 stack_reshape.4
  137.9 7.0 %collective-permute-done.22 = f32[128,256]{1,0:T(8,128)} collective-permute-done((f32[128,256]{1,0:T(8,128)}, f32[128,256]{1,0:T(8,128)}, u32[]{:S(2)}, u32[]{:S(2)}) %collective-permute-start.22) | collective-permute-done | bytes 131104 | tf_op jit(solution)/shard_map/ppermute | solution.py:60
  144.9 1.7 %maximum_select_fusion = f32[2,128,256]{2,1,0:T(8,128)} fusion(f32[1,128,256]{2,1,0:T(8,128)} %bitcast.19, f32[1,128,256]{2,1,0:T(8,128)S(1)} %stack_reshape.4, pred[]{:T(512)S(6)} %eq.19), kind=kLoop, calls=%fused_computation.5 | loop fusion | flops 196608 | bytes 524289 | tf_op jit(solution)/shard_map/jit(_where)/select_n | solution.py:374
  146.6 1.7 %collective-permute-start.23 = (f32[2,128,256]{2,1,0:T(8,128)}, f32[2,128,256]{2,1,0:T(8,128)}, u32[]{:S(2)}, u32[]{:S(2)}) collective-permute-start(f32[2,128,256]{2,1,0:T(8,128)} %maximum_select_fusion), channel_id=1, source_target_pairs={{0,1},{1,0},{2,3},{3,2},{4,5},{5,4},{6,7},{7,6},{8,9},{9,8},{10,11... | collective-permute-start | bytes 786440 | tf_op jit(solution)/shard_map/ppermute | solution.py:60
  148.3 0.6 fusion.2
  148.9 0.2 split_products.1
  149.1 0.1 collective-permute-start.20
  149.2 0.6 collective-permute-done.23
  149.8 1.1 broadcast_select_fusion.1
  151.1 9.9 %collective-permute-start.21 = (bf16[2,256,128]{2,1,0:T(8,128)(2,1)S(1)}, bf16[2,256,128]{2,1,0:T(8,128)(2,1)S(1)}, u32[]{:S(2)}, u32[]{:S(2)}) collective-permute-start(bf16[2,256,128]{2,1,0:T(8,128)(2,1)S(1)} %fusion.1), channel_id=1, source_target_pairs={{0,2},{1,3},{2,0},{3,1},{4,6},{5,7},{6,4},{7,5},{8,10},{9,11},{10,... | collective-permute-start | bytes 393224 | tf_op jit(solution)/shard_map/ppermute | solution.py:60
  161.0 0.8 slice_bitcast_fusion
  161.9 2.7 %collective-permute-done.21.got_ref = bf16[2,256,128]{2,1,0:T(8,128)(2,1)S(1)} collective-permute-done((bf16[2,256,128]{2,1,0:T(8,128)(2,1)S(1)}, bf16[2,256,128]{2,1,0:T(8,128)(2,1)S(1)}, u32[]{:S(2)}, u32[]{:S(2)}) %collective-permute-start.21) | collective-permute-done | bytes 131104 | tf_op jit(solution)/shard_map/ppermute | solution.py:60
  164.6 0.8 final_rows.1
  (75 shorter events, 0.5 us)
Async XLA Ops:
  0.6 35.3 %collective-permute-start.5 = (bf16[1024,256]{1,0:T(8,128)(2,1)}, bf16[1024,256]{1,0:T(8,128)(2,1)S(1)}, u32[]{:S(2)}, u32[]{:S(2)}) collective-permute-start(bf16[1024,256]{1,0:T(8,128)(2,1)} %param.10), channel_id=1, source_target_pairs={{104,0},{73,1},{42,2},{11,3},{108,4},{77,5},{46,6},{15,7},{0,8},{9... | collective-permute-start | bytes 1572872 | tf_op jit(solution)/shard_map/ppermute | solution.py:60
  3.8 32.2 %collective-permute-start.4 = (bf16[1024,256]{1,0:T(8,128)(2,1)}, bf16[1024,256]{1,0:T(8,128)(2,1)S(1)}, u32[]{:S(2)}, u32[]{:S(2)}) collective-permute-start(bf16[1024,256]{1,0:T(8,128)(2,1)} %param.10), channel_id=1, source_target_pairs={{110,0},{79,1},{44,2},{13,3},{106,4},{73,5},{40,6},{11,7},{4,8},{1... | collective-permute-start | bytes 1572872 | tf_op jit(solution)/shard_map/ppermute | solution.py:60
  8.9 31.3 %collective-permute-start.6 = (bf16[1024,256]{1,0:T(8,128)(2,1)}, bf16[1024,256]{1,0:T(8,128)(2,1)S(1)}, u32[]{:S(2)}, u32[]{:S(2)}) collective-permute-start(bf16[1024,256]{1,0:T(8,128)(2,1)} %param.10), channel_id=1, source_target_pairs={{0,0},{97,1},{66,2},{35,3},{4,4},{101,5},{70,6},{39,7},{8,8},{105,... | collective-permute-start | bytes 1572872 | tf_op jit(solution)/shard_map/ppermute | solution.py:60
  10.8 30.9 %collective-permute-start.1 = (bf16[1024,256]{1,0:T(8,128)(2,1)}, bf16[1024,256]{1,0:T(8,128)(2,1)S(1)}, u32[]{:S(2)}, u32[]{:S(2)}) collective-permute-start(bf16[1024,256]{1,0:T(8,128)(2,1)} %param.10), channel_id=1, source_target_pairs={{102,0},{69,1},{36,2},{7,3},{0,4},{99,5},{66,6},{33,7},{110,8},{77... | collective-permute-start | bytes 1572872 | tf_op jit(solution)/shard_map/ppermute | solution.py:60
  12.1 29.6 %collective-permute-start = (bf16[1024,256]{1,0:T(8,128)(2,1)}, bf16[1024,256]{1,0:T(8,128)(2,1)S(1)}, u32[]{:S(2)}, u32[]{:S(2)}) collective-permute-start(bf16[1024,256]{1,0:T(8,128)(2,1)} %param.10), channel_id=1, source_target_pairs={{120,0},{89,1},{58,2},{27,3},{124,4},{93,5},{62,6},{31,7},{112,8},... | collective-permute-start | bytes 1572872 | tf_op jit(solution)/shard_map/ppermute | solution.py:60
  36.0 4.3 %copy-start.4 = (bf16[1024,256]{1,0:T(8,128)(2,1)}, bf16[1024,256]{1,0:T(8,128)(2,1)S(1)}, u32[]{:S(2)}) copy-start(bf16[1024,256]{1,0:T(8,128)(2,1)S(1)} %collective-permute-done.5.refs_2_.refs_3_) | copy-start | bytes 1572868
  36.0 4.3 %copy-start = (bf16[1024,256]{1,0:T(8,128)(2,1)}, bf16[1024,256]{1,0:T(8,128)(2,1)S(1)}, u32[]{:S(2)}) copy-start(bf16[1024,256]{1,0:T(8,128)(2,1)S(1)} %collective-permute-done.4.refs_0_) | copy-start | bytes 1572868
  40.2 0.8 copy-start.6
  41.1 3.3 %copy-start.1 = (bf16[1024,256]{1,0:T(8,128)(2,1)S(1)}, bf16[1024,256]{1,0:T(8,128)(2,1)}, u32[]{:S(2)}) copy-start(bf16[1024,256]{1,0:T(8,128)(2,1)} %hold.3.refs_1_.refs_6_) | copy-start | bytes 1572868
  41.1 3.3 %copy-start.5 = (bf16[1024,256]{1,0:T(8,128)(2,1)S(1)}, bf16[1024,256]{1,0:T(8,128)(2,1)}, u32[]{:S(2)}) copy-start(bf16[1024,256]{1,0:T(8,128)(2,1)} %copy-done.4) | copy-start | bytes 1572868
  41.1 3.3 %copy-start.7 = (bf16[1024,256]{1,0:T(8,128)(2,1)S(1)}, bf16[1024,256]{1,0:T(8,128)(2,1)}, u32[]{:S(2)}) copy-start(bf16[1024,256]{1,0:T(8,128)(2,1)} %copy-done.6) | copy-start | bytes 1572868
  41.1 16.7 %collective-permute-start.7 = (bf16[1024,256]{1,0:T(8,128)(2,1)}, bf16[1024,256]{1,0:T(8,128)(2,1)S(1)}, u32[]{:S(2)}, u32[]{:S(2)}) collective-permute-start(bf16[1024,256]{1,0:T(8,128)(2,1)} %hold.3.refs_1_.refs_6_), channel_id=1, source_target_pairs={{120,0},{121,1},{122,2},{123,3},{124,4},{125,5},{126,6},{127,7},{1... | collective-permute-start | bytes 1572872 | tf_op jit(solution)/shard_map/ppermute | solution.py:60
  41.7 0.8 copy-start.8
  42.5 0.8 copy-start.2
  43.3 14.5 %collective-permute-start.3 = (bf16[1024,256]{1,0:T(8,128)(2,1)}, bf16[1024,256]{1,0:T(8,128)(2,1)S(1)}, u32[]{:S(2)}, u32[]{:S(2)}) collective-permute-start(bf16[1024,256]{1,0:T(8,128)(2,1)} %hold.2.refs_0_.refs_5_), channel_id=1, source_target_pairs={{8,0},{9,1},{10,2},{11,3},{12,4},{13,5},{14,6},{15,7},{0,8},{1,9},... | collective-permute-start | bytes 1572872 | tf_op jit(solution)/shard_map/ppermute | solution.py:60
  43.3 14.5 %collective-permute-start.2 = (bf16[1024,256]{1,0:T(8,128)(2,1)}, bf16[1024,256]{1,0:T(8,128)(2,1)}, u32[]{:S(2)}, u32[]{:S(2)}) collective-permute-start(bf16[1024,256]{1,0:T(8,128)(2,1)} %hold.2.refs_0_.refs_5_), channel_id=1, source_target_pairs={{4,0},{5,1},{6,2},{7,3},{0,4},{1,5},{2,6},{3,7},{12,8},{13,9},{14,... | collective-permute-start | bytes 1572872 | tf_op jit(solution)/shard_map/ppermute | solution.py:60
  44.4 1.1 copy-start.3
  45.4 1.0 copy-start.9
  46.5 17.5 %copy-start.16 = (s32[1024]{0:T(1024)S(1)}, s32[1024]{0:T(1024)}, u32[]{:S(2)}) copy-start(s32[1024]{0:T(1024)} %param.14) | copy-start | bytes 12292
  46.5 17.6 %copy-start.17 = (s32[1024]{0:T(1024)S(1)}, s32[1024]{0:T(1024)}, u32[]{:S(2)}) copy-start(s32[1024]{0:T(1024)} %param.15) | copy-start | bytes 12292
  46.5 32.9 %copy-start.10 = (bf16[256,256]{1,0:T(8,128)(2,1)S(1)}, bf16[256,256]{1,0:T(8,128)(2,1)}, u32[]{:S(2)}) copy-start(bf16[256,256]{1,0:T(8,128)(2,1)} %ws_ref.1) | copy-start | bytes 393220
  46.5 32.9 %copy-start.12 = (f32[256]{0:T(256)S(1)}, f32[256]{0:T(256)}, u32[]{:S(2)}) copy-start(f32[256]{0:T(256)} %param.19) | copy-start | bytes 3076
  53.5 10.6 %copy-start.14 = (bf16[1024,256]{1,0:T(8,128)(2,1)S(1)}, bf16[1024,256]{1,0:T(8,128)(2,1)}, u32[]{:S(2)}) copy-start(bf16[1024,256]{1,0:T(8,128)(2,1)} %param.10) | copy-start | bytes 1572868
  53.5 19.6 %copy-start.15 = (bf16[1024,256]{1,0:T(8,128)(2,1)S(1)}, bf16[1024,256]{1,0:T(8,128)(2,1)}, u32[]{:S(2)}) copy-start(bf16[1024,256]{1,0:T(8,128)(2,1)} %param.16) | copy-start | bytes 1572868
  53.5 25.9 %copy-start.11 = (bf16[256,256]{1,0:T(8,128)(2,1)S(1)}, bf16[256,256]{1,0:T(8,128)(2,1)}, u32[]{:S(2)}) copy-start(bf16[256,256]{1,0:T(8,128)(2,1)} %wn_ref.1) | copy-start | bytes 393220
  63.6 1.6 collective-permute-start.8
  65.3 14.1 %collective-permute-start.9 = (bf16[2,256,256]{2,1,0:T(8,128)(2,1)S(1)}, bf16[2,256,256]{2,1,0:T(8,128)(2,1)S(1)}, u32[]{:S(2)}, u32[]{:S(2)}) collective-permute-start(bf16[2,256,256]{2,1,0:T(8,128)(2,1)S(1)} %add_convert_fusion.own_ref), channel_id=1, source_target_pairs={{0,2},{1,3},{2,0},{3,1},{4,6},{5,7},{6,4},{7,5},{8,10},{9,11},{10,... | collective-permute-start | bytes 786440 | tf_op jit(solution)/shard_map/ppermute | solution.py:60
  81.0 2.0 %collective-permute-start.14 = (f32[136,256]{1,0:T(8,128)S(1)}, f32[136,256]{1,0:T(8,128)S(1)}, u32[]{:S(2)}, u32[]{:S(2)}) collective-permute-start(f32[136,256]{1,0:T(8,128)S(1)} %pad_maximum_fusion), channel_id=1, source_target_pairs={{0,1},{1,0},{2,3},{3,2},{4,5},{5,4},{6,7},{7,6},{8,9},{9,8},{10,11... | collective-permute-start | bytes 417800 | tf_op jit(solution)/shard_map/ppermute | solution.py:60
  82.0 1.5 collective-permute-start.10
  88.3 16.4 %collective-permute-start.13 = (bf16[8,256,128]{2,1,0:T(8,128)(2,1)S(1)}, bf16[8,256,128]{2,1,0:T(8,128)(2,1)S(1)}, u32[]{:S(2)}, u32[]{:S(2)}) collective-permute-start(bf16[8,256,128]{2,1,0:T(8,128)(2,1)S(1)} %get-tuple-element.23), channel_id=1, source_target_pairs={{0,8},{1,9},{2,10},{3,11},{4,12},{5,13},{6,14},{7,15},{8,0},{9,1},... | collective-permute-start | bytes 1572872 | tf_op jit(solution)/shard_map/ppermute | solution.py:60
  89.8 18.4 %collective-permute-start.17 = (bf16[8,256,128]{2,1,0:T(8,128)(2,1)}, bf16[8,256,128]{2,1,0:T(8,128)(2,1)S(1)}, u32[]{:S(2)}, u32[]{:S(2)}) collective-permute-start(bf16[8,256,128]{2,1,0:T(8,128)(2,1)} %get-tuple-element.25), channel_id=1, source_target_pairs={{0,4},{1,5},{2,6},{3,7},{4,0},{5,1},{6,2},{7,3},{8,12},{9,13},{10,... | collective-permute-start | bytes 1572872 | tf_op jit(solution)/shard_map/ppermute | solution.py:60
  91.4 13.3 %all-to-all-start = ((bf16[32,6,256]{2,1,0:T(8,128)(2,1)}), bf16[32,6,256]{2,1,0:T(8,128)(2,1)S(1)}, u32[]{:S(2)}, u32[]{:S(2)}) async-start(bf16[32,6,256]{2,1,0:T(8,128)(2,1)} %pad_maximum_fusion.2), calls=%async_computation | async-start | bytes 262144 | tf_op jit(solution)/shard_map/all_to_all | solution.py:364
  95.5 28.1 %collective-permute-start.12 = (bf16[8,256,128]{2,1,0:T(8,128)(2,1)}, bf16[8,256,128]{2,1,0:T(8,128)(2,1)S(1)}, u32[]{:S(2)}, u32[]{:S(2)}) collective-permute-start(bf16[8,256,128]{2,1,0:T(8,128)(2,1)} %get-tuple-element.22), channel_id=1, source_target_pairs={{0,8},{1,9},{2,10},{3,11},{4,12},{5,13},{6,14},{7,15},{8,0},{9,1},... | collective-permute-start | bytes 1572872 | tf_op jit(solution)/shard_map/ppermute | solution.py:60
  107.0 16.6 %collective-permute-start.15 = (bf16[8,256,128]{2,1,0:T(8,128)(2,1)S(1)}, bf16[8,256,128]{2,1,0:T(8,128)(2,1)S(1)}, u32[]{:S(2)}, u32[]{:S(2)}) collective-permute-start(bf16[8,256,128]{2,1,0:T(8,128)(2,1)S(1)} %backward_product.6), channel_id=1, source_target_pairs={{0,4},{1,5},{2,6},{3,7},{4,0},{5,1},{6,2},{7,3},{8,12},{9,13},{10,... | collective-permute-start | bytes 1572872 | tf_op jit(solution)/shard_map/ppermute | solution.py:60
  111.3 17.1 %collective-permute-start.18 = (bf16[8,256,128]{2,1,0:T(8,128)(2,1)}, bf16[8,256,128]{2,1,0:T(8,128)(2,1)}, u32[]{:S(2)}, u32[]{:S(2)}) collective-permute-start(bf16[8,256,128]{2,1,0:T(8,128)(2,1)} %backward_product.8), channel_id=1, source_target_pairs={{0,104},{1,105},{2,106},{3,107},{4,108},{5,109},{6,110},{7,111},{8... | collective-permute-start | bytes 1572872 | tf_op jit(solution)/shard_map/ppermute | solution.py:60
  113.7 22.5 %all-to-all-start.1 = ((f32[32,4,256]{2,1,0:T(4,128)}), f32[32,4,256]{2,1,0:T(4,128)S(1)}, u32[]{:S(2)}, u32[]{:S(2)}) async-start(f32[32,4,256]{2,1,0:T(4,128)} %broadcast_in_dim.11), calls=%async_computation.1 | async-start | bytes 262144 | tf_op jit(solution)/shard_map/all_to_all | solution.py:372
  117.9 31.0 %collective-permute-start.11 = (bf16[8,256,128]{2,1,0:T(8,128)(2,1)S(1)}, bf16[8,256,128]{2,1,0:T(8,128)(2,1)S(1)}, u32[]{:S(2)}, u32[]{:S(2)}) collective-permute-start(bf16[8,256,128]{2,1,0:T(8,128)(2,1)S(1)} %get-tuple-element.21), channel_id=1, source_target_pairs={{0,100},{1,71},{2,38},{3,5},{4,0},{5,99},{6,66},{7,33},{8,108},{9,... | collective-permute-start | bytes 1572872 | tf_op jit(solution)/shard_map/ppermute | solution.py:60
  126.0 22.9 %collective-permute-start.16 = (bf16[8,256,128]{2,1,0:T(8,128)(2,1)S(1)}, bf16[8,256,128]{2,1,0:T(8,128)(2,1)S(1)}, u32[]{:S(2)}, u32[]{:S(2)}) collective-permute-start(bf16[8,256,128]{2,1,0:T(8,128)(2,1)S(1)} %backward_product.7), channel_id=1, source_target_pairs={{0,120},{1,89},{2,58},{3,27},{4,124},{5,93},{6,62},{7,31},{8,112},... | collective-permute-start | bytes 1572872 | tf_op jit(solution)/shard_map/ppermute | solution.py:60
  131.8 17.1 %collective-permute-start.19 = (bf16[8,256,128]{2,1,0:T(8,128)(2,1)S(1)}, bf16[8,256,128]{2,1,0:T(8,128)(2,1)S(1)}, u32[]{:S(2)}, u32[]{:S(2)}) collective-permute-start(bf16[8,256,128]{2,1,0:T(8,128)(2,1)S(1)} %backward_product.9), channel_id=1, source_target_pairs={{0,0},{1,97},{2,66},{3,35},{4,4},{5,101},{6,70},{7,39},{8,8},{9,10... | collective-permute-start | bytes 1572872 | tf_op jit(solution)/shard_map/ppermute | solution.py:60
  136.2 0.7 copy-start.13
  136.9 8.0 %collective-permute-start.22 = (f32[128,256]{1,0:T(8,128)}, f32[128,256]{1,0:T(8,128)}, u32[]{:S(2)}, u32[]{:S(2)}) collective-permute-start(f32[128,256]{1,0:T(8,128)} %reshape.61), channel_id=1, source_target_pairs={{0,2},{1,3},{2,0},{3,1},{4,6},{5,7},{6,4},{7,5},{8,10},{9,11},{10,... | collective-permute-start | bytes 393224 | tf_op jit(solution)/shard_map/ppermute | solution.py:60
  146.6 3.2 %collective-permute-start.23 = (f32[2,128,256]{2,1,0:T(8,128)}, f32[2,128,256]{2,1,0:T(8,128)}, u32[]{:S(2)}, u32[]{:S(2)}) collective-permute-start(f32[2,128,256]{2,1,0:T(8,128)} %maximum_select_fusion), channel_id=1, source_target_pairs={{0,1},{1,0},{2,3},{3,2},{4,5},{5,4},{6,7},{7,6},{8,9},{9,8},{10,11... | collective-permute-start | bytes 786440 | tf_op jit(solution)/shard_map/ppermute | solution.py:60
  149.1 1.9 %collective-permute-start.20 = (bf16[2,2,256,128]{3,2,1,0:T(8,128)(2,1)S(1)}, bf16[2,2,256,128]{3,2,1,0:T(8,128)(2,1)S(1)}, u32[]{:S(2)}, u32[]{:S(2)}) collective-permute-start(bf16[2,2,256,128]{3,2,1,0:T(8,128)(2,1)S(1)} %get-tuple-element.27), channel_id=1, source_target_pairs={{0,1},{1,0},{2,3},{3,2},{4,5},{5,4},{6,7},{7,6},{8,9},{9,8},{10,11... | collective-permute-start | bytes 786440 | tf_op jit(solution)/shard_map/ppermute | solution.py:60
  151.1 13.5 %collective-permute-start.21 = (bf16[2,256,128]{2,1,0:T(8,128)(2,1)S(1)}, bf16[2,256,128]{2,1,0:T(8,128)(2,1)S(1)}, u32[]{:S(2)}, u32[]{:S(2)}) collective-permute-start(bf16[2,256,128]{2,1,0:T(8,128)(2,1)S(1)} %fusion.1), channel_id=1, source_target_pairs={{0,2},{1,3},{2,0},{3,1},{4,6},{5,7},{6,4},{7,5},{8,10},{9,11},{10,... | collective-permute-start | bytes 393224 | tf_op jit(solution)/shard_map/ppermute | solution.py:60

commit v8 on v7

--- a/solution.py
+++ b/solution.py
@@ -22,7 +22,7 @@
 GROUPS = ((6, 3, 1, 2, 0), (7, 4, 5))
 HELD = ((6, (1,)), (3, (2, 0)))
 BACK = ((5, 3, 4, 1), (7,), (2,), (6,), (0,))
-LATER = (7,)
+LATER = (2,)
 
 
 def index_of(y, x, zl, zh, core):
@@ -329,6 +329,27 @@
         input_output_aliases={0: 0},
         name="hold",
     )(along, *after)
+
+
+def merge_body(zh_ref, kept_ref, got_ref, mine_ref, sent_ref):
+    zh = zh_ref[0]
+    mine_ref[...] = kept_ref[zh] + got_ref[zh].astype(jnp.float32)
+    sent = kept_ref[1 - zh] + got_ref[1 - zh].astype(jnp.float32)
+    sent_ref[...] = sent.astype(jnp.bfloat16)
+
+
+def merge_call(zh, kept, got):
+    return pl.pallas_call(
+        merge_body,
+        out_shape=(
+            jax.ShapeDtypeStruct((2, F, BS), jnp.float32),
+            jax.ShapeDtypeStruct((2, F, BS), jnp.bfloat16),
+        ),
+        in_specs=[SMEM, WHOLE, WHOLE],
+        out_specs=(WHOLE, WHOLE),
+        compiler_params=params(SMALL),
+        name="merge_products",
+    )(zh, kept, got)
 
 
 def final_body(kept_ref, got_ref, term_ref, out_ref):
@@ -455,9 +476,8 @@
             else:
                 extra.setdefault(k ^ BACK_PLAN[k], []).append(moved)
     kept, away = split_call(core[None], list(arrived.values()))
-    chip = kept + send(away, flip_pairs(dcore=1)).astype(jnp.float32)
-    got = send(pick(chip, 1 - zh).astype(jnp.bfloat16), flip_pairs(dzh=1))
-    grad_features = final_call(pick(chip, zh), got, own_term)
+    mine, sent = merge_call(zh[None], kept, send(away, flip_pairs(dcore=1)))
+    grad_features = final_call(mine, send(sent, flip_pairs(dzh=1)), own_term)
     grad_self, grad_neigh, grad_bias = weight_grads(
         parts, zh, core, rows * lax.axis_size("blk")
     )

time: 166 us -> 164 us (0.988)
  other arithmetic: 4.48 us -> 2.39 us
    all_to_all x1, waiting for transfers between devices: 7.91 us -> 0.01 us  [weight_shares(): return lax.all_to_all(jnp.concatenate([rows, bias_rows], 1), 'blk', 0, 0)]
    ppermute x24, waiting for transfers between devices: 28.1 us -> 34.9 us  [send(): return lax.ppermute(value, AXES, pairs)]
  transfers between devices with their start and end apart: 26 -> 26, of which waited for: 11 -> 12; matrix products, arithmetic and copies ran while one was open for 6% -> 4% of each run, Pallas kernels for 23% -> 26%
where the time goes in v8:
time: 164 us; the launch traced here: 162 us
  starting transfers between devices  64.6 us (39%)
  Pallas kernels  50.4 us (31%)
  waiting for transfers between devices  34.9 us (21%)
  local copies, waits for them, and re-layouts  8.98 us (5%)
  other arithmetic  2.39 us (1%)
    ppermute x24, starting transfers between devices, send(): return lax.ppermute(value, AXES, pairs)  55.7 us
    ppermute x24, waiting for transfers between devices, send(): return lax.ppermute(value, AXES, pairs)  34.9 us
    pallas_call x1, Pallas kernels, assemble_call(): pl.pallas_call(functools.partial(assemble_body, n), out_shape=jax.ShapeDt...  19.2 us
    pallas_call x5, Pallas kernels, backward_call(): pl.pallas_call(functools.partial(backward_body, tuple(places), added), ou...  15.9 us
    pallas_call x2, Pallas kernels, forward_call(): pl.pallas_call(functools.partial(forward_body, n, start, first, last), ou...  12.8 us
    unnamed x38, local copies, waits for them, and re-layouts  6.23 us
    all_to_all x1, starting transfers between devices, weight_grads(): half = lax.all_to_all(spread, 'blk', 0, 0).reshape(F // 2, F)  4.82 us
    all_to_all x1, starting transfers between devices, weight_shares(): return lax.all_to_all(jnp.concatenate([rows, bias_rows], 1), 'blk', 0, 0)  4.05 us
  transfers between devices with their start and end apart: 26, of which 12 were waited for; matrix products, arithmetic and copies ran while one was open for 4% of the time, Pallas kernels for 26%

profile of v8, /device:TPU:1, one launch (start us, length us, event | category | flops | bytes accessed | tf_op | source)
XLA Modules:
  0.0 162.4 jit_solution(17897660003285237727)
XLA Ops:
  0.6 3.1 %collective-permute-start.5 = (bf16[1024,256]{1,0:T(8,128)(2,1)}, bf16[1024,256]{1,0:T(8,128)(2,1)S(1)}, u32[]{:S(2)}, u32[]{:S(2)}) collective-permute-start(bf16[1024,256]{1,0:T(8,128)(2,1)} %param.10), channel_id=1, source_target_pairs={{104,0},{73,1},{42,2},{11,3},{108,4},{77,5},{46,6},{15,7},{0,8},{9... | collective-permute-start | bytes 1572872 | tf_op jit(solution)/shard_map/ppermute | solution.py:60
  3.8 5.2 %collective-permute-start.4 = (bf16[1024,256]{1,0:T(8,128)(2,1)}, bf16[1024,256]{1,0:T(8,128)(2,1)S(1)}, u32[]{:S(2)}, u32[]{:S(2)}) collective-permute-start(bf16[1024,256]{1,0:T(8,128)(2,1)} %param.10), channel_id=1, source_target_pairs={{110,0},{79,1},{44,2},{13,3},{106,4},{73,5},{40,6},{11,7},{4,8},{1... | collective-permute-start | bytes 1572872 | tf_op jit(solution)/shard_map/ppermute | solution.py:60
  8.9 1.9 %collective-permute-start.6 = (bf16[1024,256]{1,0:T(8,128)(2,1)}, bf16[1024,256]{1,0:T(8,128)(2,1)S(1)}, u32[]{:S(2)}, u32[]{:S(2)}) collective-permute-start(bf16[1024,256]{1,0:T(8,128)(2,1)} %param.10), channel_id=1, source_target_pairs={{0,0},{97,1},{66,2},{35,3},{4,4},{101,5},{70,6},{39,7},{8,8},{105,... | collective-permute-start | bytes 1572872 | tf_op jit(solution)/shard_map/ppermute | solution.py:60
  10.8 1.3 collective-permute-start.1
  12.1 2.7 %collective-permute-start = (bf16[1024,256]{1,0:T(8,128)(2,1)}, bf16[1024,256]{1,0:T(8,128)(2,1)S(1)}, u32[]{:S(2)}, u32[]{:S(2)}) collective-permute-start(bf16[1024,256]{1,0:T(8,128)(2,1)} %param.10), channel_id=1, source_target_pairs={{120,0},{89,1},{58,2},{27,3},{124,4},{93,5},{62,6},{31,7},{112,8},... | collective-permute-start | bytes 1572872 | tf_op jit(solution)/shard_map/ppermute | solution.py:60
  14.9 0.8 reshape.52.counts_ref
  15.6 0.9 copy.22
  16.5 0.1 reshape.51.cols_ref
  16.7 0.1 stack.42.sel_ref
  16.8 19.2 %assemble_adjacency.1.refs_1_.adj_ref = bf16[8,8,1024,128]{3,2,1,0:T(8,128)(2,1)} custom-call(s32[8]{0:T(128)S(1)} %stack.42.sel_ref, s32[384]{0:T(512)S(1)} %reshape.51.cols_ref, s32[64]{0:T(128)S(1)} %reshape.52.counts_ref, bf16[8,8,6,128,128]{4,3,2,1,0:T(8,128)(2,1)} %tiles_ref.1), custom_call_target="tpu_custom_call" | custom-call | flops 4294967296 | bytes 25165824 | tf_op jit(solution)/shard_map/assemble_adjacency/pallas_call | solution.py:117
  36.0 4.2 %collective-permute-done.6.refs_3_.refs_4_ = bf16[1024,256]{1,0:T(8,128)(2,1)S(1)} collective-permute-done((bf16[1024,256]{1,0:T(8,128)(2,1)}, bf16[1024,256]{1,0:T(8,128)(2,1)S(1)}, u32[]{:S(2)}, u32[]{:S(2)}) %collective-permute-start.6) | collective-permute-done | bytes 524320 | tf_op jit(solution)/shard_map/ppermute | solution.py:60
  40.3 0.8 copy-done.6
  41.1 0.7 collective-permute-done.1.refs_2_
  41.7 0.8 copy-done.8
  42.6 0.8 copy-done.2
  43.4 1.0 collective-permute-start.2
  44.4 1.1 copy-done.3
  45.4 1.0 copy-done.9
  46.5 7.0 %forward_product.2.refs_3_ = f32[1024,256]{1,0:T(8,128)S(1)} custom-call(s32[1]{0:T(128)} %bitcast.1.core_ref, bf16[8,8,1024,128]{3,2,1,0:T(8,128)(2,1)} %assemble_adjacency.1.refs_1_.adj_ref, bf16[1024,256]{1,0:T(8,128)(2,1)S(1)} %copy-done.3, bf16[1024,256]{1,0:T(8,128)(2,1)S(1)} %copy-done.1, bf16[1024,256]{1,0:T(8,128)(2,1)S(1)} %copy-done.9, ...), custom_call_target="tpu_custom_call" | custom-call | flops 2684354560 | bytes 15728640 | tf_op jit(solution)/shard_map/forward_product/pallas_call | solution.py:186
  53.5 4.3 %collective-permute-done.7.refs_2_ = bf16[1024,256]{1,0:T(8,128)(2,1)S(1)} collective-permute-done((bf16[1024,256]{1,0:T(8,128)(2,1)}, bf16[1024,256]{1,0:T(8,128)(2,1)S(1)}, u32[]{:S(2)}, u32[]{:S(2)}) %collective-permute-start.7) | collective-permute-done | bytes 524320 | tf_op jit(solution)/shard_map/ppermute | solution.py:60
  57.8 5.8 %forward_product.3 = (f32[2,256,256]{2,1,0:T(8,128)S(1)}, bf16[2,256,256]{2,1,0:T(8,128)(2,1)S(1)}) custom-call(s32[1]{0:T(128)} %bitcast.1.core_ref, bf16[8,8,1024,128]{3,2,1,0:T(8,128)(2,1)} %assemble_adjacency.1.refs_1_.adj_ref, bf16[1024,256]{1,0:T(8,128)(2,1)} %collective-permute-done.2.refs_0_, bf16[1024,256]{1,0:T(8,128)(2,1)S(1)} %collective-permute-done.3.refs_1_, ...), custom_call_target="tpu_custom_call" | custom-call | flops 1610612736 | bytes 9437184 | tf_op jit(solution)/shard_map/forward_product/pallas_call | solution.py:186
  63.6 0.4 collective-permute-start.8
  64.1 1.1 collective-permute-done.8
  65.2 0.1 add_convert_fusion.own_ref
  65.3 7.7 %collective-permute-start.9 = (bf16[2,256,256]{2,1,0:T(8,128)(2,1)S(1)}, bf16[2,256,256]{2,1,0:T(8,128)(2,1)S(1)}, u32[]{:S(2)}, u32[]{:S(2)}) collective-permute-start(bf16[2,256,256]{2,1,0:T(8,128)(2,1)S(1)} %add_convert_fusion.own_ref), channel_id=1, source_target_pairs={{0,2},{1,3},{2,0},{3,1},{4,6},{5,7},{6,4},{7,5},{8,10},{9,11},{10,... | collective-permute-start | bytes 786440 | tf_op jit(solution)/shard_map/ppermute | solution.py:60
  73.0 0.1 bitcast_multiply_fusion.cot_ref
  73.2 6.2 %collective-permute-done.9.got_ref = bf16[2,256,256]{2,1,0:T(8,128)(2,1)S(1)} collective-permute-done((bf16[2,256,256]{2,1,0:T(8,128)(2,1)S(1)}, bf16[2,256,256]{2,1,0:T(8,128)(2,1)S(1)}, u32[]{:S(2)}, u32[]{:S(2)}) %collective-permute-start.9) | collective-permute-done | bytes 262176 | tf_op jit(solution)/shard_map/ppermute | solution.py:60
  79.4 1.6 dense_rows.1
  81.0 0.9 collective-permute-start.10
  81.9 0.3 collective-permute-start.17
  82.2 0.8 collective-permute-done.10.got_ref
  83.0 4.8 %backward_product.5 = (bf16[8,256,128]{2,1,0:T(8,128)(2,1)S(1)}, bf16[8,256,128]{2,1,0:T(8,128)(2,1)}, bf16[8,256,128]{2,1,0:T(8,128)(2,1)}, bf16[8,256,128]{2,1,0:T(8,128)(2,1)S(1)}) custom-call(s32[1]{0:T(128)} %bitcast.1.core_ref, bf16[8,8,1024,128]{3,2,1,0:T(8,128)(2,1)} %assemble_adjacency.1.refs_1_.adj_ref, ...), custom_call_target="tpu_custom_call" | custom-call | flops 2147483648 | bytes 12582912 | tf_op jit(solution)/shard_map/backward_product/pallas_call | solution.py:277
  87.8 0.8 copy-done.13
  88.6 1.5 collective-permute-start.13
  90.1 0.9 collective-permute-start.16
  91.1 0.7 pad_maximum_fusion.2
  91.8 4.1 %all-to-all-start = ((bf16[32,6,256]{2,1,0:T(8,128)(2,1)}), bf16[32,6,256]{2,1,0:T(8,128)(2,1)S(1)}, u32[]{:S(2)}, u32[]{:S(2)}) async-start(bf16[32,6,256]{2,1,0:T(8,128)(2,1)} %pad_maximum_fusion.2), calls=%async_computation | async-start | bytes 262144 | tf_op jit(solution)/shard_map/all_to_all | solution.py:385
  95.9 1.3 collective-permute-start.12
  97.2 4.6 %collective-permute-done.13.rest_0_ = bf16[8,256,128]{2,1,0:T(8,128)(2,1)S(1)} collective-permute-done((bf16[8,256,128]{2,1,0:T(8,128)(2,1)S(1)}, bf16[8,256,128]{2,1,0:T(8,128)(2,1)S(1)}, u32[]{:S(2)}, u32[]{:S(2)}) %collective-permute-start.13) | collective-permute-done | bytes 524320 | tf_op jit(solution)/shard_map/ppermute | solution.py:60
  101.7 3.1 %backward_product.6 = bf16[8,256,128]{2,1,0:T(8,128)(2,1)} custom-call(s32[1]{0:T(128)} %bitcast.1.core_ref, bf16[8,8,1024,128]{3,2,1,0:T(8,128)(2,1)} %assemble_adjacency.1.refs_1_.adj_ref, bf16[2,256,256]{2,1,0:T(8,128)(2,1)S(1)} %get-tuple-element.22.own_ref, bf16[2,256,256]{2,1,0:T(8,128)(2,1)S(1)} %collective-permute-done.10.got_ref, ...), custom_call_target="tpu_custom_call" | custom-call | flops 536870912 | bytes 3145728 | tf_op jit(solution)/shard_map/backward_product/pallas_call | solution.py:277
  104.9 0.9 collective-permute-start.14
  105.8 2.3 %backward_product.8 = bf16[8,256,128]{2,1,0:T(8,128)(2,1)S(1)} custom-call(s32[1]{0:T(128)} %bitcast.1.core_ref, bf16[8,8,1024,128]{3,2,1,0:T(8,128)(2,1)} %assemble_adjacency.1.refs_1_.adj_ref, bf16[2,256,256]{2,1,0:T(8,128)(2,1)S(1)} %get-tuple-element.22.own_ref, bf16[2,256,256]{2,1,0:T(8,128)(2,1)S(1)} %collective-permute-done.10.got_ref, ...), custom_call_target="tpu_custom_call" | custom-call | flops 536870912 | bytes 3145728 | tf_op jit(solution)/shard_map/backward_product/pallas_call | solution.py:277
  108.1 0.9 collective-permute-start.18
  109.0 0.7 broadcast_in_dim.14
  109.7 4.8 %all-to-all-start.1 = ((f32[32,4,256]{2,1,0:T(4,128)}), f32[32,4,256]{2,1,0:T(4,128)S(1)}, u32[]{:S(2)}, u32[]{:S(2)}) async-start(f32[32,4,256]{2,1,0:T(4,128)} %broadcast_in_dim.14), calls=%async_computation.1 | async-start | bytes 262144 | tf_op jit(solution)/shard_map/all_to_all | solution.py:393
  114.5 5.5 %collective-permute-start.11 = (bf16[8,256,128]{2,1,0:T(8,128)(2,1)}, bf16[8,256,128]{2,1,0:T(8,128)(2,1)S(1)}, u32[]{:S(2)}, u32[]{:S(2)}) collective-permute-start(bf16[8,256,128]{2,1,0:T(8,128)(2,1)} %copy-done.13), channel_id=1, source_target_pairs={{0,100},{1,71},{2,38},{3,5},{4,0},{5,99},{6,66},{7,33},{8,108},{9,... | collective-permute-start | bytes 1572872 | tf_op jit(solution)/shard_map/ppermute | solution.py:60
  120.0 2.3 %backward_product.7 = bf16[8,256,128]{2,1,0:T(8,128)(2,1)S(1)} custom-call(s32[1]{0:T(128)} %bitcast.1.core_ref, bf16[8,8,1024,128]{3,2,1,0:T(8,128)(2,1)} %assemble_adjacency.1.refs_1_.adj_ref, bf16[2,256,256]{2,1,0:T(8,128)(2,1)S(1)} %get-tuple-element.22.own_ref, bf16[2,256,256]{2,1,0:T(8,128)(2,1)S(1)} %collective-permute-done.10.got_ref, ...), custom_call_target="tpu_custom_call" | custom-call | flops 536870912 | bytes 3145728 | tf_op jit(solution)/shard_map/backward_product/pallas_call | solution.py:277
  122.4 2.5 %collective-permute-start.15 = (bf16[8,256,128]{2,1,0:T(8,128)(2,1)S(1)}, bf16[8,256,128]{2,1,0:T(8,128)(2,1)S(1)}, u32[]{:S(2)}, u32[]{:S(2)}) collective-permute-start(bf16[8,256,128]{2,1,0:T(8,128)(2,1)S(1)} %backward_product.7), channel_id=1, source_target_pairs={{0,120},{1,89},{2,58},{3,27},{4,124},{5,93},{6,62},{7,31},{8,112},... | collective-permute-start | bytes 1572872 | tf_op jit(solution)/shard_map/ppermute | solution.py:60
  124.8 1.2 collective-permute-done.18.rest_0_
  126.0 3.4 %backward_product.9 = bf16[8,256,128]{2,1,0:T(8,128)(2,1)S(1)} custom-call(s32[1]{0:T(128)} %bitcast.1.core_ref, bf16[8,8,1024,128]{3,2,1,0:T(8,128)(2,1)} %assemble_adjacency.1.refs_1_.adj_ref, bf16[2,256,256]{2,1,0:T(8,128)(2,1)S(1)} %get-tuple-element.22.own_ref, bf16[2,256,256]{2,1,0:T(8,128)(2,1)S(1)} %collective-permute-done.10.got_ref, ...), custom_call_target="tpu_custom_call" | custom-call | flops 536870912 | bytes 3145728 | tf_op jit(solution)/shard_map/backward_product/pallas_call | solution.py:277
  129.4 3.2 %collective-permute-start.19 = (bf16[8,256,128]{2,1,0:T(8,128)(2,1)S(1)}, bf16[8,256,128]{2,1,0:T(8,128)(2,1)S(1)}, u32[]{:S(2)}, u32[]{:S(2)}) collective-permute-start(bf16[8,256,128]{2,1,0:T(8,128)(2,1)S(1)} %backward_product.9), channel_id=1, source_target_pairs={{0,0},{1,97},{2,66},{3,35},{4,4},{5,101},{6,70},{7,39},{8,8},{9,10... | collective-permute-start | bytes 1572872 | tf_op jit(solution)/shard_map/ppermute | solution.py:60
  132.6 1.7 %collective-permute-start.22 = (f32[128,256]{1,0:T(8,128)S(1)}, f32[128,256]{1,0:T(8,128)S(1)}, u32[]{:S(2)}, u32[]{:S(2)}) collective-permute-start(f32[128,256]{1,0:T(8,128)S(1)} %reshape.60), channel_id=1, source_target_pairs={{0,2},{1,3},{2,0},{3,1},{4,6},{5,7},{6,4},{7,5},{8,10},{9,11},{10,... | collective-permute-start | bytes 393224 | tf_op jit(solution)/shard_map/ppermute | solution.py:60
  134.4 4.3 %collective-permute-done.22 = f32[128,256]{1,0:T(8,128)S(1)} collective-permute-done((f32[128,256]{1,0:T(8,128)S(1)}, f32[128,256]{1,0:T(8,128)S(1)}, u32[]{:S(2)}, u32[]{:S(2)}) %collective-permute-start.22) | collective-permute-done | bytes 131104 | tf_op jit(solution)/shard_map/ppermute | solution.py:60
  138.6 0.7 maximum_select_fusion
  139.4 1.5 collective-permute-start.23
  140.9 0.6 fusion.1
  141.5 3.4 %collective-permute-done.19.rest_2_ = bf16[8,256,128]{2,1,0:T(8,128)(2,1)S(1)} collective-permute-done((bf16[8,256,128]{2,1,0:T(8,128)(2,1)S(1)}, bf16[8,256,128]{2,1,0:T(8,128)(2,1)S(1)}, u32[]{:S(2)}, u32[]{:S(2)}) %collective-permute-start.19) | collective-permute-done | bytes 524320 | tf_op jit(solution)/shard_map/ppermute | solution.py:60
  144.9 0.2 split_products.1
  145.0 0.1 collective-permute-start.20
  145.2 1.4 collective-permute-done.20.got_ref
  146.7 11.3 %collective-permute-start.21 = (bf16[2,256,128]{2,1,0:T(8,128)(2,1)S(1)}, bf16[2,256,128]{2,1,0:T(8,128)(2,1)S(1)}, u32[]{:S(2)}, u32[]{:S(2)}) collective-permute-start(bf16[2,256,128]{2,1,0:T(8,128)(2,1)S(1)} %get-tuple-element.31), channel_id=1, source_target_pairs={{0,2},{1,3},{2,0},{3,1},{4,6},{5,7},{6,4},{7,5},{8,10},{9,11},{10,... | collective-permute-start | bytes 393224 | tf_op jit(solution)/shard_map/ppermute | solution.py:60
  158.0 0.8 slice_bitcast_fusion
  158.8 2.7 %collective-permute-done.21.got_ref = bf16[2,256,128]{2,1,0:T(8,128)(2,1)S(1)} collective-permute-done((bf16[2,256,128]{2,1,0:T(8,128)(2,1)S(1)}, bf16[2,256,128]{2,1,0:T(8,128)(2,1)S(1)}, u32[]{:S(2)}, u32[]{:S(2)}) %collective-permute-start.21) | collective-permute-done | bytes 131104 | tf_op jit(solution)/shard_map/ppermute | solution.py:60
  161.6 0.8 final_rows.1
  (73 shorter events, 0.6 us)
Async XLA Ops:
  0.6 35.3 %collective-permute-start.5 = (bf16[1024,256]{1,0:T(8,128)(2,1)}, bf16[1024,256]{1,0:T(8,128)(2,1)S(1)}, u32[]{:S(2)}, u32[]{:S(2)}) collective-permute-start(bf16[1024,256]{1,0:T(8,128)(2,1)} %param.10), channel_id=1, source_target_pairs={{104,0},{73,1},{42,2},{11,3},{108,4},{77,5},{46,6},{15,7},{0,8},{9... | collective-permute-start | bytes 1572872 | tf_op jit(solution)/shard_map/ppermute | solution.py:60
  3.8 32.2 %collective-permute-start.4 = (bf16[1024,256]{1,0:T(8,128)(2,1)}, bf16[1024,256]{1,0:T(8,128)(2,1)S(1)}, u32[]{:S(2)}, u32[]{:S(2)}) collective-permute-start(bf16[1024,256]{1,0:T(8,128)(2,1)} %param.10), channel_id=1, source_target_pairs={{110,0},{79,1},{44,2},{13,3},{106,4},{73,5},{40,6},{11,7},{4,8},{1... | collective-permute-start | bytes 1572872 | tf_op jit(solution)/shard_map/ppermute | solution.py:60
  8.9 31.3 %collective-permute-start.6 = (bf16[1024,256]{1,0:T(8,128)(2,1)}, bf16[1024,256]{1,0:T(8,128)(2,1)S(1)}, u32[]{:S(2)}, u32[]{:S(2)}) collective-permute-start(bf16[1024,256]{1,0:T(8,128)(2,1)} %param.10), channel_id=1, source_target_pairs={{0,0},{97,1},{66,2},{35,3},{4,4},{101,5},{70,6},{39,7},{8,8},{105,... | collective-permute-start | bytes 1572872 | tf_op jit(solution)/shard_map/ppermute | solution.py:60
  10.8 30.9 %collective-permute-start.1 = (bf16[1024,256]{1,0:T(8,128)(2,1)}, bf16[1024,256]{1,0:T(8,128)(2,1)S(1)}, u32[]{:S(2)}, u32[]{:S(2)}) collective-permute-start(bf16[1024,256]{1,0:T(8,128)(2,1)} %param.10), channel_id=1, source_target_pairs={{102,0},{69,1},{36,2},{7,3},{0,4},{99,5},{66,6},{33,7},{110,8},{77... | collective-permute-start | bytes 1572872 | tf_op jit(solution)/shard_map/ppermute | solution.py:60
  12.1 29.6 %collective-permute-start = (bf16[1024,256]{1,0:T(8,128)(2,1)}, bf16[1024,256]{1,0:T(8,128)(2,1)S(1)}, u32[]{:S(2)}, u32[]{:S(2)}) collective-permute-start(bf16[1024,256]{1,0:T(8,128)(2,1)} %param.10), channel_id=1, source_target_pairs={{120,0},{89,1},{58,2},{27,3},{124,4},{93,5},{62,6},{31,7},{112,8},... | collective-permute-start | bytes 1572872 | tf_op jit(solution)/shard_map/ppermute | solution.py:60
  36.0 4.3 %copy-start.4 = (bf16[1024,256]{1,0:T(8,128)(2,1)}, bf16[1024,256]{1,0:T(8,128)(2,1)S(1)}, u32[]{:S(2)}) copy-start(bf16[1024,256]{1,0:T(8,128)(2,1)S(1)} %collective-permute-done.5.refs_2_.refs_3_) | copy-start | bytes 1572868
  36.0 4.3 %copy-start = (bf16[1024,256]{1,0:T(8,128)(2,1)}, bf16[1024,256]{1,0:T(8,128)(2,1)S(1)}, u32[]{:S(2)}) copy-start(bf16[1024,256]{1,0:T(8,128)(2,1)S(1)} %collective-permute-done.4.refs_0_) | copy-start | bytes 1572868
  40.2 0.8 copy-start.6
  41.1 3.3 %copy-start.1 = (bf16[1024,256]{1,0:T(8,128)(2,1)S(1)}, bf16[1024,256]{1,0:T(8,128)(2,1)}, u32[]{:S(2)}) copy-start(bf16[1024,256]{1,0:T(8,128)(2,1)} %hold.3.refs_1_.refs_6_) | copy-start | bytes 1572868
  41.1 3.3 %copy-start.5 = (bf16[1024,256]{1,0:T(8,128)(2,1)S(1)}, bf16[1024,256]{1,0:T(8,128)(2,1)}, u32[]{:S(2)}) copy-start(bf16[1024,256]{1,0:T(8,128)(2,1)} %copy-done.4) | copy-start | bytes 1572868
  41.1 3.3 %copy-start.7 = (bf16[1024,256]{1,0:T(8,128)(2,1)S(1)}, bf16[1024,256]{1,0:T(8,128)(2,1)}, u32[]{:S(2)}) copy-start(bf16[1024,256]{1,0:T(8,128)(2,1)} %copy-done.6) | copy-start | bytes 1572868
  41.1 16.7 %collective-permute-start.7 = (bf16[1024,256]{1,0:T(8,128)(2,1)}, bf16[1024,256]{1,0:T(8,128)(2,1)S(1)}, u32[]{:S(2)}, u32[]{:S(2)}) collective-permute-start(bf16[1024,256]{1,0:T(8,128)(2,1)} %hold.3.refs_1_.refs_6_), channel_id=1, source_target_pairs={{120,0},{121,1},{122,2},{123,3},{124,4},{125,5},{126,6},{127,7},{1... | collective-permute-start | bytes 1572872 | tf_op jit(solution)/shard_map/ppermute | solution.py:60
  41.7 0.8 copy-start.8
  42.6 0.8 copy-start.2
  43.3 14.4 %collective-permute-start.3 = (bf16[1024,256]{1,0:T(8,128)(2,1)}, bf16[1024,256]{1,0:T(8,128)(2,1)S(1)}, u32[]{:S(2)}, u32[]{:S(2)}) collective-permute-start(bf16[1024,256]{1,0:T(8,128)(2,1)} %hold.2.refs_0_.refs_5_), channel_id=1, source_target_pairs={{8,0},{9,1},{10,2},{11,3},{12,4},{13,5},{14,6},{15,7},{0,8},{1,9},... | collective-permute-start | bytes 1572872 | tf_op jit(solution)/shard_map/ppermute | solution.py:60
  43.4 14.4 %collective-permute-start.2 = (bf16[1024,256]{1,0:T(8,128)(2,1)}, bf16[1024,256]{1,0:T(8,128)(2,1)}, u32[]{:S(2)}, u32[]{:S(2)}) collective-permute-start(bf16[1024,256]{1,0:T(8,128)(2,1)} %hold.2.refs_0_.refs_5_), channel_id=1, source_target_pairs={{4,0},{5,1},{6,2},{7,3},{0,4},{1,5},{2,6},{3,7},{12,8},{13,9},{14,... | collective-permute-start | bytes 1572872 | tf_op jit(solution)/shard_map/ppermute | solution.py:60
  44.4 1.1 copy-start.3
  45.4 1.0 copy-start.9
  46.5 17.5 %copy-start.16 = (s32[1024]{0:T(1024)S(1)}, s32[1024]{0:T(1024)}, u32[]{:S(2)}) copy-start(s32[1024]{0:T(1024)} %param.14) | copy-start | bytes 12292
  46.5 17.5 %copy-start.17 = (s32[1024]{0:T(1024)S(1)}, s32[1024]{0:T(1024)}, u32[]{:S(2)}) copy-start(s32[1024]{0:T(1024)} %param.15) | copy-start | bytes 12292
  46.5 32.9 %copy-start.10 = (bf16[256,256]{1,0:T(8,128)(2,1)S(1)}, bf16[256,256]{1,0:T(8,128)(2,1)}, u32[]{:S(2)}) copy-start(bf16[256,256]{1,0:T(8,128)(2,1)} %ws_ref.1) | copy-start | bytes 393220
  46.5 32.9 %copy-start.12 = (f32[256]{0:T(256)S(1)}, f32[256]{0:T(256)}, u32[]{:S(2)}) copy-start(f32[256]{0:T(256)} %param.19) | copy-start | bytes 3076
  53.5 10.6 %copy-start.14 = (bf16[1024,256]{1,0:T(8,128)(2,1)S(1)}, bf16[1024,256]{1,0:T(8,128)(2,1)}, u32[]{:S(2)}) copy-start(bf16[1024,256]{1,0:T(8,128)(2,1)} %param.10) | copy-start | bytes 1572868
  53.5 19.6 %copy-start.15 = (bf16[1024,256]{1,0:T(8,128)(2,1)S(1)}, bf16[1024,256]{1,0:T(8,128)(2,1)}, u32[]{:S(2)}) copy-start(bf16[1024,256]{1,0:T(8,128)(2,1)} %param.16) | copy-start | bytes 1572868
  53.5 25.9 %copy-start.11 = (bf16[256,256]{1,0:T(8,128)(2,1)S(1)}, bf16[256,256]{1,0:T(8,128)(2,1)}, u32[]{:S(2)}) copy-start(bf16[256,256]{1,0:T(8,128)(2,1)} %wn_ref.1) | copy-start | bytes 393220
  63.6 1.6 collective-permute-start.8
  65.3 14.1 %collective-permute-start.9 = (bf16[2,256,256]{2,1,0:T(8,128)(2,1)S(1)}, bf16[2,256,256]{2,1,0:T(8,128)(2,1)S(1)}, u32[]{:S(2)}, u32[]{:S(2)}) collective-permute-start(bf16[2,256,256]{2,1,0:T(8,128)(2,1)S(1)} %add_convert_fusion.own_ref), channel_id=1, source_target_pairs={{0,2},{1,3},{2,0},{3,1},{4,6},{5,7},{6,4},{7,5},{8,10},{9,11},{10,... | collective-permute-start | bytes 786440 | tf_op jit(solution)/shard_map/ppermute | solution.py:60
  81.0 2.0 %collective-permute-start.10 = (bf16[2,256,256]{2,1,0:T(8,128)(2,1)S(1)}, bf16[2,256,256]{2,1,0:T(8,128)(2,1)S(1)}, u32[]{:S(2)}, u32[]{:S(2)}) collective-permute-start(bf16[2,256,256]{2,1,0:T(8,128)(2,1)S(1)} %get-tuple-element.22.own_ref), channel_id=1, source_target_pairs={{0,1},{1,0},{2,3},{3,2},{4,5},{5,4},{6,7},{7,6},{8,9},{9,8},{10,11... | collective-permute-start | bytes 786440 | tf_op jit(solution)/shard_map/ppermute | solution.py:60
  81.9 8.1 %collective-permute-start.17 = (f32[136,256]{1,0:T(8,128)S(1)}, f32[136,256]{1,0:T(8,128)S(1)}, u32[]{:S(2)}, u32[]{:S(2)}) collective-permute-start(f32[136,256]{1,0:T(8,128)S(1)} %pad_maximum_fusion), channel_id=1, source_target_pairs={{0,1},{1,0},{2,3},{3,2},{4,5},{5,4},{6,7},{7,6},{8,9},{9,8},{10,11... | collective-permute-start | bytes 417800 | tf_op jit(solution)/shard_map/ppermute | solution.py:60
  87.8 0.8 copy-start.13
  88.6 13.1 %collective-permute-start.13 = (bf16[8,256,128]{2,1,0:T(8,128)(2,1)S(1)}, bf16[8,256,128]{2,1,0:T(8,128)(2,1)S(1)}, u32[]{:S(2)}, u32[]{:S(2)}) collective-permute-start(bf16[8,256,128]{2,1,0:T(8,128)(2,1)S(1)} %get-tuple-element.25), channel_id=1, source_target_pairs={{0,8},{1,9},{2,10},{3,11},{4,12},{5,13},{6,14},{7,15},{8,0},{9,1},... | collective-permute-start | bytes 1572872 | tf_op jit(solution)/shard_map/ppermute | solution.py:60
  90.1 15.6 %collective-permute-start.16 = (bf16[8,256,128]{2,1,0:T(8,128)(2,1)}, bf16[8,256,128]{2,1,0:T(8,128)(2,1)S(1)}, u32[]{:S(2)}, u32[]{:S(2)}) collective-permute-start(bf16[8,256,128]{2,1,0:T(8,128)(2,1)} %get-tuple-element.26), channel_id=1, source_target_pairs={{0,4},{1,5},{2,6},{3,7},{4,0},{5,1},{6,2},{7,3},{8,12},{9,13},{10,... | collective-permute-start | bytes 1572872 | tf_op jit(solution)/shard_map/ppermute | solution.py:60
  91.8 13.9 %all-to-all-start = ((bf16[32,6,256]{2,1,0:T(8,128)(2,1)}), bf16[32,6,256]{2,1,0:T(8,128)(2,1)S(1)}, u32[]{:S(2)}, u32[]{:S(2)}) async-start(bf16[32,6,256]{2,1,0:T(8,128)(2,1)} %pad_maximum_fusion.2), calls=%async_computation | async-start | bytes 262144 | tf_op jit(solution)/shard_map/all_to_all | solution.py:385
  95.9 24.1 %collective-permute-start.12 = (bf16[8,256,128]{2,1,0:T(8,128)(2,1)}, bf16[8,256,128]{2,1,0:T(8,128)(2,1)S(1)}, u32[]{:S(2)}, u32[]{:S(2)}) collective-permute-start(bf16[8,256,128]{2,1,0:T(8,128)(2,1)} %get-tuple-element.24), channel_id=1, source_target_pairs={{0,8},{1,9},{2,10},{3,11},{4,12},{5,13},{6,14},{7,15},{8,0},{9,1},... | collective-permute-start | bytes 1572872 | tf_op jit(solution)/shard_map/ppermute | solution.py:60
  104.9 15.2 %collective-permute-start.14 = (bf16[8,256,128]{2,1,0:T(8,128)(2,1)}, bf16[8,256,128]{2,1,0:T(8,128)(2,1)S(1)}, u32[]{:S(2)}, u32[]{:S(2)}) collective-permute-start(bf16[8,256,128]{2,1,0:T(8,128)(2,1)} %backward_product.6), channel_id=1, source_target_pairs={{0,4},{1,5},{2,6},{3,7},{4,0},{5,1},{6,2},{7,3},{8,12},{9,13},{10,... | collective-permute-start | bytes 1572872 | tf_op jit(solution)/shard_map/ppermute | solution.py:60
  108.1 17.9 %collective-permute-start.18 = (bf16[8,256,128]{2,1,0:T(8,128)(2,1)S(1)}, bf16[8,256,128]{2,1,0:T(8,128)(2,1)}, u32[]{:S(2)}, u32[]{:S(2)}) collective-permute-start(bf16[8,256,128]{2,1,0:T(8,128)(2,1)S(1)} %backward_product.8), channel_id=1, source_target_pairs={{0,104},{1,105},{2,106},{3,107},{4,108},{5,109},{6,110},{7,111},{8... | collective-permute-start | bytes 1572872 | tf_op jit(solution)/shard_map/ppermute | solution.py:60
  109.7 22.9 %all-to-all-start.1 = ((f32[32,4,256]{2,1,0:T(4,128)}), f32[32,4,256]{2,1,0:T(4,128)S(1)}, u32[]{:S(2)}, u32[]{:S(2)}) async-start(f32[32,4,256]{2,1,0:T(4,128)} %broadcast_in_dim.14), calls=%async_computation.1 | async-start | bytes 262144 | tf_op jit(solution)/shard_map/all_to_all | solution.py:393
  114.5 26.9 %collective-permute-start.11 = (bf16[8,256,128]{2,1,0:T(8,128)(2,1)}, bf16[8,256,128]{2,1,0:T(8,128)(2,1)S(1)}, u32[]{:S(2)}, u32[]{:S(2)}) collective-permute-start(bf16[8,256,128]{2,1,0:T(8,128)(2,1)} %copy-done.13), channel_id=1, source_target_pairs={{0,100},{1,71},{2,38},{3,5},{4,0},{5,99},{6,66},{7,33},{8,108},{9,... | collective-permute-start | bytes 1572872 | tf_op jit(solution)/shard_map/ppermute | solution.py:60
  122.4 19.1 %collective-permute-start.15 = (bf16[8,256,128]{2,1,0:T(8,128)(2,1)S(1)}, bf16[8,256,128]{2,1,0:T(8,128)(2,1)S(1)}, u32[]{:S(2)}, u32[]{:S(2)}) collective-permute-start(bf16[8,256,128]{2,1,0:T(8,128)(2,1)S(1)} %backward_product.7), channel_id=1, source_target_pairs={{0,120},{1,89},{2,58},{3,27},{4,124},{5,93},{6,62},{7,31},{8,112},... | collective-permute-start | bytes 1572872 | tf_op jit(solution)/shard_map/ppermute | solution.py:60
  129.4 15.5 %collective-permute-start.19 = (bf16[8,256,128]{2,1,0:T(8,128)(2,1)S(1)}, bf16[8,256,128]{2,1,0:T(8,128)(2,1)S(1)}, u32[]{:S(2)}, u32[]{:S(2)}) collective-permute-start(bf16[8,256,128]{2,1,0:T(8,128)(2,1)S(1)} %backward_product.9), channel_id=1, source_target_pairs={{0,0},{1,97},{2,66},{3,35},{4,4},{5,101},{6,70},{7,39},{8,8},{9,10... | collective-permute-start | bytes 1572872 | tf_op jit(solution)/shard_map/ppermute | solution.py:60
  132.6 6.0 %collective-permute-start.22 = (f32[128,256]{1,0:T(8,128)S(1)}, f32[128,256]{1,0:T(8,128)S(1)}, u32[]{:S(2)}, u32[]{:S(2)}) collective-permute-start(f32[128,256]{1,0:T(8,128)S(1)} %reshape.60), channel_id=1, source_target_pairs={{0,2},{1,3},{2,0},{3,1},{4,6},{5,7},{6,4},{7,5},{8,10},{9,11},{10,... | collective-permute-start | bytes 393224 | tf_op jit(solution)/shard_map/ppermute | solution.py:60
  139.4 5.8 %collective-permute-start.23 = (f32[2,128,256]{2,1,0:T(8,128)}, f32[2,128,256]{2,1,0:T(8,128)S(1)}, u32[]{:S(2)}, u32[]{:S(2)}) collective-permute-start(f32[2,128,256]{2,1,0:T(8,128)} %maximum_select_fusion), channel_id=1, source_target_pairs={{0,1},{1,0},{2,3},{3,2},{4,5},{5,4},{6,7},{7,6},{8,9},{9,8},{10,11... | collective-permute-start | bytes 786440 | tf_op jit(solution)/shard_map/ppermute | solution.py:60
  145.0 1.6 collective-permute-start.20
  146.7 14.9 %collective-permute-start.21 = (bf16[2,256,128]{2,1,0:T(8,128)(2,1)S(1)}, bf16[2,256,128]{2,1,0:T(8,128)(2,1)S(1)}, u32[]{:S(2)}, u32[]{:S(2)}) collective-permute-start(bf16[2,256,128]{2,1,0:T(8,128)(2,1)S(1)} %get-tuple-element.31), channel_id=1, source_target_pairs={{0,2},{1,3},{2,0},{3,1},{4,6},{5,7},{6,4},{7,5},{8,10},{9,11},{10,... | collective-permute-start | bytes 393224 | tf_op jit(solution)/shard_map/ppermute | solution.py:60

commit v9 on v8

--- a/solution.py
+++ b/solution.py
@@ -23,6 +23,7 @@
 HELD = ((6, (1,)), (3, (2, 0)))
 BACK = ((5, 3, 4, 1), (7,), (2,), (6,), (0,))
 LATER = (2,)
+AFTER = {6: (1,)}
 
 
 def index_of(y, x, zl, zh, core):
@@ -466,7 +467,7 @@
             back_own,
             back_got,
             extra.get(group[0], []),
-            [parts] if group[0] in LATER else [],
+            [parts] if group[0] in LATER else [arrived[k] for k in AFTER.get(group[0], ())],
         )
         for k, product in zip(group, made):
             pairs = column_pairs(k, BACK_PLAN, BACK_CROSS)

time: 164 us -> 163 us (level)
  waiting for transfers between devices: 34.9 us -> 28.8 us
  starting transfers between devices: 64.6 us -> 68.8 us
    ppermute x24, waiting for transfers between devices: 34.9 us -> 28.7 us  [send(): return lax.ppermute(value, AXES, pairs)]
    ppermute x24, starting transfers between devices: 55.7 us -> 58.2 us  [send(): return lax.ppermute(value, AXES, pairs)]
    all_to_all x1, starting transfers between devices: 4.82 us -> 6.54 us  [weight_grads(): half = lax.all_to_all(spread, 'blk', 0, 0).reshape(F // 2, F)]
    unnamed x38 -> x40, local copies, waits for them, and re-layouts: 6.23 us -> 7.27 us
  transfers between devices with their start and end apart: 26 -> 26, of which waited for: 12 -> 13; matrix products, arithmetic and copies ran while one was open for 4% -> 4% of each run, Pallas kernels for 26% -> 26%
where the time goes in v9:
time: 163 us; the launch traced here: 162 us
  starting transfers between devices  68.8 us (42%)
  Pallas kernels  50.7 us (31%)
  waiting for transfers between devices  28.8 us (18%)
  local copies, waits for them, and re-layouts  10 us (6%)
  other arithmetic  2.39 us (1%)
    ppermute x24, starting transfers between devices, send(): return lax.ppermute(value, AXES, pairs)  58.2 us
    ppermute x24, waiting for transfers between devices, send(): return lax.ppermute(value, AXES, pairs)  28.7 us
    pallas_call x1, Pallas kernels, assemble_call(): pl.pallas_call(functools.partial(assemble_body, n), out_shape=jax.ShapeDt...  19.2 us
    pallas_call x5, Pallas kernels, backward_call(): pl.pallas_call(functools.partial(backward_body, tuple(places), added), ou...  16.2 us
    pallas_call x2, Pallas kernels, forward_call(): pl.pallas_call(functools.partial(forward_body, n, start, first, last), ou...  12.8 us
    unnamed x40, local copies, waits for them, and re-layouts  7.27 us
    all_to_all x1, starting transfers between devices, weight_grads(): half = lax.all_to_all(spread, 'blk', 0, 0).reshape(F // 2, F)  6.54 us
    all_to_all x1, starting transfers between devices, weight_shares(): return lax.all_to_all(jnp.concatenate([rows, bias_rows], 1), 'blk', 0, 0)  4.05 us
  transfers between devices with their start and end apart: 26, of which 13 were waited for; matrix products, arithmetic and copies ran while one was open for 4% of the time, Pallas kernels for 26%

profile of v9, /device:TPU:1, one launch (start us, length us, event | category | flops | bytes accessed | tf_op | source)
XLA Modules:
  0.0 161.8 jit_solution(12716025613488184387)
XLA Ops:
  0.6 3.1 %collective-permute-start.5 = (bf16[1024,256]{1,0:T(8,128)(2,1)}, bf16[1024,256]{1,0:T(8,128)(2,1)S(1)}, u32[]{:S(2)}, u32[]{:S(2)}) collective-permute-start(bf16[1024,256]{1,0:T(8,128)(2,1)} %param.10), channel_id=1, source_target_pairs={{104,0},{73,1},{42,2},{11,3},{108,4},{77,5},{46,6},{15,7},{0,8},{9... | collective-permute-start | bytes 1572872 | tf_op jit(solution)/shard_map/ppermute | solution.py:61
  3.8 5.2 %collective-permute-start.4 = (bf16[1024,256]{1,0:T(8,128)(2,1)}, bf16[1024,256]{1,0:T(8,128)(2,1)S(1)}, u32[]{:S(2)}, u32[]{:S(2)}) collective-permute-start(bf16[1024,256]{1,0:T(8,128)(2,1)} %param.10), channel_id=1, source_target_pairs={{110,0},{79,1},{44,2},{13,3},{106,4},{73,5},{40,6},{11,7},{4,8},{1... | collective-permute-start | bytes 1572872 | tf_op jit(solution)/shard_map/ppermute | solution.py:61
  8.9 1.9 %collective-permute-start.6 = (bf16[1024,256]{1,0:T(8,128)(2,1)}, bf16[1024,256]{1,0:T(8,128)(2,1)S(1)}, u32[]{:S(2)}, u32[]{:S(2)}) collective-permute-start(bf16[1024,256]{1,0:T(8,128)(2,1)} %param.10), channel_id=1, source_target_pairs={{0,0},{97,1},{66,2},{35,3},{4,4},{101,5},{70,6},{39,7},{8,8},{105,... | collective-permute-start | bytes 1572872 | tf_op jit(solution)/shard_map/ppermute | solution.py:61
  10.8 1.3 collective-permute-start.1
  12.1 2.7 %collective-permute-start = (bf16[1024,256]{1,0:T(8,128)(2,1)}, bf16[1024,256]{1,0:T(8,128)(2,1)S(1)}, u32[]{:S(2)}, u32[]{:S(2)}) collective-permute-start(bf16[1024,256]{1,0:T(8,128)(2,1)} %param.10), channel_id=1, source_target_pairs={{120,0},{89,1},{58,2},{27,3},{124,4},{93,5},{62,6},{31,7},{112,8},... | collective-permute-start | bytes 1572872 | tf_op jit(solution)/shard_map/ppermute | solution.py:61
  14.9 0.8 reshape.52.counts_ref
  15.6 0.9 copy.22
  16.5 0.1 reshape.51.cols_ref
  16.7 0.1 stack.42.sel_ref
  16.8 19.2 %assemble_adjacency.1.refs_1_.adj_ref = bf16[8,8,1024,128]{3,2,1,0:T(8,128)(2,1)} custom-call(s32[8]{0:T(128)S(1)} %stack.42.sel_ref, s32[384]{0:T(512)S(1)} %reshape.51.cols_ref, s32[64]{0:T(128)S(1)} %reshape.52.counts_ref, bf16[8,8,6,128,128]{4,3,2,1,0:T(8,128)(2,1)} %tiles_ref.1), custom_call_target="tpu_custom_call" | custom-call | flops 4294967296 | bytes 25165824 | tf_op jit(solution)/shard_map/assemble_adjacency/pallas_call | solution.py:118
  36.0 4.2 %collective-permute-done.6.refs_3_.refs_4_ = bf16[1024,256]{1,0:T(8,128)(2,1)S(1)} collective-permute-done((bf16[1024,256]{1,0:T(8,128)(2,1)}, bf16[1024,256]{1,0:T(8,128)(2,1)S(1)}, u32[]{:S(2)}, u32[]{:S(2)}) %collective-permute-start.6) | collective-permute-done | bytes 524320 | tf_op jit(solution)/shard_map/ppermute | solution.py:61
  40.3 0.8 copy-done.6
  41.1 0.7 collective-permute-done.1.refs_2_
  41.7 0.8 copy-done.8
  42.5 0.8 copy-done.2
  43.3 1.0 collective-permute-start.2
  44.4 1.1 copy-done.3
  45.4 1.0 copy-done.9
  46.5 7.0 %forward_product.2.refs_3_ = f32[1024,256]{1,0:T(8,128)S(1)} custom-call(s32[1]{0:T(128)} %bitcast.1.core_ref, bf16[8,8,1024,128]{3,2,1,0:T(8,128)(2,1)} %assemble_adjacency.1.refs_1_.adj_ref, bf16[1024,256]{1,0:T(8,128)(2,1)S(1)} %copy-done.3, bf16[1024,256]{1,0:T(8,128)(2,1)S(1)} %copy-done.1, bf16[1024,256]{1,0:T(8,128)(2,1)S(1)} %copy-done.9, ...), custom_call_target="tpu_custom_call" | custom-call | flops 2684354560 | bytes 15728640 | tf_op jit(solution)/shard_map/forward_product/pallas_call | solution.py:187
  53.5 4.3 %collective-permute-done.7.refs_2_ = bf16[1024,256]{1,0:T(8,128)(2,1)S(1)} collective-permute-done((bf16[1024,256]{1,0:T(8,128)(2,1)}, bf16[1024,256]{1,0:T(8,128)(2,1)S(1)}, u32[]{:S(2)}, u32[]{:S(2)}) %collective-permute-start.7) | collective-permute-done | bytes 524320 | tf_op jit(solution)/shard_map/ppermute | solution.py:61
  57.8 5.8 %forward_product.3 = (f32[2,256,256]{2,1,0:T(8,128)S(1)}, bf16[2,256,256]{2,1,0:T(8,128)(2,1)S(1)}) custom-call(s32[1]{0:T(128)} %bitcast.1.core_ref, bf16[8,8,1024,128]{3,2,1,0:T(8,128)(2,1)} %assemble_adjacency.1.refs_1_.adj_ref, bf16[1024,256]{1,0:T(8,128)(2,1)} %collective-permute-done.2.refs_0_, bf16[1024,256]{1,0:T(8,128)(2,1)S(1)} %collective-permute-done.3.refs_1_, ...), custom_call_target="tpu_custom_call" | custom-call | flops 1610612736 | bytes 9437184 | tf_op jit(solution)/shard_map/forward_product/pallas_call | solution.py:187
  63.6 0.4 collective-permute-start.8
  64.1 1.1 collective-permute-done.8
  65.3 7.7 %collective-permute-start.9 = (bf16[2,256,256]{2,1,0:T(8,128)(2,1)S(1)}, bf16[2,256,256]{2,1,0:T(8,128)(2,1)S(1)}, u32[]{:S(2)}, u32[]{:S(2)}) collective-permute-start(bf16[2,256,256]{2,1,0:T(8,128)(2,1)S(1)} %add_convert_fusion.own_ref), channel_id=1, source_target_pairs={{0,2},{1,3},{2,0},{3,1},{4,6},{5,7},{6,4},{7,5},{8,10},{9,11},{10,... | collective-permute-start | bytes 786440 | tf_op jit(solution)/shard_map/ppermute | solution.py:61
  73.0 0.1 bitcast_multiply_fusion.cot_ref
  73.2 6.2 %collective-permute-done.9.got_ref = bf16[2,256,256]{2,1,0:T(8,128)(2,1)S(1)} collective-permute-done((bf16[2,256,256]{2,1,0:T(8,128)(2,1)S(1)}, bf16[2,256,256]{2,1,0:T(8,128)(2,1)S(1)}, u32[]{:S(2)}, u32[]{:S(2)}) %collective-permute-start.9) | collective-permute-done | bytes 262176 | tf_op jit(solution)/shard_map/ppermute | solution.py:61
  79.4 1.6 dense_rows.1
  81.0 0.9 collective-permute-start.10
  81.9 0.3 collective-permute-start.17
  82.2 0.8 collective-permute-done.10.got_ref
  83.0 5.3 %backward_product.5 = (bf16[8,256,128]{2,1,0:T(8,128)(2,1)S(1)}, bf16[8,256,128]{2,1,0:T(8,128)(2,1)}, bf16[8,256,128]{2,1,0:T(8,128)(2,1)}, bf16[8,256,128]{2,1,0:T(8,128)(2,1)}) custom-call(s32[1]{0:T(128)} %bitcast.1.core_ref, bf16[8,8,1024,128]{3,2,1,0:T(8,128)(2,1)} %assemble_adjacency.1.refs_1_.adj_ref, ...), custom_call_target="tpu_custom_call" | custom-call | flops 2147483648 | bytes 12582912 | tf_op jit(solution)/shard_map/backward_product/pallas_call | solution.py:278
  88.3 1.5 collective-permute-start.13
  89.9 0.9 collective-permute-start.16
  90.9 0.7 pad_maximum_fusion.2
  91.6 4.1 %all-to-all-start = ((bf16[32,6,256]{2,1,0:T(8,128)(2,1)}), bf16[32,6,256]{2,1,0:T(8,128)(2,1)S(1)}, u32[]{:S(2)}, u32[]{:S(2)}) async-start(bf16[32,6,256]{2,1,0:T(8,128)(2,1)} %pad_maximum_fusion.2), calls=%async_computation | async-start | bytes 262144 | tf_op jit(solution)/shard_map/all_to_all | solution.py:386
  95.7 5.9 %collective-permute-start.11 = (bf16[8,256,128]{2,1,0:T(8,128)(2,1)}, bf16[8,256,128]{2,1,0:T(8,128)(2,1)S(1)}, u32[]{:S(2)}, u32[]{:S(2)}) collective-permute-start(bf16[8,256,128]{2,1,0:T(8,128)(2,1)} %get-tuple-element.23), channel_id=1, source_target_pairs={{0,100},{1,71},{2,38},{3,5},{4,0},{5,99},{6,66},{7,33},{8,108},{9,... | collective-permute-start | bytes 1572872 | tf_op jit(solution)/shard_map/ppermute | solution.py:61
  101.6 1.2 collective-permute-start.12
  102.8 3.1 %backward_product.6 = bf16[8,256,128]{2,1,0:T(8,128)(2,1)} custom-call(s32[1]{0:T(128)} %bitcast.1.core_ref, bf16[8,8,1024,128]{3,2,1,0:T(8,128)(2,1)} %assemble_adjacency.1.refs_1_.adj_ref, bf16[2,256,256]{2,1,0:T(8,128)(2,1)S(1)} %get-tuple-element.22.own_ref, bf16[2,256,256]{2,1,0:T(8,128)(2,1)S(1)} %collective-permute-done.10.got_ref, ...), custom_call_target="tpu_custom_call" | custom-call | flops 536870912 | bytes 3145728 | tf_op jit(solution)/shard_map/backward_product/pallas_call | solution.py:278
  106.0 0.1 all-to-all-done.rest_1_
  106.1 3.1 %backward_product.8 = bf16[8,256,128]{2,1,0:T(8,128)(2,1)} custom-call(s32[1]{0:T(128)} %bitcast.1.core_ref, bf16[8,8,1024,128]{3,2,1,0:T(8,128)(2,1)} %assemble_adjacency.1.refs_1_.adj_ref, bf16[2,256,256]{2,1,0:T(8,128)(2,1)S(1)} %get-tuple-element.22.own_ref, bf16[2,256,256]{2,1,0:T(8,128)(2,1)S(1)} %collective-permute-done.10.got_ref, ...), custom_call_target="tpu_custom_call" | custom-call | flops 536870912 | bytes 3145728 | tf_op jit(solution)/shard_map/backward_product/pallas_call | solution.py:278
  109.2 0.8 collective-permute-start.18
  110.1 0.7 broadcast_in_dim.14
  110.7 6.5 %all-to-all-start.1 = ((f32[32,4,256]{2,1,0:T(4,128)}), f32[32,4,256]{2,1,0:T(4,128)S(1)}, u32[]{:S(2)}, u32[]{:S(2)}) async-start(f32[32,4,256]{2,1,0:T(4,128)} %broadcast_in_dim.14), calls=%async_computation.1 | async-start | bytes 262144 | tf_op jit(solution)/shard_map/all_to_all | solution.py:394
  117.3 2.9 %collective-permute-done.14.rest_1_ = bf16[8,256,128]{2,1,0:T(8,128)(2,1)S(1)} collective-permute-done((bf16[8,256,128]{2,1,0:T(8,128)(2,1)}, bf16[8,256,128]{2,1,0:T(8,128)(2,1)S(1)}, u32[]{:S(2)}, u32[]{:S(2)}) %collective-permute-start.14) | collective-permute-done | bytes 524320 | tf_op jit(solution)/shard_map/ppermute | solution.py:61
  120.2 2.3 %backward_product.7 = bf16[8,256,128]{2,1,0:T(8,128)(2,1)S(1)} custom-call(s32[1]{0:T(128)} %bitcast.1.core_ref, bf16[8,8,1024,128]{3,2,1,0:T(8,128)(2,1)} %assemble_adjacency.1.refs_1_.adj_ref, bf16[2,256,256]{2,1,0:T(8,128)(2,1)S(1)} %get-tuple-element.22.own_ref, bf16[2,256,256]{2,1,0:T(8,128)(2,1)S(1)} %collective-permute-done.10.got_ref, ...), custom_call_target="tpu_custom_call" | custom-call | flops 536870912 | bytes 3145728 | tf_op jit(solution)/shard_map/backward_product/pallas_call | solution.py:278
  122.5 3.4 %collective-permute-start.15 = (bf16[8,256,128]{2,1,0:T(8,128)(2,1)S(1)}, bf16[8,256,128]{2,1,0:T(8,128)(2,1)S(1)}, u32[]{:S(2)}, u32[]{:S(2)}) collective-permute-start(bf16[8,256,128]{2,1,0:T(8,128)(2,1)S(1)} %backward_product.7), channel_id=1, source_target_pairs={{0,120},{1,89},{2,58},{3,27},{4,124},{5,93},{6,62},{7,31},{8,112},... | collective-permute-start | bytes 1572872 | tf_op jit(solution)/shard_map/ppermute | solution.py:61
  125.9 0.1 collective-permute-done.18.rest_0_
  126.1 0.8 copy-done.10
  126.9 1.0 copy-done.11
  127.9 2.3 %backward_product.9 = bf16[8,256,128]{2,1,0:T(8,128)(2,1)S(1)} custom-call(s32[1]{0:T(128)} %bitcast.1.core_ref, bf16[8,8,1024,128]{3,2,1,0:T(8,128)(2,1)} %assemble_adjacency.1.refs_1_.adj_ref, bf16[2,256,256]{2,1,0:T(8,128)(2,1)S(1)} %get-tuple-element.22.own_ref, bf16[2,256,256]{2,1,0:T(8,128)(2,1)S(1)} %collective-permute-done.10.got_ref, ...), custom_call_target="tpu_custom_call" | custom-call | flops 536870912 | bytes 3145728 | tf_op jit(solution)/shard_map/backward_product/pallas_call | solution.py:278
  130.2 3.6 %collective-permute-start.19 = (bf16[8,256,128]{2,1,0:T(8,128)(2,1)S(1)}, bf16[8,256,128]{2,1,0:T(8,128)(2,1)S(1)}, u32[]{:S(2)}, u32[]{:S(2)}) collective-permute-start(bf16[8,256,128]{2,1,0:T(8,128)(2,1)S(1)} %backward_product.9), channel_id=1, source_target_pairs={{0,0},{1,97},{2,66},{3,35},{4,4},{5,101},{6,70},{7,39},{8,8},{9,10... | collective-permute-start | bytes 1572872 | tf_op jit(solution)/shard_map/ppermute | solution.py:61
  133.8 1.2 collective-permute-start.22
  135.1 4.2 %collective-permute-done.22 = f32[128,256]{1,0:T(8,128)S(1)} collective-permute-done((f32[128,256]{1,0:T(8,128)S(1)}, f32[128,256]{1,0:T(8,128)S(1)}, u32[]{:S(2)}, u32[]{:S(2)}) %collective-permute-start.22) | collective-permute-done | bytes 131104 | tf_op jit(solution)/shard_map/ppermute | solution.py:61
  139.2 0.7 maximum_select_fusion
  140.0 3.7 %collective-permute-start.23 = (f32[2,128,256]{2,1,0:T(8,128)}, f32[2,128,256]{2,1,0:T(8,128)S(1)}, u32[]{:S(2)}, u32[]{:S(2)}) collective-permute-start(f32[2,128,256]{2,1,0:T(8,128)} %maximum_select_fusion), channel_id=1, source_target_pairs={{0,1},{1,0},{2,3},{3,2},{4,5},{5,4},{6,7},{7,6},{8,9},{9,8},{10,11... | collective-permute-start | bytes 786440 | tf_op jit(solution)/shard_map/ppermute | solution.py:61
  143.7 0.6 fusion.1
  144.3 0.2 split_products.1
  144.5 0.1 collective-permute-start.20
  144.6 0.5 collective-permute-done.23
  145.2 0.9 collective-permute-done.20.got_ref
  146.1 11.3 %collective-permute-start.21 = (bf16[2,256,128]{2,1,0:T(8,128)(2,1)S(1)}, bf16[2,256,128]{2,1,0:T(8,128)(2,1)S(1)}, u32[]{:S(2)}, u32[]{:S(2)}) collective-permute-start(bf16[2,256,128]{2,1,0:T(8,128)(2,1)S(1)} %get-tuple-element.31), channel_id=1, source_target_pairs={{0,2},{1,3},{2,0},{3,1},{4,6},{5,7},{6,4},{7,5},{8,10},{9,11},{10,... | collective-permute-start | bytes 393224 | tf_op jit(solution)/shard_map/ppermute | solution.py:61
  157.5 0.8 slice_bitcast_fusion
  158.3 2.7 %collective-permute-done.21.got_ref = bf16[2,256,128]{2,1,0:T(8,128)(2,1)S(1)} collective-permute-done((bf16[2,256,128]{2,1,0:T(8,128)(2,1)S(1)}, bf16[2,256,128]{2,1,0:T(8,128)(2,1)S(1)}, u32[]{:S(2)}, u32[]{:S(2)}) %collective-permute-start.21) | collective-permute-done | bytes 131104 | tf_op jit(solution)/shard_map/ppermute | solution.py:61
  161.0 0.8 final_rows.1
  (75 shorter events, 0.7 us)
Async XLA Ops:
  0.6 35.3 %collective-permute-start.5 = (bf16[1024,256]{1,0:T(8,128)(2,1)}, bf16[1024,256]{1,0:T(8,128)(2,1)S(1)}, u32[]{:S(2)}, u32[]{:S(2)}) collective-permute-start(bf16[1024,256]{1,0:T(8,128)(2,1)} %param.10), channel_id=1, source_target_pairs={{104,0},{73,1},{42,2},{11,3},{108,4},{77,5},{46,6},{15,7},{0,8},{9... | collective-permute-start | bytes 1572872 | tf_op jit(solution)/shard_map/ppermute | solution.py:61
  3.8 32.2 %collective-permute-start.4 = (bf16[1024,256]{1,0:T(8,128)(2,1)}, bf16[1024,256]{1,0:T(8,128)(2,1)S(1)}, u32[]{:S(2)}, u32[]{:S(2)}) collective-permute-start(bf16[1024,256]{1,0:T(8,128)(2,1)} %param.10), channel_id=1, source_target_pairs={{110,0},{79,1},{44,2},{13,3},{106,4},{73,5},{40,6},{11,7},{4,8},{1... | collective-permute-start | bytes 1572872 | tf_op jit(solution)/shard_map/ppermute | solution.py:61
  8.9 31.3 %collective-permute-start.6 = (bf16[1024,256]{1,0:T(8,128)(2,1)}, bf16[1024,256]{1,0:T(8,128)(2,1)S(1)}, u32[]{:S(2)}, u32[]{:S(2)}) collective-permute-start(bf16[1024,256]{1,0:T(8,128)(2,1)} %param.10), channel_id=1, source_target_pairs={{0,0},{97,1},{66,2},{35,3},{4,4},{101,5},{70,6},{39,7},{8,8},{105,... | collective-permute-start | bytes 1572872 | tf_op jit(solution)/shard_map/ppermute | solution.py:61
  10.8 30.9 %collective-permute-start.1 = (bf16[1024,256]{1,0:T(8,128)(2,1)}, bf16[1024,256]{1,0:T(8,128)(2,1)S(1)}, u32[]{:S(2)}, u32[]{:S(2)}) collective-permute-start(bf16[1024,256]{1,0:T(8,128)(2,1)} %param.10), channel_id=1, source_target_pairs={{102,0},{69,1},{36,2},{7,3},{0,4},{99,5},{66,6},{33,7},{110,8},{77... | collective-permute-start | bytes 1572872 | tf_op jit(solution)/shard_map/ppermute | solution.py:61
  12.1 29.6 %collective-permute-start = (bf16[1024,256]{1,0:T(8,128)(2,1)}, bf16[1024,256]{1,0:T(8,128)(2,1)S(1)}, u32[]{:S(2)}, u32[]{:S(2)}) collective-permute-start(bf16[1024,256]{1,0:T(8,128)(2,1)} %param.10), channel_id=1, source_target_pairs={{120,0},{89,1},{58,2},{27,3},{124,4},{93,5},{62,6},{31,7},{112,8},... | collective-permute-start | bytes 1572872 | tf_op jit(solution)/shard_map/ppermute | solution.py:61
  36.0 4.3 %copy-start.4 = (bf16[1024,256]{1,0:T(8,128)(2,1)}, bf16[1024,256]{1,0:T(8,128)(2,1)S(1)}, u32[]{:S(2)}) copy-start(bf16[1024,256]{1,0:T(8,128)(2,1)S(1)} %collective-permute-done.5.refs_2_.refs_3_) | copy-start | bytes 1572868
  36.0 4.2 %copy-start = (bf16[1024,256]{1,0:T(8,128)(2,1)}, bf16[1024,256]{1,0:T(8,128)(2,1)S(1)}, u32[]{:S(2)}) copy-start(bf16[1024,256]{1,0:T(8,128)(2,1)S(1)} %collective-permute-done.4.refs_0_) | copy-start | bytes 1572868
  40.2 0.8 copy-start.6
  41.1 3.3 %copy-start.1 = (bf16[1024,256]{1,0:T(8,128)(2,1)S(1)}, bf16[1024,256]{1,0:T(8,128)(2,1)}, u32[]{:S(2)}) copy-start(bf16[1024,256]{1,0:T(8,128)(2,1)} %hold.3.refs_1_.refs_6_) | copy-start | bytes 1572868
  41.1 3.3 %copy-start.5 = (bf16[1024,256]{1,0:T(8,128)(2,1)S(1)}, bf16[1024,256]{1,0:T(8,128)(2,1)}, u32[]{:S(2)}) copy-start(bf16[1024,256]{1,0:T(8,128)(2,1)} %copy-done.4) | copy-start | bytes 1572868
  41.1 3.3 %copy-start.7 = (bf16[1024,256]{1,0:T(8,128)(2,1)S(1)}, bf16[1024,256]{1,0:T(8,128)(2,1)}, u32[]{:S(2)}) copy-start(bf16[1024,256]{1,0:T(8,128)(2,1)} %copy-done.6) | copy-start | bytes 1572868
  41.1 16.7 %collective-permute-start.7 = (bf16[1024,256]{1,0:T(8,128)(2,1)}, bf16[1024,256]{1,0:T(8,128)(2,1)S(1)}, u32[]{:S(2)}, u32[]{:S(2)}) collective-permute-start(bf16[1024,256]{1,0:T(8,128)(2,1)} %hold.3.refs_1_.refs_6_), channel_id=1, source_target_pairs={{120,0},{121,1},{122,2},{123,3},{124,4},{125,5},{126,6},{127,7},{1... | collective-permute-start | bytes 1572872 | tf_op jit(solution)/shard_map/ppermute | solution.py:61
  41.7 0.8 copy-start.8
  42.5 0.8 copy-start.2
  43.3 14.4 %collective-permute-start.3 = (bf16[1024,256]{1,0:T(8,128)(2,1)}, bf16[1024,256]{1,0:T(8,128)(2,1)S(1)}, u32[]{:S(2)}, u32[]{:S(2)}) collective-permute-start(bf16[1024,256]{1,0:T(8,128)(2,1)} %hold.2.refs_0_.refs_5_), channel_id=1, source_target_pairs={{8,0},{9,1},{10,2},{11,3},{12,4},{13,5},{14,6},{15,7},{0,8},{1,9},... | collective-permute-start | bytes 1572872 | tf_op jit(solution)/shard_map/ppermute | solution.py:61
  43.3 14.4 %collective-permute-start.2 = (bf16[1024,256]{1,0:T(8,128)(2,1)}, bf16[1024,256]{1,0:T(8,128)(2,1)}, u32[]{:S(2)}, u32[]{:S(2)}) collective-permute-start(bf16[1024,256]{1,0:T(8,128)(2,1)} %hold.2.refs_0_.refs_5_), channel_id=1, source_target_pairs={{4,0},{5,1},{6,2},{7,3},{0,4},{1,5},{2,6},{3,7},{12,8},{13,9},{14,... | collective-permute-start | bytes 1572872 | tf_op jit(solution)/shard_map/ppermute | solution.py:61
  44.4 1.1 copy-start.3
  45.4 1.0 copy-start.9
  46.5 17.5 %copy-start.17 = (s32[1024]{0:T(1024)S(1)}, s32[1024]{0:T(1024)}, u32[]{:S(2)}) copy-start(s32[1024]{0:T(1024)} %param.14) | copy-start | bytes 12292
  46.5 17.5 %copy-start.18 = (s32[1024]{0:T(1024)S(1)}, s32[1024]{0:T(1024)}, u32[]{:S(2)}) copy-start(s32[1024]{0:T(1024)} %param.15) | copy-start | bytes 12292
  46.5 32.9 %copy-start.12 = (bf16[256,256]{1,0:T(8,128)(2,1)S(1)}, bf16[256,256]{1,0:T(8,128)(2,1)}, u32[]{:S(2)}) copy-start(bf16[256,256]{1,0:T(8,128)(2,1)} %ws_ref.1) | copy-start | bytes 393220
  46.5 32.9 %copy-start.14 = (f32[256]{0:T(256)S(1)}, f32[256]{0:T(256)}, u32[]{:S(2)}) copy-start(f32[256]{0:T(256)} %param.19) | copy-start | bytes 3076
  53.5 10.6 %copy-start.15 = (bf16[1024,256]{1,0:T(8,128)(2,1)S(1)}, bf16[1024,256]{1,0:T(8,128)(2,1)}, u32[]{:S(2)}) copy-start(bf16[1024,256]{1,0:T(8,128)(2,1)} %param.10) | copy-start | bytes 1572868
  53.5 19.6 %copy-start.16 = (bf16[1024,256]{1,0:T(8,128)(2,1)S(1)}, bf16[1024,256]{1,0:T(8,128)(2,1)}, u32[]{:S(2)}) copy-start(bf16[1024,256]{1,0:T(8,128)(2,1)} %param.16) | copy-start | bytes 1572868
  53.5 25.9 %copy-start.13 = (bf16[256,256]{1,0:T(8,128)(2,1)S(1)}, bf16[256,256]{1,0:T(8,128)(2,1)}, u32[]{:S(2)}) copy-start(bf16[256,256]{1,0:T(8,128)(2,1)} %wn_ref.1) | copy-start | bytes 393220
  63.6 1.6 collective-permute-start.8
  65.3 14.1 %collective-permute-start.9 = (bf16[2,256,256]{2,1,0:T(8,128)(2,1)S(1)}, bf16[2,256,256]{2,1,0:T(8,128)(2,1)S(1)}, u32[]{:S(2)}, u32[]{:S(2)}) collective-permute-start(bf16[2,256,256]{2,1,0:T(8,128)(2,1)S(1)} %add_convert_fusion.own_ref), channel_id=1, source_target_pairs={{0,2},{1,3},{2,0},{3,1},{4,6},{5,7},{6,4},{7,5},{8,10},{9,11},{10,... | collective-permute-start | bytes 786440 | tf_op jit(solution)/shard_map/ppermute | solution.py:61
  81.0 2.0 %collective-permute-start.10 = (bf16[2,256,256]{2,1,0:T(8,128)(2,1)S(1)}, bf16[2,256,256]{2,1,0:T(8,128)(2,1)S(1)}, u32[]{:S(2)}, u32[]{:S(2)}) collective-permute-start(bf16[2,256,256]{2,1,0:T(8,128)(2,1)S(1)} %get-tuple-element.22.own_ref), channel_id=1, source_target_pairs={{0,1},{1,0},{2,3},{3,2},{4,5},{5,4},{6,7},{7,6},{8,9},{9,8},{10,11... | collective-permute-start | bytes 786440 | tf_op jit(solution)/shard_map/ppermute | solution.py:61
  81.9 7.9 %collective-permute-start.17 = (f32[136,256]{1,0:T(8,128)S(1)}, f32[136,256]{1,0:T(8,128)S(1)}, u32[]{:S(2)}, u32[]{:S(2)}) collective-permute-start(f32[136,256]{1,0:T(8,128)S(1)} %pad_maximum_fusion), channel_id=1, source_target_pairs={{0,1},{1,0},{2,3},{3,2},{4,5},{5,4},{6,7},{7,6},{8,9},{9,8},{10,11... | collective-permute-start | bytes 417800 | tf_op jit(solution)/shard_map/ppermute | solution.py:61
  88.3 14.4 %collective-permute-start.13 = (bf16[8,256,128]{2,1,0:T(8,128)(2,1)S(1)}, bf16[8,256,128]{2,1,0:T(8,128)(2,1)S(1)}, u32[]{:S(2)}, u32[]{:S(2)}) collective-permute-start(bf16[8,256,128]{2,1,0:T(8,128)(2,1)S(1)} %get-tuple-element.25), channel_id=1, source_target_pairs={{0,8},{1,9},{2,10},{3,11},{4,12},{5,13},{6,14},{7,15},{8,0},{9,1},... | collective-permute-start | bytes 1572872 | tf_op jit(solution)/shard_map/ppermute | solution.py:61
  89.9 16.2 %collective-permute-start.16 = (bf16[8,256,128]{2,1,0:T(8,128)(2,1)}, bf16[8,256,128]{2,1,0:T(8,128)(2,1)S(1)}, u32[]{:S(2)}, u32[]{:S(2)}) collective-permute-start(bf16[8,256,128]{2,1,0:T(8,128)(2,1)} %get-tuple-element.26), channel_id=1, source_target_pairs={{0,4},{1,5},{2,6},{3,7},{4,0},{5,1},{6,2},{7,3},{8,12},{9,13},{10,... | collective-permute-start | bytes 1572872 | tf_op jit(solution)/shard_map/ppermute | solution.py:61
  91.6 14.5 %all-to-all-start = ((bf16[32,6,256]{2,1,0:T(8,128)(2,1)}), bf16[32,6,256]{2,1,0:T(8,128)(2,1)S(1)}, u32[]{:S(2)}, u32[]{:S(2)}) async-start(bf16[32,6,256]{2,1,0:T(8,128)(2,1)} %pad_maximum_fusion.2), calls=%async_computation | async-start | bytes 262144 | tf_op jit(solution)/shard_map/all_to_all | solution.py:386
  95.7 21.6 %collective-permute-start.11 = (bf16[8,256,128]{2,1,0:T(8,128)(2,1)}, bf16[8,256,128]{2,1,0:T(8,128)(2,1)S(1)}, u32[]{:S(2)}, u32[]{:S(2)}) collective-permute-start(bf16[8,256,128]{2,1,0:T(8,128)(2,1)} %get-tuple-element.23), channel_id=1, source_target_pairs={{0,100},{1,71},{2,38},{3,5},{4,0},{5,99},{6,66},{7,33},{8,108},{9,... | collective-permute-start | bytes 1572872 | tf_op jit(solution)/shard_map/ppermute | solution.py:61
  101.6 15.7 %collective-permute-start.12 = (bf16[8,256,128]{2,1,0:T(8,128)(2,1)}, bf16[8,256,128]{2,1,0:T(8,128)(2,1)S(1)}, u32[]{:S(2)}, u32[]{:S(2)}) collective-permute-start(bf16[8,256,128]{2,1,0:T(8,128)(2,1)} %get-tuple-element.24), channel_id=1, source_target_pairs={{0,8},{1,9},{2,10},{3,11},{4,12},{5,13},{6,14},{7,15},{8,0},{9,1},... | collective-permute-start | bytes 1572872 | tf_op jit(solution)/shard_map/ppermute | solution.py:61
  105.9 14.3 %collective-permute-start.14 = (bf16[8,256,128]{2,1,0:T(8,128)(2,1)}, bf16[8,256,128]{2,1,0:T(8,128)(2,1)S(1)}, u32[]{:S(2)}, u32[]{:S(2)}) collective-permute-start(bf16[8,256,128]{2,1,0:T(8,128)(2,1)} %backward_product.6), channel_id=1, source_target_pairs={{0,4},{1,5},{2,6},{3,7},{4,0},{5,1},{6,2},{7,3},{8,12},{9,13},{10,... | collective-permute-start | bytes 1572872 | tf_op jit(solution)/shard_map/ppermute | solution.py:61
  109.2 16.9 %collective-permute-start.18 = (bf16[8,256,128]{2,1,0:T(8,128)(2,1)}, bf16[8,256,128]{2,1,0:T(8,128)(2,1)S(1)}, u32[]{:S(2)}, u32[]{:S(2)}) collective-permute-start(bf16[8,256,128]{2,1,0:T(8,128)(2,1)} %backward_product.8), channel_id=1, source_target_pairs={{0,104},{1,105},{2,106},{3,107},{4,108},{5,109},{6,110},{7,111},{8... | collective-permute-start | bytes 1572872 | tf_op jit(solution)/shard_map/ppermute | solution.py:61
  110.7 23.0 %all-to-all-start.1 = ((f32[32,4,256]{2,1,0:T(4,128)}), f32[32,4,256]{2,1,0:T(4,128)S(1)}, u32[]{:S(2)}, u32[]{:S(2)}) async-start(f32[32,4,256]{2,1,0:T(4,128)} %broadcast_in_dim.14), calls=%async_computation.1 | async-start | bytes 262144 | tf_op jit(solution)/shard_map/all_to_all | solution.py:394
  122.5 21.7 %collective-permute-start.15 = (bf16[8,256,128]{2,1,0:T(8,128)(2,1)S(1)}, bf16[8,256,128]{2,1,0:T(8,128)(2,1)S(1)}, u32[]{:S(2)}, u32[]{:S(2)}) collective-permute-start(bf16[8,256,128]{2,1,0:T(8,128)(2,1)S(1)} %backward_product.7), channel_id=1, source_target_pairs={{0,120},{1,89},{2,58},{3,27},{4,124},{5,93},{6,62},{7,31},{8,112},... | collective-permute-start | bytes 1572872 | tf_op jit(solution)/shard_map/ppermute | solution.py:61
  126.1 0.8 copy-start.10
  126.9 1.0 copy-start.11
  130.2 14.1 %collective-permute-start.19 = (bf16[8,256,128]{2,1,0:T(8,128)(2,1)S(1)}, bf16[8,256,128]{2,1,0:T(8,128)(2,1)S(1)}, u32[]{:S(2)}, u32[]{:S(2)}) collective-permute-start(bf16[8,256,128]{2,1,0:T(8,128)(2,1)S(1)} %backward_product.9), channel_id=1, source_target_pairs={{0,0},{1,97},{2,66},{3,35},{4,4},{5,101},{6,70},{7,39},{8,8},{9,10... | collective-permute-start | bytes 1572872 | tf_op jit(solution)/shard_map/ppermute | solution.py:61
  133.8 5.4 %collective-permute-start.22 = (f32[128,256]{1,0:T(8,128)S(1)}, f32[128,256]{1,0:T(8,128)S(1)}, u32[]{:S(2)}, u32[]{:S(2)}) collective-permute-start(f32[128,256]{1,0:T(8,128)S(1)} %reshape.60), channel_id=1, source_target_pairs={{0,2},{1,3},{2,0},{3,1},{4,6},{5,7},{6,4},{7,5},{8,10},{9,11},{10,... | collective-permute-start | bytes 393224 | tf_op jit(solution)/shard_map/ppermute | solution.py:61
  140.0 5.1 %collective-permute-start.23 = (f32[2,128,256]{2,1,0:T(8,128)}, f32[2,128,256]{2,1,0:T(8,128)S(1)}, u32[]{:S(2)}, u32[]{:S(2)}) collective-permute-start(f32[2,128,256]{2,1,0:T(8,128)} %maximum_select_fusion), channel_id=1, source_target_pairs={{0,1},{1,0},{2,3},{3,2},{4,5},{5,4},{6,7},{7,6},{8,9},{9,8},{10,11... | collective-permute-start | bytes 786440 | tf_op jit(solution)/shard_map/ppermute | solution.py:61
  144.5 1.6 collective-permute-start.20
  146.1 14.9 %collective-permute-start.21 = (bf16[2,256,128]{2,1,0:T(8,128)(2,1)S(1)}, bf16[2,256,128]{2,1,0:T(8,128)(2,1)S(1)}, u32[]{:S(2)}, u32[]{:S(2)}) collective-permute-start(bf16[2,256,128]{2,1,0:T(8,128)(2,1)S(1)} %get-tuple-element.31), channel_id=1, source_target_pairs={{0,2},{1,3},{2,0},{3,1},{4,6},{5,7},{6,4},{7,5},{8,10},{9,11},{10,... | collective-permute-start | bytes 393224 | tf_op jit(solution)/shard_map/ppermute | solution.py:61
